TPU v7x, 32 devices: a whole 2x2x4 slice. The times are simulated.
32 devices in a mesh: groups: 2 (over x), wide: 16 (over z, y, core).
Axes of the slice: x: 2, y: 2, z: 4, core: 2. Of those that a mesh axis runs over, the one named last changes fastest.
Arguments:
- cell_index: int32 [3, 65536], P(None, 'wide'), may hold values from 0 to 127, as said below
- station_index: int32 [2, 1024], P(None, 'groups'), parts along dimension 1, may hold values from 0 to 127, as said below
- observed: float32 [5, 1024], P(None, 'groups'), parts along dimension 1, may hold values from -6 to 6
- comp_weight: float32 [5], replicated, may hold values from 0.25 to 4
- counts: int32 [16, 512], P('groups'), parts along dimension 0, may hold values from 0 to 3, as said below
Outputs:
- models: float32 [16, 65536], P('groups', 'wide'), parts along dimension 0
There are 2 independent parts, one for each index of `groups`. A program takes and returns all parts, laid end to end along the dimension named above; an argument that names none is the same for every part. Nothing has to cross between parts.
Inputs may be any that keep to these rules, and one draw needn't show every extreme that they name: `cell_index`: each of the 128 x 32 x 16 grid places holds exactly one cell. Row 0 is below 128, row 1 below 32, row 2 below 16. `station_index`: row 0 is below 128, row 1 below 32. `counts`: bootstrap weights: row b holds how often each station is taken in resample b.
All inputs are finite; a program needn't handle non-finite values.
Results may differ from a plain program's by a relative error of at most 0.006.
Values may be sent and summed in bfloat16 or wider, within the bound.
No kernel may reach another device: no remote copies, remote signals or barrier semaphores. Data moves between devices by JAX's collectives and lax.ppermute only.
A program may use at most 64 MiB of HBM per device.

v0:
```python
import jax
import jax.numpy as jnp
from jax import lax
from jax.sharding import PartitionSpec as P

IRLS = 2
CG_STEPS = 2


station_height = 2.0
focusing = 0.1
damping = 0.0002


def sensitivity(cell_block, station_index):
    cell_x = cell_block[0].astype(jnp.float32) + 0.5
    cell_y = cell_block[1].astype(jnp.float32) + 0.5
    cell_z = cell_block[2].astype(jnp.float32) + 0.5
    station_x = station_index[0].astype(jnp.float32) + 0.5
    station_y = station_index[1].astype(jnp.float32) + 0.5
    delta_x = cell_x[None, :] - station_x[:, None]
    delta_y = cell_y[None, :] - station_y[:, None]
    delta_z = jnp.broadcast_to(cell_z[None, :] + station_height, delta_x.shape)
    radius2 = delta_x * delta_x + delta_y * delta_y + delta_z * delta_z
    strength = 1.0 / (radius2 * radius2 * jnp.sqrt(radius2))
    components = [
        (3.0 * delta_x * delta_x - radius2) * strength,
        3.0 * delta_x * delta_y * strength,
        3.0 * delta_x * delta_z * strength,
        (3.0 * delta_y * delta_y - radius2) * strength,
        3.0 * delta_y * delta_z * strength,
    ]
    return jnp.concatenate(components, axis=0).astype(jnp.bfloat16)


def local(cell_index, station_index, observed, comp_weight, counts):
    bootstrap = counts.shape[0]
    stations = station_index.shape[1]
    cells_here = cell_index.shape[1]
    total_rows = 5 * stations
    sens_tile = sensitivity(cell_index, station_index)
    weights = (counts.astype(jnp.float32)[:, None, :] * comp_weight[None, :, None]).reshape(
        bootstrap, total_rows
    )
    data_rows = observed.reshape(1, total_rows)
    depth_z = cell_index[2].astype(jnp.float32) + 0.5
    depth_weight = (station_height / (depth_z + station_height)) ** 3

    def predict(field):
        field_bf = field.astype(jnp.bfloat16)
        partial_rows = jnp.einsum(
            "bc,rc->br", field_bf, sens_tile, preferred_element_type=jnp.float32
        )
        return lax.psum(partial_rows, "wide")

    def back_project(values_bf):
        return jnp.dot(values_bf, sens_tile, preferred_element_type=jnp.float32)

    models = jnp.zeros((bootstrap, cells_here), jnp.float32)
    for outer_step in range(IRLS):
        penalty = damping * depth_weight[None, :] / (models * models + focusing * focusing)
        if outer_step == 0:
            misfit = weights * data_rows
        else:
            misfit = weights * (data_rows - predict(models))
        residual = back_project(misfit.astype(jnp.bfloat16)) - penalty * models
        direction = residual
        norm_now = lax.psum(jnp.sum(residual * residual, axis=1), "wide")
        for inner_step in range(CG_STEPS):
            image_rows = predict(direction)
            weighted = weights * image_rows
            value = jnp.sum(weighted * image_rows, axis=1)
            cell_part = jnp.sum(penalty * direction * direction, axis=1)
            carried = weighted.astype(jnp.bfloat16)
            curvature = lax.psum(cell_part, "wide") + value
            step_size = norm_now / curvature
            applied = back_project(carried) + penalty * direction
            models = models + step_size[:, None] * direction
            residual = residual - step_size[:, None] * applied
            norm_next = lax.psum(jnp.sum(residual * residual, axis=1), "wide")
            direction = residual + (norm_next / norm_now)[:, None] * direction
            norm_now = norm_next
    return models


def solution(mesh):
    in_specs = (P(None, "wide"), P(None, "groups"), P(None, "groups"), P(), P("groups", None))
    out_specs = P("groups", "wide")
    return jax.shard_map(local, mesh=mesh, in_specs=in_specs, out_specs=out_specs, check_vma=False)
```

profile of v0, /device:TPU:0, one launch (start us, length us, event | category | flops | bytes accessed | tf_op | source)
XLA Modules:
  0.0 631.1 jit_solution(8078778675300478170)
XLA Ops:
  6.5 1.0 fusion.48
  7.6 0.8 convert_add_fusion.4
  8.3 7.0 %fusion.26 = bf16[2560,4096]{1,0:T(8,128)(2,1)} fusion(f32[4096]{0:T(1024)S(1)} %bitcast.30, f32[512]{0:T(512)S(1)} %bitcast.51, f32[4096]{0:T(1024)S(1)} %bitcast.35, f32[512]{0:T(512)S(1)} %bitcast.46, f32[4096]{0:T(1024)S(1)} %bitcast.25), kind=kLoop, calls=%fused_computation.39 | loop fusion | flops 29360128 | bytes 4247552
  15.4 6.8 %fusion.23 = bf16[2560,4096]{1,0:T(8,128)(2,1)} fusion(bf16[2560,4096]{1,0:T(8,128)(2,1)} %fusion.26, f32[512]{0:T(512)S(1)} %bitcast.52, f32[4096]{0:T(1024)S(1)} %bitcast.36, f32[512]{0:T(512)S(1)} %bitcast.47, f32[4096]{0:T(1024)S(1)} %bitcast.26, f32[4096]{0:T(1024)S(1)} %bitcast.31), kind=kLoop, calls=%fused_computation.36 | loop fusion | flops 27262976 | bytes 4247552
  22.2 6.5 %fusion.25 = bf16[2560,4096]{1,0:T(8,128)(2,1)} fusion(bf16[2560,4096]{1,0:T(8,128)(2,1)} %fusion.23, f32[4096]{0:T(1024)S(1)} %bitcast.44, f32[512]{0:T(512)S(1)} %bitcast.48, f32[4096]{0:T(1024)S(1)} %bitcast.27, f32[4096]{0:T(1024)S(1)} %bitcast.32, f32[512]{0:T(512)S(1)} %bitcast.53, f32[4096]{0:T(1024)S(1)} %bitcast.37), kind=kLoop, calls=%fused_computation.38 | loop fusion | flops 25165824 | bytes 4263936
  28.7 7.1 %fusion.24 = bf16[2560,4096]{1,0:T(8,128)(2,1)} fusion(bf16[2560,4096]{1,0:T(8,128)(2,1)} %fusion.25, f32[4096]{0:T(1024)S(1)} %bitcast.33, f32[512]{0:T(512)S(1)} %bitcast.54, f32[4096]{0:T(1024)S(1)} %bitcast.38, f32[512]{0:T(512)S(1)} %bitcast.49, f32[4096]{0:T(1024)S(1)} %bitcast.28), kind=kLoop, calls=%fused_computation.37 | loop fusion | flops 29360128 | bytes 4247552
  35.7 6.5 %fusion.22 = bf16[2560,4096]{1,0:T(8,128)(2,1)} fusion(bf16[2560,4096]{1,0:T(8,128)(2,1)} %fusion.24, f32[4096]{0:T(1024)S(1)} %bitcast.45, f32[512]{0:T(512)S(1)} %bitcast.55, f32[4096]{0:T(1024)S(1)} %bitcast.39, f32[4096]{0:T(1024)S(1)} %bitcast.34, f32[512]{0:T(512)S(1)} %bitcast.50, f32[4096]{0:T(1024)S(1)} %bitcast.29), kind=kLoop, calls=%fused_computation.35 | loop fusion | flops 25165824 | bytes 4263936 | tf_op jit(solution)/shard_map/concatenate | solution.py:33
  42.3 8.6 %fusion.27 = (f32[8]{0:T(128)S(1)}, f32[8]{0:T(128)S(1)}, f32[8,4096]{1,0:T(8,128)S(1)}) fusion(f32[4096]{0:T(1024)S(1)} %get-tuple-element.18, f32[4096]{0:T(1024)S(1)} %get-tuple-element.19, bf16[2560,4096]{1,0:T(8,128)(2,1)} %fusion.22, f32[8,2560]{1,0:T(8,128)S(1)} %bitcast.17, f32[2560]{0:T(1024)S(1)} %mul.245, f32[2560]{0:T(1024)S(1)} %mul.242), kind=kOutput, calls=%fused_computation.43 | convolution fusion | flops 168030208 | bytes 21237824 | tf_op jit(solution)/shard_map/dot_general | solution.py:57
  50.9 10.4 %fusion.40 = f32[8,2560]{1,0:T(8,128)} fusion(bf16[2560,4096]{1,0:T(8,128)(2,1)} %fusion.22, f32[8,4096]{1,0:T(8,128)S(1)} %get-tuple-element.22), kind=kOutput, calls=%fused_computation.74 | convolution fusion | flops 167804928 | bytes 21184512 | tf_op jit(solution)/shard_map/bc,rc->br/dot_general | solution.py:51
  61.4 34.9 %all-reduce.1 = (f32[8]{0:T(128)S(1)}, f32[8]{0:T(128)S(1)}) all-reduce(f32[8]{0:T(128)S(1)} %get-tuple-element.8, f32[8]{0:T(128)S(1)} %get-tuple-element.7), channel_id=1, replica_groups=mesh['groups'=2,'wide'=16] {'wide'}, use_global_device_ids=true, to_apply=%region_1.0 | all-reduce | flops 16 | bytes 128 | tf_op jit(solution)/shard_map/psum | solution.py:68
  96.3 53.1 %all-reduce.8.cloned.1.call-done = f32[8,2560]{1,0:T(8,128)} async-done(((f32[8,2560]{1,0:T(8,128)}), f32[8,2560]{1,0:T(8,128)}) %all-reduce.8.cloned.1.call-update) | async-done | bytes 81936 | tf_op jit(solution)/shard_map/psum | solution.py:54
  149.5 1.0 multiply_reduce_fusion.6
  150.5 8.6 %multiply_reduce_fusion.3 = (f32[8]{0:T(128)S(1)}, f32[8,4096]{1,0:T(8,128)S(1)}) fusion(f32[8,4096]{1,0:T(8,128)S(1)} %get-tuple-element.22, f32[4096]{0:T(1024)S(1)} %get-tuple-element.18, bf16[2560,4096]{1,0:T(8,128)(2,1)} %fusion.22, f32[8,2560]{1,0:T(8,128)} %all-reduce.8.cloned.1.call-done, f32[8,2560]{1,0:T(8,128)S(1)} %bitcast.19, ...), kind=kOutput, calls=%fused_computation.54 | convolution fusion | flops 168030208 | bytes 21424192 | tf_op jit(solution)/shard_map/dot_general | solution.py:57
  159.1 32.4 %psum.94 = f32[8]{0:T(128)S(1)} all-reduce(f32[8]{0:T(128)S(1)} %get-tuple-element.23), channel_id=1, replica_groups=mesh['groups'=2,'wide'=16] {'wide'}, use_global_device_ids=true, to_apply=%region_7.0 | all-reduce | flops 8 | bytes 64 | tf_op jit(solution)/shard_map/psum | solution.py:80
  191.5 10.4 %fusion.38 = f32[8,2560]{1,0:T(8,128)} fusion(bf16[2560,4096]{1,0:T(8,128)(2,1)} %fusion.22, f32[8,4096]{1,0:T(8,128)S(1)} %get-tuple-element.24, f32[8,4096]{1,0:T(8,128)S(1)} %get-tuple-element.22, f32[8]{0:T(128)S(1)} %div.57), kind=kOutput, calls=%fused_computation.72 | convolution fusion | flops 167870464 | bytes 21315616 | tf_op jit(solution)/shard_map/bc,rc->br/dot_general | solution.py:51
  202.2 29.7 %psum.95 = f32[8]{0:T(128)S(1)} all-reduce(f32[8]{0:T(128)S(1)} %fusion.28), channel_id=1, replica_groups=mesh['groups'=2,'wide'=16] {'wide'}, use_global_device_ids=true, to_apply=%region_9.0 | all-reduce | flops 8 | bytes 64 | tf_op jit(solution)/shard_map/psum | solution.py:75
  231.9 52.6 %all-reduce.10.cloned.1.call-done = f32[8,2560]{1,0:T(8,128)} async-done(((f32[8,2560]{1,0:T(8,128)}), f32[8,2560]{1,0:T(8,128)}) %all-reduce.10.cloned.1.call-update) | async-done | bytes 81936 | tf_op jit(solution)/shard_map/psum | solution.py:54
  284.6 1.0 fusion.30
  285.7 10.4 %fusion.36 = f32[8,2560]{1,0:T(8,128)} fusion(bf16[2560,4096]{1,0:T(8,128)(2,1)} %fusion.22, f32[8,4096]{1,0:T(8,128)S(1)} %multiply_add_fusion.2), kind=kOutput, calls=%fused_computation.70 | convolution fusion | flops 167804928 | bytes 21184512 | tf_op jit(solution)/shard_map/bc,rc->br/dot_general | solution.py:51
  296.2 86.2 %all-reduce.12.cloned.1.call-done = f32[8,2560]{1,0:T(8,128)} async-done(((f32[8,2560]{1,0:T(8,128)}), f32[8,2560]{1,0:T(8,128)}) %all-reduce.12.cloned.1.call-update) | async-done | bytes 81936 | tf_op jit(solution)/shard_map/psum | solution.py:54
  382.4 8.6 %multiply_reduce_fusion.1 = (f32[8]{0:T(128)S(1)}, f32[8]{0:T(128)S(1)}, f32[8,4096]{1,0:T(8,128)S(1)}) fusion(f32[8,4096]{1,0:T(8,128)S(1)} %multiply_add_fusion.2, f32[4096]{0:T(1024)S(1)} %bitcast.41, bf16[2560,4096]{1,0:T(8,128)(2,1)} %fusion.22, f32[8,2560]{1,0:T(8,128)} %all-reduce.12.cloned.1.call-done, f32[8,2560]{1,0:T(8,128)S(1)} %bitcast.21, ...), kind=kOutput, calls=%fused_computation.49 | convolution fusion | flops 168181760 | bytes 21434432 | tf_op jit(solution)/shard_map/dot_general | solution.py:57
  391.0 10.4 %fusion.34 = f32[8,2560]{1,0:T(8,128)} fusion(bf16[2560,4096]{1,0:T(8,128)(2,1)} %fusion.22, f32[8,4096]{1,0:T(8,128)S(1)} %get-tuple-element.25), kind=kOutput, calls=%fused_computation.68 | convolution fusion | flops 167804928 | bytes 21184512 | tf_op jit(solution)/shard_map/bc,rc->br/dot_general | solution.py:51
  401.5 32.4 %all-reduce = (f32[8]{0:T(128)S(1)}, f32[8]{0:T(128)S(1)}) all-reduce(f32[8]{0:T(128)S(1)} %get-tuple-element.6, f32[8]{0:T(128)S(1)} %get-tuple-element.5), channel_id=1, replica_groups=mesh['groups'=2,'wide'=16] {'wide'}, use_global_device_ids=true, to_apply=%region_14.0 | all-reduce | flops 16 | bytes 128 | tf_op jit(solution)/shard_map/psum | solution.py:68
  434.0 53.8 %all-reduce.14.cloned.1.call-done = f32[8,2560]{1,0:T(8,128)} async-done(((f32[8,2560]{1,0:T(8,128)}), f32[8,2560]{1,0:T(8,128)}) %all-reduce.14.cloned.1.call-update) | async-done | bytes 81936 | tf_op jit(solution)/shard_map/psum | solution.py:54
  487.8 1.0 multiply_reduce_fusion.5
  488.8 8.6 %multiply_reduce_fusion = (f32[8]{0:T(128)S(1)}, f32[8,4096]{1,0:T(8,128)S(1)}) fusion(f32[8,4096]{1,0:T(8,128)S(1)} %get-tuple-element.25, f32[8,4096]{1,0:T(8,128)S(1)} %multiply_add_fusion.2, f32[4096]{0:T(1024)S(1)} %bitcast.42, bf16[2560,4096]{1,0:T(8,128)(2,1)} %fusion.22, f32[8,2560]{1,0:T(8,128)} %all-reduce.14.cloned.1.call-done, ...), kind=kOutput, calls=%fused_computation.48 | convolution fusion | flops 168128512 | bytes 21555264 | tf_op jit(solution)/shard_map/dot_general | solution.py:57
  497.4 32.4 %psum.101 = f32[8]{0:T(128)S(1)} all-reduce(f32[8]{0:T(128)S(1)} %get-tuple-element.26), channel_id=1, replica_groups=mesh['groups'=2,'wide'=16] {'wide'}, use_global_device_ids=true, to_apply=%region_20.0 | all-reduce | flops 8 | bytes 64 | tf_op jit(solution)/shard_map/psum | solution.py:80
  529.8 10.4 %fusion.32 = f32[8,2560]{1,0:T(8,128)} fusion(bf16[2560,4096]{1,0:T(8,128)(2,1)} %fusion.22, f32[8,4096]{1,0:T(8,128)S(1)} %get-tuple-element.27, f32[8,4096]{1,0:T(8,128)S(1)} %get-tuple-element.25, f32[8]{0:T(128)S(1)} %div.62), kind=kOutput, calls=%fused_computation.66 | convolution fusion | flops 167870464 | bytes 21315616 | tf_op jit(solution)/shard_map/bc,rc->br/dot_general | solution.py:51
  540.5 29.5 %psum.102 = f32[8]{0:T(128)S(1)} all-reduce(f32[8]{0:T(128)S(1)} %fusion.29), channel_id=1, replica_groups=mesh['groups'=2,'wide'=16] {'wide'}, use_global_device_ids=true, to_apply=%region_22.0 | all-reduce | flops 8 | bytes 64 | tf_op jit(solution)/shard_map/psum | solution.py:75
  570.0 52.8 %all-reduce.16.cloned.1.call-done = f32[8,2560]{1,0:T(8,128)} async-done(((f32[8,2560]{1,0:T(8,128)}), f32[8,2560]{1,0:T(8,128)}) %all-reduce.16.cloned.1.call-update) | async-done | bytes 81936 | tf_op jit(solution)/shard_map/psum | solution.py:54
  622.8 1.0 fusion.31
  623.8 0.8 multiply_add_fusion
  (31 shorter events, 0.9 us)
Async XLA Ops:
  6.5 142.9 %all-reduce.8.cloned.1.call-start = ((), (), s32[]{:S(2)}) async-start(), calls=%async_computation | async-start | bytes 163840 | tf_op jit(solution)/shard_map/psum | solution.py:54
  15.4 26.8 %copy-start.1 = (s32[8,512]{1,0:T(8,128)S(1)}, s32[8,512]{1,0:T(8,128)}, u32[]{:S(2)}) copy-start(s32[8,512]{1,0:T(8,128)} %param.9) | copy-start | bytes 49156
  15.4 26.8 %copy-start.2 = (f32[5]{0:T(128)S(1)}, f32[5]{0:T(128)}, u32[]{:S(2)}) copy-start(f32[5]{0:T(128)} %param.8) | copy-start | bytes 64
  15.4 26.9 %copy-start = (f32[5,512]{1,0:T(8,128)S(1)}, f32[5,512]{1,0:T(8,128)}, u32[]{:S(2)}) copy-start(f32[5,512]{1,0:T(8,128)} %param.7) | copy-start | bytes 30724
  61.4 223.2 %all-reduce.10.cloned.1.call-start = ((), (), s32[]{:S(2)}) async-start(), calls=%async_computation.1 | async-start | bytes 163840 | tf_op jit(solution)/shard_map/psum | solution.py:54
  202.0 180.5 %all-reduce.12.cloned.1.call-start = ((), (), s32[]{:S(2)}) async-start(), calls=%async_computation.2 | async-start | bytes 163840 | tf_op jit(solution)/shard_map/psum | solution.py:54
  296.2 191.6 %all-reduce.14.cloned.1.call-start = ((), (), s32[]{:S(2)}) async-start(), calls=%async_computation.3 | async-start | bytes 163840 | tf_op jit(solution)/shard_map/psum | solution.py:54
  401.5 221.3 %all-reduce.16.cloned.1.call-start = ((), (), s32[]{:S(2)}) async-start(), calls=%async_computation.4 | async-start | bytes 163840 | tf_op jit(solution)/shard_map/psum | solution.py:54
Sparse Core Ops, SparseCore 0:
  61.5 87.9 all-reduce.7
  202.1 82.4 all-reduce.9
  296.3 86.1 all-reduce.11
  401.6 86.1 all-reduce.13
  540.4 82.3 all-reduce.15
where the time goes:
time: 632 us; the launch traced here: 631 us
  waiting for transfers between devices  299 us (47%)
  blocking collectives  191 us (30%)
  matrix products  86.5 us (14%)
  other arithmetic  41.1 us (7%)
  between operations  13.2 us (2%)
    psum x5, waiting for transfers between devices, predict(): return lax.psum(partial_rows, 'wide')  299 us
    psum x2, blocking collectives, local(): norm_now = lax.psum(jnp.sum(residual * residual, axis=1), 'wide')  67.4 us
    psum x2, blocking collectives, local(): norm_next = lax.psum(jnp.sum(residual * residual, axis=1), 'wide')  64.8 us
    psum x2, blocking collectives, local(): curvature = lax.psum(cell_part, 'wide') + value  59.2 us
    dot_general x5, matrix products, predict(): jnp.einsum('bc,rc->br', field_bf, sens_tile, preferred_element_type=jnp.f...  52.1 us
    dot_general x4, matrix products, back_project(): return jnp.dot(values_bf, sens_tile, preferred_element_type=jnp.float32)  34.4 us
    unnamed x4, other arithmetic  27.4 us
  transfers between devices with their start and end apart: 5, of which 5 were waited for; matrix products, arithmetic and copies ran while one was open for 0% of the time, Pallas kernels for 0%

commit v1 on v0

v1 whole, which is shorter than its diff:
```python
import functools

import jax
import jax.numpy as jnp
import ml_dtypes
import numpy as np
from jax import lax
from jax.experimental import pallas as pl
from jax.experimental.pallas import tpu as pltpu
from jax.sharding import PartitionSpec as P

IRLS = 2
CG_STEPS = 2
GRID = 128
DEPTHS = 16
LANES = 128
TEAM = 2

station_height = 2.0
focusing = 0.1
damping = 0.0002

PARITY = ((0, 0), (1, 1), (1, 0), (0, 0), (0, 1))
BF = jnp.bfloat16
F32 = jnp.float32


def offset_table(grid_y):
    one = np.float32
    dx = np.arange(GRID, dtype=one)[:, None, None]
    dy = np.arange(grid_y, dtype=one)[None, :, None]
    dz = (np.arange(DEPTHS, dtype=one) + one(0.5) + one(station_height))[None, None, :]
    radius2 = dx * dx + dy * dy + dz * dz
    strength = one(1) / (radius2 * radius2 * np.sqrt(radius2))
    three = one(3)
    kinds = [
        (three * dx * dx - radius2) * strength,
        three * dx * dy * strength,
        three * dx * dz * strength,
        (three * dy * dy - radius2) * strength,
        three * dy * dz * strength,
    ]
    return [k.astype(ml_dtypes.bfloat16).astype(np.float64) for k in kinds]


def angles(size):
    return 2 * np.pi * np.outer(np.arange(size), np.arange(size) + 0.5) / (2 * size)


def basis(size):
    return np.concatenate([np.cos(angles(size)), np.sin(angles(size))], axis=1)


def spectrum(values, odd, size):
    if odd:
        trig = 2 * np.sin(angles(size))
    else:
        trig = np.cos(angles(size)) * np.where(np.arange(size) == 0, 1, 2)[:, None]
    return np.tensordot(trig.T / size, values, axes=(1, 0))


def split(matrix):
    high = matrix.astype(ml_dtypes.bfloat16)
    low = (matrix - high.astype(np.float64)).astype(ml_dtypes.bfloat16)
    return high, low


@functools.lru_cache(maxsize=None)
def constants(grid_y):
    group = LANES // grid_y
    table = []
    for values, (odd_x, odd_y) in zip(offset_table(grid_y), PARITY):
        t = spectrum(values, odd_x, GRID)
        t = np.moveaxis(spectrum(np.moveaxis(t, 1, 0), odd_y, grid_y), 0, 1)
        table.append(np.moveaxis(t, 2, 0))
    table = np.tile(np.stack(table), (1, 1, 1, group)).astype(np.float32)

    base_x = basis(GRID)
    base_y = basis(grid_y)
    field_y = np.zeros((LANES, 2, LANES))
    station_y = np.zeros((grid_y, 2, LANES))
    for b in range(group):
        lanes = slice(b * grid_y, (b + 1) * grid_y)
        for half in range(2):
            part = base_y[:, half * grid_y : (half + 1) * grid_y]
            field_y[lanes, half, lanes] = part
            station_y[:, half, lanes] = part
    field_y = field_y.reshape(LANES, 2 * LANES)
    station_y = station_y.reshape(grid_y, 2 * LANES)
    spread = np.zeros((5, LANES, 2, LANES))
    for b in range(group):
        for c in range(5):
            spread[c, b * grid_y + c, :, b * grid_y : (b + 1) * grid_y] = 1
    spread = spread.reshape(5, LANES, 2 * LANES).astype(ml_dtypes.bfloat16)
    same = np.kron(np.eye(group), np.ones((grid_y, grid_y))).astype(np.float32)
    regroup = np.zeros((group, group, grid_y, group, group, grid_y))
    for b in range(group):
        for z in range(group):
            regroup[z, b, :, b, z, :] = np.eye(grid_y)
    regroup = regroup.reshape(group * LANES, group * LANES).astype(ml_dtypes.bfloat16)
    y_high, y_low = split(field_y)
    x_high, x_low = split(base_x.T)
    return dict(
        table=table,
        base_x=split(base_x)[0],
        base_xt2=np.concatenate([x_high, x_low], axis=1),
        field_y2=np.concatenate([y_high, y_low], axis=0),
        field_yt=split(field_y.T)[0],
        station_y2=np.stack(split(station_y)),
        spread=spread,
        gather_back=np.ascontiguousarray(spread.transpose(0, 2, 1)),
        same=same,
        regroup=regroup,
    )


def dot(a, b):
    return jnp.dot(a, b, preferred_element_type=F32)


def solve_kernel(
    grid_y,
    slot_ref,
    comp_ref,
    station_ref,
    observed_ref,
    counts_ref,
    table_ref,
    base_x_ref,
    base_xt2_ref,
    field_y2_ref,
    field_yt_ref,
    station_y2_ref,
    spread_ref,
    back_ref,
    same_ref,
    regroup_ref,
    out_ref,
    pick_x,
    pick_xt,
    pick_y,
    weights,
    data,
    pred,
    image,
    values,
    rows,
    spec_q,
    spec_f,
    spec_g,
    models,
    residual,
    direction,
    penalty,
    applied,
):
    group = LANES // grid_y
    stations = station_ref.shape[1]
    first = (slot_ref[0] * pl.num_programs(0) + pl.program_id(0)) * group

    station_x = station_ref[0:1, :]
    station_y = station_ref[1:2, :]
    place_x = (lax.broadcasted_iota(jnp.int32, (GRID, stations), 0) == station_x).astype(F32)
    place_y = (lax.broadcasted_iota(jnp.int32, (LANES, stations), 0) == station_y).astype(F32)
    pick_xt[...] = dot(base_xt2_ref[:, :GRID], place_x.astype(BF)).astype(BF)
    pick_x[...] = dot(jnp.transpose(place_x).astype(BF), base_x_ref[...]).astype(BF)
    place_yt = jnp.transpose(place_y)[:, :grid_y].astype(BF)
    pick_y[...] = dot(place_yt, station_y2_ref[0]) + dot(place_yt, station_y2_ref[1])

    rows[...] = jnp.zeros_like(rows)
    for b in range(group):
        count = counts_ref[pl.ds(first + b, 1), :].astype(F32)
        for c in range(5):
            rows[b * grid_y + c : b * grid_y + c + 1, :] = count * comp_ref[c]
    weights[...] = jnp.transpose(rows[...])
    for b in range(group):
        rows[b * grid_y : b * grid_y + 5, :] = observed_ref[...]
    data[...] = jnp.transpose(rows[...])

    def back_project():
        q = values[...]
        for c, (odd_x, odd_y) in enumerate(PARITY):
            v = (dot(q, spread_ref[c]) * pick_y[...]).astype(BF)
            spec = dot(pick_xt[...], v)
            for hx in range(2):
                for hy in range(2):
                    part = spec[hx * GRID : (hx + 1) * GRID, hy * LANES : (hy + 1) * LANES]
                    spec_q[c, hx, hy] = -part if (odd_x * hx + odd_y * hy) % 2 else part

        block = 4

        @pl.loop(0, DEPTHS // block)
        def _(zb):
            @pl.loop(0, GRID // 16)
            def _(tile):
                at = pl.ds(pl.multiple_of(tile * 16, 16), 16)
                q = [[[spec_q[c, hx, hy, at, :] for hy in range(2)] for hx in range(2)] for c in range(5)]
                for zi in range(block):
                    t = [table_ref[c, zb * block + zi, at, :] for c in range(5)]
                    for hx in range(2):
                        for hy in range(2):
                            total = None
                            for c, (odd_x, odd_y) in enumerate(PARITY):
                                term = t[c] * q[c][hx ^ odd_x][hy ^ odd_y]
                                total = term if total is None else total + term
                            spec_g[zi, pl.ds(pl.multiple_of(hx * GRID + tile * 16, 16), 16),
                                   hy * LANES : (hy + 1) * LANES] = total.astype(BF)

            for zi in range(block):
                along_x = dot(base_x_ref[...], spec_g[zi]).astype(BF)
                applied[zb * block + zi] = dot(along_x, field_yt_ref[...])

    def predict():
        @pl.loop(0, DEPTHS)
        def _(z):
            d = direction[z].astype(BF)
            y = dot(jnp.concatenate([d, d], axis=1), field_y2_ref[...]).astype(BF)
            spec_f[z] = dot(base_xt2_ref[...], jnp.concatenate([y, y], axis=0))

        @pl.loop(0, GRID // 8)
        def _(tile):
            at = [pl.ds(pl.multiple_of(hx * GRID + tile * 8, 8), 8) for hx in range(2)]
            total = [[[None] * 2 for _ in range(2)] for _ in range(5)]
            for z in range(DEPTHS):
                f = [[spec_f[z, at[hx], hy * LANES : (hy + 1) * LANES] for hy in range(2)] for hx in range(2)]
                for c, (odd_x, odd_y) in enumerate(PARITY):
                    t = table_ref[c, z, at[0], :]
                    for hx in range(2):
                        for hy in range(2):
                            term = t * f[hx ^ odd_x][hy ^ odd_y]
                            old = total[c][hx][hy]
                            total[c][hx][hy] = term if old is None else old + term
            for c, (odd_x, odd_y) in enumerate(PARITY):
                for hx in range(2):
                    for hy in range(2):
                        part = total[c][hx][hy]
                        part = -part if (odd_x * hx + odd_y * hy) % 2 else part
                        spec_q[c, hx, hy, pl.ds(pl.multiple_of(tile * 8, 8), 8), :] = part

        for c in range(5):
            q = jnp.concatenate(
                [jnp.concatenate([spec_q[c, hx, 0], spec_q[c, hx, 1]], axis=1) for hx in range(2)], axis=0
            ).astype(BF)
            part = (dot(pick_x[...], q) * pick_y[...]).astype(BF)
            part = dot(part, back_ref[c])
            if c == 0:
                image[...] = part
            else:
                image[...] += part

    def fold(a):
        return jnp.sum(a.reshape(a.shape[0] // 8, 8, LANES), axis=0)

    def total_of(partial):
        sums = jnp.dot(partial, same_ref[...], precision=lax.Precision.HIGHEST, preferred_element_type=F32)
        return jnp.sum(sums, axis=0, keepdims=True)

    def depth_weight(z):
        depth = z.astype(F32) + 0.5 + station_height
        ratio = station_height / jnp.full((1, LANES), depth, F32)
        return ratio * ratio * ratio

    zero = jnp.zeros((8, LANES), F32)

    @pl.loop(0, DEPTHS)
    def _(z):
        models[z] = jnp.zeros((GRID, LANES), F32)

    pred[...] = jnp.zeros_like(pred)

    def outer(_, carry):
        values[...] = (weights[...] * (data[...] - pred[...])).astype(BF)
        back_project()

        def start(z, carry):
            norm, cross = carry
            m = models[z]
            p = damping * depth_weight(z) / (m * m + focusing * focusing)
            penalty[z] = p
            r = applied[z] - p * m
            residual[z] = r
            direction[z] = r
            return norm + fold(r * r), cross + fold(p * r * r)

        norm, cross = lax.fori_loop(0, DEPTHS, start, (zero, zero))
        norm = total_of(norm)
        for inner in range(CG_STEPS):
            predict()
            weighted = weights[...] * image[...]
            step = norm / total_of(cross + fold(weighted * image[...]))
            pred[...] += step * image[...]
            if inner == CG_STEPS - 1:

                def last(z, carry):
                    models[z] += step * direction[z]
                    return carry

                lax.fori_loop(0, DEPTHS, last, 0)
                break
            values[...] = weighted.astype(BF)
            back_project()

            def update(z, carry):
                d = direction[z]
                models[z] += step * d
                r = residual[z] - step * (applied[z] + penalty[z] * d)
                residual[z] = r
                return carry + fold(r * r)

            new = total_of(lax.fori_loop(0, DEPTHS, update, zero))
            ratio = new / norm

            def turn(z, carry):
                d = residual[z] + ratio * direction[z]
                direction[z] = d
                return carry + fold(penalty[z] * d * d)

            cross = lax.fori_loop(0, DEPTHS, turn, zero)
            norm = new
        return carry

    lax.fori_loop(0, IRLS, outer, 0)

    for zq in range(DEPTHS // group):
        m = jnp.concatenate([models[zq * group + zi].astype(BF) for zi in range(group)], axis=1)
        m = dot(m, regroup_ref[...]).astype(BF)
        for b in range(group):
            out_ref[b, :, zq * LANES : (zq + 1) * LANES] = m[:, b * LANES : (b + 1) * LANES]


def solve(slot, comp_weight, station_index, observed, counts, boots, grid_y):
    group = LANES // grid_y
    stations = station_index.shape[1]
    consts = {k: jnp.asarray(v) for k, v in constants(grid_y).items()}
    vmem = pltpu.VMEM
    steps = boots // group
    whole = lambda a: pl.BlockSpec(a.shape, lambda i, n=a.ndim: (0,) * n)
    smem = pl.BlockSpec(memory_space=pltpu.SMEM)
    field = vmem((DEPTHS, GRID, LANES), F32)
    at_stations = vmem((stations, LANES), F32)
    arrays = [station_index, observed, counts] + list(consts.values())
    return pl.pallas_call(
        functools.partial(solve_kernel, grid_y),
        out_shape=jax.ShapeDtypeStruct((boots, GRID, DEPTHS * grid_y), BF),
        grid=(steps,),
        in_specs=[smem, smem] + [whole(a) for a in arrays],
        out_specs=pl.BlockSpec((group, GRID, DEPTHS * grid_y), lambda i: (i, 0, 0)),
        scratch_shapes=[
            vmem((stations, 2 * GRID), BF),
            vmem((2 * GRID, stations), BF),
            vmem((stations, 2 * LANES), F32),
            at_stations,
            at_stations,
            at_stations,
            at_stations,
            vmem((stations, LANES), BF),
            vmem((LANES, stations), F32),
            vmem((5, 2, 2, GRID, LANES), F32),
            vmem((DEPTHS, 2 * GRID, 2 * LANES), F32),
            vmem((4, 2 * GRID, 2 * LANES), BF),
            field,
            field,
            field,
            field,
            field,
        ],
        compiler_params=pltpu.CompilerParams(vmem_limit_bytes=48 * 1024 * 1024),
        cost_estimate=pl.CostEstimate(flops=10**10, bytes_accessed=10**7, transcendentals=0),
        name="solve",
    )(slot, comp_weight, *arrays)


def pick_kernel(grid_y, models_ref, cell_ref, out_ref):
    boots, _, depth_places = models_ref.shape
    cells = cell_ref.shape[1]
    cell_x = cell_ref[0:1, :]
    place = cell_ref[2:3, :] * grid_y + cell_ref[1:2, :]
    here = lax.broadcasted_iota(jnp.int32, (depth_places, cells), 0) == place
    chosen = jnp.where(here, 1.0, 0.0).astype(BF)
    at_x = lax.broadcasted_iota(jnp.int32, (GRID, cells), 0) == cell_x
    for b in range(boots):
        found = dot(models_ref[b], chosen)
        out_ref[b : b + 1, :] = jnp.sum(jnp.where(at_x, found, 0.0), axis=0, keepdims=True)


def pick(models, cells, grid_y):
    boots, _, depth_places = models.shape
    count = cells.shape[1]
    chunk = 512
    return pl.pallas_call(
        functools.partial(pick_kernel, grid_y),
        out_shape=jax.ShapeDtypeStruct((boots, count), F32),
        grid=(count // chunk,),
        in_specs=[
            pl.BlockSpec(models.shape, lambda i: (0, 0, 0)),
            pl.BlockSpec((3, chunk), lambda i: (0, i)),
        ],
        out_specs=pl.BlockSpec((boots, chunk), lambda i: (0, i)),
        compiler_params=pltpu.CompilerParams(vmem_limit_bytes=48 * 1024 * 1024),
        cost_estimate=pl.CostEstimate(
            flops=2 * boots * GRID * depth_places * count, bytes_accessed=10**6, transcendentals=0
        ),
        name="pick",
    )(models, cells)


def local(wide, cell_index, station_index, observed, comp_weight, counts):
    boots = counts.shape[0]
    grid_y = cell_index.shape[1] * wide // (GRID * DEPTHS)
    group = LANES // grid_y
    team = TEAM if wide % TEAM == 0 and boots % (TEAM * group) == 0 else 1
    mine = boots // team
    slot = lax.axis_index("wide") % team
    models = solve(
        slot.astype(jnp.int32).reshape(1), comp_weight, station_index, observed, counts, mine, grid_y
    )
    own = pick(models, cell_index, grid_y)
    if team == 1:
        return own
    pairs = [(i, i ^ 1) for i in range(wide)]
    theirs = pick(models, lax.ppermute(cell_index, "wide", pairs), grid_y)
    other = lax.ppermute(theirs, "wide", pairs)
    return jnp.concatenate(
        [jnp.where(slot == 0, own, other), jnp.where(slot == 0, other, own)], axis=0
    )


def solution(mesh):
    in_specs = (P(None, "wide"), P(None, "groups"), P(None, "groups"), P(), P("groups", None))
    out_specs = P("groups", "wide")
    fn = functools.partial(local, mesh.shape["wide"])
    return jax.shard_map(fn, mesh=mesh, in_specs=in_specs, out_specs=out_specs, check_vma=False)
```

time: 632 us -> 84.4 us (0.13)
  waiting for transfers between devices: 299 us -> 0.01 us
  blocking collectives: 191 us -> 0 us
  matrix products: 86.5 us -> 0 us
  Pallas kernels: 0 us -> 71.3 us
  other arithmetic: 41.1 us -> 0.71 us
  between operations: 13.2 us -> 0.08 us
  local copies, waits for them, and re-layouts: 0.1 us -> 10.8 us
    psum x5 -> x0, waiting for transfers between devices: 299 us -> none  [predict(): return lax.psum(partial_rows, 'wide')]
    psum x6 -> x0, blocking collectives: 191 us -> none  [the longest x2 67.4 us: local(): norm_now = lax.psum(jnp.sum(residual * residual, axis=1), 'wide')]
    dot_general x9 -> x0, matrix products: 86.5 us -> none  [the longest x5 52.1 us: predict(): jnp.einsum('bc,rc->br', field_bf, sens_tile, preferred_element_type=jnp.f...]
    pallas_call x0 -> x3, Pallas kernels: none -> 71.3 us  [the longest x1 63.3 us: solve(): pl.pallas_call(functools.partial(solve_kernel, grid_y), out_shape=jax.Sha...]
    unnamed x4 -> x0, other arithmetic: 27.4 us -> none
    unnamed x6 -> x28, local copies, waits for them, and re-layouts: 0.01 us -> 10.8 us
  transfers between devices with their start and end apart: 5 -> 2, of which waited for: 5 -> 0; matrix products, arithmetic and copies ran while one was open for 0% -> 0% of each run, Pallas kernels for 0% -> 81%
where the time goes in v1:
time: 84.4 us; the launch traced here: 83.5 us
  Pallas kernels  71.3 us (84%)
  local copies, waits for them, and re-layouts  10.8 us (13%)
    pallas_call x1, Pallas kernels, solve(): pl.pallas_call(functools.partial(solve_kernel, grid_y), out_shape=jax.Sha...  63.3 us
    unnamed x28, local copies, waits for them, and re-layouts  10.8 us
    pallas_call x2, Pallas kernels, pick(): pl.pallas_call(functools.partial(pick_kernel, grid_y), out_shape=jax.Shap...  8.03 us
  transfers between devices with their start and end apart: 2, of which 0 were waited for; matrix products, arithmetic and copies ran while one was open for 0% of the time, Pallas kernels for 81%

profile of v1, /device:TPU:0, one launch (start us, length us, event | category | flops | bytes accessed | tf_op | source)
XLA Modules:
  0.0 83.5 jit_solution(11247465687800641115)
XLA Ops:
  0.0 0.5 collective-permute-start
  0.5 0.0 copy-start.1
  0.5 0.7 copy-done.1
  1.2 0.0 copy-start.2
  1.2 0.7 copy-done.2
  1.9 0.0 copy-start.3
  1.9 0.7 copy-done.3
  2.6 0.0 copy-start.4
  2.6 0.7 copy-done.4
  3.2 0.0 copy-start.5
  3.2 1.0 %copy-done.5 = bf16[512,512]{1,0:T(8,128)(2,1)S(1)} copy-done((bf16[512,512]{1,0:T(8,128)(2,1)S(1)}, bf16[512,512]{1,0:T(8,128)(2,1)}, u32[]{:S(2)}) %copy-start.5) | copy-done | bytes 524312
  4.3 0.0 copy-start.6
  4.3 1.0 %copy-done.6 = bf16[5,256,128]{2,1,0:T(8,128)(2,1)S(1)} copy-done((bf16[5,256,128]{2,1,0:T(8,128)(2,1)S(1)}, bf16[5,256,128]{2,1,0:T(8,128)(2,1)}, u32[]{:S(2)}) %copy-start.6) | copy-done | bytes 327704
  5.2 0.0 copy-start.7
  5.2 1.0 %copy-done.7 = bf16[5,128,256]{2,1,0:T(8,128)(2,1)S(1)} copy-done((bf16[5,128,256]{2,1,0:T(8,128)(2,1)S(1)}, bf16[5,128,256]{2,1,0:T(8,128)(2,1)}, u32[]{:S(2)}) %copy-start.7) | copy-done | bytes 327704
  6.2 0.0 copy-start.8
  6.2 0.9 %copy-done.8 = bf16[256,256]{1,0:T(8,128)(2,1)S(1)} copy-done((bf16[256,256]{1,0:T(8,128)(2,1)S(1)}, bf16[256,256]{1,0:T(8,128)(2,1)}, u32[]{:S(2)}) %copy-start.8) | copy-done | bytes 131096
  7.1 0.0 copy-start.9
  7.1 0.9 %copy-done.9 = bf16[256,256]{1,0:T(8,128)(2,1)S(1)} copy-done((bf16[256,256]{1,0:T(8,128)(2,1)S(1)}, bf16[256,256]{1,0:T(8,128)(2,1)}, u32[]{:S(2)}) %copy-start.9) | copy-done | bytes 131096
  8.0 0.8 %copy-done.10 = f32[128,128]{1,0:T(8,128)S(1)} copy-done((f32[128,128]{1,0:T(8,128)S(1)}, f32[128,128]{1,0:T(8,128)}, u32[]{:S(2)}) %copy-start.10) | copy-done | bytes 65560
  8.9 0.8 %copy-done.11 = bf16[256,128]{1,0:T(8,128)(2,1)S(1)} copy-done((bf16[256,128]{1,0:T(8,128)(2,1)S(1)}, bf16[256,128]{1,0:T(8,128)(2,1)}, u32[]{:S(2)}) %copy-start.11) | copy-done | bytes 65560
  9.7 0.8 %copy-done.12 = bf16[128,256]{1,0:T(8,128)(2,1)S(1)} copy-done((bf16[128,256]{1,0:T(8,128)(2,1)S(1)}, bf16[128,256]{1,0:T(8,128)(2,1)}, u32[]{:S(2)}) %copy-start.12) | copy-done | bytes 65560
  10.6 0.8 copy-done.13
  11.3 63.3 %solve.1.models_ref = bf16[4,128,512]{2,1,0:T(8,128)(2,1)S(1)} custom-call(s32[1]{0:T(128)} %bitcast.slot_ref, f32[5]{0:T(128)S(1)} %copy-done.4, s32[2,512]{1,0:T(2,128)S(1)} %copy-done.3, f32[5,512]{1,0:T(8,128)S(1)} %copy-done.1, s32[8,512]{1,0:T(8,128)S(1)} %copy-done.2, f32[5,16,128,128]{3,2,1,0:T(8,128)} %constant.38.clone.table_ref, ...), custom_call_target="tpu_custom_call" | custom-call | flops 10000000000 | bytes 10000000 | tf_op jit(solution)/shard_map/solve/pallas_call | solution.py:342
  74.6 0.0 copy-start
  74.6 0.0 collective-permute-done.cell_ref
  74.6 4.0 %pick.3 = f32[4,4096]{1,0:T(4,128)S(1)} custom-call(bf16[4,128,512]{2,1,0:T(8,128)(2,1)S(1)} %solve.1.models_ref, s32[3,4096]{1,0:T(4,128)S(1)} %collective-permute-done.cell_ref), custom_call_target="tpu_custom_call" | custom-call | flops 2147483648 | bytes 1000000 | tf_op jit(solution)/shard_map/pick/pallas_call | solution.py:390
  78.7 0.1 collective-permute-start.1
  78.8 0.0 copy-done
  78.8 4.0 %pick.2 = f32[4,4096]{1,0:T(4,128)S(1)} custom-call(bf16[4,128,512]{2,1,0:T(8,128)(2,1)S(1)} %solve.1.models_ref, s32[3,4096]{1,0:T(4,128)S(1)} %copy-done), custom_call_target="tpu_custom_call" | custom-call | flops 2147483648 | bytes 1000000 | tf_op jit(solution)/shard_map/pick/pallas_call | solution.py:390
  82.8 0.0 collective-permute-done.1
  82.8 0.7 pad_maximum_fusion
  (5 shorter events, 0.0 us)
Async XLA Ops:
  0.0 74.6 %collective-permute-start = (s32[3,4096]{1,0:T(4,128)}, s32[3,4096]{1,0:T(4,128)S(1)}, u32[]{:S(2)}, u32[]{:S(2)}) collective-permute-start(s32[3,4096]{1,0:T(4,128)} %cell_ref.1), channel_id=1, source_target_pairs={{0,1},{1,0},{2,3},{3,2},{4,5},{5,4},{6,7},{7,6},{8,9},{9,8},{10,11... | collective-permute-start | bytes 147464 | tf_op jit(solution)/shard_map/ppermute | solution.py:421
  0.5 0.7 copy-start.1
  1.2 0.7 copy-start.2
  1.9 0.7 copy-start.3
  2.6 0.7 copy-start.4
  3.2 1.0 %copy-start.5 = (bf16[512,512]{1,0:T(8,128)(2,1)S(1)}, bf16[512,512]{1,0:T(8,128)(2,1)}, u32[]{:S(2)}) copy-start(bf16[512,512]{1,0:T(8,128)(2,1)} %constant.47.clone.regroup_ref) | copy-start | bytes 1572868
  4.3 1.0 %copy-start.6 = (bf16[5,256,128]{2,1,0:T(8,128)(2,1)S(1)}, bf16[5,256,128]{2,1,0:T(8,128)(2,1)}, u32[]{:S(2)}) copy-start(bf16[5,256,128]{2,1,0:T(8,128)(2,1)} %constant.45.clone.back_ref) | copy-start | bytes 983044
  5.2 1.0 %copy-start.7 = (bf16[5,128,256]{2,1,0:T(8,128)(2,1)S(1)}, bf16[5,128,256]{2,1,0:T(8,128)(2,1)}, u32[]{:S(2)}) copy-start(bf16[5,128,256]{2,1,0:T(8,128)(2,1)} %constant.44.clone.spread_ref) | copy-start | bytes 983044
  6.2 0.9 %copy-start.8 = (bf16[256,256]{1,0:T(8,128)(2,1)S(1)}, bf16[256,256]{1,0:T(8,128)(2,1)}, u32[]{:S(2)}) copy-start(bf16[256,256]{1,0:T(8,128)(2,1)} %constant.41.clone.field_y2_ref) | copy-start | bytes 393220
  7.1 0.9 %copy-start.9 = (bf16[256,256]{1,0:T(8,128)(2,1)S(1)}, bf16[256,256]{1,0:T(8,128)(2,1)}, u32[]{:S(2)}) copy-start(bf16[256,256]{1,0:T(8,128)(2,1)} %constant.40.clone.base_xt2_ref) | copy-start | bytes 393220
  8.0 0.8 %copy-start.10 = (f32[128,128]{1,0:T(8,128)S(1)}, f32[128,128]{1,0:T(8,128)}, u32[]{:S(2)}) copy-start(f32[128,128]{1,0:T(8,128)} %constant.46.clone.same_ref) | copy-start | bytes 196612
  8.9 0.8 %copy-start.11 = (bf16[256,128]{1,0:T(8,128)(2,1)S(1)}, bf16[256,128]{1,0:T(8,128)(2,1)}, u32[]{:S(2)}) copy-start(bf16[256,128]{1,0:T(8,128)(2,1)} %constant.42.clone.field_yt_ref) | copy-start | bytes 196612
  9.7 0.8 %copy-start.12 = (bf16[128,256]{1,0:T(8,128)(2,1)S(1)}, bf16[128,256]{1,0:T(8,128)(2,1)}, u32[]{:S(2)}) copy-start(bf16[128,256]{1,0:T(8,128)(2,1)} %constant.39.clone.base_x_ref) | copy-start | bytes 196612
  10.6 0.8 copy-start.13
  74.6 4.2 %copy-start = (s32[3,4096]{1,0:T(4,128)S(1)}, s32[3,4096]{1,0:T(4,128)}, u32[]{:S(2)}) copy-start(s32[3,4096]{1,0:T(4,128)} %cell_ref.1) | copy-start | bytes 147460
  78.7 4.1 %collective-permute-start.1 = (f32[4,4096]{1,0:T(4,128)S(1)}, f32[4,4096]{1,0:T(4,128)S(1)}, u32[]{:S(2)}, u32[]{:S(2)}) collective-permute-start(f32[4,4096]{1,0:T(4,128)S(1)} %pick.3), channel_id=1, source_target_pairs={{0,1},{1,0},{2,3},{3,2},{4,5},{5,4},{6,7},{7,6},{8,9},{9,8},{10,11... | collective-permute-start | bytes 196616 | tf_op jit(solution)/shard_map/ppermute | solution.py:422

commit v2 on v1

v2 whole, which is shorter than its diff:
```python
import functools

import jax
import jax.numpy as jnp
import ml_dtypes
import numpy as np
from jax import lax
from jax.experimental import pallas as pl
from jax.experimental.pallas import tpu as pltpu
from jax.sharding import PartitionSpec as P

IRLS = 2
CG_STEPS = 2
GRID = 128
DEPTHS = 16
LANES = 128
TEAM = 4

station_height = 2.0
focusing = 0.1
damping = 0.0002

PARITY = ((0, 0), (1, 1), (1, 0), (0, 0), (0, 1))
BF = jnp.bfloat16
F32 = jnp.float32


def offset_table(grid_y):
    one = np.float32
    dx = np.arange(GRID, dtype=one)[:, None, None]
    dy = np.arange(grid_y, dtype=one)[None, :, None]
    dz = (np.arange(DEPTHS, dtype=one) + one(0.5) + one(station_height))[None, None, :]
    radius2 = dx * dx + dy * dy + dz * dz
    strength = one(1) / (radius2 * radius2 * np.sqrt(radius2))
    three = one(3)
    kinds = [
        (three * dx * dx - radius2) * strength,
        three * dx * dy * strength,
        three * dx * dz * strength,
        (three * dy * dy - radius2) * strength,
        three * dy * dz * strength,
    ]
    return [k.astype(ml_dtypes.bfloat16).astype(np.float64) for k in kinds]


def angles(size):
    return 2 * np.pi * np.outer(np.arange(size), np.arange(size) + 0.5) / (2 * size)


def basis(size):
    return np.concatenate([np.cos(angles(size)), np.sin(angles(size))], axis=1)


def spectrum(values, odd, size):
    if odd:
        trig = 2 * np.sin(angles(size))
    else:
        trig = np.cos(angles(size)) * np.where(np.arange(size) == 0, 1, 2)[:, None]
    return np.tensordot(trig.T / size, values, axes=(1, 0))


def split(matrix):
    high = matrix.astype(ml_dtypes.bfloat16)
    low = (matrix - high.astype(np.float64)).astype(ml_dtypes.bfloat16)
    return high, low


@functools.lru_cache(maxsize=None)
def constants(grid_y, boots):
    deep = LANES // grid_y // boots
    slabs = DEPTHS // deep
    table = []
    for values, (odd_x, odd_y) in zip(offset_table(grid_y), PARITY):
        t = spectrum(values, odd_x, GRID)
        t = np.moveaxis(spectrum(np.moveaxis(t, 1, 0), odd_y, grid_y), 0, 1)
        t = np.moveaxis(t, 2, 0).reshape(slabs, deep, GRID, 1, grid_y).transpose(0, 2, 1, 3, 4)
        table.append(np.tile(t, (1, 1, 1, boots, 1)).reshape(slabs, GRID, LANES))
    table = np.stack(table).astype(np.float32)

    base_x = basis(GRID)
    base_y = basis(grid_y).reshape(grid_y, 2, grid_y)
    copies = deep * boots
    field_y = np.einsum("ab,yhl->ayhbl", np.eye(copies), base_y).reshape(LANES, 2 * LANES)
    station_y = np.einsum("b,yhl->yhbl", np.ones(copies), base_y).reshape(grid_y, 2 * LANES)
    spread = np.zeros((6, deep, boots, grid_y, deep, boots, grid_y))
    for c in range(5):
        for b in range(boots):
            spread[c, 0, b, c, :, b, :] = 1
    spread = spread.reshape(3, 2, LANES, LANES)
    back = spread.transpose(0, 1, 3, 2).reshape(3, 2 * LANES, LANES)
    spread = spread.transpose(0, 2, 1, 3).reshape(3, LANES, 2 * LANES)
    same = np.einsum("ab,dc,yz->dayczb", np.eye(boots), np.ones((deep, deep)), np.ones((grid_y, grid_y)))
    same = same.transpose(0, 1, 2, 3, 5, 4).reshape(LANES, LANES)
    regroup = np.einsum("st,de,ab,yz->sdaybtez", *[np.eye(n) for n in (boots, deep, boots, grid_y)])
    regroup = regroup.reshape(boots * LANES, boots * LANES)
    y_high, y_low = split(field_y)
    x_high, x_low = split(base_x.T)
    half = lambda a: a.astype(ml_dtypes.bfloat16)
    return dict(
        table=table,
        base_x=half(base_x),
        base_xt2=np.concatenate([x_high, x_low], axis=1),
        field_y2=np.concatenate([y_high, y_low], axis=0),
        field_yt=half(field_y.T),
        station_y2=np.stack(split(station_y)),
        spread=half(spread),
        back=half(back),
        same=same.astype(np.float32),
        regroup=half(regroup),
    )


def dot(a, b):
    return jnp.dot(a, b, preferred_element_type=F32)


def solve_kernel(grid_y, boots, n_const, slot_ref, comp_ref, station_ref, observed_ref, counts_ref, *refs):
    sources, out_ref = refs[:n_const], refs[n_const]
    held = refs[n_const + 1 : 2 * n_const + 1]
    (
        copied,
        pick_x,
        pick_xt,
        pick_y,
        weights,
        data,
        pred,
        image,
        values,
        rows,
        spec_q,
        spec_i,
        spec_f,
        spec_g,
        models,
        residual,
        direction,
        penalty,
        applied,
    ) = refs[2 * n_const + 1 :]
    copies = [pltpu.make_async_copy(s, h, copied.at[i]) for i, (s, h) in enumerate(zip(sources, held))]
    first_step = pl.program_id(0) == 0

    @pl.when(first_step)
    def _():
        for copy in copies:
            copy.start()

    (table_ref, base_x_ref, base_xt2_ref, field_y2_ref, field_yt_ref) = held[:5]
    (station_y2_ref, spread_ref, back_ref, same_ref, regroup_ref) = held[5:]
    deep = LANES // grid_y // boots
    slabs = DEPTHS // deep
    stations = station_ref.shape[1]
    first = (slot_ref[0] * pl.num_programs(0) + pl.program_id(0)) * boots

    rows[...] = jnp.zeros_like(rows)
    for b in range(boots):
        rows[b * grid_y : b * grid_y + 5, :] = observed_ref[...]
    data[...] = jnp.transpose(rows[...])
    for b in range(boots):
        count = counts_ref[pl.ds(first + b, 1), :].astype(F32)
        for c in range(5):
            rows[b * grid_y + c : b * grid_y + c + 1, :] = count * comp_ref[c]
    weights[...] = jnp.transpose(rows[...])

    station_x = station_ref[0:1, :]
    station_y = station_ref[1:2, :]
    place_x = (lax.broadcasted_iota(jnp.int32, (GRID, stations), 0) == station_x).astype(F32)
    place_y = (lax.broadcasted_iota(jnp.int32, (LANES, stations), 0) == station_y).astype(F32)
    place_xt = jnp.transpose(place_x).astype(BF)
    place_yt = jnp.transpose(place_y)[:, :grid_y].astype(BF)

    @pl.when(first_step)
    def _():
        for copy in copies[1:]:
            copy.wait()

    pick_xt[...] = dot(base_xt2_ref[:, :GRID], place_x.astype(BF)).astype(BF)
    pick_x[...] = dot(place_xt, base_x_ref[...]).astype(BF)
    pick_y[...] = dot(place_yt, station_y2_ref[0]) + dot(place_yt, station_y2_ref[1])

    @pl.when(first_step)
    def _():
        copies[0].wait()

    def back_project():
        q = values[...]
        for c, (odd_x, odd_y) in enumerate(PARITY):
            if c % 2 == 0:
                spreads = dot(q, spread_ref[c // 2])
            e = spreads[:, c % 2 * LANES : (c % 2 + 1) * LANES]
            v = jnp.concatenate([e * pick_y[:, :LANES], e * pick_y[:, LANES:]], axis=1).astype(BF)
            spec = dot(pick_xt[...], v)
            for hx in range(2):
                for hy in range(2):
                    part = spec[hx * GRID : (hx + 1) * GRID, hy * LANES : (hy + 1) * LANES]
                    spec_q[c, hx, hy] = -part if (odd_x * hx + odd_y * hy) % 2 else part

        @pl.loop(0, GRID // 16)
        def _(tile):
            at = pl.ds(pl.multiple_of(tile * 16, 16), 16)
            for hx in range(2):
                q = [[spec_q[c, hx ^ PARITY[c][0], hy, at, :] for hy in range(2)] for c in range(5)]
                to = pl.ds(pl.multiple_of(hx * GRID + tile * 16, 16), 16)
                for z in range(slabs):
                    t = [table_ref[c, z, at, :] for c in range(5)]
                    for hy in range(2):
                        total = None
                        for c in range(5):
                            term = t[c] * q[c][hy ^ PARITY[c][1]]
                            total = term if total is None else total + term
                        spec_g[z, to, hy * LANES : (hy + 1) * LANES] = total.astype(BF)

        for z in range(slabs):
            along_x = dot(base_x_ref[...], spec_g[z]).astype(BF)
            applied[z] = dot(along_x, field_yt_ref[...])

    def predict():
        d = direction[...].reshape(slabs * GRID, LANES).astype(BF)
        y = dot(jnp.concatenate([d, d], axis=1), field_y2_ref[...]).astype(BF)
        for z in range(slabs):
            part = y[z * GRID : (z + 1) * GRID]
            spec_f[z] = dot(base_xt2_ref[...], jnp.concatenate([part, part], axis=0))

        @pl.loop(0, GRID // 16)
        def _(tile):
            done = []
            for sub in range(2):
                at = [pl.ds(pl.multiple_of(hx * GRID + tile * 16 + sub * 8, 8), 8) for hx in range(2)]
                total = [[[None] * 2 for _ in range(2)] for _ in range(5)]
                for z in range(slabs):
                    f = [[spec_f[z, at[hx], hy * LANES : (hy + 1) * LANES] for hy in range(2)] for hx in range(2)]
                    for c, (odd_x, odd_y) in enumerate(PARITY):
                        t = table_ref[c, z, at[0], :]
                        for hx in range(2):
                            for hy in range(2):
                                term = t * f[hx ^ odd_x][hy ^ odd_y]
                                old = total[c][hx][hy]
                                total[c][hx][hy] = term if old is None else old + term
                done.append(total)
            for c, (odd_x, odd_y) in enumerate(PARITY):
                for hx in range(2):
                    to = pl.ds(pl.multiple_of(hx * GRID + tile * 16, 16), 16)
                    for hy in range(2):
                        part = jnp.concatenate([done[sub][c][hx][hy] for sub in range(2)], axis=0)
                        part = -part if (odd_x * hx + odd_y * hy) % 2 else part
                        spec_i[c, to, hy * LANES : (hy + 1) * LANES] = part.astype(BF)

        total = None
        pair = []
        for c in range(5):
            part = dot(pick_x[...], spec_i[c]) * pick_y[...]
            pair.append((part[:, :LANES] + part[:, LANES:]).astype(BF))
            if c % 2 or c == 4:
                if c == 4:
                    part = dot(pair[0], back_ref[2, :LANES, :])
                else:
                    part = dot(jnp.concatenate(pair, axis=1), back_ref[c // 2])
                total = part if total is None else total + part
                pair = []
        image[...] = total

    def fold(a):
        return jnp.sum(a.reshape(a.shape[0] // 8, 8, LANES), axis=0)

    def total_of(partial):
        if boots == 1:
            return jnp.broadcast_to(jnp.sum(partial, keepdims=True), (1, LANES))
        sums = jnp.dot(partial, same_ref[...], precision=lax.Precision.HIGHEST, preferred_element_type=F32)
        return jnp.sum(sums, axis=0, keepdims=True)

    def depth_weight(z):
        within = lax.broadcasted_iota(jnp.int32, (1, LANES), 1) // (boots * grid_y)
        depth = (within + z * deep).astype(F32) + 0.5 + station_height
        ratio = station_height / depth
        return ratio * ratio * ratio

    models[...] = jnp.zeros_like(models)
    pred[...] = jnp.zeros_like(pred)

    def outer(_, carry):
        values[...] = (weights[...] * (data[...] - pred[...])).astype(BF)
        back_project()
        norm = cross = jnp.zeros((8, LANES), F32)
        for z in range(slabs):
            m = models[z]
            p = damping * depth_weight(z) / (m * m + focusing * focusing)
            penalty[z] = p
            r = applied[z] - p * m
            residual[z] = r
            direction[z] = r
            norm += fold(r * r)
            cross += fold(p * r * r)
        norm = total_of(norm)
        for inner in range(CG_STEPS):
            predict()
            weighted = weights[...] * image[...]
            step = norm / total_of(cross + fold(weighted * image[...]))
            pred[...] += step * image[...]
            if inner == CG_STEPS - 1:
                for z in range(slabs):
                    models[z] += step * direction[z]
                break
            values[...] = weighted.astype(BF)
            back_project()
            new = jnp.zeros((8, LANES), F32)
            for z in range(slabs):
                d = direction[z]
                models[z] += step * d
                r = residual[z] - step * (applied[z] + penalty[z] * d)
                residual[z] = r
                new += fold(r * r)
            new = total_of(new)
            ratio = new / norm
            cross = jnp.zeros((8, LANES), F32)
            for z in range(slabs):
                d = residual[z] + ratio * direction[z]
                direction[z] = d
                cross += fold(penalty[z] * d * d)
            norm = new
        return carry

    lax.fori_loop(0, IRLS, outer, 0)

    for group in range(slabs // boots):
        m = jnp.concatenate([models[group * boots + i].astype(BF) for i in range(boots)], axis=1)
        if boots > 1:
            m = dot(m, regroup_ref[...]).astype(BF)
        for b in range(boots):
            out_ref[b, :, group * LANES : (group + 1) * LANES] = m[:, b * LANES : (b + 1) * LANES]


def solve(slot, comp_weight, station_index, observed, counts, mine, grid_y):
    boots = min(mine, LANES // grid_y)
    slabs = DEPTHS * grid_y * boots // LANES
    stations = station_index.shape[1]
    consts = [jnp.asarray(v) for v in constants(grid_y, boots).values()]
    vmem = pltpu.VMEM
    whole = lambda a: pl.BlockSpec(a.shape, lambda i, n=a.ndim: (0,) * n)
    smem = pl.BlockSpec(memory_space=pltpu.SMEM)
    field = vmem((slabs, GRID, LANES), F32)
    at_stations = vmem((stations, LANES), F32)
    inputs = [station_index, observed, counts]
    return pl.pallas_call(
        functools.partial(solve_kernel, grid_y, boots, len(consts)),
        out_shape=jax.ShapeDtypeStruct((mine, GRID, DEPTHS * grid_y), BF),
        grid=(mine // boots,),
        in_specs=[smem, smem]
        + [whole(a) for a in inputs]
        + [pl.BlockSpec(memory_space=pl.ANY) for _ in consts],
        out_specs=pl.BlockSpec((boots, GRID, DEPTHS * grid_y), lambda i: (i, 0, 0)),
        scratch_shapes=[vmem(a.shape, a.dtype) for a in consts]
        + [
            pltpu.SemaphoreType.DMA((len(consts),)),
            vmem((stations, 2 * GRID), BF),
            vmem((2 * GRID, stations), BF),
            vmem((stations, 2 * LANES), F32),
            at_stations,
            at_stations,
            at_stations,
            at_stations,
            vmem((stations, LANES), BF),
            vmem((LANES, stations), F32),
            vmem((5, 2, 2, GRID, LANES), F32),
            vmem((5, 2 * GRID, 2 * LANES), BF),
            vmem((slabs, 2 * GRID, 2 * LANES), F32),
            vmem((slabs, 2 * GRID, 2 * LANES), BF),
            field,
            field,
            field,
            field,
            field,
        ],
        compiler_params=pltpu.CompilerParams(vmem_limit_bytes=60 * 1024 * 1024),
        cost_estimate=pl.CostEstimate(flops=10**10, bytes_accessed=10**7, transcendentals=0),
        name="solve",
    )(slot, comp_weight, *inputs, *consts)


def pick_kernel(grid_y, count, models_ref, *refs):
    boots = models_ref.shape[0]
    for cell_ref, out_ref in zip(refs[:count], refs[count:]):
        cells = cell_ref.shape[1]
        place = cell_ref[...].astype(F32)
        wide = lambda row, rows: jnp.broadcast_to(row, (rows, cells)).astype(BF)
        y_row = wide(place[1:2], grid_y)
        z_row = wide(place[2:3], grid_y)
        here_y = lax.broadcasted_iota(jnp.int32, (grid_y, cells), 0).astype(F32).astype(BF) == y_row
        here_y = jnp.where(here_y, jnp.ones_like(y_row), jnp.zeros_like(y_row))
        chosen = jnp.concatenate(
            [jnp.where(z_row == jnp.full_like(z_row, z), here_y, jnp.zeros_like(here_y)) for z in range(DEPTHS)],
            axis=0,
        )
        at_x = lax.broadcasted_iota(jnp.int32, (GRID, cells), 0) == cell_ref[0:1, :]
        for b in range(boots):
            found = dot(models_ref[b], chosen)
            out_ref[b : b + 1, :] = jnp.sum(jnp.where(at_x, found, 0.0), axis=0, keepdims=True)


def pick(models, cells, grid_y):
    boots, _, depth_places = models.shape
    count = cells[0].shape[1]
    chunk = 512
    return pl.pallas_call(
        functools.partial(pick_kernel, grid_y, len(cells)),
        out_shape=[jax.ShapeDtypeStruct((boots, count), F32)] * len(cells),
        grid=(count // chunk,),
        in_specs=[pl.BlockSpec(models.shape, lambda i: (0, 0, 0))]
        + [pl.BlockSpec((3, chunk), lambda i: (0, i))] * len(cells),
        out_specs=[pl.BlockSpec((boots, chunk), lambda i: (0, i))] * len(cells),
        compiler_params=pltpu.CompilerParams(vmem_limit_bytes=48 * 1024 * 1024),
        cost_estimate=pl.CostEstimate(
            flops=2 * boots * GRID * depth_places * count * len(cells), bytes_accessed=10**6, transcendentals=0
        ),
        name="pick",
    )(models, *cells)


def local(wide, cell_index, station_index, observed, comp_weight, counts):
    boots = counts.shape[0]
    grid_y = cell_index.shape[1] * wide // (GRID * DEPTHS)
    team = TEAM if wide % TEAM == 0 and boots % TEAM == 0 else 1
    slot = lax.axis_index("wide").astype(jnp.int32) & (team - 1)

    def swap(a, k):
        return lax.ppermute(a, "wide", [(i, i ^ k) for i in range(wide)])

    theirs = [swap(cell_index, k) for k in range(1, team)]
    models = solve(slot.reshape(1), comp_weight, station_index, observed, counts, boots // team, grid_y)
    sent = [swap(a, k + 1) for k, a in enumerate(pick(models, theirs, grid_y))] if theirs else []
    got = jnp.stack([*pick(models, [cell_index], grid_y), *sent])
    bit = 1
    while bit < team:
        pairs = got.reshape((team // (2 * bit), 2, bit) + got.shape[1:])
        got = jnp.where(slot & bit != 0, pairs[:, ::-1], pairs).reshape(got.shape)
        bit *= 2
    return got.reshape(boots, -1)


def solution(mesh):
    in_specs = (P(None, "wide"), P(None, "groups"), P(None, "groups"), P(), P("groups", None))
    out_specs = P("groups", "wide")
    fn = functools.partial(local, mesh.shape["wide"])
    return jax.shard_map(fn, mesh=mesh, in_specs=in_specs, out_specs=out_specs, check_vma=False)
```

time: 84.4 us -> 39.9 us (0.47)
  Pallas kernels: 71.3 us -> 31.7 us
  local copies, waits for them, and re-layouts: 10.8 us -> 1.7 us
  starting transfers between devices: 0.56 us -> 5.18 us
    pallas_call x3, Pallas kernels: 71.3 us -> 31.7 us  [the longest x1 23.7 us: solve(): pl.pallas_call(functools.partial(solve_kernel, grid_y, boots, len(consts)...]
    unnamed x28 -> x4, local copies, waits for them, and re-layouts: 10.8 us -> 0.95 us
    ppermute x2 -> x6, starting transfers between devices: 0.56 us -> 5.18 us  [swap(): return lax.ppermute(a, 'wide', [(i, i ^ k) for i in range(wide)])]
  transfers between devices with their start and end apart: 2 -> 6, of which waited for: 0 -> 1; matrix products, arithmetic and copies ran while one was open for 0% -> 0% of each run, Pallas kernels for 81% -> 67%
where the time goes in v2:
time: 39.9 us; the launch traced here: 39.6 us
  Pallas kernels  31.7 us (79%)
  starting transfers between devices  5.18 us (13%)
  local copies, waits for them, and re-layouts  1.7 us (4%)
  waiting for transfers between devices  0.82 us (2%)
    pallas_call x1, Pallas kernels, solve(): pl.pallas_call(functools.partial(solve_kernel, grid_y, boots, len(consts)...  23.7 us
    pallas_call x2, Pallas kernels, pick(): pl.pallas_call(functools.partial(pick_kernel, grid_y, len(cells)), out_sh...  7.91 us
    ppermute x6, starting transfers between devices, swap(): return lax.ppermute(a, 'wide', [(i, i ^ k) for i in range(wide)])  5.18 us
    unnamed x4, local copies, waits for them, and re-layouts  0.95 us
    ppermute x6, waiting for transfers between devices, swap(): return lax.ppermute(a, 'wide', [(i, i ^ k) for i in range(wide)])  0.82 us
  transfers between devices with their start and end apart: 6, of which 1 were waited for; matrix products, arithmetic and copies ran while one was open for 0% of the time, Pallas kernels for 67%

profile of v2, /device:TPU:0, one launch (start us, length us, event | category | flops | bytes accessed | tf_op | source)
XLA Modules:
  0.0 39.6 jit_solution(14713255266398106311)
XLA Ops:
  0.0 0.5 %collective-permute-start = (s32[3,4096]{1,0:T(4,128)}, s32[3,4096]{1,0:T(4,128)S(1)}, u32[]{:S(2)}, u32[]{:S(2)}) collective-permute-start(s32[3,4096]{1,0:T(4,128)} %refs_0_.2), channel_id=1, source_target_pairs={{0,1},{1,0},{2,3},{3,2},{4,5},{5,4},{6,7},{7,6},{8,9},{9,8},{10,11... | collective-permute-start | bytes 147464 | tf_op jit(solution)/shard_map/ppermute | solution.py:426
  0.5 2.5 %collective-permute-start.1 = (s32[3,4096]{1,0:T(4,128)}, s32[3,4096]{1,0:T(4,128)S(1)}, u32[]{:S(2)}, u32[]{:S(2)}) collective-permute-start(s32[3,4096]{1,0:T(4,128)} %refs_0_.2), channel_id=1, source_target_pairs={{0,2},{1,3},{2,0},{3,1},{4,6},{5,7},{6,4},{7,5},{8,10},{9,11},{10,... | collective-permute-start | bytes 147464 | tf_op jit(solution)/shard_map/ppermute | solution.py:426
  3.0 0.1 collective-permute-start.2
  3.1 23.7 %solve.1.models_ref = bf16[2,128,512]{2,1,0:T(8,128)(2,1)} custom-call(s32[1]{0:T(128)} %bitcast.slot_ref, f32[5]{0:T(128)} %comp_ref.1, s32[2,512]{1,0:T(2,128)} %station_ref.1, f32[5,512]{1,0:T(8,128)} %observed_ref.1, s32[8,512]{1,0:T(8,128)} %counts_ref.1, f32[5,8,128,128]{3,2,1,0:T(8,128)} %constant.32.clone.refs_0_, ...), custom_call_target="tpu_custom_call" | custom-call | flops 10000000000 | bytes 10000000 | tf_op jit(solution)/shard_map/solve/pallas_call | solution.py:344
  26.9 0.0 copy-start
  26.9 0.0 collective-permute-done.refs_0_
  26.9 0.0 collective-permute-done.1.refs_1_
  26.9 0.0 collective-permute-done.2.refs_2_
  26.9 0.0 copy-start.1
  26.9 0.9 %copy-done.1 = bf16[2,128,512]{2,1,0:T(8,128)(2,1)S(1)} copy-done((bf16[2,128,512]{2,1,0:T(8,128)(2,1)S(1)}, bf16[2,128,512]{2,1,0:T(8,128)(2,1)}, u32[]{:S(2)}) %copy-start.1) | copy-done | bytes 262168
  27.9 5.2 %pick.3 = (f32[2,4096]{1,0:T(2,128)S(1)}, f32[2,4096]{1,0:T(2,128)S(1)}, f32[2,4096]{1,0:T(2,128)S(1)}) custom-call(bf16[2,128,512]{2,1,0:T(8,128)(2,1)S(1)} %copy-done.1, s32[3,4096]{1,0:T(4,128)S(1)} %collective-permute-done.refs_0_, s32[3,4096]{1,0:T(4,128)S(1)} %collective-permute-done.1.refs_1_, s32[3,4096]{1,0:T(4,128)S(1)} %collective-permute-done.2.refs_2_), custom_call_target="tpu_custom_call" | custom-call | flops 3221225472 | bytes 1000000 | tf_op jit(solution)/shard_map/pick/pallas_call | solution.py:404
  33.1 0.1 collective-permute-start.3
  33.2 1.9 %collective-permute-start.4 = (f32[2,4096]{1,0:T(2,128)S(1)}, f32[2,4096]{1,0:T(2,128)S(1)}, u32[]{:S(2)}, u32[]{:S(2)}) collective-permute-start(f32[2,4096]{1,0:T(2,128)S(1)} %get-tuple-element.9), channel_id=1, source_target_pairs={{0,2},{1,3},{2,0},{3,1},{4,6},{5,7},{6,4},{7,5},{8,10},{9,11},{10,... | collective-permute-start | bytes 98312 | tf_op jit(solution)/shard_map/ppermute | solution.py:426
  35.1 0.0 collective-permute-start.5
  35.1 0.0 copy-done
  35.1 2.7 %pick.2 = f32[2,4096]{1,0:T(2,128)S(1)} custom-call(bf16[2,128,512]{2,1,0:T(8,128)(2,1)S(1)} %copy-done.1, s32[3,4096]{1,0:T(4,128)S(1)} %copy-done), custom_call_target="tpu_custom_call" | custom-call | flops 1073741824 | bytes 1000000 | tf_op jit(solution)/shard_map/pick/pallas_call | solution.py:404
  37.9 0.0 collective-permute-done.3
  37.9 0.0 collective-permute-done.4
  37.9 0.8 %collective-permute-done.5 = f32[2,4096]{1,0:T(2,128)S(1)} collective-permute-done((f32[2,4096]{1,0:T(2,128)S(1)}, f32[2,4096]{1,0:T(2,128)S(1)}, u32[]{:S(2)}, u32[]{:S(2)}) %collective-permute-start.5) | collective-permute-done | bytes 32800 | tf_op jit(solution)/shard_map/ppermute | solution.py:426
  38.7 0.1 pad_maximum_fusion
  38.8 0.1 fusion
  38.8 0.1 reverse_select_fusion
  38.9 0.7 %reshape_reshape.7 = f32[8,4096]{1,0:T(8,128)} reshape(f32[1,2,2,2,4096]{4,3,2,1,0:T(2,128)S(1)} %reverse_select_fusion) | data formatting | bytes 262144 | tf_op jit(solution)/shard_map/reshape;reshape | solution.py:437
Async XLA Ops:
  0.0 26.9 %collective-permute-start = (s32[3,4096]{1,0:T(4,128)}, s32[3,4096]{1,0:T(4,128)S(1)}, u32[]{:S(2)}, u32[]{:S(2)}) collective-permute-start(s32[3,4096]{1,0:T(4,128)} %refs_0_.2), channel_id=1, source_target_pairs={{0,1},{1,0},{2,3},{3,2},{4,5},{5,4},{6,7},{7,6},{8,9},{9,8},{10,11... | collective-permute-start | bytes 147464 | tf_op jit(solution)/shard_map/ppermute | solution.py:426
  0.5 26.4 %collective-permute-start.1 = (s32[3,4096]{1,0:T(4,128)}, s32[3,4096]{1,0:T(4,128)S(1)}, u32[]{:S(2)}, u32[]{:S(2)}) collective-permute-start(s32[3,4096]{1,0:T(4,128)} %refs_0_.2), channel_id=1, source_target_pairs={{0,2},{1,3},{2,0},{3,1},{4,6},{5,7},{6,4},{7,5},{8,10},{9,11},{10,... | collective-permute-start | bytes 147464 | tf_op jit(solution)/shard_map/ppermute | solution.py:426
  3.0 23.9 %collective-permute-start.2 = (s32[3,4096]{1,0:T(4,128)}, s32[3,4096]{1,0:T(4,128)S(1)}, u32[]{:S(2)}, u32[]{:S(2)}) collective-permute-start(s32[3,4096]{1,0:T(4,128)} %refs_0_.2), channel_id=1, source_target_pairs={{0,3},{1,2},{2,1},{3,0},{4,7},{5,6},{6,5},{7,4},{8,11},{9,10},{10,... | collective-permute-start | bytes 147464 | tf_op jit(solution)/shard_map/ppermute | solution.py:426
  26.9 8.3 %copy-start = (s32[3,4096]{1,0:T(4,128)S(1)}, s32[3,4096]{1,0:T(4,128)}, u32[]{:S(2)}) copy-start(s32[3,4096]{1,0:T(4,128)} %refs_0_.2) | copy-start | bytes 147460
  26.9 1.0 %copy-start.1 = (bf16[2,128,512]{2,1,0:T(8,128)(2,1)S(1)}, bf16[2,128,512]{2,1,0:T(8,128)(2,1)}, u32[]{:S(2)}) copy-start(bf16[2,128,512]{2,1,0:T(8,128)(2,1)} %solve.1.models_ref) | copy-start | bytes 786436
  33.1 4.8 %collective-permute-start.3 = (f32[2,4096]{1,0:T(2,128)S(1)}, f32[2,4096]{1,0:T(2,128)S(1)}, u32[]{:S(2)}, u32[]{:S(2)}) collective-permute-start(f32[2,4096]{1,0:T(2,128)S(1)} %get-tuple-element.8), channel_id=1, source_target_pairs={{0,1},{1,0},{2,3},{3,2},{4,5},{5,4},{6,7},{7,6},{8,9},{9,8},{10,11... | collective-permute-start | bytes 98312 | tf_op jit(solution)/shard_map/ppermute | solution.py:426
  33.2 4.7 %collective-permute-start.4 = (f32[2,4096]{1,0:T(2,128)S(1)}, f32[2,4096]{1,0:T(2,128)S(1)}, u32[]{:S(2)}, u32[]{:S(2)}) collective-permute-start(f32[2,4096]{1,0:T(2,128)S(1)} %get-tuple-element.9), channel_id=1, source_target_pairs={{0,2},{1,3},{2,0},{3,1},{4,6},{5,7},{6,4},{7,5},{8,10},{9,11},{10,... | collective-permute-start | bytes 98312 | tf_op jit(solution)/shard_map/ppermute | solution.py:426
  35.1 3.6 %collective-permute-start.5 = (f32[2,4096]{1,0:T(2,128)S(1)}, f32[2,4096]{1,0:T(2,128)S(1)}, u32[]{:S(2)}, u32[]{:S(2)}) collective-permute-start(f32[2,4096]{1,0:T(2,128)S(1)} %get-tuple-element.10), channel_id=1, source_target_pairs={{0,3},{1,2},{2,1},{3,0},{4,7},{5,6},{6,5},{7,4},{8,11},{9,10},{10,... | collective-permute-start | bytes 98312 | tf_op jit(solution)/shard_map/ppermute | solution.py:426

commit v3 on v2

--- a/solution.py
+++ b/solution.py
@@ -14,7 +14,7 @@
 GRID = 128
 DEPTHS = 16
 LANES = 128
-TEAM = 4
+TEAM = 8
 
 station_height = 2.0
 focusing = 0.1

time: 39.9 us -> 46.5 us (1.17)
  starting transfers between devices: 5.18 us -> 15.1 us
  Pallas kernels: 31.7 us -> 26.2 us
  local copies, waits for them, and re-layouts: 1.7 us -> 3.66 us
    ppermute x6 -> x14, starting transfers between devices: 5.18 us -> 15.1 us  [swap(): return lax.ppermute(a, 'wide', [(i, i ^ k) for i in range(wide)])]
    pallas_call x1, Pallas kernels: 23.7 us -> 18.2 us  [solve(): pl.pallas_call(functools.partial(solve_kernel, grid_y, boots, len(consts)...]
    rev x0 -> x1, local copies, waits for them, and re-layouts: none -> 1.03 us  [local(): got = jnp.where(slot & bit != 0, pairs[:, ::-1], pairs).reshape(got.shape)]
    another operation x0 -> x3, local copies, waits for them, and re-layouts: none -> 0.94 us
    ppermute x6 -> x14, waiting for transfers between devices: 0.82 us -> 0.98 us  [swap(): return lax.ppermute(a, 'wide', [(i, i ^ k) for i in range(wide)])]
  transfers between devices with their start and end apart: 6 -> 14, of which waited for: 1 -> 2; matrix products, arithmetic and copies ran while one was open for 0% -> 1% of each run, Pallas kernels for 67% -> 44%
where the time goes in v3:
time: 46.5 us; the launch traced here: 46.2 us
  Pallas kernels  26.2 us (56%)
  starting transfers between devices  15.1 us (32%)
  local copies, waits for them, and re-layouts  3.66 us (8%)
  waiting for transfers between devices  0.98 us (2%)
    pallas_call x1, Pallas kernels, solve(): pl.pallas_call(functools.partial(solve_kernel, grid_y, boots, len(consts)...  18.2 us
    ppermute x14, starting transfers between devices, swap(): return lax.ppermute(a, 'wide', [(i, i ^ k) for i in range(wide)])  15.1 us
    pallas_call x2, Pallas kernels, pick(): pl.pallas_call(functools.partial(pick_kernel, grid_y, len(cells)), out_sh...  8.04 us
    rev x1, local copies, waits for them, and re-layouts, local(): got = jnp.where(slot & bit != 0, pairs[:, ::-1], pairs).reshape(got.shape)  1.03 us
    ppermute x14, waiting for transfers between devices, swap(): return lax.ppermute(a, 'wide', [(i, i ^ k) for i in range(wide)])  0.98 us
  transfers between devices with their start and end apart: 14, of which 2 were waited for; matrix products, arithmetic and copies ran while one was open for 1% of the time, Pallas kernels for 44%

profile of v3, /device:TPU:0, one launch (start us, length us, event | category | flops | bytes accessed | tf_op | source)
XLA Modules:
  0.0 46.2 jit_solution(12646246443686129895)
XLA Ops:
  0.0 0.5 collective-permute-start
  0.5 2.5 %collective-permute-start.1 = (s32[3,4096]{1,0:T(4,128)}, s32[3,4096]{1,0:T(4,128)S(1)}, u32[]{:S(2)}, u32[]{:S(2)}) collective-permute-start(s32[3,4096]{1,0:T(4,128)} %refs_0_.2), channel_id=1, source_target_pairs={{0,2},{1,3},{2,0},{3,1},{4,6},{5,7},{6,4},{7,5},{8,10},{9,11},{10,... | collective-permute-start | bytes 147464 | tf_op jit(solution)/shard_map/ppermute | solution.py:426
  3.0 0.1 collective-permute-start.2
  3.1 1.8 %collective-permute-start.3 = (s32[3,4096]{1,0:T(4,128)}, s32[3,4096]{1,0:T(4,128)S(1)}, u32[]{:S(2)}, u32[]{:S(2)}) collective-permute-start(s32[3,4096]{1,0:T(4,128)} %refs_0_.2), channel_id=1, source_target_pairs={{0,4},{1,5},{2,6},{3,7},{4,0},{5,1},{6,2},{7,3},{8,12},{9,13},{10,... | collective-permute-start | bytes 147464 | tf_op jit(solution)/shard_map/ppermute | solution.py:426
  4.9 0.0 collective-permute-start.4
  4.9 0.0 collective-permute-done.refs_0_
  4.9 2.6 %collective-permute-start.5 = (s32[3,4096]{1,0:T(4,128)}, s32[3,4096]{1,0:T(4,128)S(1)}, u32[]{:S(2)}, u32[]{:S(2)}) collective-permute-start(s32[3,4096]{1,0:T(4,128)} %refs_0_.2), channel_id=1, source_target_pairs={{0,6},{1,7},{2,4},{3,5},{4,2},{5,3},{6,0},{7,1},{8,14},{9,15},{10,... | collective-permute-start | bytes 147464 | tf_op jit(solution)/shard_map/ppermute | solution.py:426
  7.5 0.0 collective-permute-done.1.refs_1_
  7.5 0.5 %collective-permute-start.6 = (s32[3,4096]{1,0:T(4,128)}, s32[3,4096]{1,0:T(4,128)S(1)}, u32[]{:S(2)}, u32[]{:S(2)}) collective-permute-start(s32[3,4096]{1,0:T(4,128)} %refs_0_.2), channel_id=1, source_target_pairs={{0,7},{1,6},{2,5},{3,4},{4,3},{5,2},{6,1},{7,0},{8,15},{9,14},{10,... | collective-permute-start | bytes 147464 | tf_op jit(solution)/shard_map/ppermute | solution.py:426
  8.0 0.6 %jit_solution_.3.refs_8_ = f32[128,128]{1,0:T(8,128)} broadcast(f32[]{:T(128)} %constant.42.clone), dimensions={} | broadcast | bytes 65540 | tf_op jit(solution)
  8.7 18.2 %solve.1.models_ref = bf16[1,128,512]{2,1,0:T(8,128)(2,1)} custom-call(s32[1]{0:T(128)} %bitcast.slot_ref, f32[5]{0:T(128)} %comp_ref.1, s32[2,512]{1,0:T(2,128)} %station_ref.1, f32[5,512]{1,0:T(8,128)} %observed_ref.1, s32[8,512]{1,0:T(8,128)} %counts_ref.1, f32[5,4,128,128]{3,2,1,0:T(8,128)} %constant.34.clone.refs_0_, ...), custom_call_target="tpu_custom_call" | custom-call | flops 10000000000 | bytes 10000000 | tf_op jit(solution)/shard_map/solve/pallas_call | solution.py:344
  26.9 0.0 copy-start
  26.9 0.0 collective-permute-done.4.refs_4_
  26.9 0.0 copy-start.1
  26.9 0.9 %copy-done.1 = bf16[1,128,512]{2,1,0:T(8,128)(2,1)S(1)} copy-done((bf16[1,128,512]{2,1,0:T(8,128)(2,1)S(1)}, bf16[1,128,512]{2,1,0:T(8,128)(2,1)}, u32[]{:S(2)}) %copy-start.1) | copy-done | bytes 131096
  27.8 5.9 %pick.3 = (f32[1,4096]{1,0:T(1,128)S(1)}, f32[1,4096]{1,0:T(1,128)S(1)}, f32[1,4096]{1,0:T(1,128)S(1)}, f32[1,4096]{1,0:T(1,128)S(1)}, f32[1,4096]{1,0:T(1,128)S...) custom-call(bf16[1,128,512]{2,1,0:T(8,128)(2,1)S(1)} %copy-done.1, s32[3,4096]{1,0:T(4,128)S(1)} %collective-permute-done.refs_0_, ...), custom_call_target="tpu_custom_call" | custom-call | flops 3758096384 | bytes 1000000 | tf_op jit(solution)/shard_map/pick/pallas_call | solution.py:404
  33.8 1.2 %collective-permute-start.7 = (f32[1,4096]{1,0:T(1,128)S(1)}, f32[1,4096]{1,0:T(1,128)S(1)}, u32[]{:S(2)}, u32[]{:S(2)}) collective-permute-start(f32[1,4096]{1,0:T(1,128)S(1)} %get-tuple-element.12), channel_id=1, source_target_pairs={{0,1},{1,0},{2,3},{3,2},{4,5},{5,4},{6,7},{7,6},{8,9},{9,8},{10,11... | collective-permute-start | bytes 49160 | tf_op jit(solution)/shard_map/ppermute | solution.py:426
  35.0 0.3 collective-permute-start.8
  35.3 1.1 %collective-permute-start.9 = (f32[1,4096]{1,0:T(1,128)S(1)}, f32[1,4096]{1,0:T(1,128)S(1)}, u32[]{:S(2)}, u32[]{:S(2)}) collective-permute-start(f32[1,4096]{1,0:T(1,128)S(1)} %get-tuple-element.14), channel_id=1, source_target_pairs={{0,3},{1,2},{2,1},{3,0},{4,7},{5,6},{6,5},{7,4},{8,11},{9,10},{10,... | collective-permute-start | bytes 49160 | tf_op jit(solution)/shard_map/ppermute | solution.py:426
  36.4 0.5 %collective-permute-start.10 = (f32[1,4096]{1,0:T(1,128)S(1)}, f32[1,4096]{1,0:T(1,128)S(1)}, u32[]{:S(2)}, u32[]{:S(2)}) collective-permute-start(f32[1,4096]{1,0:T(1,128)S(1)} %get-tuple-element.15), channel_id=1, source_target_pairs={{0,4},{1,5},{2,6},{3,7},{4,0},{5,1},{6,2},{7,3},{8,12},{9,13},{10,... | collective-permute-start | bytes 49160 | tf_op jit(solution)/shard_map/ppermute | solution.py:426
  37.0 1.6 %collective-permute-start.11 = (f32[1,4096]{1,0:T(1,128)S(1)}, f32[1,4096]{1,0:T(1,128)S(1)}, u32[]{:S(2)}, u32[]{:S(2)}) collective-permute-start(f32[1,4096]{1,0:T(1,128)S(1)} %get-tuple-element.16), channel_id=1, source_target_pairs={{0,5},{1,4},{2,7},{3,6},{4,1},{5,0},{6,3},{7,2},{8,13},{9,12},{10,... | collective-permute-start | bytes 49160 | tf_op jit(solution)/shard_map/ppermute | solution.py:426
  38.5 1.3 %collective-permute-start.12 = (f32[1,4096]{1,0:T(1,128)S(1)}, f32[1,4096]{1,0:T(1,128)S(1)}, u32[]{:S(2)}, u32[]{:S(2)}) collective-permute-start(f32[1,4096]{1,0:T(1,128)S(1)} %get-tuple-element.17), channel_id=1, source_target_pairs={{0,6},{1,7},{2,4},{3,5},{4,2},{5,3},{6,0},{7,1},{8,14},{9,15},{10,... | collective-permute-start | bytes 49160 | tf_op jit(solution)/shard_map/ppermute | solution.py:426
  39.8 1.0 %collective-permute-start.13 = (f32[1,4096]{1,0:T(1,128)S(1)}, f32[1,4096]{1,0:T(1,128)S(1)}, u32[]{:S(2)}, u32[]{:S(2)}) collective-permute-start(f32[1,4096]{1,0:T(1,128)S(1)} %get-tuple-element.18), channel_id=1, source_target_pairs={{0,7},{1,6},{2,5},{3,4},{4,3},{5,2},{6,1},{7,0},{8,15},{9,14},{10,... | collective-permute-start | bytes 49160 | tf_op jit(solution)/shard_map/ppermute | solution.py:426
  40.8 2.1 %pick.2 = f32[1,4096]{1,0:T(1,128)S(1)} custom-call(bf16[1,128,512]{2,1,0:T(8,128)(2,1)S(1)} %copy-done.1, s32[3,4096]{1,0:T(4,128)S(1)} %copy-done), custom_call_target="tpu_custom_call" | custom-call | flops 536870912 | bytes 1000000 | tf_op jit(solution)/shard_map/pick/pallas_call | solution.py:404
  43.0 0.2 collective-permute-done.12
  43.2 0.8 %collective-permute-done.13 = f32[1,4096]{1,0:T(1,128)S(1)} collective-permute-done((f32[1,4096]{1,0:T(1,128)S(1)}, f32[1,4096]{1,0:T(1,128)S(1)}, u32[]{:S(2)}, u32[]{:S(2)}) %collective-permute-start.13) | collective-permute-done | bytes 16416 | tf_op jit(solution)/shard_map/ppermute | solution.py:426
  43.9 0.2 stack.35
  44.1 0.1 reshape.7
  44.2 1.0 %rev.9 = f32[4,2,1,1,4096]{4,1,0,3,2:T(2,128)S(1)} reverse(f32[4,2,1,1,4096]{4,1,0,3,2:T(2,128)S(1)} %reshape.7), dimensions={1} | reverse | bytes 262144 | tf_op jit(solution)/shard_map/rev | solution.py:435
  45.3 0.1 reverse_select_fusion.1
  45.4 0.1 reshape_reshape.10
  45.5 0.7 %reshape_reshape.11 = f32[8,4096]{1,0:T(8,128)} reshape(f32[1,2,4,1,4096]{4,2,1,3,0:T(4,128)S(1)} %reverse_select_fusion) | data formatting | bytes 262144 | tf_op jit(solution)/shard_map/reshape;reshape | solution.py:437
  (12 shorter events, 0.1 us)
Async XLA Ops:
  0.0 4.9 %collective-permute-start = (s32[3,4096]{1,0:T(4,128)}, s32[3,4096]{1,0:T(4,128)S(1)}, u32[]{:S(2)}, u32[]{:S(2)}) collective-permute-start(s32[3,4096]{1,0:T(4,128)} %refs_0_.2), channel_id=1, source_target_pairs={{0,1},{1,0},{2,3},{3,2},{4,5},{5,4},{6,7},{7,6},{8,9},{9,8},{10,11... | collective-permute-start | bytes 147464 | tf_op jit(solution)/shard_map/ppermute | solution.py:426
  0.5 7.0 %collective-permute-start.1 = (s32[3,4096]{1,0:T(4,128)}, s32[3,4096]{1,0:T(4,128)S(1)}, u32[]{:S(2)}, u32[]{:S(2)}) collective-permute-start(s32[3,4096]{1,0:T(4,128)} %refs_0_.2), channel_id=1, source_target_pairs={{0,2},{1,3},{2,0},{3,1},{4,6},{5,7},{6,4},{7,5},{8,10},{9,11},{10,... | collective-permute-start | bytes 147464 | tf_op jit(solution)/shard_map/ppermute | solution.py:426
  3.0 23.9 %collective-permute-start.2 = (s32[3,4096]{1,0:T(4,128)}, s32[3,4096]{1,0:T(4,128)S(1)}, u32[]{:S(2)}, u32[]{:S(2)}) collective-permute-start(s32[3,4096]{1,0:T(4,128)} %refs_0_.2), channel_id=1, source_target_pairs={{0,3},{1,2},{2,1},{3,0},{4,7},{5,6},{6,5},{7,4},{8,11},{9,10},{10,... | collective-permute-start | bytes 147464 | tf_op jit(solution)/shard_map/ppermute | solution.py:426
  3.1 23.8 %collective-permute-start.3 = (s32[3,4096]{1,0:T(4,128)}, s32[3,4096]{1,0:T(4,128)S(1)}, u32[]{:S(2)}, u32[]{:S(2)}) collective-permute-start(s32[3,4096]{1,0:T(4,128)} %refs_0_.2), channel_id=1, source_target_pairs={{0,4},{1,5},{2,6},{3,7},{4,0},{5,1},{6,2},{7,3},{8,12},{9,13},{10,... | collective-permute-start | bytes 147464 | tf_op jit(solution)/shard_map/ppermute | solution.py:426
  4.9 22.0 %collective-permute-start.4 = (s32[3,4096]{1,0:T(4,128)}, s32[3,4096]{1,0:T(4,128)S(1)}, u32[]{:S(2)}, u32[]{:S(2)}) collective-permute-start(s32[3,4096]{1,0:T(4,128)} %refs_0_.2), channel_id=1, source_target_pairs={{0,5},{1,4},{2,7},{3,6},{4,1},{5,0},{6,3},{7,2},{8,13},{9,12},{10,... | collective-permute-start | bytes 147464 | tf_op jit(solution)/shard_map/ppermute | solution.py:426
  4.9 22.0 %collective-permute-start.5 = (s32[3,4096]{1,0:T(4,128)}, s32[3,4096]{1,0:T(4,128)S(1)}, u32[]{:S(2)}, u32[]{:S(2)}) collective-permute-start(s32[3,4096]{1,0:T(4,128)} %refs_0_.2), channel_id=1, source_target_pairs={{0,6},{1,7},{2,4},{3,5},{4,2},{5,3},{6,0},{7,1},{8,14},{9,15},{10,... | collective-permute-start | bytes 147464 | tf_op jit(solution)/shard_map/ppermute | solution.py:426
  7.5 19.4 %collective-permute-start.6 = (s32[3,4096]{1,0:T(4,128)}, s32[3,4096]{1,0:T(4,128)S(1)}, u32[]{:S(2)}, u32[]{:S(2)}) collective-permute-start(s32[3,4096]{1,0:T(4,128)} %refs_0_.2), channel_id=1, source_target_pairs={{0,7},{1,6},{2,5},{3,4},{4,3},{5,2},{6,1},{7,0},{8,15},{9,14},{10,... | collective-permute-start | bytes 147464 | tf_op jit(solution)/shard_map/ppermute | solution.py:426
  26.9 14.0 %copy-start = (s32[3,4096]{1,0:T(4,128)S(1)}, s32[3,4096]{1,0:T(4,128)}, u32[]{:S(2)}) copy-start(s32[3,4096]{1,0:T(4,128)} %refs_0_.2) | copy-start | bytes 147460
  26.9 0.9 %copy-start.1 = (bf16[1,128,512]{2,1,0:T(8,128)(2,1)S(1)}, bf16[1,128,512]{2,1,0:T(8,128)(2,1)}, u32[]{:S(2)}) copy-start(bf16[1,128,512]{2,1,0:T(8,128)(2,1)} %solve.1.models_ref) | copy-start | bytes 393220
  33.8 4.8 %collective-permute-start.7 = (f32[1,4096]{1,0:T(1,128)S(1)}, f32[1,4096]{1,0:T(1,128)S(1)}, u32[]{:S(2)}, u32[]{:S(2)}) collective-permute-start(f32[1,4096]{1,0:T(1,128)S(1)} %get-tuple-element.12), channel_id=1, source_target_pairs={{0,1},{1,0},{2,3},{3,2},{4,5},{5,4},{6,7},{7,6},{8,9},{9,8},{10,11... | collective-permute-start | bytes 49160 | tf_op jit(solution)/shard_map/ppermute | solution.py:426
  35.0 4.8 %collective-permute-start.8 = (f32[1,4096]{1,0:T(1,128)S(1)}, f32[1,4096]{1,0:T(1,128)S(1)}, u32[]{:S(2)}, u32[]{:S(2)}) collective-permute-start(f32[1,4096]{1,0:T(1,128)S(1)} %get-tuple-element.13), channel_id=1, source_target_pairs={{0,2},{1,3},{2,0},{3,1},{4,6},{5,7},{6,4},{7,5},{8,10},{9,11},{10,... | collective-permute-start | bytes 49160 | tf_op jit(solution)/shard_map/ppermute | solution.py:426
  35.3 7.6 %collective-permute-start.9 = (f32[1,4096]{1,0:T(1,128)S(1)}, f32[1,4096]{1,0:T(1,128)S(1)}, u32[]{:S(2)}, u32[]{:S(2)}) collective-permute-start(f32[1,4096]{1,0:T(1,128)S(1)} %get-tuple-element.14), channel_id=1, source_target_pairs={{0,3},{1,2},{2,1},{3,0},{4,7},{5,6},{6,5},{7,4},{8,11},{9,10},{10,... | collective-permute-start | bytes 49160 | tf_op jit(solution)/shard_map/ppermute | solution.py:426
  36.4 6.5 %collective-permute-start.10 = (f32[1,4096]{1,0:T(1,128)S(1)}, f32[1,4096]{1,0:T(1,128)S(1)}, u32[]{:S(2)}, u32[]{:S(2)}) collective-permute-start(f32[1,4096]{1,0:T(1,128)S(1)} %get-tuple-element.15), channel_id=1, source_target_pairs={{0,4},{1,5},{2,6},{3,7},{4,0},{5,1},{6,2},{7,3},{8,12},{9,13},{10,... | collective-permute-start | bytes 49160 | tf_op jit(solution)/shard_map/ppermute | solution.py:426
  37.0 6.0 %collective-permute-start.11 = (f32[1,4096]{1,0:T(1,128)S(1)}, f32[1,4096]{1,0:T(1,128)S(1)}, u32[]{:S(2)}, u32[]{:S(2)}) collective-permute-start(f32[1,4096]{1,0:T(1,128)S(1)} %get-tuple-element.16), channel_id=1, source_target_pairs={{0,5},{1,4},{2,7},{3,6},{4,1},{5,0},{6,3},{7,2},{8,13},{9,12},{10,... | collective-permute-start | bytes 49160 | tf_op jit(solution)/shard_map/ppermute | solution.py:426
  38.5 4.6 %collective-permute-start.12 = (f32[1,4096]{1,0:T(1,128)S(1)}, f32[1,4096]{1,0:T(1,128)S(1)}, u32[]{:S(2)}, u32[]{:S(2)}) collective-permute-start(f32[1,4096]{1,0:T(1,128)S(1)} %get-tuple-element.17), channel_id=1, source_target_pairs={{0,6},{1,7},{2,4},{3,5},{4,2},{5,3},{6,0},{7,1},{8,14},{9,15},{10,... | collective-permute-start | bytes 49160 | tf_op jit(solution)/shard_map/ppermute | solution.py:426
  39.8 4.1 %collective-permute-start.13 = (f32[1,4096]{1,0:T(1,128)S(1)}, f32[1,4096]{1,0:T(1,128)S(1)}, u32[]{:S(2)}, u32[]{:S(2)}) collective-permute-start(f32[1,4096]{1,0:T(1,128)S(1)} %get-tuple-element.18), channel_id=1, source_target_pairs={{0,7},{1,6},{2,5},{3,4},{4,3},{5,2},{6,1},{7,0},{8,15},{9,14},{10,... | collective-permute-start | bytes 49160 | tf_op jit(solution)/shard_map/ppermute | solution.py:426

commit v4 on v2

--- a/solution.py
+++ b/solution.py
@@ -15,6 +15,7 @@
 DEPTHS = 16
 LANES = 128
 TEAM = 4
+BLOCK = 4
 
 station_height = 2.0
 focusing = 0.1
@@ -128,6 +129,7 @@
         image,
         values,
         rows,
+        sums,
         spec_q,
         spec_i,
         spec_f,
@@ -152,6 +154,7 @@
     slabs = DEPTHS // deep
     stations = station_ref.shape[1]
     first = (slot_ref[0] * pl.num_programs(0) + pl.program_id(0)) * boots
+    blocks = [list(range(z, z + BLOCK)) for z in range(0, slabs, BLOCK)]
 
     rows[...] = jnp.zeros_like(rows)
     for b in range(boots):
@@ -162,6 +165,7 @@
         for c in range(5):
             rows[b * grid_y + c : b * grid_y + c + 1, :] = count * comp_ref[c]
     weights[...] = jnp.transpose(rows[...])
+    values[...] = (weights[...] * data[...]).astype(BF)
 
     station_x = station_ref[0:1, :]
     station_y = station_ref[1:2, :]
@@ -196,55 +200,65 @@
                     part = spec[hx * GRID : (hx + 1) * GRID, hy * LANES : (hy + 1) * LANES]
                     spec_q[c, hx, hy] = -part if (odd_x * hx + odd_y * hy) % 2 else part
 
-        @pl.loop(0, GRID // 16)
-        def _(tile):
-            at = pl.ds(pl.multiple_of(tile * 16, 16), 16)
-            for hx in range(2):
-                q = [[spec_q[c, hx ^ PARITY[c][0], hy, at, :] for hy in range(2)] for c in range(5)]
-                to = pl.ds(pl.multiple_of(hx * GRID + tile * 16, 16), 16)
-                for z in range(slabs):
-                    t = [table_ref[c, z, at, :] for c in range(5)]
-                    for hy in range(2):
-                        total = None
+        for block in blocks:
+            for row in range(0, GRID, 16):
+                at = slice(row, row + 16)
+                for hx in range(2):
+                    q = [[spec_q[c, hx ^ PARITY[c][0], hy, at, :] for hy in range(2)] for c in range(5)]
+                    to = slice(hx * GRID + row, hx * GRID + row + 16)
+                    for z in block:
+                        t = [table_ref[c, z, at, :] for c in range(5)]
+                        for hy in range(2):
+                            total = None
+                            for c in range(5):
+                                term = t[c] * q[c][hy ^ PARITY[c][1]]
+                                total = term if total is None else total + term
+                            spec_g[z, to, hy * LANES : (hy + 1) * LANES] = total.astype(BF)
+            for z in block:
+                along_x = dot(base_x_ref[...], spec_g[z]).astype(BF)
+                applied[z] = dot(along_x, field_yt_ref[...])
+
+    def predict():
+        for block in blocks:
+            r = residual[block[0] : block[-1] + 1].reshape(BLOCK * GRID, LANES).astype(BF)
+            y = dot(jnp.concatenate([r, r], axis=1), field_y2_ref[...]).astype(BF)
+            for i, z in enumerate(block):
+                part = y[i * GRID : (i + 1) * GRID]
+                spec_f[z] = dot(base_xt2_ref[...], jnp.concatenate([part, part], axis=0))
+            for row in range(0, GRID, 16):
+                done = []
+                for sub in range(row, row + 16, 8):
+                    at = [slice(hx * GRID + sub, hx * GRID + sub + 8) for hx in range(2)]
+                    total = [[[None] * 2 for _ in range(2)] for _ in range(5)]
+                    if block is not blocks[0]:
+                        total = [
+                            [[spec_q[c, hx, hy, at[0], :] for hy in range(2)] for hx in range(2)] for c in range(5)
+                        ]
+                    for z in block:
+                        f = [[spec_f[z, at[hx], hy * LANES : (hy + 1) * LANES] for hy in range(2)] for hx in range(2)]
+                        for c, (odd_x, odd_y) in enumerate(PARITY):
+                            t = table_ref[c, z, at[0], :]
+                            for hx in range(2):
+                                for hy in range(2):
+                                    term = t * f[hx ^ odd_x][hy ^ odd_y]
+                                    old = total[c][hx][hy]
+                                    total[c][hx][hy] = term if old is None else old + term
+                    if block is not blocks[-1]:
                         for c in range(5):
-                            term = t[c] * q[c][hy ^ PARITY[c][1]]
-                            total = term if total is None else total + term
-                        spec_g[z, to, hy * LANES : (hy + 1) * LANES] = total.astype(BF)
-
-        for z in range(slabs):
-            along_x = dot(base_x_ref[...], spec_g[z]).astype(BF)
-            applied[z] = dot(along_x, field_yt_ref[...])
-
-    def predict():
-        d = direction[...].reshape(slabs * GRID, LANES).astype(BF)
-        y = dot(jnp.concatenate([d, d], axis=1), field_y2_ref[...]).astype(BF)
-        for z in range(slabs):
-            part = y[z * GRID : (z + 1) * GRID]
-            spec_f[z] = dot(base_xt2_ref[...], jnp.concatenate([part, part], axis=0))
-
-        @pl.loop(0, GRID // 16)
-        def _(tile):
-            done = []
-            for sub in range(2):
-                at = [pl.ds(pl.multiple_of(hx * GRID + tile * 16 + sub * 8, 8), 8) for hx in range(2)]
-                total = [[[None] * 2 for _ in range(2)] for _ in range(5)]
-                for z in range(slabs):
-                    f = [[spec_f[z, at[hx], hy * LANES : (hy + 1) * LANES] for hy in range(2)] for hx in range(2)]
-                    for c, (odd_x, odd_y) in enumerate(PARITY):
-                        t = table_ref[c, z, at[0], :]
-                        for hx in range(2):
-                            for hy in range(2):
-                                term = t * f[hx ^ odd_x][hy ^ odd_y]
-                                old = total[c][hx][hy]
-                                total[c][hx][hy] = term if old is None else old + term
-                done.append(total)
-            for c, (odd_x, odd_y) in enumerate(PARITY):
-                for hx in range(2):
-                    to = pl.ds(pl.multiple_of(hx * GRID + tile * 16, 16), 16)
-                    for hy in range(2):
-                        part = jnp.concatenate([done[sub][c][hx][hy] for sub in range(2)], axis=0)
-                        part = -part if (odd_x * hx + odd_y * hy) % 2 else part
-                        spec_i[c, to, hy * LANES : (hy + 1) * LANES] = part.astype(BF)
+                            for hx in range(2):
+                                for hy in range(2):
+                                    spec_q[c, hx, hy, at[0], :] = total[c][hx][hy]
+                    done.append(total)
+                if block is not blocks[-1]:
+                    continue
+                for c, (odd_x, odd_y) in enumerate(PARITY):
+                    for hx in range(2):
+                        for hy in range(2):
+                            part = jnp.concatenate([done[sub][c][hx][hy] for sub in range(2)], axis=0)
+                            part = -part if (odd_x * hx + odd_y * hy) % 2 else part
+                            spec_i[c, hx * GRID + row : hx * GRID + row + 16, hy * LANES : (hy + 1) * LANES] = (
+                                part.astype(BF)
+                            )
 
         total = None
         pair = []
@@ -258,7 +272,7 @@
                     part = dot(jnp.concatenate(pair, axis=1), back_ref[c // 2])
                 total = part if total is None else total + part
                 pair = []
-        image[...] = total
+        return total
 
     def fold(a):
         return jnp.sum(a.reshape(a.shape[0] // 8, 8, LANES), axis=0)
@@ -276,58 +290,64 @@
         return ratio * ratio * ratio
 
     models[...] = jnp.zeros_like(models)
+    direction[...] = jnp.zeros_like(direction)
     pred[...] = jnp.zeros_like(pred)
-
-    def outer(_, carry):
-        values[...] = (weights[...] * (data[...] - pred[...])).astype(BF)
+    image[...] = jnp.zeros_like(image)
+
+    def round_of(index, carry):
+        old_norm, old_step = carry
+        fresh = index % CG_STEPS == 0
         back_project()
-        norm = cross = jnp.zeros((8, LANES), F32)
+
+        @pl.when(fresh)
+        def _():
+            norm = jnp.zeros((8, LANES), F32)
+            for z in range(slabs):
+                m = models[z]
+                p = damping * depth_weight(z) / (m * m + focusing * focusing)
+                penalty[z] = p
+                r = applied[z] - p * m
+                residual[z] = r
+                norm += fold(r * r)
+            sums[...] = norm
+
+        @pl.when(jnp.logical_not(fresh))
+        def _():
+            norm = jnp.zeros((8, LANES), F32)
+            for z in range(slabs):
+                r = residual[z] - old_step * (applied[z] + penalty[z] * direction[z])
+                residual[z] = r
+                norm += fold(r * r)
+            sums[...] = norm
+
+        norm = total_of(sums[...])
+        ratio = jnp.where(fresh, 0.0, norm / old_norm)
+        cross = jnp.zeros((8, LANES), F32)
         for z in range(slabs):
-            m = models[z]
-            p = damping * depth_weight(z) / (m * m + focusing * focusing)
-            penalty[z] = p
-            r = applied[z] - p * m
-            residual[z] = r
-            direction[z] = r
-            norm += fold(r * r)
-            cross += fold(p * r * r)
-        norm = total_of(norm)
-        for inner in range(CG_STEPS):
-            predict()
-            weighted = weights[...] * image[...]
-            step = norm / total_of(cross + fold(weighted * image[...]))
-            pred[...] += step * image[...]
-            if inner == CG_STEPS - 1:
-                for z in range(slabs):
-                    models[z] += step * direction[z]
-                break
-            values[...] = weighted.astype(BF)
-            back_project()
-            new = jnp.zeros((8, LANES), F32)
-            for z in range(slabs):
-                d = direction[z]
-                models[z] += step * d
-                r = residual[z] - step * (applied[z] + penalty[z] * d)
-                residual[z] = r
-                new += fold(r * r)
-            new = total_of(new)
-            ratio = new / norm
-            cross = jnp.zeros((8, LANES), F32)
-            for z in range(slabs):
-                d = residual[z] + ratio * direction[z]
-                direction[z] = d
-                cross += fold(penalty[z] * d * d)
-            norm = new
-        return carry
-
-    lax.fori_loop(0, IRLS, outer, 0)
+            d = residual[z] + ratio * direction[z]
+            direction[z] = d
+            cross += fold(penalty[z] * d * d)
+        here = predict() + ratio * image[...]
+        image[...] = here
+        step = norm / total_of(cross + fold(weights[...] * here * here))
+        for z in range(slabs):
+            models[z] += step * direction[z]
+        now = pred[...] + step * here
+        pred[...] = now
+        values[...] = (weights[...] * jnp.where(fresh, here, data[...] - now)).astype(BF)
+        return norm, step
+
+    one = jnp.ones((1, LANES), F32)
+    lax.fori_loop(0, IRLS * CG_STEPS, round_of, (one, one))
 
     for group in range(slabs // boots):
         m = jnp.concatenate([models[group * boots + i].astype(BF) for i in range(boots)], axis=1)
         if boots > 1:
             m = dot(m, regroup_ref[...]).astype(BF)
         for b in range(boots):
-            out_ref[b, :, group * LANES : (group + 1) * LANES] = m[:, b * LANES : (b + 1) * LANES]
+            out_ref[b * GRID : (b + 1) * GRID, group * LANES : (group + 1) * LANES] = (
+                m[:, b * LANES : (b + 1) * LANES]
+            )
 
 
 def solve(slot, comp_weight, station_index, observed, counts, mine, grid_y):
@@ -343,12 +363,12 @@
     inputs = [station_index, observed, counts]
     return pl.pallas_call(
         functools.partial(solve_kernel, grid_y, boots, len(consts)),
-        out_shape=jax.ShapeDtypeStruct((mine, GRID, DEPTHS * grid_y), BF),
+        out_shape=jax.ShapeDtypeStruct((mine * GRID, DEPTHS * grid_y), BF),
         grid=(mine // boots,),
         in_specs=[smem, smem]
         + [whole(a) for a in inputs]
-        + [pl.BlockSpec(memory_space=pl.ANY) for _ in consts],
-        out_specs=pl.BlockSpec((boots, GRID, DEPTHS * grid_y), lambda i: (i, 0, 0)),
+        + [pl.BlockSpec(memory_space=pltpu.HBM) for _ in consts],
+        out_specs=pl.BlockSpec((boots * GRID, DEPTHS * grid_y), lambda i: (i, 0)),
         scratch_shapes=[vmem(a.shape, a.dtype) for a in consts]
         + [
             pltpu.SemaphoreType.DMA((len(consts),)),
@@ -361,6 +381,7 @@
             at_stations,
             vmem((stations, LANES), BF),
             vmem((LANES, stations), F32),
+            vmem((8, LANES), F32),
             vmem((5, 2, 2, GRID, LANES), F32),
             vmem((5, 2 * GRID, 2 * LANES), BF),
             vmem((slabs, 2 * GRID, 2 * LANES), F32),
@@ -371,46 +392,55 @@
             field,
             field,
         ],
-        compiler_params=pltpu.CompilerParams(vmem_limit_bytes=60 * 1024 * 1024),
+        compiler_params=pltpu.CompilerParams(vmem_limit_bytes=40 * 1024 * 1024),
         cost_estimate=pl.CostEstimate(flops=10**10, bytes_accessed=10**7, transcendentals=0),
         name="solve",
     )(slot, comp_weight, *inputs, *consts)
 
 
-def pick_kernel(grid_y, count, models_ref, *refs):
-    boots = models_ref.shape[0]
-    for cell_ref, out_ref in zip(refs[:count], refs[count:]):
-        cells = cell_ref.shape[1]
-        place = cell_ref[...].astype(F32)
-        wide = lambda row, rows: jnp.broadcast_to(row, (rows, cells)).astype(BF)
+def pick_kernel(grid_y, boots, count, models_ref, *refs):
+    chunk = 512
+
+    def pick_chunk(cell_ref, out_ref, at):
+        cells = cell_ref[:, at]
+        place = cells.astype(F32)
+        wide = lambda row, rows: jnp.broadcast_to(row, (rows, chunk)).astype(BF)
         y_row = wide(place[1:2], grid_y)
         z_row = wide(place[2:3], grid_y)
-        here_y = lax.broadcasted_iota(jnp.int32, (grid_y, cells), 0).astype(F32).astype(BF) == y_row
+        here_y = lax.broadcasted_iota(jnp.int32, (grid_y, chunk), 0).astype(F32).astype(BF) == y_row
         here_y = jnp.where(here_y, jnp.ones_like(y_row), jnp.zeros_like(y_row))
         chosen = jnp.concatenate(
             [jnp.where(z_row == jnp.full_like(z_row, z), here_y, jnp.zeros_like(here_y)) for z in range(DEPTHS)],
             axis=0,
         )
-        at_x = lax.broadcasted_iota(jnp.int32, (GRID, cells), 0) == cell_ref[0:1, :]
+        at_x = lax.broadcasted_iota(jnp.int32, (GRID, chunk), 0) == cells[0:1]
+        found = dot(models_ref[...], chosen)
         for b in range(boots):
-            found = dot(models_ref[b], chosen)
-            out_ref[b : b + 1, :] = jnp.sum(jnp.where(at_x, found, 0.0), axis=0, keepdims=True)
+            part = jnp.where(at_x, found[b * GRID : (b + 1) * GRID], 0.0)
+            out_ref[b : b + 1, at] = jnp.sum(part, axis=0, keepdims=True)
+
+    per = max(1, 4 // count)
+
+    @pl.loop(0, refs[0].shape[1] // (per * chunk))
+    def _(step):
+        for i in range(per):
+            at = pl.ds(pl.multiple_of((step * per + i) * chunk, chunk), chunk)
+            for cell_ref, out_ref in zip(refs[:count], refs[count:]):
+                pick_chunk(cell_ref, out_ref, at)
 
 
 def pick(models, cells, grid_y):
-    boots, _, depth_places = models.shape
+    boots = models.shape[0] // GRID
     count = cells[0].shape[1]
-    chunk = 512
+    vmem = pl.BlockSpec(memory_space=pltpu.VMEM)
     return pl.pallas_call(
-        functools.partial(pick_kernel, grid_y, len(cells)),
+        functools.partial(pick_kernel, grid_y, boots, len(cells)),
         out_shape=[jax.ShapeDtypeStruct((boots, count), F32)] * len(cells),
-        grid=(count // chunk,),
-        in_specs=[pl.BlockSpec(models.shape, lambda i: (0, 0, 0))]
-        + [pl.BlockSpec((3, chunk), lambda i: (0, i))] * len(cells),
-        out_specs=[pl.BlockSpec((boots, chunk), lambda i: (0, i))] * len(cells),
-        compiler_params=pltpu.CompilerParams(vmem_limit_bytes=48 * 1024 * 1024),
+        in_specs=[vmem] * (1 + len(cells)),
+        out_specs=[vmem] * len(cells),
+        compiler_params=pltpu.CompilerParams(vmem_limit_bytes=40 * 1024 * 1024),
         cost_estimate=pl.CostEstimate(
-            flops=2 * boots * GRID * depth_places * count * len(cells), bytes_accessed=10**6, transcendentals=0
+            flops=2 * models.size * count * len(cells), bytes_accessed=10**6, transcendentals=0
         ),
         name="pick",
     )(models, *cells)
@@ -428,13 +458,14 @@
     theirs = [swap(cell_index, k) for k in range(1, team)]
     models = solve(slot.reshape(1), comp_weight, station_index, observed, counts, boots // team, grid_y)
     sent = [swap(a, k + 1) for k, a in enumerate(pick(models, theirs, grid_y))] if theirs else []
-    got = jnp.stack([*pick(models, [cell_index], grid_y), *sent])
-    bit = 1
-    while bit < team:
-        pairs = got.reshape((team // (2 * bit), 2, bit) + got.shape[1:])
-        got = jnp.where(slot & bit != 0, pairs[:, ::-1], pairs).reshape(got.shape)
-        bit *= 2
-    return got.reshape(boots, -1)
+    got = [*pick(models, [cell_index], grid_y), *sent]
+    blocks = []
+    for member in range(team):
+        block = got[member]
+        for other in range(1, team):
+            block = jnp.where(slot == other, got[member ^ other], block)
+        blocks.append(block)
+    return jnp.concatenate(blocks, axis=0)
 
 
 def solution(mesh):

time: 39.9 us -> 51.3 us (1.29)
  local copies, waits for them, and re-layouts: 1.7 us -> 12.4 us
  Pallas kernels: 31.7 us -> 30.3 us
  waiting for transfers between devices: 0.82 us -> 2.06 us
  other arithmetic: 0.17 us -> 0.78 us
    unnamed x4 -> x30, local copies, waits for them, and re-layouts: 0.95 us -> 12.4 us
    pallas_call x2, Pallas kernels: 7.91 us -> 6.58 us  [pick(): pl.pallas_call(functools.partial(pick_kernel, grid_y, boots, len(cells)),...]
    ppermute x6, waiting for transfers between devices: 0.82 us -> 2.06 us  [swap(): return lax.ppermute(a, 'wide', [(i, i ^ k) for i in range(wide)])]
    another operation x1 -> x0, local copies, waits for them, and re-layouts: 0.75 us -> none  [local(): return got.reshape(boots, -1)]
    concatenate x0 -> x1, other arithmetic: none -> 0.72 us  [local(): return jnp.concatenate(blocks, axis=0)]
  transfers between devices with their start and end apart: 6 -> 6, of which waited for: 1 -> 1; matrix products, arithmetic and copies ran while one was open for 0% -> 0% of each run, Pallas kernels for 67% -> 50%
where the time goes in v4:
time: 51.3 us; the launch traced here: 50.7 us
  Pallas kernels  30.3 us (59%)
  local copies, waits for them, and re-layouts  12.4 us (24%)
  starting transfers between devices  5.06 us (10%)
  waiting for transfers between devices  2.06 us (4%)
  other arithmetic  0.78 us (2%)
    pallas_call x1, Pallas kernels, solve(): pl.pallas_call(functools.partial(solve_kernel, grid_y, boots, len(consts)...  23.7 us
    unnamed x30, local copies, waits for them, and re-layouts  12.4 us
    pallas_call x2, Pallas kernels, pick(): pl.pallas_call(functools.partial(pick_kernel, grid_y, boots, len(cells)),...  6.58 us
    ppermute x6, starting transfers between devices, swap(): return lax.ppermute(a, 'wide', [(i, i ^ k) for i in range(wide)])  5.06 us
    ppermute x6, waiting for transfers between devices, swap(): return lax.ppermute(a, 'wide', [(i, i ^ k) for i in range(wide)])  2.06 us
  transfers between devices with their start and end apart: 6, of which 1 were waited for; matrix products, arithmetic and copies ran while one was open for 0% of the time, Pallas kernels for 50%

profile of v4, /device:TPU:0, one launch (start us, length us, event | category | flops | bytes accessed | tf_op | source)
XLA Modules:
  0.0 50.7 jit_solution(8487281629118574733)
XLA Ops:
  0.0 0.5 collective-permute-start
  0.5 2.5 %collective-permute-start.1 = (s32[3,4096]{1,0:T(4,128)}, s32[3,4096]{1,0:T(4,128)S(1)}, u32[]{:S(2)}, u32[]{:S(2)}) collective-permute-start(s32[3,4096]{1,0:T(4,128)} %refs_0_.2), channel_id=1, source_target_pairs={{0,2},{1,3},{2,0},{3,1},{4,6},{5,7},{6,4},{7,5},{8,10},{9,11},{10,... | collective-permute-start | bytes 147464 | tf_op jit(solution)/shard_map/ppermute | solution.py:456
  3.0 0.1 collective-permute-start.2
  3.1 0.7 %copy-done.1 = f32[5,512]{1,0:T(8,128)S(1)} copy-done((f32[5,512]{1,0:T(8,128)S(1)}, f32[5,512]{1,0:T(8,128)}, u32[]{:S(2)}) %copy-start.1) | copy-done | bytes 10264
  3.8 0.7 %copy-done.2 = s32[8,512]{1,0:T(8,128)S(1)} copy-done((s32[8,512]{1,0:T(8,128)S(1)}, s32[8,512]{1,0:T(8,128)}, u32[]{:S(2)}) %copy-start.2) | copy-done | bytes 16408
  4.6 0.7 %copy-done.3 = s32[2,512]{1,0:T(2,128)S(1)} copy-done((s32[2,512]{1,0:T(2,128)S(1)}, s32[2,512]{1,0:T(2,128)}, u32[]{:S(2)}) %copy-start.3) | copy-done | bytes 4120
  5.2 0.7 %copy-done.4 = f32[5]{0:T(128)S(1)} copy-done((f32[5]{0:T(128)S(1)}, f32[5]{0:T(128)}, u32[]{:S(2)}) %copy-start.4) | copy-done | bytes 44
  5.9 1.7 %copy-done.5 = f32[5,8,128,128]{3,2,1,0:T(8,128)S(1)} copy-done((f32[5,8,128,128]{3,2,1,0:T(8,128)S(1)}, f32[5,8,128,128]{3,2,1,0:T(8,128)}, u32[]{:S(2)}) %copy-start.5) | copy-done | bytes 2621464
  7.6 0.9 %copy-done.6 = bf16[3,128,256]{2,1,0:T(8,128)(2,1)S(1)} copy-done((bf16[3,128,256]{2,1,0:T(8,128)(2,1)S(1)}, bf16[3,128,256]{2,1,0:T(8,128)(2,1)}, u32[]{:S(2)}) %copy-start.6) | copy-done | bytes 196632
  8.6 0.9 %copy-done.7 = bf16[3,256,128]{2,1,0:T(8,128)(2,1)S(1)} copy-done((bf16[3,256,128]{2,1,0:T(8,128)(2,1)S(1)}, bf16[3,256,128]{2,1,0:T(8,128)(2,1)}, u32[]{:S(2)}) %copy-start.7) | copy-done | bytes 196632
  9.5 0.9 %copy-done.8 = bf16[256,256]{1,0:T(8,128)(2,1)S(1)} copy-done((bf16[256,256]{1,0:T(8,128)(2,1)S(1)}, bf16[256,256]{1,0:T(8,128)(2,1)}, u32[]{:S(2)}) %copy-start.8) | copy-done | bytes 131096
  10.4 0.9 %copy-done.9 = bf16[256,256]{1,0:T(8,128)(2,1)S(1)} copy-done((bf16[256,256]{1,0:T(8,128)(2,1)S(1)}, bf16[256,256]{1,0:T(8,128)(2,1)}, u32[]{:S(2)}) %copy-start.9) | copy-done | bytes 131096
  11.3 0.9 %copy-done.10 = bf16[256,256]{1,0:T(8,128)(2,1)S(1)} copy-done((bf16[256,256]{1,0:T(8,128)(2,1)S(1)}, bf16[256,256]{1,0:T(8,128)(2,1)}, u32[]{:S(2)}) %copy-start.10) | copy-done | bytes 131096
  12.2 0.8 %copy-done.11 = bf16[128,256]{1,0:T(8,128)(2,1)S(1)} copy-done((bf16[128,256]{1,0:T(8,128)(2,1)S(1)}, bf16[128,256]{1,0:T(8,128)(2,1)}, u32[]{:S(2)}) %copy-start.11) | copy-done | bytes 65560
  13.0 0.8 %copy-done.12 = bf16[256,128]{1,0:T(8,128)(2,1)S(1)} copy-done((bf16[256,128]{1,0:T(8,128)(2,1)S(1)}, bf16[256,128]{1,0:T(8,128)(2,1)}, u32[]{:S(2)}) %copy-start.12) | copy-done | bytes 65560
  13.9 0.8 %copy-done.13 = f32[128,128]{1,0:T(8,128)S(1)} copy-done((f32[128,128]{1,0:T(8,128)S(1)}, f32[128,128]{1,0:T(8,128)}, u32[]{:S(2)}) %copy-start.13) | copy-done | bytes 65560
  14.7 0.8 %copy-done.14 = bf16[2,32,256]{2,1,0:T(8,128)(2,1)S(1)} copy-done((bf16[2,32,256]{2,1,0:T(8,128)(2,1)S(1)}, bf16[2,32,256]{2,1,0:T(8,128)(2,1)}, u32[]{:S(2)}) %copy-start.14) | copy-done | bytes 32792
  15.5 23.7 %solve.1.models_ref = bf16[256,512]{1,0:T(8,128)(2,1)S(1)} custom-call(s32[1]{0:T(128)} %bitcast.slot_ref, f32[5]{0:T(128)S(1)} %copy-done.4, s32[2,512]{1,0:T(2,128)S(1)} %copy-done.3, f32[5,512]{1,0:T(8,128)S(1)} %copy-done.1, s32[8,512]{1,0:T(8,128)S(1)} %copy-done.2, f32[5,8,128,128]{3,2,1,0:T(8,128)S(1)} %copy-done.5, bf16[128,256]{1,0:T(8,128)(2,1)S(1)} %copy-done.11, ...), custom_call_target="tpu_custom_call" | custom-call | flops 10000000000 | bytes 10000000 | tf_op jit(solution)/shard_map/solve/pallas_call | solution.py:364
  39.2 0.0 copy-start
  39.2 0.0 collective-permute-done.refs_0_
  39.2 0.0 collective-permute-done.1.refs_1_
  39.2 0.0 collective-permute-done.2.refs_2_
  39.3 5.0 %pick.2 = (f32[2,4096]{1,0:T(2,128)S(1)}, f32[2,4096]{1,0:T(2,128)S(1)}, f32[2,4096]{1,0:T(2,128)S(1)}) custom-call(bf16[256,512]{1,0:T(8,128)(2,1)S(1)} %solve.1.models_ref, s32[3,4096]{1,0:T(4,128)S(1)} %collective-permute-done.refs_0_, s32[3,4096]{1,0:T(4,128)S(1)} %collective-permute-done.1.refs_1_, s32[3,4096]{1,0:T(4,128)S(1)} %collective-permute-done.2.refs_2_), custom_call_target="tpu_custom_call" | custom-call | flops 3221225472 | bytes 1000000 | tf_op jit(solution)/shard_map/pick/pallas_call | solution.py:436
  44.3 1.7 %collective-permute-start.3 = (f32[2,4096]{1,0:T(2,128)S(1)}, f32[2,4096]{1,0:T(2,128)S(1)}, u32[]{:S(2)}, u32[]{:S(2)}) collective-permute-start(f32[2,4096]{1,0:T(2,128)S(1)} %get-tuple-element.8), channel_id=1, source_target_pairs={{0,3},{1,2},{2,1},{3,0},{4,7},{5,6},{6,5},{7,4},{8,11},{9,10},{10,... | collective-permute-start | bytes 98312 | tf_op jit(solution)/shard_map/ppermute | solution.py:456
  46.0 0.2 collective-permute-start.4
  46.1 0.1 collective-permute-start.5
  46.2 1.6 %pick.3 = f32[2,4096]{1,0:T(2,128)S(1)} custom-call(bf16[256,512]{1,0:T(8,128)(2,1)S(1)} %solve.1.models_ref, s32[3,4096]{1,0:T(4,128)S(1)} %copy-done), custom_call_target="tpu_custom_call" | custom-call | flops 1073741824 | bytes 1000000 | tf_op jit(solution)/shard_map/pick/pallas_call | solution.py:436
  47.8 0.0 collective-permute-done.3
  47.8 2.0 %collective-permute-done.4 = f32[2,4096]{1,0:T(2,128)S(1)} collective-permute-done((f32[2,4096]{1,0:T(2,128)S(1)}, f32[2,4096]{1,0:T(2,128)S(1)}, u32[]{:S(2)}, u32[]{:S(2)}) %collective-permute-start.4) | collective-permute-done | bytes 32800 | tf_op jit(solution)/shard_map/ppermute | solution.py:456
  49.9 0.0 collective-permute-done.5
  49.9 0.1 select_select_fusion.3
  49.9 0.7 %pad_maximum_fusion = f32[8,4096]{1,0:T(8,128)} fusion(f32[2,4096]{1,0:T(2,128)S(1)} %get-tuple-element.12, f32[2,4096]{1,0:T(2,128)S(1)} %get-tuple-element.13, f32[2,4096]{1,0:T(2,128)S(1)} %get-tuple-element.14, f32[2,4096]{1,0:T(2,128)S(1)} %get-tuple-element.11), kind=kLoop, calls=%fused_computation | loop fusion | flops 98304 | bytes 262144 | tf_op jit(solution)/shard_map/concatenate | solution.py:468
  (15 shorter events, 0.0 us)
Async XLA Ops:
  0.0 39.2 %collective-permute-start = (s32[3,4096]{1,0:T(4,128)}, s32[3,4096]{1,0:T(4,128)S(1)}, u32[]{:S(2)}, u32[]{:S(2)}) collective-permute-start(s32[3,4096]{1,0:T(4,128)} %refs_0_.2), channel_id=1, source_target_pairs={{0,1},{1,0},{2,3},{3,2},{4,5},{5,4},{6,7},{7,6},{8,9},{9,8},{10,11... | collective-permute-start | bytes 147464 | tf_op jit(solution)/shard_map/ppermute | solution.py:456
  0.5 38.8 %collective-permute-start.1 = (s32[3,4096]{1,0:T(4,128)}, s32[3,4096]{1,0:T(4,128)S(1)}, u32[]{:S(2)}, u32[]{:S(2)}) collective-permute-start(s32[3,4096]{1,0:T(4,128)} %refs_0_.2), channel_id=1, source_target_pairs={{0,2},{1,3},{2,0},{3,1},{4,6},{5,7},{6,4},{7,5},{8,10},{9,11},{10,... | collective-permute-start | bytes 147464 | tf_op jit(solution)/shard_map/ppermute | solution.py:456
  3.0 36.3 %collective-permute-start.2 = (s32[3,4096]{1,0:T(4,128)}, s32[3,4096]{1,0:T(4,128)S(1)}, u32[]{:S(2)}, u32[]{:S(2)}) collective-permute-start(s32[3,4096]{1,0:T(4,128)} %refs_0_.2), channel_id=1, source_target_pairs={{0,3},{1,2},{2,1},{3,0},{4,7},{5,6},{6,5},{7,4},{8,11},{9,10},{10,... | collective-permute-start | bytes 147464 | tf_op jit(solution)/shard_map/ppermute | solution.py:456
  3.1 0.7 %copy-start.1 = (f32[5,512]{1,0:T(8,128)S(1)}, f32[5,512]{1,0:T(8,128)}, u32[]{:S(2)}) copy-start(f32[5,512]{1,0:T(8,128)} %observed_ref.1) | copy-start | bytes 30724
  3.8 0.7 %copy-start.2 = (s32[8,512]{1,0:T(8,128)S(1)}, s32[8,512]{1,0:T(8,128)}, u32[]{:S(2)}) copy-start(s32[8,512]{1,0:T(8,128)} %counts_ref.1) | copy-start | bytes 49156
  4.6 0.7 %copy-start.3 = (s32[2,512]{1,0:T(2,128)S(1)}, s32[2,512]{1,0:T(2,128)}, u32[]{:S(2)}) copy-start(s32[2,512]{1,0:T(2,128)} %station_ref.1) | copy-start | bytes 12292
  5.2 0.7 %copy-start.4 = (f32[5]{0:T(128)S(1)}, f32[5]{0:T(128)}, u32[]{:S(2)}) copy-start(f32[5]{0:T(128)} %comp_ref.1) | copy-start | bytes 64
  5.9 1.7 %copy-start.5 = (f32[5,8,128,128]{3,2,1,0:T(8,128)S(1)}, f32[5,8,128,128]{3,2,1,0:T(8,128)}, u32[]{:S(2)}) copy-start(f32[5,8,128,128]{3,2,1,0:T(8,128)} %constant.30.clone.refs_0_) | copy-start | bytes 7864324
  7.6 0.9 %copy-start.6 = (bf16[3,128,256]{2,1,0:T(8,128)(2,1)S(1)}, bf16[3,128,256]{2,1,0:T(8,128)(2,1)}, u32[]{:S(2)}) copy-start(bf16[3,128,256]{2,1,0:T(8,128)(2,1)} %constant.36.clone.refs_6_) | copy-start | bytes 589828
  8.6 0.9 %copy-start.7 = (bf16[3,256,128]{2,1,0:T(8,128)(2,1)S(1)}, bf16[3,256,128]{2,1,0:T(8,128)(2,1)}, u32[]{:S(2)}) copy-start(bf16[3,256,128]{2,1,0:T(8,128)(2,1)} %constant.37.clone.refs_7_) | copy-start | bytes 589828
  9.5 0.9 %copy-start.8 = (bf16[256,256]{1,0:T(8,128)(2,1)S(1)}, bf16[256,256]{1,0:T(8,128)(2,1)}, u32[]{:S(2)}) copy-start(bf16[256,256]{1,0:T(8,128)(2,1)} %constant.32.clone.refs_2_) | copy-start | bytes 393220
  10.4 0.9 %copy-start.9 = (bf16[256,256]{1,0:T(8,128)(2,1)S(1)}, bf16[256,256]{1,0:T(8,128)(2,1)}, u32[]{:S(2)}) copy-start(bf16[256,256]{1,0:T(8,128)(2,1)} %constant.33.clone.refs_3_) | copy-start | bytes 393220
  11.3 0.9 %copy-start.10 = (bf16[256,256]{1,0:T(8,128)(2,1)S(1)}, bf16[256,256]{1,0:T(8,128)(2,1)}, u32[]{:S(2)}) copy-start(bf16[256,256]{1,0:T(8,128)(2,1)} %constant.39.clone.refs_9_) | copy-start | bytes 393220
  12.2 0.8 %copy-start.11 = (bf16[128,256]{1,0:T(8,128)(2,1)S(1)}, bf16[128,256]{1,0:T(8,128)(2,1)}, u32[]{:S(2)}) copy-start(bf16[128,256]{1,0:T(8,128)(2,1)} %constant.31.clone.refs_1_) | copy-start | bytes 196612
  13.0 0.8 %copy-start.12 = (bf16[256,128]{1,0:T(8,128)(2,1)S(1)}, bf16[256,128]{1,0:T(8,128)(2,1)}, u32[]{:S(2)}) copy-start(bf16[256,128]{1,0:T(8,128)(2,1)} %constant.34.clone.refs_4_) | copy-start | bytes 196612
  13.9 0.8 %copy-start.13 = (f32[128,128]{1,0:T(8,128)S(1)}, f32[128,128]{1,0:T(8,128)}, u32[]{:S(2)}) copy-start(f32[128,128]{1,0:T(8,128)} %constant.38.clone.refs_8_) | copy-start | bytes 196612
  14.7 0.8 %copy-start.14 = (bf16[2,32,256]{2,1,0:T(8,128)(2,1)S(1)}, bf16[2,32,256]{2,1,0:T(8,128)(2,1)}, u32[]{:S(2)}) copy-start(bf16[2,32,256]{2,1,0:T(8,128)(2,1)} %constant.35.clone.refs_5_) | copy-start | bytes 98308
  39.2 7.0 %copy-start = (s32[3,4096]{1,0:T(4,128)S(1)}, s32[3,4096]{1,0:T(4,128)}, u32[]{:S(2)}) copy-start(s32[3,4096]{1,0:T(4,128)} %refs_0_.2) | copy-start | bytes 147460
  44.3 3.5 %collective-permute-start.3 = (f32[2,4096]{1,0:T(2,128)S(1)}, f32[2,4096]{1,0:T(2,128)S(1)}, u32[]{:S(2)}, u32[]{:S(2)}) collective-permute-start(f32[2,4096]{1,0:T(2,128)S(1)} %get-tuple-element.8), channel_id=1, source_target_pairs={{0,3},{1,2},{2,1},{3,0},{4,7},{5,6},{6,5},{7,4},{8,11},{9,10},{10,... | collective-permute-start | bytes 98312 | tf_op jit(solution)/shard_map/ppermute | solution.py:456
  46.0 3.9 %collective-permute-start.4 = (f32[2,4096]{1,0:T(2,128)S(1)}, f32[2,4096]{1,0:T(2,128)S(1)}, u32[]{:S(2)}, u32[]{:S(2)}) collective-permute-start(f32[2,4096]{1,0:T(2,128)S(1)} %get-tuple-element.9), channel_id=1, source_target_pairs={{0,2},{1,3},{2,0},{3,1},{4,6},{5,7},{6,4},{7,5},{8,10},{9,11},{10,... | collective-permute-start | bytes 98312 | tf_op jit(solution)/shard_map/ppermute | solution.py:456
  46.1 3.7 %collective-permute-start.5 = (f32[2,4096]{1,0:T(2,128)S(1)}, f32[2,4096]{1,0:T(2,128)S(1)}, u32[]{:S(2)}, u32[]{:S(2)}) collective-permute-start(f32[2,4096]{1,0:T(2,128)S(1)} %get-tuple-element.10), channel_id=1, source_target_pairs={{0,1},{1,0},{2,3},{3,2},{4,5},{5,4},{6,7},{7,6},{8,9},{9,8},{10,11... | collective-permute-start | bytes 98312 | tf_op jit(solution)/shard_map/ppermute | solution.py:456

commit v5 on v4

--- a/solution.py
+++ b/solution.py
@@ -16,6 +16,7 @@
 LANES = 128
 TEAM = 4
 BLOCK = 4
+CHUNK = 512
 
 station_height = 2.0
 focusing = 0.1
@@ -83,13 +84,13 @@
     copies = deep * boots
     field_y = np.einsum("ab,yhl->ayhbl", np.eye(copies), base_y).reshape(LANES, 2 * LANES)
     station_y = np.einsum("b,yhl->yhbl", np.ones(copies), base_y).reshape(grid_y, 2 * LANES)
-    spread = np.zeros((6, deep, boots, grid_y, deep, boots, grid_y))
+    spread = np.zeros((5, deep, boots, grid_y, deep, boots, grid_y))
     for c in range(5):
         for b in range(boots):
             spread[c, 0, b, c, :, b, :] = 1
-    spread = spread.reshape(3, 2, LANES, LANES)
-    back = spread.transpose(0, 1, 3, 2).reshape(3, 2 * LANES, LANES)
-    spread = spread.transpose(0, 2, 1, 3).reshape(3, LANES, 2 * LANES)
+    spread = spread.reshape(5, LANES, LANES)
+    back = spread.transpose(0, 2, 1).reshape(5 * LANES, LANES)
+    spread = spread.transpose(1, 0, 2).reshape(LANES, 5 * LANES)
     same = np.einsum("ab,dc,yz->dayczb", np.eye(boots), np.ones((deep, deep)), np.ones((grid_y, grid_y)))
     same = same.transpose(0, 1, 2, 3, 5, 4).reshape(LANES, LANES)
     regroup = np.einsum("st,de,ab,yz->sdaybtez", *[np.eye(n) for n in (boots, deep, boots, grid_y)])
@@ -115,9 +116,11 @@
     return jnp.dot(a, b, preferred_element_type=F32)
 
 
-def solve_kernel(grid_y, boots, n_const, slot_ref, comp_ref, station_ref, observed_ref, counts_ref, *refs):
-    sources, out_ref = refs[:n_const], refs[n_const]
-    held = refs[n_const + 1 : 2 * n_const + 1]
+def solve_kernel(grid_y, boots, n_const, team, slot_ref, comp_ref, station_ref, observed_ref, counts_ref, *refs):
+    cell_refs, refs = refs[:team], refs[team:]
+    sources, refs = refs[:n_const], refs[n_const:]
+    out_refs, refs = refs[:team], refs[team:]
+    held, refs = refs[:n_const], refs[n_const:]
     (
         copied,
         pick_x,
@@ -139,7 +142,8 @@
         direction,
         penalty,
         applied,
-    ) = refs[2 * n_const + 1 :]
+        found_in,
+    ) = refs
     copies = [pltpu.make_async_copy(s, h, copied.at[i]) for i, (s, h) in enumerate(zip(sources, held))]
     first_step = pl.program_id(0) == 0
 
@@ -188,16 +192,17 @@
         copies[0].wait()
 
     def back_project():
-        q = values[...]
+        spreads = dot(values[...], spread_ref[...])
+        parts = []
+        for c in range(5):
+            e = spreads[:, c * LANES : (c + 1) * LANES]
+            parts += [e * pick_y[:, :LANES], e * pick_y[:, LANES:]]
+        spec = dot(pick_xt[...], jnp.concatenate(parts, axis=1).astype(BF))
         for c, (odd_x, odd_y) in enumerate(PARITY):
-            if c % 2 == 0:
-                spreads = dot(q, spread_ref[c // 2])
-            e = spreads[:, c % 2 * LANES : (c % 2 + 1) * LANES]
-            v = jnp.concatenate([e * pick_y[:, :LANES], e * pick_y[:, LANES:]], axis=1).astype(BF)
-            spec = dot(pick_xt[...], v)
             for hx in range(2):
                 for hy in range(2):
-                    part = spec[hx * GRID : (hx + 1) * GRID, hy * LANES : (hy + 1) * LANES]
+                    lane = (2 * c + hy) * LANES
+                    part = spec[hx * GRID : (hx + 1) * GRID, lane : lane + LANES]
                     spec_q[c, hx, hy] = -part if (odd_x * hx + odd_y * hy) % 2 else part
 
         for block in blocks:
@@ -213,18 +218,20 @@
                             for c in range(5):
                                 term = t[c] * q[c][hy ^ PARITY[c][1]]
                                 total = term if total is None else total + term
-                            spec_g[z, to, hy * LANES : (hy + 1) * LANES] = total.astype(BF)
-            for z in block:
-                along_x = dot(base_x_ref[...], spec_g[z]).astype(BF)
-                applied[z] = dot(along_x, field_yt_ref[...])
+                            lane = (2 * z + hy) * LANES
+                            spec_g[to, lane : lane + LANES] = total.astype(BF)
+            along_x = dot(base_x_ref[...], spec_g[:, block[0] * 2 * LANES : (block[-1] + 1) * 2 * LANES]).astype(BF)
+            along_x = jnp.concatenate([along_x[:, i * 2 * LANES : (i + 1) * 2 * LANES] for i in range(BLOCK)], axis=0)
+            applied[block[0] : block[-1] + 1] = dot(along_x, field_yt_ref[...]).reshape(BLOCK, GRID, LANES)
 
     def predict():
         for block in blocks:
             r = residual[block[0] : block[-1] + 1].reshape(BLOCK * GRID, LANES).astype(BF)
             y = dot(jnp.concatenate([r, r], axis=1), field_y2_ref[...]).astype(BF)
-            for i, z in enumerate(block):
-                part = y[i * GRID : (i + 1) * GRID]
-                spec_f[z] = dot(base_xt2_ref[...], jnp.concatenate([part, part], axis=0))
+            y = jnp.concatenate([y[i * GRID : (i + 1) * GRID] for i in range(BLOCK)], axis=1)
+            spec_f[:, block[0] * 2 * LANES : (block[-1] + 1) * 2 * LANES] = dot(
+                base_xt2_ref[...], jnp.concatenate([y, y], axis=0)
+            )
             for row in range(0, GRID, 16):
                 done = []
                 for sub in range(row, row + 16, 8):
@@ -235,7 +242,8 @@
                             [[spec_q[c, hx, hy, at[0], :] for hy in range(2)] for hx in range(2)] for c in range(5)
                         ]
                     for z in block:
-                        f = [[spec_f[z, at[hx], hy * LANES : (hy + 1) * LANES] for hy in range(2)] for hx in range(2)]
+                        lane = 2 * z * LANES
+                        f = [[spec_f[at[hx], lane + hy * LANES : lane + (hy + 1) * LANES] for hy in range(2)] for hx in range(2)]
                         for c, (odd_x, odd_y) in enumerate(PARITY):
                             t = table_ref[c, z, at[0], :]
                             for hx in range(2):
@@ -256,23 +264,17 @@
                         for hy in range(2):
                             part = jnp.concatenate([done[sub][c][hx][hy] for sub in range(2)], axis=0)
                             part = -part if (odd_x * hx + odd_y * hy) % 2 else part
-                            spec_i[c, hx * GRID + row : hx * GRID + row + 16, hy * LANES : (hy + 1) * LANES] = (
-                                part.astype(BF)
-                            )
-
-        total = None
-        pair = []
+                            lane = (2 * c + hy) * LANES
+                            spec_i[hx * GRID + row : hx * GRID + row + 16, lane : lane + LANES] = part.astype(BF)
+
+        picked = dot(pick_x[...], spec_i[...])
+        parts = []
         for c in range(5):
-            part = dot(pick_x[...], spec_i[c]) * pick_y[...]
-            pair.append((part[:, :LANES] + part[:, LANES:]).astype(BF))
-            if c % 2 or c == 4:
-                if c == 4:
-                    part = dot(pair[0], back_ref[2, :LANES, :])
-                else:
-                    part = dot(jnp.concatenate(pair, axis=1), back_ref[c // 2])
-                total = part if total is None else total + part
-                pair = []
-        return total
+            lane = 2 * c * LANES
+            cosines = picked[:, lane : lane + LANES] * pick_y[:, :LANES]
+            sines = picked[:, lane + LANES : lane + 2 * LANES] * pick_y[:, LANES:]
+            parts.append((cosines + sines).astype(BF))
+        return dot(jnp.concatenate(parts, axis=1), back_ref[...])
 
     def fold(a):
         return jnp.sum(a.reshape(a.shape[0] // 8, 8, LANES), axis=0)
@@ -345,30 +347,54 @@
         if boots > 1:
             m = dot(m, regroup_ref[...]).astype(BF)
         for b in range(boots):
-            out_ref[b * GRID : (b + 1) * GRID, group * LANES : (group + 1) * LANES] = (
+            found_in[b * GRID : (b + 1) * GRID, group * LANES : (group + 1) * LANES] = (
                 m[:, b * LANES : (b + 1) * LANES]
             )
 
-
-def solve(slot, comp_weight, station_index, observed, counts, mine, grid_y):
+    @pl.loop(0, cell_refs[0].shape[1] // CHUNK)
+    def _(step):
+        at = pl.ds(pl.multiple_of(step * CHUNK, CHUNK), CHUNK)
+        for cell_ref, out_ref in zip(cell_refs, out_refs):
+            cells = cell_ref[:, at]
+            place = cells.astype(F32)
+            wide = lambda row, rows: jnp.broadcast_to(row, (rows, CHUNK)).astype(BF)
+            y_row = wide(place[1:2], grid_y)
+            z_row = wide(place[2:3], grid_y)
+            here_y = lax.broadcasted_iota(jnp.int32, (grid_y, CHUNK), 0).astype(F32).astype(BF) == y_row
+            here_y = jnp.where(here_y, jnp.ones_like(y_row), jnp.zeros_like(y_row))
+            chosen = jnp.concatenate(
+                [jnp.where(z_row == jnp.full_like(z_row, z), here_y, jnp.zeros_like(here_y)) for z in range(DEPTHS)],
+                axis=0,
+            )
+            at_x = lax.broadcasted_iota(jnp.int32, (GRID, CHUNK), 0) == cells[0:1]
+            found = dot(found_in[...], chosen)
+            parts = [
+                jnp.sum(jnp.where(at_x, found[b * GRID : (b + 1) * GRID], 0.0), axis=0, keepdims=True)
+                for b in range(boots)
+            ]
+            out_ref[0, :, at] = jnp.concatenate(parts, axis=0).astype(BF)
+
+
+def solve(slot, comp_weight, station_index, observed, counts, cells, mine, grid_y):
     boots = min(mine, LANES // grid_y)
     slabs = DEPTHS * grid_y * boots // LANES
     stations = station_index.shape[1]
+    count = cells[0].shape[1]
     consts = [jnp.asarray(v) for v in constants(grid_y, boots).values()]
     vmem = pltpu.VMEM
     whole = lambda a: pl.BlockSpec(a.shape, lambda i, n=a.ndim: (0,) * n)
     smem = pl.BlockSpec(memory_space=pltpu.SMEM)
     field = vmem((slabs, GRID, LANES), F32)
     at_stations = vmem((stations, LANES), F32)
-    inputs = [station_index, observed, counts]
+    inputs = [station_index, observed, counts, *cells]
     return pl.pallas_call(
-        functools.partial(solve_kernel, grid_y, boots, len(consts)),
-        out_shape=jax.ShapeDtypeStruct((mine * GRID, DEPTHS * grid_y), BF),
+        functools.partial(solve_kernel, grid_y, boots, len(consts), len(cells)),
+        out_shape=[jax.ShapeDtypeStruct((mine // boots, boots, count), BF)] * len(cells),
         grid=(mine // boots,),
         in_specs=[smem, smem]
         + [whole(a) for a in inputs]
-        + [pl.BlockSpec(memory_space=pltpu.HBM) for _ in consts],
-        out_specs=pl.BlockSpec((boots * GRID, DEPTHS * grid_y), lambda i: (i, 0)),
+        + [pl.BlockSpec(memory_space=pl.ANY) for _ in consts],
+        out_specs=[pl.BlockSpec((1, boots, count), lambda i: (i, 0, 0))] * len(cells),
         scratch_shapes=[vmem(a.shape, a.dtype) for a in consts]
         + [
             pltpu.SemaphoreType.DMA((len(consts),)),
@@ -383,67 +409,20 @@
             vmem((LANES, stations), F32),
             vmem((8, LANES), F32),
             vmem((5, 2, 2, GRID, LANES), F32),
-            vmem((5, 2 * GRID, 2 * LANES), BF),
-            vmem((slabs, 2 * GRID, 2 * LANES), F32),
-            vmem((slabs, 2 * GRID, 2 * LANES), BF),
+            vmem((2 * GRID, 10 * LANES), BF),
+            vmem((2 * GRID, slabs * 2 * LANES), F32),
+            vmem((2 * GRID, slabs * 2 * LANES), BF),
             field,
             field,
             field,
             field,
             field,
+            vmem((boots * GRID, DEPTHS * grid_y), BF),
         ],
-        compiler_params=pltpu.CompilerParams(vmem_limit_bytes=40 * 1024 * 1024),
+        compiler_params=pltpu.CompilerParams(vmem_limit_bytes=60 * 1024 * 1024),
         cost_estimate=pl.CostEstimate(flops=10**10, bytes_accessed=10**7, transcendentals=0),
         name="solve",
     )(slot, comp_weight, *inputs, *consts)
-
-
-def pick_kernel(grid_y, boots, count, models_ref, *refs):
-    chunk = 512
-
-    def pick_chunk(cell_ref, out_ref, at):
-        cells = cell_ref[:, at]
-        place = cells.astype(F32)
-        wide = lambda row, rows: jnp.broadcast_to(row, (rows, chunk)).astype(BF)
-        y_row = wide(place[1:2], grid_y)
-        z_row = wide(place[2:3], grid_y)
-        here_y = lax.broadcasted_iota(jnp.int32, (grid_y, chunk), 0).astype(F32).astype(BF) == y_row
-        here_y = jnp.where(here_y, jnp.ones_like(y_row), jnp.zeros_like(y_row))
-        chosen = jnp.concatenate(
-            [jnp.where(z_row == jnp.full_like(z_row, z), here_y, jnp.zeros_like(here_y)) for z in range(DEPTHS)],
-            axis=0,
-        )
-        at_x = lax.broadcasted_iota(jnp.int32, (GRID, chunk), 0) == cells[0:1]
-        found = dot(models_ref[...], chosen)
-        for b in range(boots):
-            part = jnp.where(at_x, found[b * GRID : (b + 1) * GRID], 0.0)
-            out_ref[b : b + 1, at] = jnp.sum(part, axis=0, keepdims=True)
-
-    per = max(1, 4 // count)
-
-    @pl.loop(0, refs[0].shape[1] // (per * chunk))
-    def _(step):
-        for i in range(per):
-            at = pl.ds(pl.multiple_of((step * per + i) * chunk, chunk), chunk)
-            for cell_ref, out_ref in zip(refs[:count], refs[count:]):
-                pick_chunk(cell_ref, out_ref, at)
-
-
-def pick(models, cells, grid_y):
-    boots = models.shape[0] // GRID
-    count = cells[0].shape[1]
-    vmem = pl.BlockSpec(memory_space=pltpu.VMEM)
-    return pl.pallas_call(
-        functools.partial(pick_kernel, grid_y, boots, len(cells)),
-        out_shape=[jax.ShapeDtypeStruct((boots, count), F32)] * len(cells),
-        in_specs=[vmem] * (1 + len(cells)),
-        out_specs=[vmem] * len(cells),
-        compiler_params=pltpu.CompilerParams(vmem_limit_bytes=40 * 1024 * 1024),
-        cost_estimate=pl.CostEstimate(
-            flops=2 * models.size * count * len(cells), bytes_accessed=10**6, transcendentals=0
-        ),
-        name="pick",
-    )(models, *cells)
 
 
 def local(wide, cell_index, station_index, observed, comp_weight, counts):
@@ -455,17 +434,16 @@
     def swap(a, k):
         return lax.ppermute(a, "wide", [(i, i ^ k) for i in range(wide)])
 
-    theirs = [swap(cell_index, k) for k in range(1, team)]
-    models = solve(slot.reshape(1), comp_weight, station_index, observed, counts, boots // team, grid_y)
-    sent = [swap(a, k + 1) for k, a in enumerate(pick(models, theirs, grid_y))] if theirs else []
-    got = [*pick(models, [cell_index], grid_y), *sent]
+    cells = [cell_index] + [swap(cell_index, k) for k in range(1, team)]
+    found = solve(slot.reshape(1), comp_weight, station_index, observed, counts, cells, boots // team, grid_y)
+    got = [found[0]] + [swap(found[k], k) for k in range(1, team)]
     blocks = []
     for member in range(team):
         block = got[member]
         for other in range(1, team):
             block = jnp.where(slot == other, got[member ^ other], block)
         blocks.append(block)
-    return jnp.concatenate(blocks, axis=0)
+    return jnp.concatenate(blocks, axis=0).reshape(boots, -1).astype(F32)
 
 
 def solution(mesh):

time: 51.3 us -> 45.2 us (0.88)
  local copies, waits for them, and re-layouts: 12.4 us -> 1.37 us
  waiting for transfers between devices: 2.06 us -> 7.48 us
    unnamed x30 -> x6, local copies, waits for them, and re-layouts: 12.4 us -> 0.62 us
    pallas_call x2 -> x0, Pallas kernels: 6.58 us -> none  [pick(): pl.pallas_call(functools.partial(pick_kernel, grid_y, boots, len(cells)),...]
    pallas_call x1, Pallas kernels: 23.7 us -> 30.1 us  [solve(): pl.pallas_call(functools.partial(solve_kernel, grid_y, boots, len(consts)...]
    ppermute x6, waiting for transfers between devices: 2.06 us -> 7.48 us  [swap(): return lax.ppermute(a, 'wide', [(i, i ^ k) for i in range(wide)])]
    convert_element_type x0 -> x1, local copies, waits for them, and re-layouts: none -> 0.75 us  [local(): return jnp.concatenate(blocks, axis=0).reshape(boots, -1).astype(F32)]
    select_n x1, other arithmetic: 0.06 us -> 0.8 us  [local(): block = jnp.where(slot == other, got[member ^ other], block)]
    concatenate x1 -> x0, other arithmetic: 0.72 us -> none  [local(): return jnp.concatenate(blocks, axis=0)]
  transfers between devices with their start and end apart: 6 -> 6, of which waited for: 1 -> 4; matrix products, arithmetic and copies ran while one was open for 0% -> 0% of each run, Pallas kernels for 50% -> 0%
where the time goes in v5:
time: 45.2 us; the launch traced here: 44.9 us
  Pallas kernels  30.1 us (67%)
  waiting for transfers between devices  7.48 us (17%)
  starting transfers between devices  5.04 us (11%)
  local copies, waits for them, and re-layouts  1.37 us (3%)
  other arithmetic  0.9 us (2%)
    pallas_call x1, Pallas kernels, solve(): pl.pallas_call(functools.partial(solve_kernel, grid_y, boots, len(consts)...  30.1 us
    ppermute x6, waiting for transfers between devices, swap(): return lax.ppermute(a, 'wide', [(i, i ^ k) for i in range(wide)])  7.48 us
    ppermute x6, starting transfers between devices, swap(): return lax.ppermute(a, 'wide', [(i, i ^ k) for i in range(wide)])  5.04 us
  transfers between devices with their start and end apart: 6, of which 4 were waited for; matrix products, arithmetic and copies ran while one was open for 0% of the time, Pallas kernels for 0%

profile of v5, /device:TPU:0, one launch (start us, length us, event | category | flops | bytes accessed | tf_op | source)
XLA Modules:
  0.0 44.9 jit_solution(11929611442210925376)
XLA Ops:
  0.0 0.5 %collective-permute-start = (s32[3,4096]{1,0:T(4,128)}, s32[3,4096]{1,0:T(4,128)S(1)}, u32[]{:S(2)}, u32[]{:S(2)}) collective-permute-start(s32[3,4096]{1,0:T(4,128)} %refs_0_.1), channel_id=1, source_target_pairs={{0,1},{1,0},{2,3},{3,2},{4,5},{5,4},{6,7},{7,6},{8,9},{9,8},{10,11... | collective-permute-start | bytes 147464 | tf_op jit(solution)/shard_map/ppermute | solution.py:435
  0.5 2.5 %collective-permute-start.1 = (s32[3,4096]{1,0:T(4,128)}, s32[3,4096]{1,0:T(4,128)S(1)}, u32[]{:S(2)}, u32[]{:S(2)}) collective-permute-start(s32[3,4096]{1,0:T(4,128)} %refs_0_.1), channel_id=1, source_target_pairs={{0,2},{1,3},{2,0},{3,1},{4,6},{5,7},{6,4},{7,5},{8,10},{9,11},{10,... | collective-permute-start | bytes 147464 | tf_op jit(solution)/shard_map/ppermute | solution.py:435
  3.0 0.1 collective-permute-start.2
  3.1 0.0 collective-permute-done.refs_1_
  3.1 0.0 copy-start
  3.1 2.8 %collective-permute-done.1.refs_2_ = s32[3,4096]{1,0:T(4,128)S(1)} collective-permute-done((s32[3,4096]{1,0:T(4,128)}, s32[3,4096]{1,0:T(4,128)S(1)}, u32[]{:S(2)}, u32[]{:S(2)}) %collective-permute-start.1) | collective-permute-done | bytes 49184 | tf_op jit(solution)/shard_map/ppermute | solution.py:435
  5.9 0.0 copy-start.1
  5.9 1.3 %collective-permute-done.2.refs_3_ = s32[3,4096]{1,0:T(4,128)S(1)} collective-permute-done((s32[3,4096]{1,0:T(4,128)}, s32[3,4096]{1,0:T(4,128)S(1)}, u32[]{:S(2)}, u32[]{:S(2)}) %collective-permute-start.2) | collective-permute-done | bytes 49184 | tf_op jit(solution)/shard_map/ppermute | solution.py:435
  7.3 0.0 copy-start.2
  7.3 0.0 copy-done
  7.3 0.0 copy-done.1
  7.3 0.6 %copy-done.2 = s32[3,4096]{1,0:T(4,128)} copy-done((s32[3,4096]{1,0:T(4,128)}, s32[3,4096]{1,0:T(4,128)S(1)}, u32[]{:S(2)}) %copy-start.2) | copy-done | bytes 49176
  7.9 30.1 %solve.1 = (bf16[1,2,4096]{2,1,0:T(2,128)(2,1)}, bf16[1,2,4096]{2,1,0:T(2,128)(2,1)}, bf16[1,2,4096]{2,1,0:T(2,128)(2,1)}, bf16[1,2,4096]{2,1,0:T(2,128)(2,1)}) custom-call(s32[1]{0:T(128)} %bitcast.slot_ref, f32[5]{0:T(128)} %comp_ref.1, s32[2,512]{1,0:T(2,128)} %station_ref.1, f32[5,512]{1,0:T(8,128)} %observed_ref.1, s32[8,512]{1,0:T(8,128)} %counts_ref.1, ...), custom_call_target="tpu_custom_call" | custom-call | flops 10000000000 | bytes 10000000 | tf_op jit(solution)/shard_map/solve/pallas_call | solution.py:390
  38.0 1.3 %collective-permute-start.3 = (bf16[1,2,4096]{2,1,0:T(2,128)(2,1)}, bf16[1,2,4096]{2,1,0:T(2,128)(2,1)S(1)}, u32[]{:S(2)}, u32[]{:S(2)}) collective-permute-start(bf16[1,2,4096]{2,1,0:T(2,128)(2,1)} %get-tuple-element.9), channel_id=1, source_target_pairs={{0,3},{1,2},{2,1},{3,0},{4,7},{5,6},{6,5},{7,4},{8,11},{9,10},{10,... | collective-permute-start | bytes 49160 | tf_op jit(solution)/shard_map/ppermute | solution.py:435
  39.3 0.5 %collective-permute-start.4 = (bf16[1,2,4096]{2,1,0:T(2,128)(2,1)}, bf16[1,2,4096]{2,1,0:T(2,128)(2,1)S(1)}, u32[]{:S(2)}, u32[]{:S(2)}) collective-permute-start(bf16[1,2,4096]{2,1,0:T(2,128)(2,1)} %get-tuple-element.10), channel_id=1, source_target_pairs={{0,2},{1,3},{2,0},{3,1},{4,6},{5,7},{6,4},{7,5},{8,10},{9,11},{10,... | collective-permute-start | bytes 49160 | tf_op jit(solution)/shard_map/ppermute | solution.py:435
  39.9 0.1 collective-permute-start.5
  39.9 1.5 %collective-permute-done.3 = bf16[1,2,4096]{2,1,0:T(2,128)(2,1)S(1)} collective-permute-done((bf16[1,2,4096]{2,1,0:T(2,128)(2,1)}, bf16[1,2,4096]{2,1,0:T(2,128)(2,1)S(1)}, u32[]{:S(2)}, u32[]{:S(2)}) %collective-permute-start.3) | collective-permute-done | bytes 16416 | tf_op jit(solution)/shard_map/ppermute | solution.py:435
  41.5 1.8 %collective-permute-done.4 = bf16[1,2,4096]{2,1,0:T(2,128)(2,1)S(1)} collective-permute-done((bf16[1,2,4096]{2,1,0:T(2,128)(2,1)}, bf16[1,2,4096]{2,1,0:T(2,128)(2,1)S(1)}, u32[]{:S(2)}, u32[]{:S(2)}) %collective-permute-start.4) | collective-permute-done | bytes 16416 | tf_op jit(solution)/shard_map/ppermute | solution.py:435
  43.3 0.0 collective-permute-done.5
  43.3 0.8 %broadcast_select_fusion.11 = (bf16[1,2,4096]{2,1,0:T(2,128)(2,1)S(1)}, bf16[1,2,4096]{2,1,0:T(2,128)(2,1)S(1)}, bf16[1,2,4096]{2,1,0:T(2,128)(2,1)S(1)}, bf16[1,2,4096]{2,1,0:T(2,128)(2,1)S(1)}) fusion(bf16[1,2,4096]{2,1,0:T(2,128)(2,1)S(1)} %collective-permute-done.3, pred[]{:T(512)S(6)} %eq.6, bf16[1,2,4096]{2,1,0:T(2,128)(2,1)S(1)} %collective-permute-done.4, ...), kind=kLoop, calls=%fused_computation.12 | loop fusion | flops 98304 | bytes 131075 | tf_op jit(solution)/shard_map/jit(_where)/select_n | solution.py:444
  44.1 0.1 maximum_convert_fusion
  44.2 0.7 %reshape.7 = f32[8,4096]{1,0:T(8,128)} reshape(f32[4,2,4096]{2,1,0:T(2,128)S(1)} %maximum_convert_fusion) | data formatting | bytes 262144 | tf_op jit(solution)/shard_map/convert_element_type | solution.py:446
Async XLA Ops:
  0.0 3.1 %collective-permute-start = (s32[3,4096]{1,0:T(4,128)}, s32[3,4096]{1,0:T(4,128)S(1)}, u32[]{:S(2)}, u32[]{:S(2)}) collective-permute-start(s32[3,4096]{1,0:T(4,128)} %refs_0_.1), channel_id=1, source_target_pairs={{0,1},{1,0},{2,3},{3,2},{4,5},{5,4},{6,7},{7,6},{8,9},{9,8},{10,11... | collective-permute-start | bytes 147464 | tf_op jit(solution)/shard_map/ppermute | solution.py:435
  0.5 5.5 %collective-permute-start.1 = (s32[3,4096]{1,0:T(4,128)}, s32[3,4096]{1,0:T(4,128)S(1)}, u32[]{:S(2)}, u32[]{:S(2)}) collective-permute-start(s32[3,4096]{1,0:T(4,128)} %refs_0_.1), channel_id=1, source_target_pairs={{0,2},{1,3},{2,0},{3,1},{4,6},{5,7},{6,4},{7,5},{8,10},{9,11},{10,... | collective-permute-start | bytes 147464 | tf_op jit(solution)/shard_map/ppermute | solution.py:435
  3.0 4.3 %collective-permute-start.2 = (s32[3,4096]{1,0:T(4,128)}, s32[3,4096]{1,0:T(4,128)S(1)}, u32[]{:S(2)}, u32[]{:S(2)}) collective-permute-start(s32[3,4096]{1,0:T(4,128)} %refs_0_.1), channel_id=1, source_target_pairs={{0,3},{1,2},{2,1},{3,0},{4,7},{5,6},{6,5},{7,4},{8,11},{9,10},{10,... | collective-permute-start | bytes 147464 | tf_op jit(solution)/shard_map/ppermute | solution.py:435
  3.1 4.1 %copy-start = (s32[3,4096]{1,0:T(4,128)}, s32[3,4096]{1,0:T(4,128)S(1)}, u32[]{:S(2)}) copy-start(s32[3,4096]{1,0:T(4,128)S(1)} %collective-permute-done.refs_1_) | copy-start | bytes 147460
  5.9 1.3 %copy-start.1 = (s32[3,4096]{1,0:T(4,128)}, s32[3,4096]{1,0:T(4,128)S(1)}, u32[]{:S(2)}) copy-start(s32[3,4096]{1,0:T(4,128)S(1)} %collective-permute-done.1.refs_2_) | copy-start | bytes 147460
  7.3 0.6 %copy-start.2 = (s32[3,4096]{1,0:T(4,128)}, s32[3,4096]{1,0:T(4,128)S(1)}, u32[]{:S(2)}) copy-start(s32[3,4096]{1,0:T(4,128)S(1)} %collective-permute-done.2.refs_3_) | copy-start | bytes 147460
  38.0 3.4 %collective-permute-start.3 = (bf16[1,2,4096]{2,1,0:T(2,128)(2,1)}, bf16[1,2,4096]{2,1,0:T(2,128)(2,1)S(1)}, u32[]{:S(2)}, u32[]{:S(2)}) collective-permute-start(bf16[1,2,4096]{2,1,0:T(2,128)(2,1)} %get-tuple-element.9), channel_id=1, source_target_pairs={{0,3},{1,2},{2,1},{3,0},{4,7},{5,6},{6,5},{7,4},{8,11},{9,10},{10,... | collective-permute-start | bytes 49160 | tf_op jit(solution)/shard_map/ppermute | solution.py:435
  39.3 3.9 %collective-permute-start.4 = (bf16[1,2,4096]{2,1,0:T(2,128)(2,1)}, bf16[1,2,4096]{2,1,0:T(2,128)(2,1)S(1)}, u32[]{:S(2)}, u32[]{:S(2)}) collective-permute-start(bf16[1,2,4096]{2,1,0:T(2,128)(2,1)} %get-tuple-element.10), channel_id=1, source_target_pairs={{0,2},{1,3},{2,0},{3,1},{4,6},{5,7},{6,4},{7,5},{8,10},{9,11},{10,... | collective-permute-start | bytes 49160 | tf_op jit(solution)/shard_map/ppermute | solution.py:435
  39.9 3.4 %collective-permute-start.5 = (bf16[1,2,4096]{2,1,0:T(2,128)(2,1)}, bf16[1,2,4096]{2,1,0:T(2,128)(2,1)S(1)}, u32[]{:S(2)}, u32[]{:S(2)}) collective-permute-start(bf16[1,2,4096]{2,1,0:T(2,128)(2,1)} %get-tuple-element.11), channel_id=1, source_target_pairs={{0,1},{1,0},{2,3},{3,2},{4,5},{5,4},{6,7},{7,6},{8,9},{9,8},{10,11... | collective-permute-start | bytes 49160 | tf_op jit(solution)/shard_map/ppermute | solution.py:435

commit v6 on v4

v6 whole, which is shorter than its diff:
```python
import functools

import jax
import jax.numpy as jnp
import ml_dtypes
import numpy as np
from jax import lax
from jax.experimental import pallas as pl
from jax.experimental.pallas import tpu as pltpu
from jax.sharding import PartitionSpec as P

IRLS = 2
CG_STEPS = 2
GRID = 128
DEPTHS = 16
LANES = 128
TEAM = 4
BLOCK = 4
CHUNK = 512
ROWS = 32

station_height = 2.0
focusing = 0.1
damping = 0.0002

PARITY = ((0, 0), (1, 1), (1, 0), (0, 0), (0, 1))
BF = jnp.bfloat16
F32 = jnp.float32


def offset_table(grid_y):
    one = np.float32
    dx = np.arange(GRID, dtype=one)[:, None, None]
    dy = np.arange(grid_y, dtype=one)[None, :, None]
    dz = (np.arange(DEPTHS, dtype=one) + one(0.5) + one(station_height))[None, None, :]
    radius2 = dx * dx + dy * dy + dz * dz
    strength = one(1) / (radius2 * radius2 * np.sqrt(radius2))
    three = one(3)
    kinds = [
        (three * dx * dx - radius2) * strength,
        three * dx * dy * strength,
        three * dx * dz * strength,
        (three * dy * dy - radius2) * strength,
        three * dy * dz * strength,
    ]
    return [k.astype(ml_dtypes.bfloat16).astype(np.float64) for k in kinds]


def angles(size):
    return 2 * np.pi * np.outer(np.arange(size), np.arange(size) + 0.5) / (2 * size)


def basis(size):
    return np.concatenate([np.cos(angles(size)), np.sin(angles(size))], axis=1)


def spectrum(values, odd, size):
    if odd:
        trig = 2 * np.sin(angles(size))
    else:
        trig = np.cos(angles(size)) * np.where(np.arange(size) == 0, 1, 2)[:, None]
    return np.tensordot(trig.T / size, values, axes=(1, 0))


def split(matrix):
    high = matrix.astype(ml_dtypes.bfloat16)
    low = (matrix - high.astype(np.float64)).astype(ml_dtypes.bfloat16)
    return high, low


class Layout:
    def __init__(self, parts):
        self.at = {}
        row = 0
        for name, rows in parts:
            self.at[name] = (row, rows)
            row += rows
        self.rows = row


def layout(grid_y, boots):
    slabs = DEPTHS * grid_y * boots // LANES
    return Layout(
        [
            ("base_x", GRID),
            ("base_xt2", 2 * GRID),
            ("field_y2", 2 * LANES),
            ("field_yt", 2 * LANES),
            ("station_y2", 2 * grid_y),
            ("spread", 3 * LANES),
            ("back", 5 * LANES),
            ("same", LANES),
            ("regroup", boots * LANES * max(1, boots // 2)),
            ("table", 5 * slabs // 2 * GRID),
        ]
    )


@functools.lru_cache(maxsize=None)
def constants(grid_y, boots):
    deep = LANES // grid_y // boots
    slabs = DEPTHS // deep
    table = []
    for values, (odd_x, odd_y) in zip(offset_table(grid_y), PARITY):
        t = spectrum(values, odd_x, GRID)
        t = np.moveaxis(spectrum(np.moveaxis(t, 1, 0), odd_y, grid_y), 0, 1)
        t = np.moveaxis(t, 2, 0).reshape(slabs, deep, GRID, 1, grid_y).transpose(0, 2, 1, 3, 4)
        table.append(np.tile(t, (1, 1, 1, boots, 1)).reshape(slabs, GRID, LANES))
    table = np.stack(table).reshape(5, slabs // 2, 2, GRID, LANES).transpose(0, 1, 3, 2, 4)

    base_x = basis(GRID)
    base_y = basis(grid_y).reshape(grid_y, 2, grid_y)
    copies = deep * boots
    field_y = np.einsum("ab,yhl->ayhbl", np.eye(copies), base_y).reshape(LANES, 2 * LANES)
    station_y = np.einsum("b,yhl->yhbl", np.ones(copies), base_y).reshape(grid_y, 2 * LANES)
    spread = np.zeros((6, deep, boots, grid_y, deep, boots, grid_y))
    for c in range(5):
        for b in range(boots):
            spread[c, 0, b, c, :, b, :] = 1
    spread = spread.reshape(6, LANES, LANES)
    back = spread[:5].transpose(0, 2, 1).reshape(5 * LANES, LANES)
    spread = spread.reshape(3, 2, LANES, LANES).transpose(0, 2, 1, 3)
    same = np.einsum("ab,dc,yz->daycbz", np.eye(boots), np.ones((deep, deep)), np.ones((grid_y, grid_y)))
    same = same.reshape(LANES, LANES)
    regroup = np.einsum("st,de,ab,yz->sdaybtez", *[np.eye(n) for n in (boots, deep, boots, grid_y)])
    regroup = regroup.reshape(boots * LANES, boots * LANES)
    if boots > 2:
        regroup = np.concatenate(np.split(regroup, boots // 2, axis=1), axis=0)
    y_high, y_low = split(field_y)
    x_high, x_low = split(base_x.T)
    parts = dict(
        base_x=base_x,
        base_xt2=np.concatenate([x_high, x_low], axis=1),
        field_y2=np.concatenate([y_high, y_low], axis=0),
        field_yt=field_y.T,
        station_y2=np.concatenate(split(station_y)),
        spread=spread.reshape(3 * LANES, 2 * LANES),
        back=back,
        same=same,
        regroup=regroup,
        table=table.reshape(-1, 2 * LANES),
    )
    where = layout(grid_y, boots)
    whole = np.zeros((max(where.rows, 1 << 14), 2 * LANES), ml_dtypes.bfloat16)
    for name, (row, rows) in where.at.items():
        part = parts[name].astype(ml_dtypes.bfloat16)
        assert part.shape[0] == rows
        whole[row : row + rows, : part.shape[1]] = part
    return whole


def dot(a, b):
    return jnp.dot(a, b, preferred_element_type=F32)


def solve_kernel(
    grid_y,
    boots,
    slot_ref,
    comp_ref,
    station_ref,
    observed_ref,
    counts_ref,
    source,
    out_ref,
    const,
    copied,
    pick_x,
    pick_xt,
    pick_y,
    weights,
    data,
    pred,
    image,
    values,
    rows,
    sums,
    spread_out,
    spec_q,
    spec_i,
    spec_f,
    spec_g,
    picked_in,
    models,
    residual,
    direction,
    penalty,
    applied,
):
    deep = LANES // grid_y // boots
    slabs = DEPTHS // deep
    where = layout(grid_y, boots)
    split_row = where.at["table"][0]
    copies = [
        pltpu.make_async_copy(source.at[a:b], const.at[a:b], copied.at[i])
        for i, (a, b) in enumerate([(0, split_row), (split_row, where.rows)])
    ]
    first_step = pl.program_id(0) == 0

    @pl.when(first_step)
    def _():
        for copy in copies:
            copy.start()

    def held(name, width=2 * LANES):
        row, count = where.at[name]
        return const[row : row + count, :width]

    def table(c, z, at):
        row = split_row + (c * (slabs // 2) + z // 2) * GRID
        return const[row + at.start : row + at.stop, z % 2 * LANES : (z % 2 + 1) * LANES]

    stations = station_ref.shape[1]
    first = (slot_ref[0] * pl.num_programs(0) + pl.program_id(0)) * boots
    blocks = [list(range(z, z + BLOCK)) for z in range(0, slabs, BLOCK)]
    pieces = [(z, slice(row, row + ROWS)) for z in range(slabs) for row in range(0, GRID, ROWS)]

    rows[...] = jnp.zeros_like(rows)
    for b in range(boots):
        rows[b * grid_y : b * grid_y + 5, :] = observed_ref[...]
    data[...] = jnp.transpose(rows[...])
    for b in range(boots):
        count = counts_ref[pl.ds(first + b, 1), :].astype(F32)
        for c in range(5):
            rows[b * grid_y + c : b * grid_y + c + 1, :] = count * comp_ref[c]
    weights[...] = jnp.transpose(rows[...])
    values[...] = (weights[...] * data[...]).astype(BF)

    station_x = station_ref[0:1, :]
    station_y = station_ref[1:2, :]
    place_x = (lax.broadcasted_iota(jnp.int32, (GRID, stations), 0) == station_x).astype(F32)
    place_y = (lax.broadcasted_iota(jnp.int32, (LANES, stations), 0) == station_y).astype(F32)
    place_xt = jnp.transpose(place_x).astype(BF)
    place_yt = jnp.transpose(place_y)[:, :grid_y].astype(BF)

    @pl.when(first_step)
    def _():
        copies[0].wait()

    pick_xt[...] = dot(held("base_xt2", GRID), place_x.astype(BF)).astype(BF)
    pick_x[...] = dot(place_xt, held("base_x")).astype(BF)
    station_y2 = held("station_y2")
    pick_y[...] = dot(place_yt, station_y2[:grid_y]) + dot(place_yt, station_y2[grid_y:])

    @pl.when(first_step)
    def _():
        copies[1].wait()

    def back_project():
        spread = held("spread")
        spread = jnp.concatenate([spread[i * LANES : (i + 1) * LANES] for i in range(3)], axis=1)
        spreads = dot(values[...], spread[:, : 5 * LANES])
        for row in range(0, stations, ROWS):
            at = slice(row, row + ROWS)
            cosines, sines = pick_y[at, :LANES], pick_y[at, LANES:]
            for c in range(5):
                e = spreads[at, c * LANES : (c + 1) * LANES]
                spread_out[at, 2 * c * LANES : (2 * c + 1) * LANES] = (e * cosines).astype(BF)
                spread_out[at, (2 * c + 1) * LANES : (2 * c + 2) * LANES] = (e * sines).astype(BF)
        spec = dot(pick_xt[...], spread_out[...])
        for c, (odd_x, odd_y) in enumerate(PARITY):
            for hx in range(2):
                for hy in range(2):
                    lane = (2 * c + hy) * LANES
                    part = spec[hx * GRID : (hx + 1) * GRID, lane : lane + LANES]
                    spec_q[c, hx, hy] = -part if (odd_x * hx + odd_y * hy) % 2 else part

        for row in range(0, GRID, 16):
            at = slice(row, row + 16)
            for hx in range(2):
                q = [[spec_q[c, hx ^ PARITY[c][0], hy, at, :] for hy in range(2)] for c in range(5)]
                to = slice(hx * GRID + row, hx * GRID + row + 16)
                for z in range(slabs):
                    t = [table(c, z, at).astype(F32) for c in range(5)]
                    for hy in range(2):
                        total = None
                        for c in range(5):
                            term = t[c] * q[c][hy ^ PARITY[c][1]]
                            total = term if total is None else total + term
                        lane = (2 * z + hy) * LANES
                        spec_g[to, lane : lane + LANES] = total.astype(BF)
        for block in blocks:
            along_x = dot(held("base_x"), spec_g[:, block[0] * 2 * LANES : (block[-1] + 1) * 2 * LANES]).astype(BF)
            along_x = jnp.concatenate([along_x[:, i * 2 * LANES : (i + 1) * 2 * LANES] for i in range(BLOCK)], axis=0)
            applied[block[0] : block[-1] + 1] = dot(along_x, held("field_yt", LANES)).reshape(BLOCK, GRID, LANES)

    def predict():
        for block in blocks:
            r = residual[block[0] : block[-1] + 1].reshape(BLOCK * GRID, LANES).astype(BF)
            y = dot(jnp.concatenate([r, r], axis=1), held("field_y2")).astype(BF)
            y = jnp.concatenate([y[i * GRID : (i + 1) * GRID] for i in range(BLOCK)], axis=1)
            spec_f[:, block[0] * 2 * LANES : (block[-1] + 1) * 2 * LANES] = dot(
                held("base_xt2"), jnp.concatenate([y, y], axis=0)
            ).astype(BF)

        for row in range(0, GRID, 16):
            at = [slice(hx * GRID + row, hx * GRID + row + 16) for hx in range(2)]
            total = [[[None] * 2 for _ in range(2)] for _ in range(5)]
            for eight in range(0, slabs, 8):
                part = [[[None] * 2 for _ in range(2)] for _ in range(5)]
                for z in range(eight, min(slabs, eight + 8)):
                    lane = 2 * z * LANES
                    f = [
                        [spec_f[at[hx], lane + hy * LANES : lane + (hy + 1) * LANES] for hy in range(2)]
                        for hx in range(2)
                    ]
                    for c, (odd_x, odd_y) in enumerate(PARITY):
                        t = table(c, z, at[0])
                        for hx in range(2):
                            for hy in range(2):
                                term = t * f[hx ^ odd_x][hy ^ odd_y]
                                old = part[c][hx][hy]
                                part[c][hx][hy] = term if old is None else old + term
                for c in range(5):
                    for hx in range(2):
                        for hy in range(2):
                            old = total[c][hx][hy]
                            new = part[c][hx][hy]
                            total[c][hx][hy] = new if old is None else old.astype(F32) + new.astype(F32)
            for c, (odd_x, odd_y) in enumerate(PARITY):
                for hx in range(2):
                    for hy in range(2):
                        part = total[c][hx][hy].astype(BF)
                        part = -part if (odd_x * hx + odd_y * hy) % 2 else part
                        lane = (2 * c + hy) * LANES
                        spec_i[at[hx], lane : lane + LANES] = part

        picked = dot(pick_x[...], spec_i[...])
        for row in range(0, stations, ROWS):
            at = slice(row, row + ROWS)
            cosines, sines = pick_y[at, :LANES], pick_y[at, LANES:]
            for c in range(5):
                lane = 2 * c * LANES
                part = picked[at, lane : lane + LANES] * cosines + picked[at, lane + LANES : lane + 2 * LANES] * sines
                picked_in[at, c * LANES : (c + 1) * LANES] = part.astype(BF)
        return dot(picked_in[...], held("back", LANES))

    def fold(a):
        return jnp.sum(a.reshape(a.shape[0] // 8, 8, LANES), axis=0)

    def total_of(partial):
        if boots == 1:
            return jnp.broadcast_to(jnp.sum(partial, keepdims=True), (1, LANES))
        sums = jnp.dot(
            partial, held("same", LANES).astype(F32), precision=lax.Precision.HIGHEST, preferred_element_type=F32
        )
        return jnp.sum(sums, axis=0, keepdims=True)

    def depth_weight(z):
        within = lax.broadcasted_iota(jnp.int32, (1, LANES), 1) // (boots * grid_y)
        depth = (within + z * deep).astype(F32) + 0.5 + station_height
        ratio = station_height / depth
        return ratio * ratio * ratio

    models[...] = jnp.zeros_like(models)
    direction[...] = jnp.zeros_like(direction)
    pred[...] = jnp.zeros_like(pred)
    image[...] = jnp.zeros_like(image)
    no_sum = jnp.zeros((8, LANES), F32)

    def round_of(index, carry):
        old_norm, old_step = carry
        fresh = index % CG_STEPS == 0
        back_project()

        @pl.when(fresh)
        def _():
            norm = no_sum
            for z, at in pieces:
                m = models[z, at]
                p = damping * depth_weight(z) / (m * m + focusing * focusing)
                penalty[z, at] = p
                r = applied[z, at] - p * m
                residual[z, at] = r
                norm += fold(r * r)
            sums[...] = norm

        @pl.when(jnp.logical_not(fresh))
        def _():
            norm = no_sum
            for z, at in pieces:
                r = residual[z, at] - old_step * (applied[z, at] + penalty[z, at] * direction[z, at])
                residual[z, at] = r
                norm += fold(r * r)
            sums[...] = norm

        norm = total_of(sums[...])
        ratio = jnp.where(fresh, 0.0, norm / old_norm)
        cross = no_sum
        for z, at in pieces:
            d = residual[z, at] + ratio * direction[z, at]
            direction[z, at] = d
            cross += fold(penalty[z, at] * d * d)
        here = predict() + ratio * image[...]
        image[...] = here
        step = norm / total_of(cross + fold(weights[...] * here * here))
        for z, at in pieces:
            models[z, at] += step * direction[z, at]
        now = pred[...] + step * here
        pred[...] = now
        values[...] = (weights[...] * jnp.where(fresh, here, data[...] - now)).astype(BF)
        return norm, step

    one = jnp.ones((1, LANES), F32)
    lax.fori_loop(0, IRLS * CG_STEPS, round_of, (one, one))

    for group in range(slabs // boots):
        m = jnp.concatenate([models[group * boots + i].astype(BF) for i in range(boots)], axis=1)
        if boots > 1:
            regroup = held("regroup")
            regroup = [regroup[i * boots * LANES : (i + 1) * boots * LANES] for i in range(boots // 2)]
            m = dot(m, jnp.concatenate(regroup, axis=1)).astype(BF)
        for b in range(boots):
            out_ref[b * GRID : (b + 1) * GRID, group * LANES : (group + 1) * LANES] = (
                m[:, b * LANES : (b + 1) * LANES]
            )


def solve(slot, comp_weight, station_index, observed, counts, mine, grid_y):
    boots = min(mine, LANES // grid_y)
    slabs = DEPTHS * grid_y * boots // LANES
    stations = station_index.shape[1]
    const = jnp.asarray(constants(grid_y, boots))
    vmem = pltpu.VMEM
    whole = lambda a: pl.BlockSpec(a.shape, lambda i, n=a.ndim: (0,) * n)
    smem = pl.BlockSpec(memory_space=pltpu.SMEM)
    field = vmem((slabs, GRID, LANES), F32)
    at_stations = vmem((stations, LANES), F32)
    inputs = [station_index, observed, counts]
    return pl.pallas_call(
        functools.partial(solve_kernel, grid_y, boots),
        out_shape=jax.ShapeDtypeStruct((mine * GRID, DEPTHS * grid_y), BF),
        grid=(mine // boots,),
        in_specs=[smem, smem] + [whole(a) for a in inputs] + [pl.BlockSpec(memory_space=pl.ANY)],
        out_specs=pl.BlockSpec((boots * GRID, DEPTHS * grid_y), lambda i: (i, 0)),
        scratch_shapes=[
            vmem((layout(grid_y, boots).rows, 2 * LANES), BF),
            pltpu.SemaphoreType.DMA((2,)),
            vmem((stations, 2 * GRID), BF),
            vmem((2 * GRID, stations), BF),
            vmem((stations, 2 * LANES), F32),
            at_stations,
            at_stations,
            at_stations,
            at_stations,
            vmem((stations, LANES), BF),
            vmem((LANES, stations), F32),
            vmem((8, LANES), F32),
            vmem((stations, 10 * LANES), BF),
            vmem((5, 2, 2, GRID, LANES), F32),
            vmem((2 * GRID, 10 * LANES), BF),
            vmem((2 * GRID, slabs * 2 * LANES), BF),
            vmem((2 * GRID, slabs * 2 * LANES), BF),
            vmem((stations, 5 * LANES), BF),
            field,
            field,
            field,
            field,
            field,
        ],
        compiler_params=pltpu.CompilerParams(vmem_limit_bytes=56 * 1024 * 1024),
        cost_estimate=pl.CostEstimate(flops=10**10, bytes_accessed=10**7, transcendentals=0),
        name="solve",
    )(slot, comp_weight, *inputs, const)


def pick_kernel(grid_y, boots, count, models_ref, *refs):
    def pick_chunk(cell_ref, out_ref, at):
        cells = cell_ref[:, at]
        place = cells.astype(F32)
        wide = lambda row, rows: jnp.broadcast_to(row, (rows, CHUNK)).astype(BF)
        y_row = wide(place[1:2], grid_y)
        z_row = wide(place[2:3], grid_y)
        here_y = lax.broadcasted_iota(jnp.int32, (grid_y, CHUNK), 0).astype(F32).astype(BF) == y_row
        here_y = jnp.where(here_y, jnp.ones_like(y_row), jnp.zeros_like(y_row))
        chosen = jnp.concatenate(
            [jnp.where(z_row == jnp.full_like(z_row, z), here_y, jnp.zeros_like(here_y)) for z in range(DEPTHS)],
            axis=0,
        )
        at_x = lax.broadcasted_iota(jnp.int32, (GRID, CHUNK), 0) == cells[0:1]
        found = dot(models_ref[...], chosen)
        parts = [
            jnp.sum(jnp.where(at_x, found[b * GRID : (b + 1) * GRID], 0.0), axis=0, keepdims=True)
            for b in range(boots)
        ]
        out_ref[:, at] = jnp.concatenate(parts, axis=0).astype(BF)

    per = max(1, 4 // count)

    @pl.loop(0, refs[0].shape[1] // (per * CHUNK))
    def _(step):
        for i in range(per):
            at = pl.ds(pl.multiple_of((step * per + i) * CHUNK, CHUNK), CHUNK)
            for cell_ref, out_ref in zip(refs[:count], refs[count:]):
                pick_chunk(cell_ref, out_ref, at)


def pick(models, cells, grid_y):
    boots = models.shape[0] // GRID
    count = cells[0].shape[1]
    vmem = pl.BlockSpec(memory_space=pltpu.VMEM)
    return pl.pallas_call(
        functools.partial(pick_kernel, grid_y, boots, len(cells)),
        out_shape=[jax.ShapeDtypeStruct((boots, count), BF)] * len(cells),
        in_specs=[vmem] * (1 + len(cells)),
        out_specs=[vmem] * len(cells),
        compiler_params=pltpu.CompilerParams(vmem_limit_bytes=40 * 1024 * 1024),
        cost_estimate=pl.CostEstimate(
            flops=2 * models.size * count * len(cells), bytes_accessed=10**6, transcendentals=0
        ),
        name="pick",
    )(models, *cells)


def local(wide, cell_index, station_index, observed, comp_weight, counts):
    boots = counts.shape[0]
    grid_y = cell_index.shape[1] * wide // (GRID * DEPTHS)
    team = TEAM if wide % TEAM == 0 and boots % TEAM == 0 else 1
    slot = lax.axis_index("wide").astype(jnp.int32) & (team - 1)

    def swap(a, k):
        return lax.ppermute(a, "wide", [(i, i ^ k) for i in range(wide)])

    theirs = [swap(cell_index, k) for k in range(1, team)]
    models = solve(slot.reshape(1), comp_weight, station_index, observed, counts, boots // team, grid_y)
    sent = [swap(a, k + 1) for k, a in enumerate(pick(models, theirs, grid_y))] if theirs else []
    got = [*pick(models, [cell_index], grid_y), *sent]
    blocks = []
    for member in range(team):
        block = got[member]
        for other in range(1, team):
            block = jnp.where(slot == other, got[member ^ other], block)
        blocks.append(block.astype(F32))
    return jnp.concatenate(blocks, axis=0)


def solution(mesh):
    in_specs = (P(None, "wide"), P(None, "groups"), P(None, "groups"), P(), P("groups", None))
    out_specs = P("groups", "wide")
    fn = functools.partial(local, mesh.shape["wide"])
    return jax.shard_map(fn, mesh=mesh, in_specs=in_specs, out_specs=out_specs, check_vma=False)
```

time: 51.3 us -> 37.3 us (0.73)
  local copies, waits for them, and re-layouts: 12.4 us -> 0.95 us
  Pallas kernels: 30.3 us -> 28.2 us
    unnamed x30 -> x4, local copies, waits for them, and re-layouts: 12.4 us -> 0.95 us
    pallas_call x1, Pallas kernels: 23.7 us -> 21.7 us  [solve(): pl.pallas_call(functools.partial(solve_kernel, grid_y, boots), out_shape=...]
  transfers between devices with their start and end apart: 6 -> 6, of which waited for: 1 -> 1; matrix products, arithmetic and copies ran while one was open for 0% -> 0% of each run, Pallas kernels for 50% -> 63%
where the time goes in v6:
time: 37.3 us; the launch traced here: 37 us
  Pallas kernels  28.2 us (76%)
  starting transfers between devices  5.06 us (14%)
  waiting for transfers between devices  1.91 us (5%)
  local copies, waits for them, and re-layouts  0.95 us (3%)
  other arithmetic  0.81 us (2%)
    pallas_call x1, Pallas kernels, solve(): pl.pallas_call(functools.partial(solve_kernel, grid_y, boots), out_shape=...  21.7 us
    pallas_call x2, Pallas kernels, pick(): pl.pallas_call(functools.partial(pick_kernel, grid_y, boots, len(cells)),...  6.48 us
    ppermute x6, starting transfers between devices, swap(): return lax.ppermute(a, 'wide', [(i, i ^ k) for i in range(wide)])  5.06 us
    ppermute x6, waiting for transfers between devices, swap(): return lax.ppermute(a, 'wide', [(i, i ^ k) for i in range(wide)])  1.91 us
    unnamed x4, local copies, waits for them, and re-layouts  0.95 us
  transfers between devices with their start and end apart: 6, of which 1 were waited for; matrix products, arithmetic and copies ran while one was open for 0% of the time, Pallas kernels for 63%

profile of v6, /device:TPU:0, one launch (start us, length us, event | category | flops | bytes accessed | tf_op | source)
XLA Modules:
  0.0 37.0 jit_solution(12331881204910137534)
XLA Ops:
  0.0 0.5 %collective-permute-start = (s32[3,4096]{1,0:T(4,128)}, s32[3,4096]{1,0:T(4,128)S(1)}, u32[]{:S(2)}, u32[]{:S(2)}) collective-permute-start(s32[3,4096]{1,0:T(4,128)} %refs_0_.1), channel_id=1, source_target_pairs={{0,1},{1,0},{2,3},{3,2},{4,5},{5,4},{6,7},{7,6},{8,9},{9,8},{10,11... | collective-permute-start | bytes 147464 | tf_op jit(solution)/shard_map/ppermute | solution.py:522
  0.5 2.5 %collective-permute-start.1 = (s32[3,4096]{1,0:T(4,128)}, s32[3,4096]{1,0:T(4,128)S(1)}, u32[]{:S(2)}, u32[]{:S(2)}) collective-permute-start(s32[3,4096]{1,0:T(4,128)} %refs_0_.1), channel_id=1, source_target_pairs={{0,2},{1,3},{2,0},{3,1},{4,6},{5,7},{6,4},{7,5},{8,10},{9,11},{10,... | collective-permute-start | bytes 147464 | tf_op jit(solution)/shard_map/ppermute | solution.py:522
  3.0 0.1 collective-permute-start.2
  3.1 21.7 %solve.1.models_ref = bf16[256,512]{1,0:T(8,128)(2,1)} custom-call(s32[1]{0:T(128)} %bitcast.slot_ref, f32[5]{0:T(128)} %comp_ref.1, s32[2,512]{1,0:T(2,128)} %station_ref.1, f32[5,512]{1,0:T(8,128)} %observed_ref.1, s32[8,512]{1,0:T(8,128)} %counts_ref.1, bf16[16384,256]{1,0:T(8,128)(2,1)} %constant.12.clone.source), custom_call_target="tpu_custom_call" | custom-call | flops 10000000000 | bytes 10000000 | tf_op jit(solution)/shard_map/solve/pallas_call | solution.py:430
  24.9 0.0 copy-start
  24.9 0.0 collective-permute-done.refs_0_
  24.9 0.0 collective-permute-done.1.refs_1_
  24.9 0.0 collective-permute-done.2.refs_2_
  24.9 0.0 copy-start.1
  24.9 0.9 %copy-done.1 = bf16[256,512]{1,0:T(8,128)(2,1)S(1)} copy-done((bf16[256,512]{1,0:T(8,128)(2,1)S(1)}, bf16[256,512]{1,0:T(8,128)(2,1)}, u32[]{:S(2)}) %copy-start.1) | copy-done | bytes 262168
  25.8 4.9 %pick.2 = (bf16[2,4096]{1,0:T(2,128)(2,1)S(1)}, bf16[2,4096]{1,0:T(2,128)(2,1)S(1)}, bf16[2,4096]{1,0:T(2,128)(2,1)S(1)}) custom-call(bf16[256,512]{1,0:T(8,128)(2,1)S(1)} %copy-done.1, s32[3,4096]{1,0:T(4,128)S(1)} %collective-permute-done.refs_0_, s32[3,4096]{1,0:T(4,128)S(1)} %collective-permute-done.1.refs_1_, s32[3,4096]{1,0:T(4,128)S(1)} %collective-permute-done.2.refs_2_), custom_call_target="tpu_custom_call" | custom-call | flops 3221225472 | bytes 1000000 | tf_op jit(solution)/shard_map/pick/pallas_call | solution.py:502
  30.8 1.7 %collective-permute-start.3 = (bf16[2,4096]{1,0:T(2,128)(2,1)S(1)}, bf16[2,4096]{1,0:T(2,128)(2,1)S(1)}, u32[]{:S(2)}, u32[]{:S(2)}) collective-permute-start(bf16[2,4096]{1,0:T(2,128)(2,1)S(1)} %get-tuple-element.8), channel_id=1, source_target_pairs={{0,3},{1,2},{2,1},{3,0},{4,7},{5,6},{6,5},{7,4},{8,11},{9,10},{10,... | collective-permute-start | bytes 49160 | tf_op jit(solution)/shard_map/ppermute | solution.py:522
  32.5 0.2 collective-permute-start.4
  32.7 0.1 collective-permute-start.5
  32.7 0.0 copy-done
  32.7 1.5 %pick.3 = bf16[2,4096]{1,0:T(2,128)(2,1)S(1)} custom-call(bf16[256,512]{1,0:T(8,128)(2,1)S(1)} %copy-done.1, s32[3,4096]{1,0:T(4,128)S(1)} %copy-done), custom_call_target="tpu_custom_call" | custom-call | flops 1073741824 | bytes 1000000 | tf_op jit(solution)/shard_map/pick/pallas_call | solution.py:502
  34.3 0.0 collective-permute-done.3
  34.3 1.9 %collective-permute-done.4 = bf16[2,4096]{1,0:T(2,128)(2,1)S(1)} collective-permute-done((bf16[2,4096]{1,0:T(2,128)(2,1)S(1)}, bf16[2,4096]{1,0:T(2,128)(2,1)S(1)}, u32[]{:S(2)}, u32[]{:S(2)}) %collective-permute-start.4) | collective-permute-done | bytes 16416 | tf_op jit(solution)/shard_map/ppermute | solution.py:522
  36.2 0.0 collective-permute-done.5
  36.2 0.1 broadcast_select_fusion.11
  36.3 0.7 %maximum_convert_fusion = f32[8,4096]{1,0:T(8,128)} fusion(bf16[2,4096]{1,0:T(2,128)(2,1)S(1)} %get-tuple-element.12, bf16[2,4096]{1,0:T(2,128)(2,1)S(1)} %get-tuple-element.13, bf16[2,4096]{1,0:T(2,128)(2,1)S(1)} %get-tuple-element.14, bf16[2,4096]{1,0:T(2,128)(2,1)S(1)} %get-tuple-element.11), kind=kLoop, calls=%fused_computation | loop fusion | flops 262144 | bytes 196608 | tf_op jit(solution)/shard_map/concatenate | solution.py:534
Async XLA Ops:
  0.0 24.9 %collective-permute-start = (s32[3,4096]{1,0:T(4,128)}, s32[3,4096]{1,0:T(4,128)S(1)}, u32[]{:S(2)}, u32[]{:S(2)}) collective-permute-start(s32[3,4096]{1,0:T(4,128)} %refs_0_.1), channel_id=1, source_target_pairs={{0,1},{1,0},{2,3},{3,2},{4,5},{5,4},{6,7},{7,6},{8,9},{9,8},{10,11... | collective-permute-start | bytes 147464 | tf_op jit(solution)/shard_map/ppermute | solution.py:522
  0.5 24.4 %collective-permute-start.1 = (s32[3,4096]{1,0:T(4,128)}, s32[3,4096]{1,0:T(4,128)S(1)}, u32[]{:S(2)}, u32[]{:S(2)}) collective-permute-start(s32[3,4096]{1,0:T(4,128)} %refs_0_.1), channel_id=1, source_target_pairs={{0,2},{1,3},{2,0},{3,1},{4,6},{5,7},{6,4},{7,5},{8,10},{9,11},{10,... | collective-permute-start | bytes 147464 | tf_op jit(solution)/shard_map/ppermute | solution.py:522
  3.0 21.9 %collective-permute-start.2 = (s32[3,4096]{1,0:T(4,128)}, s32[3,4096]{1,0:T(4,128)S(1)}, u32[]{:S(2)}, u32[]{:S(2)}) collective-permute-start(s32[3,4096]{1,0:T(4,128)} %refs_0_.1), channel_id=1, source_target_pairs={{0,3},{1,2},{2,1},{3,0},{4,7},{5,6},{6,5},{7,4},{8,11},{9,10},{10,... | collective-permute-start | bytes 147464 | tf_op jit(solution)/shard_map/ppermute | solution.py:522
  24.9 7.9 %copy-start = (s32[3,4096]{1,0:T(4,128)S(1)}, s32[3,4096]{1,0:T(4,128)}, u32[]{:S(2)}) copy-start(s32[3,4096]{1,0:T(4,128)} %refs_0_.1) | copy-start | bytes 147460
  24.9 1.0 %copy-start.1 = (bf16[256,512]{1,0:T(8,128)(2,1)S(1)}, bf16[256,512]{1,0:T(8,128)(2,1)}, u32[]{:S(2)}) copy-start(bf16[256,512]{1,0:T(8,128)(2,1)} %solve.1.models_ref) | copy-start | bytes 786436
  30.8 3.5 %collective-permute-start.3 = (bf16[2,4096]{1,0:T(2,128)(2,1)S(1)}, bf16[2,4096]{1,0:T(2,128)(2,1)S(1)}, u32[]{:S(2)}, u32[]{:S(2)}) collective-permute-start(bf16[2,4096]{1,0:T(2,128)(2,1)S(1)} %get-tuple-element.8), channel_id=1, source_target_pairs={{0,3},{1,2},{2,1},{3,0},{4,7},{5,6},{6,5},{7,4},{8,11},{9,10},{10,... | collective-permute-start | bytes 49160 | tf_op jit(solution)/shard_map/ppermute | solution.py:522
  32.5 3.7 %collective-permute-start.4 = (bf16[2,4096]{1,0:T(2,128)(2,1)S(1)}, bf16[2,4096]{1,0:T(2,128)(2,1)S(1)}, u32[]{:S(2)}, u32[]{:S(2)}) collective-permute-start(bf16[2,4096]{1,0:T(2,128)(2,1)S(1)} %get-tuple-element.9), channel_id=1, source_target_pairs={{0,2},{1,3},{2,0},{3,1},{4,6},{5,7},{6,4},{7,5},{8,10},{9,11},{10,... | collective-permute-start | bytes 49160 | tf_op jit(solution)/shard_map/ppermute | solution.py:522
  32.7 3.6 %collective-permute-start.5 = (bf16[2,4096]{1,0:T(2,128)(2,1)S(1)}, bf16[2,4096]{1,0:T(2,128)(2,1)S(1)}, u32[]{:S(2)}, u32[]{:S(2)}) collective-permute-start(bf16[2,4096]{1,0:T(2,128)(2,1)S(1)} %get-tuple-element.10), channel_id=1, source_target_pairs={{0,1},{1,0},{2,3},{3,2},{4,5},{5,4},{6,7},{7,6},{8,9},{9,8},{10,11... | collective-permute-start | bytes 49160 | tf_op jit(solution)/shard_map/ppermute | solution.py:522

commit v7 on v6

--- a/solution.py
+++ b/solution.py
@@ -15,7 +15,7 @@
 DEPTHS = 16
 LANES = 128
 TEAM = 4
-BLOCK = 4
+BLOCK = 2
 CHUNK = 512
 ROWS = 32
 
@@ -112,13 +112,17 @@
     base_y = basis(grid_y).reshape(grid_y, 2, grid_y)
     copies = deep * boots
     field_y = np.einsum("ab,yhl->ayhbl", np.eye(copies), base_y).reshape(LANES, 2 * LANES)
-    station_y = np.einsum("b,yhl->yhbl", np.ones(copies), base_y).reshape(grid_y, 2 * LANES)
-    spread = np.zeros((6, deep, boots, grid_y, deep, boots, grid_y))
+    compact = deep == 2
+    near = 1 if compact else deep
+    station_y = np.einsum("b,yhl->yhbl", np.ones(near * boots), base_y).reshape(grid_y, -1)
+    halves = 2 if compact else 1
+    spread = np.zeros((5, deep, boots, grid_y, halves, near, boots, grid_y))
     for c in range(5):
         for b in range(boots):
-            spread[c, 0, b, c, :, b, :] = 1
-    spread = spread.reshape(6, LANES, LANES)
-    back = spread[:5].transpose(0, 2, 1).reshape(5 * LANES, LANES)
+            spread[c, 0, b, c, :, :, b, :] = 1
+    spread = spread.reshape(5, LANES, LANES)
+    back = spread.transpose(0, 2, 1).reshape(5 * LANES, LANES)
+    spread = np.concatenate([spread, np.zeros((1, LANES, LANES))])
     spread = spread.reshape(3, 2, LANES, LANES).transpose(0, 2, 1, 3)
     same = np.einsum("ab,dc,yz->daycbz", np.eye(boots), np.ones((deep, deep)), np.ones((grid_y, grid_y)))
     same = same.reshape(LANES, LANES)
@@ -153,6 +157,21 @@
     return jnp.dot(a, b, preferred_element_type=F32)
 
 
+def interleave(ahead, behind):
+    for stage in range(len(ahead) + 1):
+        first = ahead[stage] if stage < len(ahead) else []
+        second = behind[stage - 1] if stage else []
+        done = 0
+        for i, step in enumerate(first):
+            step()
+            upto = (i + 1) * len(second) // len(first)
+            for other in second[done:upto]:
+                other()
+            done = upto
+        for other in second[done:]:
+            other()
+
+
 def solve_kernel(
     grid_y,
     boots,
@@ -180,6 +199,7 @@
     spec_i,
     spec_f,
     spec_g,
+    spec_a,
     picked_in,
     models,
     residual,
@@ -191,6 +211,9 @@
     slabs = DEPTHS // deep
     where = layout(grid_y, boots)
     split_row = where.at["table"][0]
+    compact = deep == 2
+    wide = LANES if compact else 2 * LANES
+    low_lanes = lax.broadcasted_iota(jnp.int32, (1, LANES), 1) < LANES // 2
     copies = [
         pltpu.make_async_copy(source.at[a:b], const.at[a:b], copied.at[i])
         for i, (a, b) in enumerate([(0, split_row), (split_row, where.rows)])
@@ -239,12 +262,14 @@
 
     pick_xt[...] = dot(held("base_xt2", GRID), place_x.astype(BF)).astype(BF)
     pick_x[...] = dot(place_xt, held("base_x")).astype(BF)
-    station_y2 = held("station_y2")
+    station_y2 = held("station_y2", wide)
     pick_y[...] = dot(place_yt, station_y2[:grid_y]) + dot(place_yt, station_y2[grid_y:])
 
     @pl.when(first_step)
     def _():
         copies[1].wait()
+
+    no_sum = jnp.zeros((8, LANES), F32)
 
     def back_project():
         spread = held("spread")
@@ -252,86 +277,121 @@
         spreads = dot(values[...], spread[:, : 5 * LANES])
         for row in range(0, stations, ROWS):
             at = slice(row, row + ROWS)
-            cosines, sines = pick_y[at, :LANES], pick_y[at, LANES:]
+            trig = [pick_y[at, lane : lane + LANES] for lane in range(0, wide, LANES)]
             for c in range(5):
                 e = spreads[at, c * LANES : (c + 1) * LANES]
-                spread_out[at, 2 * c * LANES : (2 * c + 1) * LANES] = (e * cosines).astype(BF)
-                spread_out[at, (2 * c + 1) * LANES : (2 * c + 2) * LANES] = (e * sines).astype(BF)
+                for i, part in enumerate(trig):
+                    lane = c * wide + i * LANES
+                    spread_out[at, lane : lane + LANES] = (e * part).astype(BF)
         spec = dot(pick_xt[...], spread_out[...])
         for c, (odd_x, odd_y) in enumerate(PARITY):
             for hx in range(2):
+                for row in range(0, GRID, ROWS):
+                    at = slice(hx * GRID + row, hx * GRID + row + ROWS)
+                    if compact:
+                        part = spec[at, c * LANES : (c + 1) * LANES]
+                        turned = pltpu.roll(part, LANES // 2, 1)
+                        parts = [jnp.where(low_lanes, part, turned), jnp.where(low_lanes, turned, part)]
+                    else:
+                        parts = [spec[at, lane : lane + LANES] for lane in (c * wide, c * wide + LANES)]
+                    for hy, part in enumerate(parts):
+                        spec_q[c, hx, hy, row : row + ROWS, :] = -part if (odd_x * hx + odd_y * hy) % 2 else part
+
+        def products(block, row):
+            at = slice(row, row + 16)
+            t = [[table(c, z, at).astype(F32) for c in range(5)] for z in block]
+            for hx in range(2):
+                to = slice(hx * GRID + row, hx * GRID + row + 16)
                 for hy in range(2):
-                    lane = (2 * c + hy) * LANES
-                    part = spec[hx * GRID : (hx + 1) * GRID, lane : lane + LANES]
-                    spec_q[c, hx, hy] = -part if (odd_x * hx + odd_y * hy) % 2 else part
-
-        for row in range(0, GRID, 16):
-            at = slice(row, row + 16)
-            for hx in range(2):
-                q = [[spec_q[c, hx ^ PARITY[c][0], hy, at, :] for hy in range(2)] for c in range(5)]
-                to = slice(hx * GRID + row, hx * GRID + row + 16)
-                for z in range(slabs):
-                    t = [table(c, z, at).astype(F32) for c in range(5)]
-                    for hy in range(2):
-                        total = None
-                        for c in range(5):
-                            term = t[c] * q[c][hy ^ PARITY[c][1]]
-                            total = term if total is None else total + term
+                    q = [spec_q[c, hx ^ PARITY[c][0], hy ^ PARITY[c][1], at, :] for c in range(5)]
+                    for z, tz in zip(block, t):
+                        total = tz[0] * q[0]
+                        for c in range(1, 5):
+                            total = total + tz[c] * q[c]
                         lane = (2 * z + hy) * LANES
                         spec_g[to, lane : lane + LANES] = total.astype(BF)
-        for block in blocks:
-            along_x = dot(held("base_x"), spec_g[:, block[0] * 2 * LANES : (block[-1] + 1) * 2 * LANES]).astype(BF)
-            along_x = jnp.concatenate([along_x[:, i * 2 * LANES : (i + 1) * 2 * LANES] for i in range(BLOCK)], axis=0)
-            applied[block[0] : block[-1] + 1] = dot(along_x, held("field_yt", LANES)).reshape(BLOCK, GRID, LANES)
+
+        along = {}
+
+        def inverse_x(z):
+            along[z] = dot(held("base_x"), spec_g[:, 2 * z * LANES : (2 * z + 2) * LANES]).astype(BF)
+
+        def inverse_y(z):
+            applied[z] = dot(along[z], held("field_yt", LANES))
+
+        interleave(
+            [[functools.partial(products, block, row) for row in range(0, GRID, 16)] for block in blocks],
+            [[functools.partial(f, z) for f in (inverse_x, inverse_y) for z in block] for block in blocks],
+        )
 
     def predict():
-        for block in blocks:
+        along = {}
+
+        def forward_y(block):
             r = residual[block[0] : block[-1] + 1].reshape(BLOCK * GRID, LANES).astype(BF)
             y = dot(jnp.concatenate([r, r], axis=1), held("field_y2")).astype(BF)
-            y = jnp.concatenate([y[i * GRID : (i + 1) * GRID] for i in range(BLOCK)], axis=1)
-            spec_f[:, block[0] * 2 * LANES : (block[-1] + 1) * 2 * LANES] = dot(
-                held("base_xt2"), jnp.concatenate([y, y], axis=0)
-            ).astype(BF)
-
-        for row in range(0, GRID, 16):
+            for i, z in enumerate(block):
+                along[z] = jnp.concatenate([y[i * GRID : (i + 1) * GRID]] * 2, axis=0)
+
+        def forward_x(z):
+            spec_f[:, 2 * z * LANES : (2 * z + 2) * LANES] = dot(held("base_xt2"), along[z]).astype(BF)
+
+        def products(block, row):
             at = [slice(hx * GRID + row, hx * GRID + row + 16) for hx in range(2)]
-            total = [[[None] * 2 for _ in range(2)] for _ in range(5)]
-            for eight in range(0, slabs, 8):
-                part = [[[None] * 2 for _ in range(2)] for _ in range(5)]
-                for z in range(eight, min(slabs, eight + 8)):
-                    lane = 2 * z * LANES
-                    f = [
-                        [spec_f[at[hx], lane + hy * LANES : lane + (hy + 1) * LANES] for hy in range(2)]
-                        for hx in range(2)
-                    ]
-                    for c, (odd_x, odd_y) in enumerate(PARITY):
-                        t = table(c, z, at[0])
-                        for hx in range(2):
-                            for hy in range(2):
-                                term = t * f[hx ^ odd_x][hy ^ odd_y]
-                                old = part[c][hx][hy]
-                                part[c][hx][hy] = term if old is None else old + term
-                for c in range(5):
-                    for hx in range(2):
-                        for hy in range(2):
-                            old = total[c][hx][hy]
-                            new = part[c][hx][hy]
-                            total[c][hx][hy] = new if old is None else old.astype(F32) + new.astype(F32)
+            begin = block[0] % 8 == 0
+            f = {
+                (z, hx, hy): spec_f[at[hx], (2 * z + hy) * LANES : (2 * z + hy + 1) * LANES]
+                for z in block
+                for hx in range(2)
+                for hy in range(2)
+            }
             for c, (odd_x, odd_y) in enumerate(PARITY):
+                t = [table(c, z, at[0]) for z in block]
                 for hx in range(2):
+                    parts = []
                     for hy in range(2):
-                        part = total[c][hx][hy].astype(BF)
-                        part = -part if (odd_x * hx + odd_y * hy) % 2 else part
-                        lane = (2 * c + hy) * LANES
-                        spec_i[at[hx], lane : lane + LANES] = part
+                        total = None if begin else spec_a[c, hx, hy, at[0], :]
+                        for z, tz in zip(block, t):
+                            term = tz * f[z, hx ^ odd_x, hy ^ odd_y]
+                            total = term if total is None else total + term
+                        if block[-1] % 8 != 7 and block is not blocks[-1]:
+                            spec_a[c, hx, hy, at[0], :] = total
+                            continue
+                        total = total.astype(F32)
+                        if block[-1] >= 8:
+                            total = total + spec_q[c, hx, hy, at[0], :]
+                        if block is not blocks[-1]:
+                            spec_q[c, hx, hy, at[0], :] = total
+                            continue
+                        parts.append(-total if (odd_x * hx + odd_y * hy) % 2 else total)
+                    if not parts:
+                        continue
+                    if compact:
+                        low, high = parts
+                        parts = [
+                            jnp.where(low_lanes, low, high)
+                            + pltpu.roll(jnp.where(low_lanes, high, low), LANES // 2, 1)
+                        ]
+                    for i, part in enumerate(parts):
+                        lane = c * wide + i * LANES
+                        spec_i[at[hx], lane : lane + LANES] = part.astype(BF)
+
+        interleave(
+            [
+                [functools.partial(forward_y, block)] + [functools.partial(forward_x, z) for z in block]
+                for block in blocks
+            ],
+            [[functools.partial(products, block, row) for row in range(0, GRID, 16)] for block in blocks],
+        )
 
         picked = dot(pick_x[...], spec_i[...])
         for row in range(0, stations, ROWS):
             at = slice(row, row + ROWS)
-            cosines, sines = pick_y[at, :LANES], pick_y[at, LANES:]
             for c in range(5):
-                lane = 2 * c * LANES
-                part = picked[at, lane : lane + LANES] * cosines + picked[at, lane + LANES : lane + 2 * LANES] * sines
+                part = None
+                for lane in range(0, wide, LANES):
+                    term = picked[at, c * wide + lane : c * wide + lane + LANES] * pick_y[at, lane : lane + LANES]
+                    part = term if part is None else part + term
                 picked_in[at, c * LANES : (c + 1) * LANES] = part.astype(BF)
         return dot(picked_in[...], held("back", LANES))
 
@@ -341,9 +401,13 @@
     def total_of(partial):
         if boots == 1:
             return jnp.broadcast_to(jnp.sum(partial, keepdims=True), (1, LANES))
-        sums = jnp.dot(
-            partial, held("same", LANES).astype(F32), precision=lax.Precision.HIGHEST, preferred_element_type=F32
-        )
+        parts = []
+        for _ in range(3):
+            part = partial.astype(BF).astype(F32)
+            parts.append(part)
+            partial = partial - part
+        parts.append(no_sum)
+        sums = dot(jnp.concatenate(parts, axis=0).astype(BF), held("same", LANES))
         return jnp.sum(sums, axis=0, keepdims=True)
 
     def depth_weight(z):
@@ -356,7 +420,6 @@
     direction[...] = jnp.zeros_like(direction)
     pred[...] = jnp.zeros_like(pred)
     image[...] = jnp.zeros_like(image)
-    no_sum = jnp.zeros((8, LANES), F32)
 
     def round_of(index, carry):
         old_norm, old_step = carry
@@ -426,6 +489,7 @@
     smem = pl.BlockSpec(memory_space=pltpu.SMEM)
     field = vmem((slabs, GRID, LANES), F32)
     at_stations = vmem((stations, LANES), F32)
+    wide = LANES if 2 * slabs == DEPTHS else 2 * LANES
     inputs = [station_index, observed, counts]
     return pl.pallas_call(
         functools.partial(solve_kernel, grid_y, boots),
@@ -438,7 +502,7 @@
             pltpu.SemaphoreType.DMA((2,)),
             vmem((stations, 2 * GRID), BF),
             vmem((2 * GRID, stations), BF),
-            vmem((stations, 2 * LANES), F32),
+            vmem((stations, wide), F32),
             at_stations,
             at_stations,
             at_stations,
@@ -446,11 +510,12 @@
             vmem((stations, LANES), BF),
             vmem((LANES, stations), F32),
             vmem((8, LANES), F32),
-            vmem((stations, 10 * LANES), BF),
+            vmem((stations, 5 * wide), BF),
             vmem((5, 2, 2, GRID, LANES), F32),
-            vmem((2 * GRID, 10 * LANES), BF),
+            vmem((2 * GRID, 5 * wide), BF),
             vmem((2 * GRID, slabs * 2 * LANES), BF),
             vmem((2 * GRID, slabs * 2 * LANES), BF),
+            vmem((5, 2, 2, GRID, LANES), BF),
             vmem((stations, 5 * LANES), BF),
             field,
             field,
@@ -523,8 +588,9 @@
 
     theirs = [swap(cell_index, k) for k in range(1, team)]
     models = solve(slot.reshape(1), comp_weight, station_index, observed, counts, boots // team, grid_y)
-    sent = [swap(a, k + 1) for k, a in enumerate(pick(models, theirs, grid_y))] if theirs else []
-    got = [*pick(models, [cell_index], grid_y), *sent]
+    far = [swap(a, k + 2) for k, a in enumerate(pick(models, theirs[1:], grid_y))] if team > 2 else []
+    near = pick(models, [cell_index] + theirs[:1], grid_y)
+    got = [near[0]] + [swap(a, 1) for a in near[1:]] + far
     blocks = []
     for member in range(team):
         block = got[member]

time: 37.3 us -> 40 us (1.072)
  Pallas kernels: 28.2 us -> 31.4 us
  waiting for transfers between devices: 1.91 us -> 1.15 us
    pallas_call x1, Pallas kernels: 21.7 us -> 25.2 us  [solve(): pl.pallas_call(functools.partial(solve_kernel, grid_y, boots), out_shape=...]
    ppermute x6, waiting for transfers between devices: 1.91 us -> 1.15 us  [swap(): return lax.ppermute(a, 'wide', [(i, i ^ k) for i in range(wide)])]
  transfers between devices with their start and end apart: 6 -> 6, of which waited for: 1 -> 1; matrix products, arithmetic and copies ran while one was open for 0% -> 0% of each run, Pallas kernels for 63% -> 79%
where the time goes in v7:
time: 40 us; the launch traced here: 39.7 us
  Pallas kernels  31.4 us (78%)
  starting transfers between devices  5.37 us (13%)
  waiting for transfers between devices  1.15 us (3%)
  local copies, waits for them, and re-layouts  0.95 us (2%)
  other arithmetic  0.81 us (2%)
    pallas_call x1, Pallas kernels, solve(): pl.pallas_call(functools.partial(solve_kernel, grid_y, boots), out_shape=...  25.2 us
    pallas_call x2, Pallas kernels, pick(): pl.pallas_call(functools.partial(pick_kernel, grid_y, boots, len(cells)),...  6.18 us
    ppermute x6, starting transfers between devices, swap(): return lax.ppermute(a, 'wide', [(i, i ^ k) for i in range(wide)])  5.37 us
    ppermute x6, waiting for transfers between devices, swap(): return lax.ppermute(a, 'wide', [(i, i ^ k) for i in range(wide)])  1.15 us
    unnamed x4, local copies, waits for them, and re-layouts  0.95 us
  transfers between devices with their start and end apart: 6, of which 1 were waited for; matrix products, arithmetic and copies ran while one was open for 0% of the time, Pallas kernels for 79%

profile of v7, /device:TPU:0, one launch (start us, length us, event | category | flops | bytes accessed | tf_op | source)
XLA Modules:
  0.0 39.7 jit_solution(9164093799056700965)
XLA Ops:
  0.0 3.0 %collective-permute-start = (s32[3,4096]{1,0:T(4,128)}, s32[3,4096]{1,0:T(4,128)S(1)}, u32[]{:S(2)}, u32[]{:S(2)}) collective-permute-start(s32[3,4096]{1,0:T(4,128)} %refs_0_.1), channel_id=1, source_target_pairs={{0,2},{1,3},{2,0},{3,1},{4,6},{5,7},{6,4},{7,5},{8,10},{9,11},{10,... | collective-permute-start | bytes 147464 | tf_op jit(solution)/shard_map/ppermute | solution.py:587
  3.0 0.0 collective-permute-start.1
  3.0 0.1 collective-permute-start.4
  3.1 0.0 copy-start
  3.1 25.2 %solve.1.models_ref = bf16[256,512]{1,0:T(8,128)(2,1)} custom-call(s32[1]{0:T(128)} %bitcast.slot_ref, f32[5]{0:T(128)} %comp_ref.1, s32[2,512]{1,0:T(2,128)} %station_ref.1, f32[5,512]{1,0:T(8,128)} %observed_ref.1, s32[8,512]{1,0:T(8,128)} %counts_ref.1, bf16[16384,256]{1,0:T(8,128)(2,1)} %constant.12.clone.source), custom_call_target="tpu_custom_call" | custom-call | flops 10000000000 | bytes 10000000 | tf_op jit(solution)/shard_map/solve/pallas_call | solution.py:494
  28.4 0.0 collective-permute-done.refs_0_
  28.4 0.0 collective-permute-done.1.refs_1_
  28.4 0.0 copy-start.1
  28.4 0.9 %copy-done.1 = bf16[256,512]{1,0:T(8,128)(2,1)S(1)} copy-done((bf16[256,512]{1,0:T(8,128)(2,1)S(1)}, bf16[256,512]{1,0:T(8,128)(2,1)}, u32[]{:S(2)}) %copy-start.1) | copy-done | bytes 262168
  29.3 3.1 %pick.2 = (bf16[2,4096]{1,0:T(2,128)(2,1)S(1)}, bf16[2,4096]{1,0:T(2,128)(2,1)S(1)}) custom-call(bf16[256,512]{1,0:T(8,128)(2,1)S(1)} %copy-done.1, s32[3,4096]{1,0:T(4,128)S(1)} %collective-permute-done.refs_0_, s32[3,4096]{1,0:T(4,128)S(1)} %collective-permute-done.1.refs_1_), custom_call_target="tpu_custom_call" | custom-call | flops 2147483648 | bytes 1000000 | tf_op jit(solution)/shard_map/pick/pallas_call | solution.py:567
  32.4 1.7 %collective-permute-start.2 = (bf16[2,4096]{1,0:T(2,128)(2,1)S(1)}, bf16[2,4096]{1,0:T(2,128)(2,1)S(1)}, u32[]{:S(2)}, u32[]{:S(2)}) collective-permute-start(bf16[2,4096]{1,0:T(2,128)(2,1)S(1)} %get-tuple-element.9), channel_id=1, source_target_pairs={{0,3},{1,2},{2,1},{3,0},{4,7},{5,6},{6,5},{7,4},{8,11},{9,10},{10,... | collective-permute-start | bytes 49160 | tf_op jit(solution)/shard_map/ppermute | solution.py:587
  34.1 0.5 %collective-permute-start.3 = (bf16[2,4096]{1,0:T(2,128)(2,1)S(1)}, bf16[2,4096]{1,0:T(2,128)(2,1)S(1)}, u32[]{:S(2)}, u32[]{:S(2)}) collective-permute-start(bf16[2,4096]{1,0:T(2,128)(2,1)S(1)} %get-tuple-element.10), channel_id=1, source_target_pairs={{0,2},{1,3},{2,0},{3,1},{4,6},{5,7},{6,4},{7,5},{8,10},{9,11},{10,... | collective-permute-start | bytes 49160 | tf_op jit(solution)/shard_map/ppermute | solution.py:587
  34.6 0.0 collective-permute-done.4.refs_1_
  34.6 0.0 copy-done
  34.6 3.1 %pick.3 = (bf16[2,4096]{1,0:T(2,128)(2,1)S(1)}, bf16[2,4096]{1,0:T(2,128)(2,1)S(1)}) custom-call(bf16[256,512]{1,0:T(8,128)(2,1)S(1)} %copy-done.1, s32[3,4096]{1,0:T(4,128)S(1)} %copy-done, s32[3,4096]{1,0:T(4,128)S(1)} %collective-permute-done.4.refs_1_), custom_call_target="tpu_custom_call" | custom-call | flops 2147483648 | bytes 1000000 | tf_op jit(solution)/shard_map/pick/pallas_call | solution.py:567
  37.7 0.1 collective-permute-start.5
  37.8 0.0 collective-permute-done.2
  37.8 0.0 collective-permute-done.3
  37.8 1.1 %collective-permute-done.5 = bf16[2,4096]{1,0:T(2,128)(2,1)S(1)} collective-permute-done((bf16[2,4096]{1,0:T(2,128)(2,1)S(1)}, bf16[2,4096]{1,0:T(2,128)(2,1)S(1)}, u32[]{:S(2)}, u32[]{:S(2)}) %collective-permute-start.5) | collective-permute-done | bytes 16416 | tf_op jit(solution)/shard_map/ppermute | solution.py:587
  38.9 0.1 broadcast_select_fusion.11
  39.0 0.7 %maximum_convert_fusion = f32[8,4096]{1,0:T(8,128)} fusion(bf16[2,4096]{1,0:T(2,128)(2,1)S(1)} %get-tuple-element.14, bf16[2,4096]{1,0:T(2,128)(2,1)S(1)} %get-tuple-element.15, bf16[2,4096]{1,0:T(2,128)(2,1)S(1)} %get-tuple-element.16, bf16[2,4096]{1,0:T(2,128)(2,1)S(1)} %get-tuple-element.13), kind=kLoop, calls=%fused_computation | loop fusion | flops 262144 | bytes 196608 | tf_op jit(solution)/shard_map/concatenate | solution.py:600
Async XLA Ops:
  0.0 28.4 %collective-permute-start = (s32[3,4096]{1,0:T(4,128)}, s32[3,4096]{1,0:T(4,128)S(1)}, u32[]{:S(2)}, u32[]{:S(2)}) collective-permute-start(s32[3,4096]{1,0:T(4,128)} %refs_0_.1), channel_id=1, source_target_pairs={{0,2},{1,3},{2,0},{3,1},{4,6},{5,7},{6,4},{7,5},{8,10},{9,11},{10,... | collective-permute-start | bytes 147464 | tf_op jit(solution)/shard_map/ppermute | solution.py:587
  3.0 25.4 %collective-permute-start.1 = (s32[3,4096]{1,0:T(4,128)}, s32[3,4096]{1,0:T(4,128)S(1)}, u32[]{:S(2)}, u32[]{:S(2)}) collective-permute-start(s32[3,4096]{1,0:T(4,128)} %refs_0_.1), channel_id=1, source_target_pairs={{0,3},{1,2},{2,1},{3,0},{4,7},{5,6},{6,5},{7,4},{8,11},{9,10},{10,... | collective-permute-start | bytes 147464 | tf_op jit(solution)/shard_map/ppermute | solution.py:587
  3.0 31.6 %collective-permute-start.4 = (s32[3,4096]{1,0:T(4,128)}, s32[3,4096]{1,0:T(4,128)S(1)}, u32[]{:S(2)}, u32[]{:S(2)}) collective-permute-start(s32[3,4096]{1,0:T(4,128)} %refs_0_.1), channel_id=1, source_target_pairs={{0,1},{1,0},{2,3},{3,2},{4,5},{5,4},{6,7},{7,6},{8,9},{9,8},{10,11... | collective-permute-start | bytes 147464 | tf_op jit(solution)/shard_map/ppermute | solution.py:587
  3.1 31.4 %copy-start = (s32[3,4096]{1,0:T(4,128)S(1)}, s32[3,4096]{1,0:T(4,128)}, u32[]{:S(2)}) copy-start(s32[3,4096]{1,0:T(4,128)} %refs_0_.1) | copy-start | bytes 147460
  28.4 1.0 %copy-start.1 = (bf16[256,512]{1,0:T(8,128)(2,1)S(1)}, bf16[256,512]{1,0:T(8,128)(2,1)}, u32[]{:S(2)}) copy-start(bf16[256,512]{1,0:T(8,128)(2,1)} %solve.1.models_ref) | copy-start | bytes 786436
  32.4 5.4 %collective-permute-start.2 = (bf16[2,4096]{1,0:T(2,128)(2,1)S(1)}, bf16[2,4096]{1,0:T(2,128)(2,1)S(1)}, u32[]{:S(2)}, u32[]{:S(2)}) collective-permute-start(bf16[2,4096]{1,0:T(2,128)(2,1)S(1)} %get-tuple-element.9), channel_id=1, source_target_pairs={{0,3},{1,2},{2,1},{3,0},{4,7},{5,6},{6,5},{7,4},{8,11},{9,10},{10,... | collective-permute-start | bytes 49160 | tf_op jit(solution)/shard_map/ppermute | solution.py:587
  34.1 3.7 %collective-permute-start.3 = (bf16[2,4096]{1,0:T(2,128)(2,1)S(1)}, bf16[2,4096]{1,0:T(2,128)(2,1)S(1)}, u32[]{:S(2)}, u32[]{:S(2)}) collective-permute-start(bf16[2,4096]{1,0:T(2,128)(2,1)S(1)} %get-tuple-element.10), channel_id=1, source_target_pairs={{0,2},{1,3},{2,0},{3,1},{4,6},{5,7},{6,4},{7,5},{8,10},{9,11},{10,... | collective-permute-start | bytes 49160 | tf_op jit(solution)/shard_map/ppermute | solution.py:587
  37.7 1.2 %collective-permute-start.5 = (bf16[2,4096]{1,0:T(2,128)(2,1)S(1)}, bf16[2,4096]{1,0:T(2,128)(2,1)S(1)}, u32[]{:S(2)}, u32[]{:S(2)}) collective-permute-start(bf16[2,4096]{1,0:T(2,128)(2,1)S(1)} %get-tuple-element.11), channel_id=1, source_target_pairs={{0,1},{1,0},{2,3},{3,2},{4,5},{5,4},{6,7},{7,6},{8,9},{9,8},{10,11... | collective-permute-start | bytes 49160 | tf_op jit(solution)/shard_map/ppermute | solution.py:587

commit v8 on v7

--- a/solution.py
+++ b/solution.py
@@ -15,8 +15,7 @@
 DEPTHS = 16
 LANES = 128
 TEAM = 4
-BLOCK = 2
-CHUNK = 512
+CHUNK = 2048
 ROWS = 32
 
 station_height = 2.0
@@ -87,7 +86,6 @@
             ("field_y2", 2 * LANES),
             ("field_yt", 2 * LANES),
             ("station_y2", 2 * grid_y),
-            ("spread", 3 * LANES),
             ("back", 5 * LANES),
             ("same", LANES),
             ("regroup", boots * LANES * max(1, boots // 2)),
@@ -122,8 +120,6 @@
             spread[c, 0, b, c, :, :, b, :] = 1
     spread = spread.reshape(5, LANES, LANES)
     back = spread.transpose(0, 2, 1).reshape(5 * LANES, LANES)
-    spread = np.concatenate([spread, np.zeros((1, LANES, LANES))])
-    spread = spread.reshape(3, 2, LANES, LANES).transpose(0, 2, 1, 3)
     same = np.einsum("ab,dc,yz->daycbz", np.eye(boots), np.ones((deep, deep)), np.ones((grid_y, grid_y)))
     same = same.reshape(LANES, LANES)
     regroup = np.einsum("st,de,ab,yz->sdaybtez", *[np.eye(n) for n in (boots, deep, boots, grid_y)])
@@ -138,7 +134,6 @@
         field_y2=np.concatenate([y_high, y_low], axis=0),
         field_yt=field_y.T,
         station_y2=np.concatenate(split(station_y)),
-        spread=spread.reshape(3 * LANES, 2 * LANES),
         back=back,
         same=same,
         regroup=regroup,
@@ -155,21 +150,6 @@
 
 def dot(a, b):
     return jnp.dot(a, b, preferred_element_type=F32)
-
-
-def interleave(ahead, behind):
-    for stage in range(len(ahead) + 1):
-        first = ahead[stage] if stage < len(ahead) else []
-        second = behind[stage - 1] if stage else []
-        done = 0
-        for i, step in enumerate(first):
-            step()
-            upto = (i + 1) * len(second) // len(first)
-            for other in second[done:upto]:
-                other()
-            done = upto
-        for other in second[done:]:
-            other()
 
 
 def solve_kernel(
@@ -193,13 +173,13 @@
     image,
     values,
     rows,
+    table_wide,
     sums,
     spread_out,
     spec_q,
     spec_i,
     spec_f,
     spec_g,
-    spec_a,
     picked_in,
     models,
     residual,
@@ -235,32 +215,32 @@
 
     stations = station_ref.shape[1]
     first = (slot_ref[0] * pl.num_programs(0) + pl.program_id(0)) * boots
-    blocks = [list(range(z, z + BLOCK)) for z in range(0, slabs, BLOCK)]
     pieces = [(z, slice(row, row + ROWS)) for z in range(slabs) for row in range(0, GRID, ROWS)]
 
     rows[...] = jnp.zeros_like(rows)
     for b in range(boots):
-        rows[b * grid_y : b * grid_y + 5, :] = observed_ref[...]
-    data[...] = jnp.transpose(rows[...])
-    for b in range(boots):
+        row = b * grid_y
+        rows[row : row + 5, :] = observed_ref[...]
         count = counts_ref[pl.ds(first + b, 1), :].astype(F32)
         for c in range(5):
-            rows[b * grid_y + c : b * grid_y + c + 1, :] = count * comp_ref[c]
-    weights[...] = jnp.transpose(rows[...])
-    values[...] = (weights[...] * data[...]).astype(BF)
-
-    station_x = station_ref[0:1, :]
-    station_y = station_ref[1:2, :]
-    place_x = (lax.broadcasted_iota(jnp.int32, (GRID, stations), 0) == station_x).astype(F32)
-    place_y = (lax.broadcasted_iota(jnp.int32, (LANES, stations), 0) == station_y).astype(F32)
-    place_xt = jnp.transpose(place_x).astype(BF)
-    place_yt = jnp.transpose(place_y)[:, :grid_y].astype(BF)
+            rows[row + 8 + c : row + 9 + c, :] = count * comp_ref[c]
+    rows[16:18, :] = station_ref[...].astype(F32)
+    turned = jnp.transpose(rows[...])
+    lane = lax.broadcasted_iota(jnp.int32, (1, LANES), 1)
+    used = lane % grid_y < 5
+    data[...] = jnp.where(used, turned, 0.0)
+    weights[...] = jnp.where(used, pltpu.roll(turned, LANES - 8, 1), 0.0)
+    values[...] = (weights[...] * data[...]).astype(BF).astype(F32)
+
+    place_x = (lax.broadcasted_iota(jnp.int32, (GRID, stations), 0) == station_ref[0:1, :]).astype(F32).astype(BF)
+    place_xt = (turned[:, 16:17] == lane.astype(F32)).astype(F32).astype(BF)
+    place_yt = (turned[:, 17:18] == lane.astype(F32)).astype(F32)[:, :grid_y].astype(BF)
 
     @pl.when(first_step)
     def _():
         copies[0].wait()
 
-    pick_xt[...] = dot(held("base_xt2", GRID), place_x.astype(BF)).astype(BF)
+    pick_xt[...] = dot(held("base_xt2", GRID), place_x).astype(BF)
     pick_x[...] = dot(place_xt, held("base_x")).astype(BF)
     station_y2 = held("station_y2", wide)
     pick_y[...] = dot(place_yt, station_y2[:grid_y]) + dot(place_yt, station_y2[grid_y:])
@@ -268,21 +248,22 @@
     @pl.when(first_step)
     def _():
         copies[1].wait()
+        for c in range(5):
+            for z in range(slabs):
+                table_wide[c, z] = table(c, z, slice(0, GRID)).astype(F32)
 
     no_sum = jnp.zeros((8, LANES), F32)
 
     def back_project():
-        spread = held("spread")
-        spread = jnp.concatenate([spread[i * LANES : (i + 1) * LANES] for i in range(3)], axis=1)
-        spreads = dot(values[...], spread[:, : 5 * LANES])
+        owner = lane // grid_y % boots * grid_y
         for row in range(0, stations, ROWS):
             at = slice(row, row + ROWS)
             trig = [pick_y[at, lane : lane + LANES] for lane in range(0, wide, LANES)]
             for c in range(5):
-                e = spreads[at, c * LANES : (c + 1) * LANES]
+                e = jnp.take_along_axis(values[at, :], jnp.broadcast_to(owner + c, (ROWS, LANES)), axis=1)
                 for i, part in enumerate(trig):
-                    lane = c * wide + i * LANES
-                    spread_out[at, lane : lane + LANES] = (e * part).astype(BF)
+                    to = c * wide + i * LANES
+                    spread_out[at, to : to + LANES] = (e * part).astype(BF)
         spec = dot(pick_xt[...], spread_out[...])
         for c, (odd_x, odd_y) in enumerate(PARITY):
             for hx in range(2):
@@ -297,75 +278,53 @@
                     for hy, part in enumerate(parts):
                         spec_q[c, hx, hy, row : row + ROWS, :] = -part if (odd_x * hx + odd_y * hy) % 2 else part
 
-        def products(block, row):
+        for row in range(0, GRID, 16):
             at = slice(row, row + 16)
-            t = [[table(c, z, at).astype(F32) for c in range(5)] for z in block]
             for hx in range(2):
+                q = [[spec_q[c, hx ^ PARITY[c][0], hy, at, :] for hy in range(2)] for c in range(5)]
                 to = slice(hx * GRID + row, hx * GRID + row + 16)
-                for hy in range(2):
-                    q = [spec_q[c, hx ^ PARITY[c][0], hy ^ PARITY[c][1], at, :] for c in range(5)]
-                    for z, tz in zip(block, t):
-                        total = tz[0] * q[0]
+                for z in range(slabs):
+                    t = [table_wide[c, z, at, :] for c in range(5)]
+                    for hy in range(2):
+                        total = t[0] * q[0][hy]
                         for c in range(1, 5):
-                            total = total + tz[c] * q[c]
-                        lane = (2 * z + hy) * LANES
-                        spec_g[to, lane : lane + LANES] = total.astype(BF)
-
-        along = {}
-
-        def inverse_x(z):
-            along[z] = dot(held("base_x"), spec_g[:, 2 * z * LANES : (2 * z + 2) * LANES]).astype(BF)
-
-        def inverse_y(z):
-            applied[z] = dot(along[z], held("field_yt", LANES))
-
-        interleave(
-            [[functools.partial(products, block, row) for row in range(0, GRID, 16)] for block in blocks],
-            [[functools.partial(f, z) for f in (inverse_x, inverse_y) for z in block] for block in blocks],
-        )
+                            total = total + t[c] * q[c][hy ^ PARITY[c][1]]
+                        spec_g[to, (2 * z + hy) * LANES : (2 * z + hy + 1) * LANES] = total.astype(BF)
+        along_x = dot(held("base_x"), spec_g[...]).astype(BF)
+        along_x = jnp.concatenate([along_x[:, 2 * z * LANES : (2 * z + 2) * LANES] for z in range(slabs)], axis=0)
+        applied[...] = dot(along_x, held("field_yt", LANES)).reshape(slabs, GRID, LANES)
 
     def predict():
-        along = {}
-
-        def forward_y(block):
-            r = residual[block[0] : block[-1] + 1].reshape(BLOCK * GRID, LANES).astype(BF)
-            y = dot(jnp.concatenate([r, r], axis=1), held("field_y2")).astype(BF)
-            for i, z in enumerate(block):
-                along[z] = jnp.concatenate([y[i * GRID : (i + 1) * GRID]] * 2, axis=0)
-
-        def forward_x(z):
-            spec_f[:, 2 * z * LANES : (2 * z + 2) * LANES] = dot(held("base_xt2"), along[z]).astype(BF)
-
-        def products(block, row):
+        r = residual[...].reshape(slabs * GRID, LANES).astype(BF)
+        y = dot(jnp.concatenate([r, r], axis=1), held("field_y2")).astype(BF)
+        y = jnp.concatenate([y[z * GRID : (z + 1) * GRID] for z in range(slabs)], axis=1)
+        spec_f[...] = dot(held("base_xt2"), jnp.concatenate([y, y], axis=0)).astype(BF)
+
+        for row in range(0, GRID, 16):
             at = [slice(hx * GRID + row, hx * GRID + row + 16) for hx in range(2)]
-            begin = block[0] % 8 == 0
-            f = {
-                (z, hx, hy): spec_f[at[hx], (2 * z + hy) * LANES : (2 * z + hy + 1) * LANES]
-                for z in block
-                for hx in range(2)
-                for hy in range(2)
-            }
+            total = [[[None] * 2 for _ in range(2)] for _ in range(5)]
+            for eight in range(0, slabs, 8):
+                part = [[[None] * 2 for _ in range(2)] for _ in range(5)]
+                for z in range(eight, min(slabs, eight + 8)):
+                    f = [
+                        [spec_f[at[hx], (2 * z + hy) * LANES : (2 * z + hy + 1) * LANES] for hy in range(2)]
+                        for hx in range(2)
+                    ]
+                    for c, (odd_x, odd_y) in enumerate(PARITY):
+                        t = table(c, z, at[0])
+                        for hx in range(2):
+                            for hy in range(2):
+                                term = t * f[hx ^ odd_x][hy ^ odd_y]
+                                old = part[c][hx][hy]
+                                part[c][hx][hy] = term if old is None else old + term
+                for c in range(5):
+                    for hx in range(2):
+                        for hy in range(2):
+                            new = part[c][hx][hy].astype(F32)
+                            total[c][hx][hy] = total[c][hx][hy] + new if eight else new
             for c, (odd_x, odd_y) in enumerate(PARITY):
-                t = [table(c, z, at[0]) for z in block]
                 for hx in range(2):
-                    parts = []
-                    for hy in range(2):
-                        total = None if begin else spec_a[c, hx, hy, at[0], :]
-                        for z, tz in zip(block, t):
-                            term = tz * f[z, hx ^ odd_x, hy ^ odd_y]
-                            total = term if total is None else total + term
-                        if block[-1] % 8 != 7 and block is not blocks[-1]:
-                            spec_a[c, hx, hy, at[0], :] = total
-                            continue
-                        total = total.astype(F32)
-                        if block[-1] >= 8:
-                            total = total + spec_q[c, hx, hy, at[0], :]
-                        if block is not blocks[-1]:
-                            spec_q[c, hx, hy, at[0], :] = total
-                            continue
-                        parts.append(-total if (odd_x * hx + odd_y * hy) % 2 else total)
-                    if not parts:
-                        continue
+                    parts = [-total[c][hx][hy] if (odd_x * hx + odd_y * hy) % 2 else total[c][hx][hy] for hy in range(2)]
                     if compact:
                         low, high = parts
                         parts = [
@@ -373,16 +332,8 @@
                             + pltpu.roll(jnp.where(low_lanes, high, low), LANES // 2, 1)
                         ]
                     for i, part in enumerate(parts):
-                        lane = c * wide + i * LANES
-                        spec_i[at[hx], lane : lane + LANES] = part.astype(BF)
-
-        interleave(
-            [
-                [functools.partial(forward_y, block)] + [functools.partial(forward_x, z) for z in block]
-                for block in blocks
-            ],
-            [[functools.partial(products, block, row) for row in range(0, GRID, 16)] for block in blocks],
-        )
+                        to = c * wide + i * LANES
+                        spec_i[at[hx], to : to + LANES] = part.astype(BF)
 
         picked = dot(pick_x[...], spec_i[...])
         for row in range(0, stations, ROWS):
@@ -461,7 +412,7 @@
             models[z, at] += step * direction[z, at]
         now = pred[...] + step * here
         pred[...] = now
-        values[...] = (weights[...] * jnp.where(fresh, here, data[...] - now)).astype(BF)
+        values[...] = (weights[...] * jnp.where(fresh, here, data[...] - now)).astype(BF).astype(F32)
         return norm, step
 
     one = jnp.ones((1, LANES), F32)
@@ -507,15 +458,15 @@
             at_stations,
             at_stations,
             at_stations,
-            vmem((stations, LANES), BF),
+            at_stations,
             vmem((LANES, stations), F32),
+            vmem((5, slabs, GRID, LANES), F32),
             vmem((8, LANES), F32),
             vmem((stations, 5 * wide), BF),
             vmem((5, 2, 2, GRID, LANES), F32),
             vmem((2 * GRID, 5 * wide), BF),
             vmem((2 * GRID, slabs * 2 * LANES), BF),
             vmem((2 * GRID, slabs * 2 * LANES), BF),
-            vmem((5, 2, 2, GRID, LANES), BF),
             vmem((stations, 5 * LANES), BF),
             field,
             field,
@@ -534,30 +485,31 @@
         cells = cell_ref[:, at]
         place = cells.astype(F32)
         wide = lambda row, rows: jnp.broadcast_to(row, (rows, CHUNK)).astype(BF)
-        y_row = wide(place[1:2], grid_y)
-        z_row = wide(place[2:3], grid_y)
-        here_y = lax.broadcasted_iota(jnp.int32, (grid_y, CHUNK), 0).astype(F32).astype(BF) == y_row
-        here_y = jnp.where(here_y, jnp.ones_like(y_row), jnp.zeros_like(y_row))
-        chosen = jnp.concatenate(
-            [jnp.where(z_row == jnp.full_like(z_row, z), here_y, jnp.zeros_like(here_y)) for z in range(DEPTHS)],
-            axis=0,
-        )
-        at_x = lax.broadcasted_iota(jnp.int32, (GRID, CHUNK), 0) == cells[0:1]
-        found = dot(models_ref[...], chosen)
-        parts = [
-            jnp.sum(jnp.where(at_x, found[b * GRID : (b + 1) * GRID], 0.0), axis=0, keepdims=True)
-            for b in range(boots)
-        ]
+        count_up = lambda rows: lax.broadcasted_iota(jnp.int32, (rows, CHUNK), 0).astype(F32).astype(BF)
+        here_y = count_up(grid_y) == wide(place[1:2], grid_y)
+        here_y = jnp.where(here_y, jnp.ones((grid_y, CHUNK), BF), jnp.zeros((grid_y, CHUNK), BF))
+        z_row = wide(place[2:3], 16)
+        none = jnp.zeros((16, CHUNK), BF)
+        chosen = []
+        for z in range(DEPTHS):
+            here_z = z_row == jnp.full((16, CHUNK), z, BF)
+            chosen += [jnp.where(here_z, here_y[i : i + 16], none) for i in range(0, grid_y, 16)]
+        found = dot(models_ref[...], jnp.concatenate(chosen, axis=0)).astype(BF)
+        at_x = count_up(GRID) == wide(place[0:1], GRID)
+        parts = []
+        for b in range(boots):
+            part = jnp.where(at_x, found[b * GRID : (b + 1) * GRID], jnp.zeros((GRID, CHUNK), BF))
+            while part.shape[0] > 16:
+                half = part.shape[0] // 2
+                part = part[:half] + part[half:]
+            parts.append(jnp.sum(part.astype(F32), axis=0, keepdims=True))
         out_ref[:, at] = jnp.concatenate(parts, axis=0).astype(BF)
 
-    per = max(1, 4 // count)
-
-    @pl.loop(0, refs[0].shape[1] // (per * CHUNK))
+    @pl.loop(0, refs[0].shape[1] // CHUNK)
     def _(step):
-        for i in range(per):
-            at = pl.ds(pl.multiple_of((step * per + i) * CHUNK, CHUNK), CHUNK)
-            for cell_ref, out_ref in zip(refs[:count], refs[count:]):
-                pick_chunk(cell_ref, out_ref, at)
+        at = pl.ds(pl.multiple_of(step * CHUNK, CHUNK), CHUNK)
+        for cell_ref, out_ref in zip(refs[:count], refs[count:]):
+            pick_chunk(cell_ref, out_ref, at)
 
 
 def pick(models, cells, grid_y):

time: 40 us -> 37.3 us (0.932)
  Pallas kernels: 31.4 us -> 28.8 us
    pallas_call x1, Pallas kernels: 25.2 us -> 23.6 us  [solve(): pl.pallas_call(functools.partial(solve_kernel, grid_y, boots), out_shape=...]
    pallas_call x2, Pallas kernels: 6.18 us -> 5.14 us  [pick(): pl.pallas_call(functools.partial(pick_kernel, grid_y, boots, len(cells)),...]
  transfers between devices with their start and end apart: 6 -> 6, of which waited for: 1 -> 2; matrix products, arithmetic and copies ran while one was open for 0% -> 0% of each run, Pallas kernels for 79% -> 78%
where the time goes in v8:
time: 37.3 us; the launch traced here: 37.1 us
  Pallas kernels  28.8 us (77%)
  starting transfers between devices  5.36 us (14%)
  waiting for transfers between devices  1.15 us (3%)
  local copies, waits for them, and re-layouts  0.95 us (3%)
  other arithmetic  0.81 us (2%)
    pallas_call x1, Pallas kernels, solve(): pl.pallas_call(functools.partial(solve_kernel, grid_y, boots), out_shape=...  23.6 us
    ppermute x6, starting transfers between devices, swap(): return lax.ppermute(a, 'wide', [(i, i ^ k) for i in range(wide)])  5.36 us
    pallas_call x2, Pallas kernels, pick(): pl.pallas_call(functools.partial(pick_kernel, grid_y, boots, len(cells)),...  5.14 us
    ppermute x6, waiting for transfers between devices, swap(): return lax.ppermute(a, 'wide', [(i, i ^ k) for i in range(wide)])  1.15 us
    unnamed x4, local copies, waits for them, and re-layouts  0.95 us
  transfers between devices with their start and end apart: 6, of which 2 were waited for; matrix products, arithmetic and copies ran while one was open for 0% of the time, Pallas kernels for 78%

profile of v8, /device:TPU:0, one launch (start us, length us, event | category | flops | bytes accessed | tf_op | source)
XLA Modules:
  0.0 37.1 jit_solution(16380830140347953831)
XLA Ops:
  0.0 3.0 %collective-permute-start = (s32[3,4096]{1,0:T(4,128)}, s32[3,4096]{1,0:T(4,128)S(1)}, u32[]{:S(2)}, u32[]{:S(2)}) collective-permute-start(s32[3,4096]{1,0:T(4,128)} %refs_0_.1), channel_id=1, source_target_pairs={{0,2},{1,3},{2,0},{3,1},{4,6},{5,7},{6,4},{7,5},{8,10},{9,11},{10,... | collective-permute-start | bytes 147464 | tf_op jit(solution)/shard_map/ppermute | solution.py:539
  3.0 0.0 collective-permute-start.1
  3.0 0.1 collective-permute-start.4
  3.1 0.0 copy-start
  3.1 23.6 %solve.1.models_ref = bf16[256,512]{1,0:T(8,128)(2,1)} custom-call(s32[1]{0:T(128)} %bitcast.slot_ref, f32[5]{0:T(128)} %comp_ref.1, s32[2,512]{1,0:T(2,128)} %station_ref.1, f32[5,512]{1,0:T(8,128)} %observed_ref.1, s32[8,512]{1,0:T(8,128)} %counts_ref.1, bf16[16384,256]{1,0:T(8,128)(2,1)} %constant.12.clone.source), custom_call_target="tpu_custom_call" | custom-call | flops 10000000000 | bytes 10000000 | tf_op jit(solution)/shard_map/solve/pallas_call | solution.py:445
  26.8 0.0 collective-permute-done.refs_0_
  26.8 0.0 collective-permute-done.1.refs_1_
  26.8 0.0 copy-start.1
  26.8 0.9 %copy-done.1 = bf16[256,512]{1,0:T(8,128)(2,1)S(1)} copy-done((bf16[256,512]{1,0:T(8,128)(2,1)S(1)}, bf16[256,512]{1,0:T(8,128)(2,1)}, u32[]{:S(2)}) %copy-start.1) | copy-done | bytes 262168
  27.7 2.6 %pick.2 = (bf16[2,4096]{1,0:T(2,128)(2,1)S(1)}, bf16[2,4096]{1,0:T(2,128)(2,1)S(1)}) custom-call(bf16[256,512]{1,0:T(8,128)(2,1)S(1)} %copy-done.1, s32[3,4096]{1,0:T(4,128)S(1)} %collective-permute-done.refs_0_, s32[3,4096]{1,0:T(4,128)S(1)} %collective-permute-done.1.refs_1_), custom_call_target="tpu_custom_call" | custom-call | flops 2147483648 | bytes 1000000 | tf_op jit(solution)/shard_map/pick/pallas_call | solution.py:519
  30.3 1.7 %collective-permute-start.2 = (bf16[2,4096]{1,0:T(2,128)(2,1)S(1)}, bf16[2,4096]{1,0:T(2,128)(2,1)S(1)}, u32[]{:S(2)}, u32[]{:S(2)}) collective-permute-start(bf16[2,4096]{1,0:T(2,128)(2,1)S(1)} %get-tuple-element.9), channel_id=1, source_target_pairs={{0,3},{1,2},{2,1},{3,0},{4,7},{5,6},{6,5},{7,4},{8,11},{9,10},{10,... | collective-permute-start | bytes 49160 | tf_op jit(solution)/shard_map/ppermute | solution.py:539
  32.0 0.5 %collective-permute-start.3 = (bf16[2,4096]{1,0:T(2,128)(2,1)S(1)}, bf16[2,4096]{1,0:T(2,128)(2,1)S(1)}, u32[]{:S(2)}, u32[]{:S(2)}) collective-permute-start(bf16[2,4096]{1,0:T(2,128)(2,1)S(1)} %get-tuple-element.10), channel_id=1, source_target_pairs={{0,2},{1,3},{2,0},{3,1},{4,6},{5,7},{6,4},{7,5},{8,10},{9,11},{10,... | collective-permute-start | bytes 49160 | tf_op jit(solution)/shard_map/ppermute | solution.py:539
  32.5 0.0 collective-permute-done.4.refs_1_
  32.5 0.0 copy-done
  32.5 2.6 %pick.3 = (bf16[2,4096]{1,0:T(2,128)(2,1)S(1)}, bf16[2,4096]{1,0:T(2,128)(2,1)S(1)}) custom-call(bf16[256,512]{1,0:T(8,128)(2,1)S(1)} %copy-done.1, s32[3,4096]{1,0:T(4,128)S(1)} %copy-done, s32[3,4096]{1,0:T(4,128)S(1)} %collective-permute-done.4.refs_1_), custom_call_target="tpu_custom_call" | custom-call | flops 2147483648 | bytes 1000000 | tf_op jit(solution)/shard_map/pick/pallas_call | solution.py:519
  35.0 0.1 collective-permute-start.5
  35.1 0.0 collective-permute-done.2
  35.1 0.6 %collective-permute-done.3 = bf16[2,4096]{1,0:T(2,128)(2,1)S(1)} collective-permute-done((bf16[2,4096]{1,0:T(2,128)(2,1)S(1)}, bf16[2,4096]{1,0:T(2,128)(2,1)S(1)}, u32[]{:S(2)}, u32[]{:S(2)}) %collective-permute-start.3) | collective-permute-done | bytes 16416 | tf_op jit(solution)/shard_map/ppermute | solution.py:539
  35.7 0.6 %collective-permute-done.5 = bf16[2,4096]{1,0:T(2,128)(2,1)S(1)} collective-permute-done((bf16[2,4096]{1,0:T(2,128)(2,1)S(1)}, bf16[2,4096]{1,0:T(2,128)(2,1)S(1)}, u32[]{:S(2)}, u32[]{:S(2)}) %collective-permute-start.5) | collective-permute-done | bytes 16416 | tf_op jit(solution)/shard_map/ppermute | solution.py:539
  36.3 0.1 broadcast_select_fusion.11
  36.4 0.7 %maximum_convert_fusion = f32[8,4096]{1,0:T(8,128)} fusion(bf16[2,4096]{1,0:T(2,128)(2,1)S(1)} %get-tuple-element.14, bf16[2,4096]{1,0:T(2,128)(2,1)S(1)} %get-tuple-element.15, bf16[2,4096]{1,0:T(2,128)(2,1)S(1)} %get-tuple-element.16, bf16[2,4096]{1,0:T(2,128)(2,1)S(1)} %get-tuple-element.13), kind=kLoop, calls=%fused_computation | loop fusion | flops 262144 | bytes 196608 | tf_op jit(solution)/shard_map/concatenate | solution.py:552
Async XLA Ops:
  0.0 26.8 %collective-permute-start = (s32[3,4096]{1,0:T(4,128)}, s32[3,4096]{1,0:T(4,128)S(1)}, u32[]{:S(2)}, u32[]{:S(2)}) collective-permute-start(s32[3,4096]{1,0:T(4,128)} %refs_0_.1), channel_id=1, source_target_pairs={{0,2},{1,3},{2,0},{3,1},{4,6},{5,7},{6,4},{7,5},{8,10},{9,11},{10,... | collective-permute-start | bytes 147464 | tf_op jit(solution)/shard_map/ppermute | solution.py:539
  3.0 23.8 %collective-permute-start.1 = (s32[3,4096]{1,0:T(4,128)}, s32[3,4096]{1,0:T(4,128)S(1)}, u32[]{:S(2)}, u32[]{:S(2)}) collective-permute-start(s32[3,4096]{1,0:T(4,128)} %refs_0_.1), channel_id=1, source_target_pairs={{0,3},{1,2},{2,1},{3,0},{4,7},{5,6},{6,5},{7,4},{8,11},{9,10},{10,... | collective-permute-start | bytes 147464 | tf_op jit(solution)/shard_map/ppermute | solution.py:539
  3.0 29.5 %collective-permute-start.4 = (s32[3,4096]{1,0:T(4,128)}, s32[3,4096]{1,0:T(4,128)S(1)}, u32[]{:S(2)}, u32[]{:S(2)}) collective-permute-start(s32[3,4096]{1,0:T(4,128)} %refs_0_.1), channel_id=1, source_target_pairs={{0,1},{1,0},{2,3},{3,2},{4,5},{5,4},{6,7},{7,6},{8,9},{9,8},{10,11... | collective-permute-start | bytes 147464 | tf_op jit(solution)/shard_map/ppermute | solution.py:539
  3.1 29.3 %copy-start = (s32[3,4096]{1,0:T(4,128)S(1)}, s32[3,4096]{1,0:T(4,128)}, u32[]{:S(2)}) copy-start(s32[3,4096]{1,0:T(4,128)} %refs_0_.1) | copy-start | bytes 147460
  26.8 1.0 %copy-start.1 = (bf16[256,512]{1,0:T(8,128)(2,1)S(1)}, bf16[256,512]{1,0:T(8,128)(2,1)}, u32[]{:S(2)}) copy-start(bf16[256,512]{1,0:T(8,128)(2,1)} %solve.1.models_ref) | copy-start | bytes 786436
  30.3 4.8 %collective-permute-start.2 = (bf16[2,4096]{1,0:T(2,128)(2,1)S(1)}, bf16[2,4096]{1,0:T(2,128)(2,1)S(1)}, u32[]{:S(2)}, u32[]{:S(2)}) collective-permute-start(bf16[2,4096]{1,0:T(2,128)(2,1)S(1)} %get-tuple-element.9), channel_id=1, source_target_pairs={{0,3},{1,2},{2,1},{3,0},{4,7},{5,6},{6,5},{7,4},{8,11},{9,10},{10,... | collective-permute-start | bytes 49160 | tf_op jit(solution)/shard_map/ppermute | solution.py:539
  32.0 3.7 %collective-permute-start.3 = (bf16[2,4096]{1,0:T(2,128)(2,1)S(1)}, bf16[2,4096]{1,0:T(2,128)(2,1)S(1)}, u32[]{:S(2)}, u32[]{:S(2)}) collective-permute-start(bf16[2,4096]{1,0:T(2,128)(2,1)S(1)} %get-tuple-element.10), channel_id=1, source_target_pairs={{0,2},{1,3},{2,0},{3,1},{4,6},{5,7},{6,4},{7,5},{8,10},{9,11},{10,... | collective-permute-start | bytes 49160 | tf_op jit(solution)/shard_map/ppermute | solution.py:539
  35.0 1.2 %collective-permute-start.5 = (bf16[2,4096]{1,0:T(2,128)(2,1)S(1)}, bf16[2,4096]{1,0:T(2,128)(2,1)S(1)}, u32[]{:S(2)}, u32[]{:S(2)}) collective-permute-start(bf16[2,4096]{1,0:T(2,128)(2,1)S(1)} %get-tuple-element.11), channel_id=1, source_target_pairs={{0,1},{1,0},{2,3},{3,2},{4,5},{5,4},{6,7},{7,6},{8,9},{9,8},{10,11... | collective-permute-start | bytes 49160 | tf_op jit(solution)/shard_map/ppermute | solution.py:539

commit v9 on v8

--- a/solution.py
+++ b/solution.py
@@ -86,6 +86,7 @@
             ("field_y2", 2 * LANES),
             ("field_yt", 2 * LANES),
             ("station_y2", 2 * grid_y),
+            ("spread", 3 * LANES),
             ("back", 5 * LANES),
             ("same", LANES),
             ("regroup", boots * LANES * max(1, boots // 2)),
@@ -120,6 +121,8 @@
             spread[c, 0, b, c, :, :, b, :] = 1
     spread = spread.reshape(5, LANES, LANES)
     back = spread.transpose(0, 2, 1).reshape(5 * LANES, LANES)
+    spread = np.concatenate([spread, np.zeros((1, LANES, LANES))])
+    spread = spread.reshape(3, 2, LANES, LANES).transpose(0, 2, 1, 3)
     same = np.einsum("ab,dc,yz->daycbz", np.eye(boots), np.ones((deep, deep)), np.ones((grid_y, grid_y)))
     same = same.reshape(LANES, LANES)
     regroup = np.einsum("st,de,ab,yz->sdaybtez", *[np.eye(n) for n in (boots, deep, boots, grid_y)])
@@ -134,6 +137,7 @@
         field_y2=np.concatenate([y_high, y_low], axis=0),
         field_yt=field_y.T,
         station_y2=np.concatenate(split(station_y)),
+        spread=spread.reshape(3 * LANES, 2 * LANES),
         back=back,
         same=same,
         regroup=regroup,
@@ -230,7 +234,7 @@
     used = lane % grid_y < 5
     data[...] = jnp.where(used, turned, 0.0)
     weights[...] = jnp.where(used, pltpu.roll(turned, LANES - 8, 1), 0.0)
-    values[...] = (weights[...] * data[...]).astype(BF).astype(F32)
+    values[...] = (weights[...] * data[...]).astype(BF)
 
     place_x = (lax.broadcasted_iota(jnp.int32, (GRID, stations), 0) == station_ref[0:1, :]).astype(F32).astype(BF)
     place_xt = (turned[:, 16:17] == lane.astype(F32)).astype(F32).astype(BF)
@@ -255,12 +259,14 @@
     no_sum = jnp.zeros((8, LANES), F32)
 
     def back_project():
-        owner = lane // grid_y % boots * grid_y
+        spread = held("spread")
+        spread = jnp.concatenate([spread[i * LANES : (i + 1) * LANES] for i in range(3)], axis=1)
+        spreads = dot(values[...], spread[:, : 5 * LANES])
         for row in range(0, stations, ROWS):
             at = slice(row, row + ROWS)
             trig = [pick_y[at, lane : lane + LANES] for lane in range(0, wide, LANES)]
             for c in range(5):
-                e = jnp.take_along_axis(values[at, :], jnp.broadcast_to(owner + c, (ROWS, LANES)), axis=1)
+                e = spreads[at, c * LANES : (c + 1) * LANES]
                 for i, part in enumerate(trig):
                     to = c * wide + i * LANES
                     spread_out[at, to : to + LANES] = (e * part).astype(BF)
@@ -412,7 +418,7 @@
             models[z, at] += step * direction[z, at]
         now = pred[...] + step * here
         pred[...] = now
-        values[...] = (weights[...] * jnp.where(fresh, here, data[...] - now)).astype(BF).astype(F32)
+        values[...] = (weights[...] * jnp.where(fresh, here, data[...] - now)).astype(BF)
         return norm, step
 
     one = jnp.ones((1, LANES), F32)
@@ -458,7 +464,7 @@
             at_stations,
             at_stations,
             at_stations,
-            at_stations,
+            vmem((stations, LANES), BF),
             vmem((LANES, stations), F32),
             vmem((5, slabs, GRID, LANES), F32),
             vmem((8, LANES), F32),

time: 37.3 us -> 35.6 us (0.954)
  Pallas kernels: 28.8 us -> 27 us
    pallas_call x1, Pallas kernels: 23.6 us -> 21.9 us  [solve(): pl.pallas_call(functools.partial(solve_kernel, grid_y, boots), out_shape=...]
  transfers between devices with their start and end apart: 6 -> 6, of which waited for: 2 -> 2; matrix products, arithmetic and copies ran while one was open for 0% -> 0% of each run, Pallas kernels for 78% -> 76%
where the time goes in v9:
time: 35.6 us; the launch traced here: 35.4 us
  Pallas kernels  27 us (76%)
  starting transfers between devices  5.36 us (15%)
  waiting for transfers between devices  1.15 us (3%)
  local copies, waits for them, and re-layouts  0.95 us (3%)
  other arithmetic  0.81 us (2%)
    pallas_call x1, Pallas kernels, solve(): pl.pallas_call(functools.partial(solve_kernel, grid_y, boots), out_shape=...  21.9 us
    ppermute x6, starting transfers between devices, swap(): return lax.ppermute(a, 'wide', [(i, i ^ k) for i in range(wide)])  5.36 us
    pallas_call x2, Pallas kernels, pick(): pl.pallas_call(functools.partial(pick_kernel, grid_y, boots, len(cells)),...  5.14 us
    ppermute x6, waiting for transfers between devices, swap(): return lax.ppermute(a, 'wide', [(i, i ^ k) for i in range(wide)])  1.15 us
    unnamed x4, local copies, waits for them, and re-layouts  0.95 us
    concatenate x1, other arithmetic, local(): return jnp.concatenate(blocks, axis=0)  0.73 us
  transfers between devices with their start and end apart: 6, of which 2 were waited for; matrix products, arithmetic and copies ran while one was open for 0% of the time, Pallas kernels for 76%

profile of v9, /device:TPU:0, one launch (start us, length us, event | category | flops | bytes accessed | tf_op | source)
XLA Modules:
  0.0 35.4 jit_solution(1130552077840581609)
XLA Ops:
  0.0 3.0 %collective-permute-start = (s32[3,4096]{1,0:T(4,128)}, s32[3,4096]{1,0:T(4,128)S(1)}, u32[]{:S(2)}, u32[]{:S(2)}) collective-permute-start(s32[3,4096]{1,0:T(4,128)} %refs_0_.1), channel_id=1, source_target_pairs={{0,2},{1,3},{2,0},{3,1},{4,6},{5,7},{6,4},{7,5},{8,10},{9,11},{10,... | collective-permute-start | bytes 147464 | tf_op jit(solution)/shard_map/ppermute | solution.py:545
  3.0 0.0 collective-permute-start.1
  3.0 0.1 collective-permute-start.4
  3.1 0.0 copy-start
  3.1 21.9 %solve.1.models_ref = bf16[256,512]{1,0:T(8,128)(2,1)} custom-call(s32[1]{0:T(128)} %bitcast.slot_ref, f32[5]{0:T(128)} %comp_ref.1, s32[2,512]{1,0:T(2,128)} %station_ref.1, f32[5,512]{1,0:T(8,128)} %observed_ref.1, s32[8,512]{1,0:T(8,128)} %counts_ref.1, bf16[16384,256]{1,0:T(8,128)(2,1)} %constant.12.clone.source), custom_call_target="tpu_custom_call" | custom-call | flops 10000000000 | bytes 10000000 | tf_op jit(solution)/shard_map/solve/pallas_call | solution.py:451
  25.0 0.0 collective-permute-done.refs_0_
  25.0 0.0 collective-permute-done.1.refs_1_
  25.1 0.0 copy-start.1
  25.1 0.9 %copy-done.1 = bf16[256,512]{1,0:T(8,128)(2,1)S(1)} copy-done((bf16[256,512]{1,0:T(8,128)(2,1)S(1)}, bf16[256,512]{1,0:T(8,128)(2,1)}, u32[]{:S(2)}) %copy-start.1) | copy-done | bytes 262168
  26.0 2.6 %pick.2 = (bf16[2,4096]{1,0:T(2,128)(2,1)S(1)}, bf16[2,4096]{1,0:T(2,128)(2,1)S(1)}) custom-call(bf16[256,512]{1,0:T(8,128)(2,1)S(1)} %copy-done.1, s32[3,4096]{1,0:T(4,128)S(1)} %collective-permute-done.refs_0_, s32[3,4096]{1,0:T(4,128)S(1)} %collective-permute-done.1.refs_1_), custom_call_target="tpu_custom_call" | custom-call | flops 2147483648 | bytes 1000000 | tf_op jit(solution)/shard_map/pick/pallas_call | solution.py:525
  28.6 1.7 %collective-permute-start.2 = (bf16[2,4096]{1,0:T(2,128)(2,1)S(1)}, bf16[2,4096]{1,0:T(2,128)(2,1)S(1)}, u32[]{:S(2)}, u32[]{:S(2)}) collective-permute-start(bf16[2,4096]{1,0:T(2,128)(2,1)S(1)} %get-tuple-element.9), channel_id=1, source_target_pairs={{0,3},{1,2},{2,1},{3,0},{4,7},{5,6},{6,5},{7,4},{8,11},{9,10},{10,... | collective-permute-start | bytes 49160 | tf_op jit(solution)/shard_map/ppermute | solution.py:545
  30.3 0.5 %collective-permute-start.3 = (bf16[2,4096]{1,0:T(2,128)(2,1)S(1)}, bf16[2,4096]{1,0:T(2,128)(2,1)S(1)}, u32[]{:S(2)}, u32[]{:S(2)}) collective-permute-start(bf16[2,4096]{1,0:T(2,128)(2,1)S(1)} %get-tuple-element.10), channel_id=1, source_target_pairs={{0,2},{1,3},{2,0},{3,1},{4,6},{5,7},{6,4},{7,5},{8,10},{9,11},{10,... | collective-permute-start | bytes 49160 | tf_op jit(solution)/shard_map/ppermute | solution.py:545
  30.7 0.0 collective-permute-done.4.refs_1_
  30.7 0.0 copy-done
  30.7 2.6 %pick.3 = (bf16[2,4096]{1,0:T(2,128)(2,1)S(1)}, bf16[2,4096]{1,0:T(2,128)(2,1)S(1)}) custom-call(bf16[256,512]{1,0:T(8,128)(2,1)S(1)} %copy-done.1, s32[3,4096]{1,0:T(4,128)S(1)} %copy-done, s32[3,4096]{1,0:T(4,128)S(1)} %collective-permute-done.4.refs_1_), custom_call_target="tpu_custom_call" | custom-call | flops 2147483648 | bytes 1000000 | tf_op jit(solution)/shard_map/pick/pallas_call | solution.py:525
  33.3 0.1 collective-permute-start.5
  33.4 0.0 collective-permute-done.2
  33.4 0.6 %collective-permute-done.3 = bf16[2,4096]{1,0:T(2,128)(2,1)S(1)} collective-permute-done((bf16[2,4096]{1,0:T(2,128)(2,1)S(1)}, bf16[2,4096]{1,0:T(2,128)(2,1)S(1)}, u32[]{:S(2)}, u32[]{:S(2)}) %collective-permute-start.3) | collective-permute-done | bytes 16416 | tf_op jit(solution)/shard_map/ppermute | solution.py:545
  34.0 0.6 %collective-permute-done.5 = bf16[2,4096]{1,0:T(2,128)(2,1)S(1)} collective-permute-done((bf16[2,4096]{1,0:T(2,128)(2,1)S(1)}, bf16[2,4096]{1,0:T(2,128)(2,1)S(1)}, u32[]{:S(2)}, u32[]{:S(2)}) %collective-permute-start.5) | collective-permute-done | bytes 16416 | tf_op jit(solution)/shard_map/ppermute | solution.py:545
  34.5 0.1 broadcast_select_fusion.11
  34.6 0.7 %maximum_convert_fusion = f32[8,4096]{1,0:T(8,128)} fusion(bf16[2,4096]{1,0:T(2,128)(2,1)S(1)} %get-tuple-element.14, bf16[2,4096]{1,0:T(2,128)(2,1)S(1)} %get-tuple-element.15, bf16[2,4096]{1,0:T(2,128)(2,1)S(1)} %get-tuple-element.16, bf16[2,4096]{1,0:T(2,128)(2,1)S(1)} %get-tuple-element.13), kind=kLoop, calls=%fused_computation | loop fusion | flops 262144 | bytes 196608 | tf_op jit(solution)/shard_map/concatenate | solution.py:558
Async XLA Ops:
  0.0 25.0 %collective-permute-start = (s32[3,4096]{1,0:T(4,128)}, s32[3,4096]{1,0:T(4,128)S(1)}, u32[]{:S(2)}, u32[]{:S(2)}) collective-permute-start(s32[3,4096]{1,0:T(4,128)} %refs_0_.1), channel_id=1, source_target_pairs={{0,2},{1,3},{2,0},{3,1},{4,6},{5,7},{6,4},{7,5},{8,10},{9,11},{10,... | collective-permute-start | bytes 147464 | tf_op jit(solution)/shard_map/ppermute | solution.py:545
  3.0 22.1 %collective-permute-start.1 = (s32[3,4096]{1,0:T(4,128)}, s32[3,4096]{1,0:T(4,128)S(1)}, u32[]{:S(2)}, u32[]{:S(2)}) collective-permute-start(s32[3,4096]{1,0:T(4,128)} %refs_0_.1), channel_id=1, source_target_pairs={{0,3},{1,2},{2,1},{3,0},{4,7},{5,6},{6,5},{7,4},{8,11},{9,10},{10,... | collective-permute-start | bytes 147464 | tf_op jit(solution)/shard_map/ppermute | solution.py:545
  3.0 27.7 %collective-permute-start.4 = (s32[3,4096]{1,0:T(4,128)}, s32[3,4096]{1,0:T(4,128)S(1)}, u32[]{:S(2)}, u32[]{:S(2)}) collective-permute-start(s32[3,4096]{1,0:T(4,128)} %refs_0_.1), channel_id=1, source_target_pairs={{0,1},{1,0},{2,3},{3,2},{4,5},{5,4},{6,7},{7,6},{8,9},{9,8},{10,11... | collective-permute-start | bytes 147464 | tf_op jit(solution)/shard_map/ppermute | solution.py:545
  3.1 27.6 %copy-start = (s32[3,4096]{1,0:T(4,128)S(1)}, s32[3,4096]{1,0:T(4,128)}, u32[]{:S(2)}) copy-start(s32[3,4096]{1,0:T(4,128)} %refs_0_.1) | copy-start | bytes 147460
  25.1 1.0 %copy-start.1 = (bf16[256,512]{1,0:T(8,128)(2,1)S(1)}, bf16[256,512]{1,0:T(8,128)(2,1)}, u32[]{:S(2)}) copy-start(bf16[256,512]{1,0:T(8,128)(2,1)} %solve.1.models_ref) | copy-start | bytes 786436
  28.6 4.8 %collective-permute-start.2 = (bf16[2,4096]{1,0:T(2,128)(2,1)S(1)}, bf16[2,4096]{1,0:T(2,128)(2,1)S(1)}, u32[]{:S(2)}, u32[]{:S(2)}) collective-permute-start(bf16[2,4096]{1,0:T(2,128)(2,1)S(1)} %get-tuple-element.9), channel_id=1, source_target_pairs={{0,3},{1,2},{2,1},{3,0},{4,7},{5,6},{6,5},{7,4},{8,11},{9,10},{10,... | collective-permute-start | bytes 49160 | tf_op jit(solution)/shard_map/ppermute | solution.py:545
  30.3 3.7 %collective-permute-start.3 = (bf16[2,4096]{1,0:T(2,128)(2,1)S(1)}, bf16[2,4096]{1,0:T(2,128)(2,1)S(1)}, u32[]{:S(2)}, u32[]{:S(2)}) collective-permute-start(bf16[2,4096]{1,0:T(2,128)(2,1)S(1)} %get-tuple-element.10), channel_id=1, source_target_pairs={{0,2},{1,3},{2,0},{3,1},{4,6},{5,7},{6,4},{7,5},{8,10},{9,11},{10,... | collective-permute-start | bytes 49160 | tf_op jit(solution)/shard_map/ppermute | solution.py:545
  33.3 1.2 %collective-permute-start.5 = (bf16[2,4096]{1,0:T(2,128)(2,1)S(1)}, bf16[2,4096]{1,0:T(2,128)(2,1)S(1)}, u32[]{:S(2)}, u32[]{:S(2)}) collective-permute-start(bf16[2,4096]{1,0:T(2,128)(2,1)S(1)} %get-tuple-element.11), channel_id=1, source_target_pairs={{0,1},{1,0},{2,3},{3,2},{4,5},{5,4},{6,7},{7,6},{8,9},{9,8},{10,11... | collective-permute-start | bytes 49160 | tf_op jit(solution)/shard_map/ppermute | solution.py:545

commit v10 on v9

--- a/solution.py
+++ b/solution.py
@@ -111,14 +111,11 @@
     base_y = basis(grid_y).reshape(grid_y, 2, grid_y)
     copies = deep * boots
     field_y = np.einsum("ab,yhl->ayhbl", np.eye(copies), base_y).reshape(LANES, 2 * LANES)
-    compact = deep == 2
-    near = 1 if compact else deep
-    station_y = np.einsum("b,yhl->yhbl", np.ones(near * boots), base_y).reshape(grid_y, -1)
-    halves = 2 if compact else 1
-    spread = np.zeros((5, deep, boots, grid_y, halves, near, boots, grid_y))
+    station_y = np.einsum("b,yhl->yhbl", np.ones(copies), base_y).reshape(grid_y, 2 * LANES)
+    spread = np.zeros((5, deep, boots, grid_y, deep, boots, grid_y))
     for c in range(5):
         for b in range(boots):
-            spread[c, 0, b, c, :, :, b, :] = 1
+            spread[c, 0, b, c, :, b, :] = 1
     spread = spread.reshape(5, LANES, LANES)
     back = spread.transpose(0, 2, 1).reshape(5 * LANES, LANES)
     spread = np.concatenate([spread, np.zeros((1, LANES, LANES))])
@@ -195,9 +192,7 @@
     slabs = DEPTHS // deep
     where = layout(grid_y, boots)
     split_row = where.at["table"][0]
-    compact = deep == 2
-    wide = LANES if compact else 2 * LANES
-    low_lanes = lax.broadcasted_iota(jnp.int32, (1, LANES), 1) < LANES // 2
+    wide = 2 * LANES
     copies = [
         pltpu.make_async_copy(source.at[a:b], const.at[a:b], copied.at[i])
         for i, (a, b) in enumerate([(0, split_row), (split_row, where.rows)])
@@ -246,7 +241,7 @@
 
     pick_xt[...] = dot(held("base_xt2", GRID), place_x).astype(BF)
     pick_x[...] = dot(place_xt, held("base_x")).astype(BF)
-    station_y2 = held("station_y2", wide)
+    station_y2 = held("station_y2")
     pick_y[...] = dot(place_yt, station_y2[:grid_y]) + dot(place_yt, station_y2[grid_y:])
 
     @pl.when(first_step)
@@ -273,16 +268,9 @@
         spec = dot(pick_xt[...], spread_out[...])
         for c, (odd_x, odd_y) in enumerate(PARITY):
             for hx in range(2):
-                for row in range(0, GRID, ROWS):
-                    at = slice(hx * GRID + row, hx * GRID + row + ROWS)
-                    if compact:
-                        part = spec[at, c * LANES : (c + 1) * LANES]
-                        turned = pltpu.roll(part, LANES // 2, 1)
-                        parts = [jnp.where(low_lanes, part, turned), jnp.where(low_lanes, turned, part)]
-                    else:
-                        parts = [spec[at, lane : lane + LANES] for lane in (c * wide, c * wide + LANES)]
-                    for hy, part in enumerate(parts):
-                        spec_q[c, hx, hy, row : row + ROWS, :] = -part if (odd_x * hx + odd_y * hy) % 2 else part
+                for hy in range(2):
+                    part = spec[hx * GRID : (hx + 1) * GRID, c * wide + hy * LANES : c * wide + (hy + 1) * LANES]
+                    spec_q[c, hx, hy] = -part if (odd_x * hx + odd_y * hy) % 2 else part
 
         for row in range(0, GRID, 16):
             at = slice(row, row + 16)
@@ -326,20 +314,14 @@
                 for c in range(5):
                     for hx in range(2):
                         for hy in range(2):
-                            new = part[c][hx][hy].astype(F32)
-                            total[c][hx][hy] = total[c][hx][hy] + new if eight else new
+                            new = part[c][hx][hy]
+                            total[c][hx][hy] = total[c][hx][hy].astype(F32) + new.astype(F32) if eight else new
             for c, (odd_x, odd_y) in enumerate(PARITY):
                 for hx in range(2):
-                    parts = [-total[c][hx][hy] if (odd_x * hx + odd_y * hy) % 2 else total[c][hx][hy] for hy in range(2)]
-                    if compact:
-                        low, high = parts
-                        parts = [
-                            jnp.where(low_lanes, low, high)
-                            + pltpu.roll(jnp.where(low_lanes, high, low), LANES // 2, 1)
-                        ]
-                    for i, part in enumerate(parts):
-                        to = c * wide + i * LANES
-                        spec_i[at[hx], to : to + LANES] = part.astype(BF)
+                    for hy in range(2):
+                        part = total[c][hx][hy].astype(BF)
+                        part = -part if (odd_x * hx + odd_y * hy) % 2 else part
+                        spec_i[at[hx], c * wide + hy * LANES : c * wide + (hy + 1) * LANES] = part
 
         picked = dot(pick_x[...], spec_i[...])
         for row in range(0, stations, ROWS):
@@ -446,7 +428,7 @@
     smem = pl.BlockSpec(memory_space=pltpu.SMEM)
     field = vmem((slabs, GRID, LANES), F32)
     at_stations = vmem((stations, LANES), F32)
-    wide = LANES if 2 * slabs == DEPTHS else 2 * LANES
+    wide = 2 * LANES
     inputs = [station_index, observed, counts]
     return pl.pallas_call(
         functools.partial(solve_kernel, grid_y, boots),
@@ -502,14 +484,11 @@
             chosen += [jnp.where(here_z, here_y[i : i + 16], none) for i in range(0, grid_y, 16)]
         found = dot(models_ref[...], jnp.concatenate(chosen, axis=0)).astype(BF)
         at_x = count_up(GRID) == wide(place[0:1], GRID)
-        parts = []
-        for b in range(boots):
-            part = jnp.where(at_x, found[b * GRID : (b + 1) * GRID], jnp.zeros((GRID, CHUNK), BF))
-            while part.shape[0] > 16:
-                half = part.shape[0] // 2
-                part = part[:half] + part[half:]
-            parts.append(jnp.sum(part.astype(F32), axis=0, keepdims=True))
-        out_ref[:, at] = jnp.concatenate(parts, axis=0).astype(BF)
+        none = jnp.zeros((GRID, CHUNK), BF)
+        parts = [jnp.where(at_x, found[b * GRID : (b + 1) * GRID], none) for b in range(boots)]
+        owner = lax.broadcasted_iota(jnp.int32, (16, boots * GRID), 1) // GRID
+        owner = (owner == lax.broadcasted_iota(jnp.int32, (16, boots * GRID), 0)).astype(F32).astype(BF)
+        out_ref[:, at] = dot(owner, jnp.concatenate(parts, axis=0))[:boots].astype(BF)
 
     @pl.loop(0, refs[0].shape[1] // CHUNK)
     def _(step):

time: 35.6 us -> 35.7 us (level)
    pallas_call x2, Pallas kernels: 5.14 us -> 6.25 us  [pick(): pl.pallas_call(functools.partial(pick_kernel, grid_y, boots, len(cells)),...]
    pallas_call x1, Pallas kernels: 21.9 us -> 21 us  [solve(): pl.pallas_call(functools.partial(solve_kernel, grid_y, boots), out_shape=...]
  transfers between devices with their start and end apart: 6 -> 6, of which waited for: 2 -> 2; matrix products, arithmetic and copies ran while one was open for 0% -> 0% of each run, Pallas kernels for 76% -> 77%
where the time goes in v10:
time: 35.7 us; the launch traced here: 35.5 us
  Pallas kernels  27.2 us (76%)
  starting transfers between devices  5.27 us (15%)
  waiting for transfers between devices  1.15 us (3%)
  local copies, waits for them, and re-layouts  0.95 us (3%)
  other arithmetic  0.81 us (2%)
    pallas_call x1, Pallas kernels, solve(): pl.pallas_call(functools.partial(solve_kernel, grid_y, boots), out_shape=...  21 us
    pallas_call x2, Pallas kernels, pick(): pl.pallas_call(functools.partial(pick_kernel, grid_y, boots, len(cells)),...  6.25 us
    ppermute x6, starting transfers between devices, swap(): return lax.ppermute(a, 'wide', [(i, i ^ k) for i in range(wide)])  5.27 us
    ppermute x6, waiting for transfers between devices, swap(): return lax.ppermute(a, 'wide', [(i, i ^ k) for i in range(wide)])  1.15 us
    unnamed x4, local copies, waits for them, and re-layouts  0.95 us
    concatenate x1, other arithmetic, local(): return jnp.concatenate(blocks, axis=0)  0.73 us
  transfers between devices with their start and end apart: 6, of which 2 were waited for; matrix products, arithmetic and copies ran while one was open for 0% of the time, Pallas kernels for 77%

profile of v10, /device:TPU:0, one launch (start us, length us, event | category | flops | bytes accessed | tf_op | source)
XLA Modules:
  0.0 35.5 jit_solution(2996066248817462376)
XLA Ops:
  0.0 3.0 %collective-permute-start = (s32[3,4096]{1,0:T(4,128)}, s32[3,4096]{1,0:T(4,128)S(1)}, u32[]{:S(2)}, u32[]{:S(2)}) collective-permute-start(s32[3,4096]{1,0:T(4,128)} %refs_0_.1), channel_id=1, source_target_pairs={{0,2},{1,3},{2,0},{3,1},{4,6},{5,7},{6,4},{7,5},{8,10},{9,11},{10,... | collective-permute-start | bytes 147464 | tf_op jit(solution)/shard_map/ppermute | solution.py:524
  3.0 0.0 collective-permute-start.1
  3.0 0.1 collective-permute-start.4
  3.1 0.0 copy-start
  3.1 21.0 %solve.1.models_ref = bf16[256,512]{1,0:T(8,128)(2,1)} custom-call(s32[1]{0:T(128)} %bitcast.slot_ref, f32[5]{0:T(128)} %comp_ref.1, s32[2,512]{1,0:T(2,128)} %station_ref.1, f32[5,512]{1,0:T(8,128)} %observed_ref.1, s32[8,512]{1,0:T(8,128)} %counts_ref.1, bf16[16384,256]{1,0:T(8,128)(2,1)} %constant.12.clone.source), custom_call_target="tpu_custom_call" | custom-call | flops 10000000000 | bytes 10000000 | tf_op jit(solution)/shard_map/solve/pallas_call | solution.py:433
  24.1 0.0 collective-permute-done.refs_0_
  24.1 0.0 collective-permute-done.1.refs_1_
  24.1 0.0 copy-start.1
  24.1 0.9 %copy-done.1 = bf16[256,512]{1,0:T(8,128)(2,1)S(1)} copy-done((bf16[256,512]{1,0:T(8,128)(2,1)S(1)}, bf16[256,512]{1,0:T(8,128)(2,1)}, u32[]{:S(2)}) %copy-start.1) | copy-done | bytes 262168
  25.1 3.1 %pick.2 = (bf16[2,4096]{1,0:T(2,128)(2,1)S(1)}, bf16[2,4096]{1,0:T(2,128)(2,1)S(1)}) custom-call(bf16[256,512]{1,0:T(8,128)(2,1)S(1)} %copy-done.1, s32[3,4096]{1,0:T(4,128)S(1)} %collective-permute-done.refs_0_, s32[3,4096]{1,0:T(4,128)S(1)} %collective-permute-done.1.refs_1_), custom_call_target="tpu_custom_call" | custom-call | flops 2147483648 | bytes 1000000 | tf_op jit(solution)/shard_map/pick/pallas_call | solution.py:504
  28.2 1.6 %collective-permute-start.2 = (bf16[2,4096]{1,0:T(2,128)(2,1)S(1)}, bf16[2,4096]{1,0:T(2,128)(2,1)S(1)}, u32[]{:S(2)}, u32[]{:S(2)}) collective-permute-start(bf16[2,4096]{1,0:T(2,128)(2,1)S(1)} %get-tuple-element.9), channel_id=1, source_target_pairs={{0,3},{1,2},{2,1},{3,0},{4,7},{5,6},{6,5},{7,4},{8,11},{9,10},{10,... | collective-permute-start | bytes 49160 | tf_op jit(solution)/shard_map/ppermute | solution.py:524
  29.8 0.5 %collective-permute-start.3 = (bf16[2,4096]{1,0:T(2,128)(2,1)S(1)}, bf16[2,4096]{1,0:T(2,128)(2,1)S(1)}, u32[]{:S(2)}, u32[]{:S(2)}) collective-permute-start(bf16[2,4096]{1,0:T(2,128)(2,1)S(1)} %get-tuple-element.10), channel_id=1, source_target_pairs={{0,2},{1,3},{2,0},{3,1},{4,6},{5,7},{6,4},{7,5},{8,10},{9,11},{10,... | collective-permute-start | bytes 49160 | tf_op jit(solution)/shard_map/ppermute | solution.py:524
  30.3 0.0 collective-permute-done.4.refs_1_
  30.3 0.0 copy-done
  30.3 3.1 %pick.3 = (bf16[2,4096]{1,0:T(2,128)(2,1)S(1)}, bf16[2,4096]{1,0:T(2,128)(2,1)S(1)}) custom-call(bf16[256,512]{1,0:T(8,128)(2,1)S(1)} %copy-done.1, s32[3,4096]{1,0:T(4,128)S(1)} %copy-done, s32[3,4096]{1,0:T(4,128)S(1)} %collective-permute-done.4.refs_1_), custom_call_target="tpu_custom_call" | custom-call | flops 2147483648 | bytes 1000000 | tf_op jit(solution)/shard_map/pick/pallas_call | solution.py:504
  33.4 0.1 collective-permute-start.5
  33.5 0.0 collective-permute-done.2
  33.5 0.1 collective-permute-done.3
  33.6 1.1 %collective-permute-done.5 = bf16[2,4096]{1,0:T(2,128)(2,1)S(1)} collective-permute-done((bf16[2,4096]{1,0:T(2,128)(2,1)S(1)}, bf16[2,4096]{1,0:T(2,128)(2,1)S(1)}, u32[]{:S(2)}, u32[]{:S(2)}) %collective-permute-start.5) | collective-permute-done | bytes 16416 | tf_op jit(solution)/shard_map/ppermute | solution.py:524
  34.6 0.1 broadcast_select_fusion.11
  34.7 0.7 %maximum_convert_fusion = f32[8,4096]{1,0:T(8,128)} fusion(bf16[2,4096]{1,0:T(2,128)(2,1)S(1)} %get-tuple-element.14, bf16[2,4096]{1,0:T(2,128)(2,1)S(1)} %get-tuple-element.15, bf16[2,4096]{1,0:T(2,128)(2,1)S(1)} %get-tuple-element.16, bf16[2,4096]{1,0:T(2,128)(2,1)S(1)} %get-tuple-element.13), kind=kLoop, calls=%fused_computation | loop fusion | flops 262144 | bytes 196608 | tf_op jit(solution)/shard_map/concatenate | solution.py:537
Async XLA Ops:
  0.0 24.1 %collective-permute-start = (s32[3,4096]{1,0:T(4,128)}, s32[3,4096]{1,0:T(4,128)S(1)}, u32[]{:S(2)}, u32[]{:S(2)}) collective-permute-start(s32[3,4096]{1,0:T(4,128)} %refs_0_.1), channel_id=1, source_target_pairs={{0,2},{1,3},{2,0},{3,1},{4,6},{5,7},{6,4},{7,5},{8,10},{9,11},{10,... | collective-permute-start | bytes 147464 | tf_op jit(solution)/shard_map/ppermute | solution.py:524
  3.0 21.2 %collective-permute-start.1 = (s32[3,4096]{1,0:T(4,128)}, s32[3,4096]{1,0:T(4,128)S(1)}, u32[]{:S(2)}, u32[]{:S(2)}) collective-permute-start(s32[3,4096]{1,0:T(4,128)} %refs_0_.1), channel_id=1, source_target_pairs={{0,3},{1,2},{2,1},{3,0},{4,7},{5,6},{6,5},{7,4},{8,11},{9,10},{10,... | collective-permute-start | bytes 147464 | tf_op jit(solution)/shard_map/ppermute | solution.py:524
  3.0 27.3 %collective-permute-start.4 = (s32[3,4096]{1,0:T(4,128)}, s32[3,4096]{1,0:T(4,128)S(1)}, u32[]{:S(2)}, u32[]{:S(2)}) collective-permute-start(s32[3,4096]{1,0:T(4,128)} %refs_0_.1), channel_id=1, source_target_pairs={{0,1},{1,0},{2,3},{3,2},{4,5},{5,4},{6,7},{7,6},{8,9},{9,8},{10,11... | collective-permute-start | bytes 147464 | tf_op jit(solution)/shard_map/ppermute | solution.py:524
  3.1 27.2 %copy-start = (s32[3,4096]{1,0:T(4,128)S(1)}, s32[3,4096]{1,0:T(4,128)}, u32[]{:S(2)}) copy-start(s32[3,4096]{1,0:T(4,128)} %refs_0_.1) | copy-start | bytes 147460
  24.1 1.0 %copy-start.1 = (bf16[256,512]{1,0:T(8,128)(2,1)S(1)}, bf16[256,512]{1,0:T(8,128)(2,1)}, u32[]{:S(2)}) copy-start(bf16[256,512]{1,0:T(8,128)(2,1)} %solve.1.models_ref) | copy-start | bytes 786436
  28.2 5.3 %collective-permute-start.2 = (bf16[2,4096]{1,0:T(2,128)(2,1)S(1)}, bf16[2,4096]{1,0:T(2,128)(2,1)S(1)}, u32[]{:S(2)}, u32[]{:S(2)}) collective-permute-start(bf16[2,4096]{1,0:T(2,128)(2,1)S(1)} %get-tuple-element.9), channel_id=1, source_target_pairs={{0,3},{1,2},{2,1},{3,0},{4,7},{5,6},{6,5},{7,4},{8,11},{9,10},{10,... | collective-permute-start | bytes 49160 | tf_op jit(solution)/shard_map/ppermute | solution.py:524
  29.8 3.7 %collective-permute-start.3 = (bf16[2,4096]{1,0:T(2,128)(2,1)S(1)}, bf16[2,4096]{1,0:T(2,128)(2,1)S(1)}, u32[]{:S(2)}, u32[]{:S(2)}) collective-permute-start(bf16[2,4096]{1,0:T(2,128)(2,1)S(1)} %get-tuple-element.10), channel_id=1, source_target_pairs={{0,2},{1,3},{2,0},{3,1},{4,6},{5,7},{6,4},{7,5},{8,10},{9,11},{10,... | collective-permute-start | bytes 49160 | tf_op jit(solution)/shard_map/ppermute | solution.py:524
  33.4 1.2 %collective-permute-start.5 = (bf16[2,4096]{1,0:T(2,128)(2,1)S(1)}, bf16[2,4096]{1,0:T(2,128)(2,1)S(1)}, u32[]{:S(2)}, u32[]{:S(2)}) collective-permute-start(bf16[2,4096]{1,0:T(2,128)(2,1)S(1)} %get-tuple-element.11), channel_id=1, source_target_pairs={{0,1},{1,0},{2,3},{3,2},{4,5},{5,4},{6,7},{7,6},{8,9},{9,8},{10,11... | collective-permute-start | bytes 49160 | tf_op jit(solution)/shard_map/ppermute | solution.py:524

commit v11 on v10

--- a/solution.py
+++ b/solution.py
@@ -78,19 +78,18 @@
 
 
 def layout(grid_y, boots):
-    slabs = DEPTHS * grid_y * boots // LANES
     return Layout(
         [
             ("base_x", GRID),
             ("base_xt2", 2 * GRID),
+            ("station_y2", 4 * grid_y),
+            ("spread", 3 * LANES),
+            ("table", 5 * DEPTHS // 2 * GRID),
             ("field_y2", 2 * LANES),
             ("field_yt", 2 * LANES),
-            ("station_y2", 2 * grid_y),
-            ("spread", 3 * LANES),
             ("back", 5 * LANES),
             ("same", LANES),
             ("regroup", boots * LANES * max(1, boots // 2)),
-            ("table", 5 * slabs // 2 * GRID),
         ]
     )
 
@@ -98,24 +97,23 @@
 @functools.lru_cache(maxsize=None)
 def constants(grid_y, boots):
     deep = LANES // grid_y // boots
-    slabs = DEPTHS // deep
+    copies = LANES // grid_y
     table = []
     for values, (odd_x, odd_y) in zip(offset_table(grid_y), PARITY):
         t = spectrum(values, odd_x, GRID)
         t = np.moveaxis(spectrum(np.moveaxis(t, 1, 0), odd_y, grid_y), 0, 1)
-        t = np.moveaxis(t, 2, 0).reshape(slabs, deep, GRID, 1, grid_y).transpose(0, 2, 1, 3, 4)
-        table.append(np.tile(t, (1, 1, 1, boots, 1)).reshape(slabs, GRID, LANES))
-    table = np.stack(table).reshape(5, slabs // 2, 2, GRID, LANES).transpose(0, 1, 3, 2, 4)
+        table.append(np.tile(np.moveaxis(t, 2, 0), (1, 1, copies)))
+    table = np.stack(table).reshape(5, DEPTHS // 2, 2, GRID, LANES).transpose(0, 1, 3, 2, 4)
 
     base_x = basis(GRID)
     base_y = basis(grid_y).reshape(grid_y, 2, grid_y)
-    copies = deep * boots
-    field_y = np.einsum("ab,yhl->ayhbl", np.eye(copies), base_y).reshape(LANES, 2 * LANES)
-    station_y = np.einsum("b,yhl->yhbl", np.ones(copies), base_y).reshape(grid_y, 2 * LANES)
-    spread = np.zeros((5, deep, boots, grid_y, deep, boots, grid_y))
+    field_y = np.einsum("de,ab,yhl->dayehbl", np.eye(deep), np.eye(boots), base_y).reshape(LANES, 2 * LANES)
+    odd_y = np.stack([-base_y[:, 1], base_y[:, 0]], axis=1)
+    station_y = [np.tile(b[:, :, None], (1, 1, boots, 1)).reshape(grid_y, -1) for b in (base_y, odd_y)]
+    spread = np.zeros((5, deep, boots, grid_y, copies, grid_y))
     for c in range(5):
-        for b in range(boots):
-            spread[c, 0, b, c, :, b, :] = 1
+        for copy in range(copies):
+            spread[c, 0, copy % boots, c, copy, :] = 1
     spread = spread.reshape(5, LANES, LANES)
     back = spread.transpose(0, 2, 1).reshape(5 * LANES, LANES)
     spread = np.concatenate([spread, np.zeros((1, LANES, LANES))])
@@ -133,7 +131,7 @@
         base_xt2=np.concatenate([x_high, x_low], axis=1),
         field_y2=np.concatenate([y_high, y_low], axis=0),
         field_yt=field_y.T,
-        station_y2=np.concatenate(split(station_y)),
+        station_y2=np.concatenate([part for b in station_y for part in split(b)]),
         spread=spread.reshape(3 * LANES, 2 * LANES),
         back=back,
         same=same,
@@ -191,11 +189,13 @@
     deep = LANES // grid_y // boots
     slabs = DEPTHS // deep
     where = layout(grid_y, boots)
-    split_row = where.at["table"][0]
-    wide = 2 * LANES
+    table_row, table_rows = where.at["table"]
+    wide = 2 * boots * grid_y
+    chunks = range(wide // LANES)
+    bounds = [0, table_row, table_row + table_rows, where.rows]
     copies = [
         pltpu.make_async_copy(source.at[a:b], const.at[a:b], copied.at[i])
-        for i, (a, b) in enumerate([(0, split_row), (split_row, where.rows)])
+        for i, (a, b) in enumerate(zip(bounds[:-1], bounds[1:]))
     ]
     first_step = pl.program_id(0) == 0
 
@@ -209,7 +209,7 @@
         return const[row : row + count, :width]
 
     def table(c, z, at):
-        row = split_row + (c * (slabs // 2) + z // 2) * GRID
+        row = table_row + (c * (DEPTHS // 2) + z // 2) * GRID
         return const[row + at.start : row + at.stop, z % 2 * LANES : (z % 2 + 1) * LANES]
 
     stations = station_ref.shape[1]
@@ -241,49 +241,55 @@
 
     pick_xt[...] = dot(held("base_xt2", GRID), place_x).astype(BF)
     pick_x[...] = dot(place_xt, held("base_x")).astype(BF)
-    station_y2 = held("station_y2")
-    pick_y[...] = dot(place_yt, station_y2[:grid_y]) + dot(place_yt, station_y2[grid_y:])
-
-    @pl.when(first_step)
-    def _():
-        copies[1].wait()
-        for c in range(5):
-            for z in range(slabs):
-                table_wide[c, z] = table(c, z, slice(0, GRID)).astype(F32)
-
+    station_y2 = held("station_y2", wide)
+    for odd in range(2):
+        high, low = [station_y2[(2 * odd + i) * grid_y : (2 * odd + i + 1) * grid_y] for i in range(2)]
+        pick_y[:, odd * wide : (odd + 1) * wide] = dot(place_yt, high) + dot(place_yt, low)
     no_sum = jnp.zeros((8, LANES), F32)
 
-    def back_project():
+    def trig(at, odd, chunk):
+        lane = odd * wide + chunk * LANES
+        return pick_y[at, lane : lane + LANES]
+
+    def back_project(index):
         spread = held("spread")
         spread = jnp.concatenate([spread[i * LANES : (i + 1) * LANES] for i in range(3)], axis=1)
         spreads = dot(values[...], spread[:, : 5 * LANES])
         for row in range(0, stations, ROWS):
             at = slice(row, row + ROWS)
-            trig = [pick_y[at, lane : lane + LANES] for lane in range(0, wide, LANES)]
+            for c, (_, odd_y) in enumerate(PARITY):
+                e = spreads[at, c * LANES : (c + 1) * LANES]
+                for chunk in chunks:
+                    to = c * wide + chunk * LANES
+                    spread_out[at, to : to + LANES] = (e * trig(at, odd_y, chunk)).astype(BF)
+        spec = dot(pick_xt[...], spread_out[...])
+        for c, (odd_x, _) in enumerate(PARITY):
+            for hx in range(2):
+                for chunk in chunks:
+                    lane = c * wide + chunk * LANES
+                    part = spec[hx * GRID : (hx + 1) * GRID, lane : lane + LANES]
+                    spec_q[c, hx, chunk] = -part if odd_x * hx else part
+
+        @pl.when(jnp.logical_and(first_step, index == 0))
+        def _():
+            copies[1].wait()
+            copies[2].wait()
             for c in range(5):
-                e = spreads[at, c * LANES : (c + 1) * LANES]
-                for i, part in enumerate(trig):
-                    to = c * wide + i * LANES
-                    spread_out[at, to : to + LANES] = (e * part).astype(BF)
-        spec = dot(pick_xt[...], spread_out[...])
-        for c, (odd_x, odd_y) in enumerate(PARITY):
-            for hx in range(2):
-                for hy in range(2):
-                    part = spec[hx * GRID : (hx + 1) * GRID, c * wide + hy * LANES : c * wide + (hy + 1) * LANES]
-                    spec_q[c, hx, hy] = -part if (odd_x * hx + odd_y * hy) % 2 else part
+                for z in range(DEPTHS):
+                    table_wide[c, z] = table(c, z, slice(0, GRID)).astype(F32)
 
         for row in range(0, GRID, 16):
             at = slice(row, row + 16)
-            for hx in range(2):
-                q = [[spec_q[c, hx ^ PARITY[c][0], hy, at, :] for hy in range(2)] for c in range(5)]
-                to = slice(hx * GRID + row, hx * GRID + row + 16)
-                for z in range(slabs):
+            for chunk in chunks:
+                q = [[spec_q[c, hx, chunk, at, :] for hx in range(2)] for c in range(5)]
+                for z in range(DEPTHS):
                     t = [table_wide[c, z, at, :] for c in range(5)]
-                    for hy in range(2):
-                        total = t[0] * q[0][hy]
+                    lane = z * wide + chunk * LANES
+                    for hx in range(2):
+                        total = t[0] * q[0][hx]
                         for c in range(1, 5):
-                            total = total + t[c] * q[c][hy ^ PARITY[c][1]]
-                        spec_g[to, (2 * z + hy) * LANES : (2 * z + hy + 1) * LANES] = total.astype(BF)
+                            total = total + t[c] * q[c][hx ^ PARITY[c][0]]
+                        spec_g[hx * GRID + row : hx * GRID + row + 16, lane : lane + LANES] = total.astype(BF)
         along_x = dot(held("base_x"), spec_g[...]).astype(BF)
         along_x = jnp.concatenate([along_x[:, 2 * z * LANES : (2 * z + 2) * LANES] for z in range(slabs)], axis=0)
         applied[...] = dot(along_x, held("field_yt", LANES)).reshape(slabs, GRID, LANES)
@@ -296,40 +302,35 @@
 
         for row in range(0, GRID, 16):
             at = [slice(hx * GRID + row, hx * GRID + row + 16) for hx in range(2)]
-            total = [[[None] * 2 for _ in range(2)] for _ in range(5)]
-            for eight in range(0, slabs, 8):
-                part = [[[None] * 2 for _ in range(2)] for _ in range(5)]
-                for z in range(eight, min(slabs, eight + 8)):
-                    f = [
-                        [spec_f[at[hx], (2 * z + hy) * LANES : (2 * z + hy + 1) * LANES] for hy in range(2)]
-                        for hx in range(2)
-                    ]
-                    for c, (odd_x, odd_y) in enumerate(PARITY):
-                        t = table(c, z, at[0])
+            for chunk in chunks:
+                total = [[None] * 2 for _ in range(5)]
+                for eight in range(0, DEPTHS, 8):
+                    part = [[None] * 2 for _ in range(5)]
+                    for z in range(eight, eight + 8):
+                        lane = z * wide + chunk * LANES
+                        f = [spec_f[at[hx], lane : lane + LANES] for hx in range(2)]
+                        for c, (odd_x, _) in enumerate(PARITY):
+                            t = table(c, z, at[0])
+                            for hx in range(2):
+                                term = t * f[hx ^ odd_x]
+                                part[c][hx] = part[c][hx] + term if z > eight else term
+                    for c in range(5):
                         for hx in range(2):
-                            for hy in range(2):
-                                term = t * f[hx ^ odd_x][hy ^ odd_y]
-                                old = part[c][hx][hy]
-                                part[c][hx][hy] = term if old is None else old + term
-                for c in range(5):
+                            total[c][hx] = total[c][hx] + part[c][hx] if eight else part[c][hx]
+                for c, (odd_x, _) in enumerate(PARITY):
+                    lane = c * wide + chunk * LANES
                     for hx in range(2):
-                        for hy in range(2):
-                            new = part[c][hx][hy]
-                            total[c][hx][hy] = total[c][hx][hy].astype(F32) + new.astype(F32) if eight else new
-            for c, (odd_x, odd_y) in enumerate(PARITY):
-                for hx in range(2):
-                    for hy in range(2):
-                        part = total[c][hx][hy].astype(BF)
-                        part = -part if (odd_x * hx + odd_y * hy) % 2 else part
-                        spec_i[at[hx], c * wide + hy * LANES : c * wide + (hy + 1) * LANES] = part
+                        part = -total[c][hx] if odd_x * hx else total[c][hx]
+                        spec_i[at[hx], lane : lane + LANES] = part
 
         picked = dot(pick_x[...], spec_i[...])
         for row in range(0, stations, ROWS):
             at = slice(row, row + ROWS)
-            for c in range(5):
+            for c, (_, odd_y) in enumerate(PARITY):
                 part = None
-                for lane in range(0, wide, LANES):
-                    term = picked[at, c * wide + lane : c * wide + lane + LANES] * pick_y[at, lane : lane + LANES]
+                for chunk in chunks:
+                    lane = c * wide + chunk * LANES
+                    term = picked[at, lane : lane + LANES] * trig(at, odd_y, chunk)
                     part = term if part is None else part + term
                 picked_in[at, c * LANES : (c + 1) * LANES] = part.astype(BF)
         return dot(picked_in[...], held("back", LANES))
@@ -337,17 +338,17 @@
     def fold(a):
         return jnp.sum(a.reshape(a.shape[0] // 8, 8, LANES), axis=0)
 
-    def total_of(partial):
-        if boots == 1:
-            return jnp.broadcast_to(jnp.sum(partial, keepdims=True), (1, LANES))
-        parts = []
-        for _ in range(3):
-            part = partial.astype(BF).astype(F32)
-            parts.append(part)
-            partial = partial - part
-        parts.append(no_sum)
-        sums = dot(jnp.concatenate(parts, axis=0).astype(BF), held("same", LANES))
-        return jnp.sum(sums, axis=0, keepdims=True)
+    def totals_of(partials):
+        rows_of = []
+        for partial in partials:
+            for _ in range(3):
+                part = partial.astype(BF).astype(F32)
+                rows_of.append(part)
+                partial = partial - part
+        if len(rows_of) % 2:
+            rows_of.append(no_sum)
+        sums = dot(jnp.concatenate(rows_of, axis=0).astype(BF), held("same", LANES))
+        return [jnp.sum(sums[i * 24 : (i + 1) * 24], axis=0, keepdims=True) for i in range(len(partials))]
 
     def depth_weight(z):
         within = lax.broadcasted_iota(jnp.int32, (1, LANES), 1) // (boots * grid_y)
@@ -361,50 +362,64 @@
     image[...] = jnp.zeros_like(image)
 
     def round_of(index, carry):
-        old_norm, old_step = carry
+        old_norm, old_step, old_curve = carry
         fresh = index % CG_STEPS == 0
-        back_project()
+        back_project(index)
 
         @pl.when(fresh)
         def _():
-            norm = no_sum
+            norm = bend = no_sum
             for z, at in pieces:
                 m = models[z, at]
                 p = damping * depth_weight(z) / (m * m + focusing * focusing)
                 penalty[z, at] = p
                 r = applied[z, at] - p * m
                 residual[z, at] = r
-                norm += fold(r * r)
-            sums[...] = norm
+                square = r * r
+                norm += fold(square)
+                bend += fold(p * square)
+            sums[0] = norm
+            sums[1] = bend
+            sums[2] = no_sum
 
         @pl.when(jnp.logical_not(fresh))
         def _():
-            norm = no_sum
+            norm = bend = cross = no_sum
             for z, at in pieces:
-                r = residual[z, at] - old_step * (applied[z, at] + penalty[z, at] * direction[z, at])
+                d = direction[z, at]
+                p = penalty[z, at]
+                pd = p * d
+                r = residual[z, at] - old_step * (applied[z, at] + pd)
                 residual[z, at] = r
-                norm += fold(r * r)
-            sums[...] = norm
-
-        norm = total_of(sums[...])
+                square = r * r
+                norm += fold(square)
+                bend += fold(p * square)
+                cross += fold(pd * r)
+            sums[0] = norm
+            sums[1] = bend
+            sums[2] = cross
+
+        here = predict()
+        weighted = weights[...] * here
+        norm, bend, cross = totals_of(
+            [sums[0], sums[1] + fold(weighted * here), sums[2] + fold(weighted * image[...])]
+        )
         ratio = jnp.where(fresh, 0.0, norm / old_norm)
-        cross = no_sum
+        curve = bend + ratio * (2.0 * cross + ratio * old_curve)
+        step = norm / curve
+        here = here + ratio * image[...]
+        image[...] = here
+        now = pred[...] + step * here
+        pred[...] = now
+        values[...] = (weights[...] * jnp.where(fresh, here, data[...] - now)).astype(BF)
         for z, at in pieces:
             d = residual[z, at] + ratio * direction[z, at]
             direction[z, at] = d
-            cross += fold(penalty[z, at] * d * d)
-        here = predict() + ratio * image[...]
-        image[...] = here
-        step = norm / total_of(cross + fold(weights[...] * here * here))
-        for z, at in pieces:
-            models[z, at] += step * direction[z, at]
-        now = pred[...] + step * here
-        pred[...] = now
-        values[...] = (weights[...] * jnp.where(fresh, here, data[...] - now)).astype(BF)
-        return norm, step
+            models[z, at] += step * d
+        return norm, step, curve
 
     one = jnp.ones((1, LANES), F32)
-    lax.fori_loop(0, IRLS * CG_STEPS, round_of, (one, one))
+    lax.fori_loop(0, IRLS * CG_STEPS, round_of, (one, one, one))
 
     for group in range(slabs // boots):
         m = jnp.concatenate([models[group * boots + i].astype(BF) for i in range(boots)], axis=1)
@@ -428,7 +443,7 @@
     smem = pl.BlockSpec(memory_space=pltpu.SMEM)
     field = vmem((slabs, GRID, LANES), F32)
     at_stations = vmem((stations, LANES), F32)
-    wide = 2 * LANES
+    wide = 2 * boots * grid_y
     inputs = [station_index, observed, counts]
     return pl.pallas_call(
         functools.partial(solve_kernel, grid_y, boots),
@@ -438,20 +453,20 @@
         out_specs=pl.BlockSpec((boots * GRID, DEPTHS * grid_y), lambda i: (i, 0)),
         scratch_shapes=[
             vmem((layout(grid_y, boots).rows, 2 * LANES), BF),
-            pltpu.SemaphoreType.DMA((2,)),
+            pltpu.SemaphoreType.DMA((3,)),
             vmem((stations, 2 * GRID), BF),
             vmem((2 * GRID, stations), BF),
-            vmem((stations, wide), F32),
+            vmem((stations, 2 * wide), F32),
             at_stations,
             at_stations,
             at_stations,
             at_stations,
             vmem((stations, LANES), BF),
             vmem((LANES, stations), F32),
-            vmem((5, slabs, GRID, LANES), F32),
-            vmem((8, LANES), F32),
+            vmem((5, DEPTHS, GRID, LANES), F32),
+            vmem((3, 8, LANES), F32),
             vmem((stations, 5 * wide), BF),
-            vmem((5, 2, 2, GRID, LANES), F32),
+            vmem((5, 2, wide // LANES, GRID, LANES), F32),
             vmem((2 * GRID, 5 * wide), BF),
             vmem((2 * GRID, slabs * 2 * LANES), BF),
             vmem((2 * GRID, slabs * 2 * LANES), BF),
@@ -484,11 +499,14 @@
             chosen += [jnp.where(here_z, here_y[i : i + 16], none) for i in range(0, grid_y, 16)]
         found = dot(models_ref[...], jnp.concatenate(chosen, axis=0)).astype(BF)
         at_x = count_up(GRID) == wide(place[0:1], GRID)
-        none = jnp.zeros((GRID, CHUNK), BF)
-        parts = [jnp.where(at_x, found[b * GRID : (b + 1) * GRID], none) for b in range(boots)]
-        owner = lax.broadcasted_iota(jnp.int32, (16, boots * GRID), 1) // GRID
-        owner = (owner == lax.broadcasted_iota(jnp.int32, (16, boots * GRID), 0)).astype(F32).astype(BF)
-        out_ref[:, at] = dot(owner, jnp.concatenate(parts, axis=0))[:boots].astype(BF)
+        parts = []
+        for b in range(boots):
+            part = jnp.where(at_x, found[b * GRID : (b + 1) * GRID], jnp.zeros((GRID, CHUNK), BF))
+            while part.shape[0] > 16:
+                half = part.shape[0] // 2
+                part = part[:half] + part[half:]
+            parts.append(jnp.sum(part.astype(F32), axis=0, keepdims=True))
+        out_ref[:, at] = jnp.concatenate(parts, axis=0).astype(BF)
 
     @pl.loop(0, refs[0].shape[1] // CHUNK)
     def _(step):
@@ -518,6 +536,8 @@
     boots = counts.shape[0]
     grid_y = cell_index.shape[1] * wide // (GRID * DEPTHS)
     team = TEAM if wide % TEAM == 0 and boots % TEAM == 0 else 1
+    while 4 * boots * grid_y < team * 2 * LANES:
+        team //= 2
     slot = lax.axis_index("wide").astype(jnp.int32) & (team - 1)
 
     def swap(a, k):

time: 35.7 us -> 36.4 us (1.020)
  Pallas kernels: 27.2 us -> 27.9 us
    pallas_call x1, Pallas kernels: 21 us -> 22.7 us  [solve(): pl.pallas_call(functools.partial(solve_kernel, grid_y, boots), out_shape=...]
    pallas_call x2, Pallas kernels: 6.25 us -> 5.14 us  [pick(): pl.pallas_call(functools.partial(pick_kernel, grid_y, boots, len(cells)),...]
where the time goes in v11:
time: 36.4 us; the launch traced here: 36.2 us
  Pallas kernels  27.9 us (77%)
  starting transfers between devices  5.36 us (15%)
  waiting for transfers between devices  1.15 us (3%)
  local copies, waits for them, and re-layouts  0.95 us (3%)
  other arithmetic  0.81 us (2%)
    pallas_call x1, Pallas kernels, solve(): pl.pallas_call(functools.partial(solve_kernel, grid_y, boots), out_shape=...  22.7 us
    ppermute x6, starting transfers between devices, swap(): return lax.ppermute(a, 'wide', [(i, i ^ k) for i in range(wide)])  5.36 us
    pallas_call x2, Pallas kernels, pick(): pl.pallas_call(functools.partial(pick_kernel, grid_y, boots, len(cells)),...  5.14 us
    ppermute x6, waiting for transfers between devices, swap(): return lax.ppermute(a, 'wide', [(i, i ^ k) for i in range(wide)])  1.15 us
    unnamed x4, local copies, waits for them, and re-layouts  0.95 us
    concatenate x1, other arithmetic, local(): return jnp.concatenate(blocks, axis=0)  0.73 us
  transfers between devices with their start and end apart: 6, of which 2 were waited for; matrix products, arithmetic and copies ran while one was open for 0% of the time, Pallas kernels for 77%

profile of v11, /device:TPU:0, one launch (start us, length us, event | category | flops | bytes accessed | tf_op | source)
XLA Modules:
  0.0 36.2 jit_solution(9337342755725567436)
XLA Ops:
  0.0 3.0 %collective-permute-start = (s32[3,4096]{1,0:T(4,128)}, s32[3,4096]{1,0:T(4,128)S(1)}, u32[]{:S(2)}, u32[]{:S(2)}) collective-permute-start(s32[3,4096]{1,0:T(4,128)} %refs_0_.1), channel_id=1, source_target_pairs={{0,2},{1,3},{2,0},{3,1},{4,6},{5,7},{6,4},{7,5},{8,10},{9,11},{10,... | collective-permute-start | bytes 147464 | tf_op jit(solution)/shard_map/ppermute | solution.py:544
  3.0 0.0 collective-permute-start.1
  3.0 0.1 collective-permute-start.4
  3.1 0.0 copy-start
  3.1 22.7 %solve.1.models_ref = bf16[256,512]{1,0:T(8,128)(2,1)} custom-call(s32[1]{0:T(128)} %bitcast.slot_ref, f32[5]{0:T(128)} %comp_ref.1, s32[2,512]{1,0:T(2,128)} %station_ref.1, f32[5,512]{1,0:T(8,128)} %observed_ref.1, s32[8,512]{1,0:T(8,128)} %counts_ref.1, bf16[16384,256]{1,0:T(8,128)(2,1)} %constant.12.clone.source), custom_call_target="tpu_custom_call" | custom-call | flops 10000000000 | bytes 10000000 | tf_op jit(solution)/shard_map/solve/pallas_call | solution.py:448
  25.9 0.0 collective-permute-done.refs_0_
  25.9 0.0 collective-permute-done.1.refs_1_
  25.9 0.0 copy-start.1
  25.9 0.9 %copy-done.1 = bf16[256,512]{1,0:T(8,128)(2,1)S(1)} copy-done((bf16[256,512]{1,0:T(8,128)(2,1)S(1)}, bf16[256,512]{1,0:T(8,128)(2,1)}, u32[]{:S(2)}) %copy-start.1) | copy-done | bytes 262168
  26.8 2.6 %pick.2 = (bf16[2,4096]{1,0:T(2,128)(2,1)S(1)}, bf16[2,4096]{1,0:T(2,128)(2,1)S(1)}) custom-call(bf16[256,512]{1,0:T(8,128)(2,1)S(1)} %copy-done.1, s32[3,4096]{1,0:T(4,128)S(1)} %collective-permute-done.refs_0_, s32[3,4096]{1,0:T(4,128)S(1)} %collective-permute-done.1.refs_1_), custom_call_target="tpu_custom_call" | custom-call | flops 2147483648 | bytes 1000000 | tf_op jit(solution)/shard_map/pick/pallas_call | solution.py:522
  29.4 1.7 %collective-permute-start.2 = (bf16[2,4096]{1,0:T(2,128)(2,1)S(1)}, bf16[2,4096]{1,0:T(2,128)(2,1)S(1)}, u32[]{:S(2)}, u32[]{:S(2)}) collective-permute-start(bf16[2,4096]{1,0:T(2,128)(2,1)S(1)} %get-tuple-element.9), channel_id=1, source_target_pairs={{0,3},{1,2},{2,1},{3,0},{4,7},{5,6},{6,5},{7,4},{8,11},{9,10},{10,... | collective-permute-start | bytes 49160 | tf_op jit(solution)/shard_map/ppermute | solution.py:544
  31.1 0.5 %collective-permute-start.3 = (bf16[2,4096]{1,0:T(2,128)(2,1)S(1)}, bf16[2,4096]{1,0:T(2,128)(2,1)S(1)}, u32[]{:S(2)}, u32[]{:S(2)}) collective-permute-start(bf16[2,4096]{1,0:T(2,128)(2,1)S(1)} %get-tuple-element.10), channel_id=1, source_target_pairs={{0,2},{1,3},{2,0},{3,1},{4,6},{5,7},{6,4},{7,5},{8,10},{9,11},{10,... | collective-permute-start | bytes 49160 | tf_op jit(solution)/shard_map/ppermute | solution.py:544
  31.5 0.0 collective-permute-done.4.refs_1_
  31.5 0.0 copy-done
  31.5 2.6 %pick.3 = (bf16[2,4096]{1,0:T(2,128)(2,1)S(1)}, bf16[2,4096]{1,0:T(2,128)(2,1)S(1)}) custom-call(bf16[256,512]{1,0:T(8,128)(2,1)S(1)} %copy-done.1, s32[3,4096]{1,0:T(4,128)S(1)} %copy-done, s32[3,4096]{1,0:T(4,128)S(1)} %collective-permute-done.4.refs_1_), custom_call_target="tpu_custom_call" | custom-call | flops 2147483648 | bytes 1000000 | tf_op jit(solution)/shard_map/pick/pallas_call | solution.py:522
  34.1 0.1 collective-permute-start.5
  34.2 0.0 collective-permute-done.2
  34.2 0.6 %collective-permute-done.3 = bf16[2,4096]{1,0:T(2,128)(2,1)S(1)} collective-permute-done((bf16[2,4096]{1,0:T(2,128)(2,1)S(1)}, bf16[2,4096]{1,0:T(2,128)(2,1)S(1)}, u32[]{:S(2)}, u32[]{:S(2)}) %collective-permute-start.3) | collective-permute-done | bytes 16416 | tf_op jit(solution)/shard_map/ppermute | solution.py:544
  34.8 0.6 %collective-permute-done.5 = bf16[2,4096]{1,0:T(2,128)(2,1)S(1)} collective-permute-done((bf16[2,4096]{1,0:T(2,128)(2,1)S(1)}, bf16[2,4096]{1,0:T(2,128)(2,1)S(1)}, u32[]{:S(2)}, u32[]{:S(2)}) %collective-permute-start.5) | collective-permute-done | bytes 16416 | tf_op jit(solution)/shard_map/ppermute | solution.py:544
  35.4 0.1 broadcast_select_fusion.11
  35.5 0.7 %maximum_convert_fusion = f32[8,4096]{1,0:T(8,128)} fusion(bf16[2,4096]{1,0:T(2,128)(2,1)S(1)} %get-tuple-element.14, bf16[2,4096]{1,0:T(2,128)(2,1)S(1)} %get-tuple-element.15, bf16[2,4096]{1,0:T(2,128)(2,1)S(1)} %get-tuple-element.16, bf16[2,4096]{1,0:T(2,128)(2,1)S(1)} %get-tuple-element.13), kind=kLoop, calls=%fused_computation | loop fusion | flops 262144 | bytes 196608 | tf_op jit(solution)/shard_map/concatenate | solution.py:557
Async XLA Ops:
  0.0 25.9 %collective-permute-start = (s32[3,4096]{1,0:T(4,128)}, s32[3,4096]{1,0:T(4,128)S(1)}, u32[]{:S(2)}, u32[]{:S(2)}) collective-permute-start(s32[3,4096]{1,0:T(4,128)} %refs_0_.1), channel_id=1, source_target_pairs={{0,2},{1,3},{2,0},{3,1},{4,6},{5,7},{6,4},{7,5},{8,10},{9,11},{10,... | collective-permute-start | bytes 147464 | tf_op jit(solution)/shard_map/ppermute | solution.py:544
  3.0 22.9 %collective-permute-start.1 = (s32[3,4096]{1,0:T(4,128)}, s32[3,4096]{1,0:T(4,128)S(1)}, u32[]{:S(2)}, u32[]{:S(2)}) collective-permute-start(s32[3,4096]{1,0:T(4,128)} %refs_0_.1), channel_id=1, source_target_pairs={{0,3},{1,2},{2,1},{3,0},{4,7},{5,6},{6,5},{7,4},{8,11},{9,10},{10,... | collective-permute-start | bytes 147464 | tf_op jit(solution)/shard_map/ppermute | solution.py:544
  3.0 28.6 %collective-permute-start.4 = (s32[3,4096]{1,0:T(4,128)}, s32[3,4096]{1,0:T(4,128)S(1)}, u32[]{:S(2)}, u32[]{:S(2)}) collective-permute-start(s32[3,4096]{1,0:T(4,128)} %refs_0_.1), channel_id=1, source_target_pairs={{0,1},{1,0},{2,3},{3,2},{4,5},{5,4},{6,7},{7,6},{8,9},{9,8},{10,11... | collective-permute-start | bytes 147464 | tf_op jit(solution)/shard_map/ppermute | solution.py:544
  3.1 28.4 %copy-start = (s32[3,4096]{1,0:T(4,128)S(1)}, s32[3,4096]{1,0:T(4,128)}, u32[]{:S(2)}) copy-start(s32[3,4096]{1,0:T(4,128)} %refs_0_.1) | copy-start | bytes 147460
  25.9 1.0 %copy-start.1 = (bf16[256,512]{1,0:T(8,128)(2,1)S(1)}, bf16[256,512]{1,0:T(8,128)(2,1)}, u32[]{:S(2)}) copy-start(bf16[256,512]{1,0:T(8,128)(2,1)} %solve.1.models_ref) | copy-start | bytes 786436
  29.4 4.8 %collective-permute-start.2 = (bf16[2,4096]{1,0:T(2,128)(2,1)S(1)}, bf16[2,4096]{1,0:T(2,128)(2,1)S(1)}, u32[]{:S(2)}, u32[]{:S(2)}) collective-permute-start(bf16[2,4096]{1,0:T(2,128)(2,1)S(1)} %get-tuple-element.9), channel_id=1, source_target_pairs={{0,3},{1,2},{2,1},{3,0},{4,7},{5,6},{6,5},{7,4},{8,11},{9,10},{10,... | collective-permute-start | bytes 49160 | tf_op jit(solution)/shard_map/ppermute | solution.py:544
  31.1 3.7 %collective-permute-start.3 = (bf16[2,4096]{1,0:T(2,128)(2,1)S(1)}, bf16[2,4096]{1,0:T(2,128)(2,1)S(1)}, u32[]{:S(2)}, u32[]{:S(2)}) collective-permute-start(bf16[2,4096]{1,0:T(2,128)(2,1)S(1)} %get-tuple-element.10), channel_id=1, source_target_pairs={{0,2},{1,3},{2,0},{3,1},{4,6},{5,7},{6,4},{7,5},{8,10},{9,11},{10,... | collective-permute-start | bytes 49160 | tf_op jit(solution)/shard_map/ppermute | solution.py:544
  34.1 1.2 %collective-permute-start.5 = (bf16[2,4096]{1,0:T(2,128)(2,1)S(1)}, bf16[2,4096]{1,0:T(2,128)(2,1)S(1)}, u32[]{:S(2)}, u32[]{:S(2)}) collective-permute-start(bf16[2,4096]{1,0:T(2,128)(2,1)S(1)} %get-tuple-element.11), channel_id=1, source_target_pairs={{0,1},{1,0},{2,3},{3,2},{4,5},{5,4},{6,7},{7,6},{8,9},{9,8},{10,11... | collective-permute-start | bytes 49160 | tf_op jit(solution)/shard_map/ppermute | solution.py:544

commit v12 on v11

--- a/solution.py
+++ b/solution.py
@@ -173,7 +173,6 @@
     values,
     rows,
     table_wide,
-    sums,
     spread_out,
     spec_q,
     spec_i,
@@ -184,7 +183,6 @@
     residual,
     direction,
     penalty,
-    applied,
 ):
     deep = LANES // grid_y // boots
     slabs = DEPTHS // deep
@@ -214,7 +212,12 @@
 
     stations = station_ref.shape[1]
     first = (slot_ref[0] * pl.num_programs(0) + pl.program_id(0)) * boots
-    pieces = [(z, slice(row, row + ROWS)) for z in range(slabs) for row in range(0, GRID, ROWS)]
+    halves = [range(half, half + slabs // 2) for half in (0, slabs // 2)]
+    half_lanes = slabs // 2 * 2 * LANES
+
+    def pieces(half):
+        return [(slab, slice(row, row + ROWS)) for slab in half for row in range(0, GRID, ROWS)]
+
 
     rows[...] = jnp.zeros_like(rows)
     for b in range(boots):
@@ -247,11 +250,19 @@
         pick_y[:, odd * wide : (odd + 1) * wide] = dot(place_yt, high) + dot(place_yt, low)
     no_sum = jnp.zeros((8, LANES), F32)
 
+    @pl.when(first_step)
+    def _():
+        copies[1].wait()
+        copies[2].wait()
+        for c in range(5):
+            for z in range(DEPTHS):
+                table_wide[c, z] = table(c, z, slice(0, GRID)).astype(F32)
+
     def trig(at, odd, chunk):
         lane = odd * wide + chunk * LANES
         return pick_y[at, lane : lane + LANES]
 
-    def back_project(index):
+    def back_project(receive):
         spread = held("spread")
         spread = jnp.concatenate([spread[i * LANES : (i + 1) * LANES] for i in range(3)], axis=1)
         spreads = dot(values[...], spread[:, : 5 * LANES])
@@ -270,58 +281,52 @@
                     part = spec[hx * GRID : (hx + 1) * GRID, lane : lane + LANES]
                     spec_q[c, hx, chunk] = -part if odd_x * hx else part
 
-        @pl.when(jnp.logical_and(first_step, index == 0))
-        def _():
-            copies[1].wait()
-            copies[2].wait()
-            for c in range(5):
-                for z in range(DEPTHS):
-                    table_wide[c, z] = table(c, z, slice(0, GRID)).astype(F32)
-
-        for row in range(0, GRID, 16):
-            at = slice(row, row + 16)
-            for chunk in chunks:
-                q = [[spec_q[c, hx, chunk, at, :] for hx in range(2)] for c in range(5)]
-                for z in range(DEPTHS):
-                    t = [table_wide[c, z, at, :] for c in range(5)]
-                    lane = z * wide + chunk * LANES
-                    for hx in range(2):
-                        total = t[0] * q[0][hx]
-                        for c in range(1, 5):
-                            total = total + t[c] * q[c][hx ^ PARITY[c][0]]
-                        spec_g[hx * GRID + row : hx * GRID + row + 16, lane : lane + LANES] = total.astype(BF)
-        along_x = dot(held("base_x"), spec_g[...]).astype(BF)
-        along_x = jnp.concatenate([along_x[:, 2 * z * LANES : (2 * z + 2) * LANES] for z in range(slabs)], axis=0)
-        applied[...] = dot(along_x, held("field_yt", LANES)).reshape(slabs, GRID, LANES)
+        for half in halves:
+            for row in range(0, GRID, 16):
+                at = slice(row, row + 16)
+                for chunk in chunks:
+                    q = [[spec_q[c, hx, chunk, at, :] for hx in range(2)] for c in range(5)]
+                    for z in range(half.start * deep, half.stop * deep):
+                        t = [table_wide[c, z, at, :] for c in range(5)]
+                        lane = z * wide + chunk * LANES
+                        for hx in range(2):
+                            total = t[0] * q[0][hx]
+                            for c in range(1, 5):
+                                total = total + t[c] * q[c][hx ^ PARITY[c][0]]
+                            spec_g[hx * GRID + row : hx * GRID + row + 16, lane : lane + LANES] = total.astype(BF)
+            lane = half.start * 2 * LANES
+            along_x = dot(held("base_x"), spec_g[:, lane : lane + half_lanes]).astype(BF)
+            along_x = [along_x[:, lane : lane + 2 * LANES] for lane in range(0, half_lanes, 2 * LANES)]
+            receive(half, dot(jnp.concatenate(along_x, axis=0), held("field_yt", LANES)))
 
     def predict():
-        r = residual[...].reshape(slabs * GRID, LANES).astype(BF)
-        y = dot(jnp.concatenate([r, r], axis=1), held("field_y2")).astype(BF)
-        y = jnp.concatenate([y[z * GRID : (z + 1) * GRID] for z in range(slabs)], axis=1)
-        spec_f[...] = dot(held("base_xt2"), jnp.concatenate([y, y], axis=0)).astype(BF)
-
-        for row in range(0, GRID, 16):
-            at = [slice(hx * GRID + row, hx * GRID + row + 16) for hx in range(2)]
-            for chunk in chunks:
-                total = [[None] * 2 for _ in range(5)]
-                for eight in range(0, DEPTHS, 8):
-                    part = [[None] * 2 for _ in range(5)]
-                    for z in range(eight, eight + 8):
+        for half in halves:
+            r = residual[half.start : half.stop].reshape(len(half) * GRID, LANES).astype(BF)
+            y = dot(jnp.concatenate([r, r], axis=1), held("field_y2")).astype(BF)
+            y = jnp.concatenate([y[i * GRID : (i + 1) * GRID] for i in range(len(half))], axis=1)
+            lane = half.start * 2 * LANES
+            spec_f[:, lane : lane + half_lanes] = dot(held("base_xt2"), jnp.concatenate([y, y], axis=0)).astype(BF)
+
+            for row in range(0, GRID, 16):
+                at = [slice(hx * GRID + row, hx * GRID + row + 16) for hx in range(2)]
+                for chunk in chunks:
+                    total = [[None] * 2 for _ in range(5)]
+                    for z in range(half.start * deep, half.stop * deep):
                         lane = z * wide + chunk * LANES
                         f = [spec_f[at[hx], lane : lane + LANES] for hx in range(2)]
                         for c, (odd_x, _) in enumerate(PARITY):
                             t = table(c, z, at[0])
                             for hx in range(2):
                                 term = t * f[hx ^ odd_x]
-                                part[c][hx] = part[c][hx] + term if z > eight else term
-                    for c in range(5):
+                                total[c][hx] = term if total[c][hx] is None else total[c][hx] + term
+                    for c, (odd_x, _) in enumerate(PARITY):
+                        lane = c * wide + chunk * LANES
                         for hx in range(2):
-                            total[c][hx] = total[c][hx] + part[c][hx] if eight else part[c][hx]
-                for c, (odd_x, _) in enumerate(PARITY):
-                    lane = c * wide + chunk * LANES
-                    for hx in range(2):
-                        part = -total[c][hx] if odd_x * hx else total[c][hx]
-                        spec_i[at[hx], lane : lane + LANES] = part
+                            part = total[c][hx]
+                            if half is not halves[0]:
+                                part = part + spec_i[at[hx], lane : lane + LANES]
+                                part = -part if odd_x * hx else part
+                            spec_i[at[hx], lane : lane + LANES] = part
 
         picked = dot(pick_x[...], spec_i[...])
         for row in range(0, stations, ROWS):
@@ -357,69 +362,70 @@
         return ratio * ratio * ratio
 
     models[...] = jnp.zeros_like(models)
-    direction[...] = jnp.zeros_like(direction)
     pred[...] = jnp.zeros_like(pred)
-    image[...] = jnp.zeros_like(image)
-
-    def round_of(index, carry):
+
+    def round_of(fresh, carry):
         old_norm, old_step, old_curve = carry
-        fresh = index % CG_STEPS == 0
-        back_project(index)
-
-        @pl.when(fresh)
-        def _():
-            norm = bend = no_sum
-            for z, at in pieces:
-                m = models[z, at]
-                p = damping * depth_weight(z) / (m * m + focusing * focusing)
-                penalty[z, at] = p
-                r = applied[z, at] - p * m
-                residual[z, at] = r
+        sums = [no_sum] * 3
+
+        def receive(half, applied):
+            norm, bend, cross = sums
+            for slab, at in pieces(half):
+                row = (slab - half.start) * GRID + at.start
+                g = applied[row : row + ROWS]
+                if fresh:
+                    m = models[slab, at]
+                    p = damping * depth_weight(slab) / (m * m + focusing * focusing)
+                    penalty[slab, at] = p
+                    r = g - p * m
+                else:
+                    p = penalty[slab, at]
+                    pd = p * direction[slab, at]
+                    r = residual[slab, at] - old_step * (g + pd)
+                    cross += fold(pd * r)
+                residual[slab, at] = r
                 square = r * r
                 norm += fold(square)
                 bend += fold(p * square)
-            sums[0] = norm
-            sums[1] = bend
-            sums[2] = no_sum
-
-        @pl.when(jnp.logical_not(fresh))
-        def _():
-            norm = bend = cross = no_sum
-            for z, at in pieces:
-                d = direction[z, at]
-                p = penalty[z, at]
-                pd = p * d
-                r = residual[z, at] - old_step * (applied[z, at] + pd)
-                residual[z, at] = r
-                square = r * r
-                norm += fold(square)
-                bend += fold(p * square)
-                cross += fold(pd * r)
-            sums[0] = norm
-            sums[1] = bend
-            sums[2] = cross
-
+            sums[:] = [norm, bend, cross]
+
+        back_project(receive)
         here = predict()
         weighted = weights[...] * here
-        norm, bend, cross = totals_of(
-            [sums[0], sums[1] + fold(weighted * here), sums[2] + fold(weighted * image[...])]
-        )
-        ratio = jnp.where(fresh, 0.0, norm / old_norm)
-        curve = bend + ratio * (2.0 * cross + ratio * old_curve)
+        norm, bend, cross = sums
+        if fresh:
+            norm, curve = totals_of([norm, bend + fold(weighted * here)])
+        else:
+            norm, bend, cross = totals_of(
+                [norm, bend + fold(weighted * here), cross + fold(weighted * image[...])]
+            )
+            ratio = norm / old_norm
+            curve = bend + ratio * (2.0 * cross + ratio * old_curve)
+            here = here + ratio * image[...]
         step = norm / curve
-        here = here + ratio * image[...]
-        image[...] = here
         now = pred[...] + step * here
         pred[...] = now
-        values[...] = (weights[...] * jnp.where(fresh, here, data[...] - now)).astype(BF)
-        for z, at in pieces:
-            d = residual[z, at] + ratio * direction[z, at]
-            direction[z, at] = d
-            models[z, at] += step * d
+        if fresh:
+            image[...] = here
+            values[...] = (weights[...] * here).astype(BF)
+        else:
+            values[...] = (weights[...] * (data[...] - now)).astype(BF)
+        for half in halves:
+            for slab, at in pieces(half):
+                d = residual[slab, at]
+                if not fresh:
+                    d = d + ratio * direction[slab, at]
+                direction[slab, at] = d
+                models[slab, at] += step * d
         return norm, step, curve
 
+    def outer(_, carry):
+        for inner in range(CG_STEPS):
+            carry = round_of(inner == 0, carry)
+        return carry
+
     one = jnp.ones((1, LANES), F32)
-    lax.fori_loop(0, IRLS * CG_STEPS, round_of, (one, one, one))
+    lax.fori_loop(0, IRLS, outer, (one, one, one))
 
     for group in range(slabs // boots):
         m = jnp.concatenate([models[group * boots + i].astype(BF) for i in range(boots)], axis=1)
@@ -464,14 +470,12 @@
             vmem((stations, LANES), BF),
             vmem((LANES, stations), F32),
             vmem((5, DEPTHS, GRID, LANES), F32),
-            vmem((3, 8, LANES), F32),
             vmem((stations, 5 * wide), BF),
             vmem((5, 2, wide // LANES, GRID, LANES), F32),
             vmem((2 * GRID, 5 * wide), BF),
             vmem((2 * GRID, slabs * 2 * LANES), BF),
             vmem((2 * GRID, slabs * 2 * LANES), BF),
             vmem((stations, 5 * LANES), BF),
-            field,
             field,
             field,
             field,

time: 36.4 us -> 33.7 us (0.926)
  Pallas kernels: 27.9 us -> 25.2 us
    pallas_call x1, Pallas kernels: 22.7 us -> 20 us  [solve(): pl.pallas_call(functools.partial(solve_kernel, grid_y, boots), out_shape=...]
  transfers between devices with their start and end apart: 6 -> 6, of which waited for: 2 -> 2; matrix products, arithmetic and copies ran while one was open for 0% -> 0% of each run, Pallas kernels for 77% -> 75%
where the time goes in v12:
time: 33.7 us; the launch traced here: 33.5 us
  Pallas kernels  25.2 us (75%)
  starting transfers between devices  5.36 us (16%)
  waiting for transfers between devices  1.15 us (3%)
  local copies, waits for them, and re-layouts  0.95 us (3%)
  other arithmetic  0.81 us (2%)
    pallas_call x1, Pallas kernels, solve(): pl.pallas_call(functools.partial(solve_kernel, grid_y, boots), out_shape=...  20 us
    ppermute x6, starting transfers between devices, swap(): return lax.ppermute(a, 'wide', [(i, i ^ k) for i in range(wide)])  5.36 us
    pallas_call x2, Pallas kernels, pick(): pl.pallas_call(functools.partial(pick_kernel, grid_y, boots, len(cells)),...  5.14 us
    ppermute x6, waiting for transfers between devices, swap(): return lax.ppermute(a, 'wide', [(i, i ^ k) for i in range(wide)])  1.15 us
    unnamed x4, local copies, waits for them, and re-layouts  0.95 us
    concatenate x1, other arithmetic, local(): return jnp.concatenate(blocks, axis=0)  0.73 us
  transfers between devices with their start and end apart: 6, of which 2 were waited for; matrix products, arithmetic and copies ran while one was open for 0% of the time, Pallas kernels for 75%

profile of v12, /device:TPU:0, one launch (start us, length us, event | category | flops | bytes accessed | tf_op | source)
XLA Modules:
  0.0 33.5 jit_solution(8816636813372810222)
XLA Ops:
  0.0 3.0 %collective-permute-start = (s32[3,4096]{1,0:T(4,128)}, s32[3,4096]{1,0:T(4,128)S(1)}, u32[]{:S(2)}, u32[]{:S(2)}) collective-permute-start(s32[3,4096]{1,0:T(4,128)} %refs_0_.1), channel_id=1, source_target_pairs={{0,2},{1,3},{2,0},{3,1},{4,6},{5,7},{6,4},{7,5},{8,10},{9,11},{10,... | collective-permute-start | bytes 147464 | tf_op jit(solution)/shard_map/ppermute | solution.py:548
  3.0 0.0 collective-permute-start.1
  3.0 0.1 collective-permute-start.4
  3.1 0.0 copy-start
  3.1 20.0 %solve.1.models_ref = bf16[256,512]{1,0:T(8,128)(2,1)} custom-call(s32[1]{0:T(128)} %bitcast.slot_ref, f32[5]{0:T(128)} %comp_ref.1, s32[2,512]{1,0:T(2,128)} %station_ref.1, f32[5,512]{1,0:T(8,128)} %observed_ref.1, s32[8,512]{1,0:T(8,128)} %counts_ref.1, bf16[16384,256]{1,0:T(8,128)(2,1)} %constant.12.clone.source), custom_call_target="tpu_custom_call" | custom-call | flops 10000000000 | bytes 10000000 | tf_op jit(solution)/shard_map/solve/pallas_call | solution.py:454
  23.2 0.0 collective-permute-done.refs_0_
  23.2 0.0 collective-permute-done.1.refs_1_
  23.2 0.0 copy-start.1
  23.2 0.9 %copy-done.1 = bf16[256,512]{1,0:T(8,128)(2,1)S(1)} copy-done((bf16[256,512]{1,0:T(8,128)(2,1)S(1)}, bf16[256,512]{1,0:T(8,128)(2,1)}, u32[]{:S(2)}) %copy-start.1) | copy-done | bytes 262168
  24.1 2.6 %pick.2 = (bf16[2,4096]{1,0:T(2,128)(2,1)S(1)}, bf16[2,4096]{1,0:T(2,128)(2,1)S(1)}) custom-call(bf16[256,512]{1,0:T(8,128)(2,1)S(1)} %copy-done.1, s32[3,4096]{1,0:T(4,128)S(1)} %collective-permute-done.refs_0_, s32[3,4096]{1,0:T(4,128)S(1)} %collective-permute-done.1.refs_1_), custom_call_target="tpu_custom_call" | custom-call | flops 2147483648 | bytes 1000000 | tf_op jit(solution)/shard_map/pick/pallas_call | solution.py:526
  26.7 1.7 %collective-permute-start.2 = (bf16[2,4096]{1,0:T(2,128)(2,1)S(1)}, bf16[2,4096]{1,0:T(2,128)(2,1)S(1)}, u32[]{:S(2)}, u32[]{:S(2)}) collective-permute-start(bf16[2,4096]{1,0:T(2,128)(2,1)S(1)} %get-tuple-element.9), channel_id=1, source_target_pairs={{0,3},{1,2},{2,1},{3,0},{4,7},{5,6},{6,5},{7,4},{8,11},{9,10},{10,... | collective-permute-start | bytes 49160 | tf_op jit(solution)/shard_map/ppermute | solution.py:548
  28.4 0.5 %collective-permute-start.3 = (bf16[2,4096]{1,0:T(2,128)(2,1)S(1)}, bf16[2,4096]{1,0:T(2,128)(2,1)S(1)}, u32[]{:S(2)}, u32[]{:S(2)}) collective-permute-start(bf16[2,4096]{1,0:T(2,128)(2,1)S(1)} %get-tuple-element.10), channel_id=1, source_target_pairs={{0,2},{1,3},{2,0},{3,1},{4,6},{5,7},{6,4},{7,5},{8,10},{9,11},{10,... | collective-permute-start | bytes 49160 | tf_op jit(solution)/shard_map/ppermute | solution.py:548
  28.8 0.0 collective-permute-done.4.refs_1_
  28.8 0.0 copy-done
  28.9 2.6 %pick.3 = (bf16[2,4096]{1,0:T(2,128)(2,1)S(1)}, bf16[2,4096]{1,0:T(2,128)(2,1)S(1)}) custom-call(bf16[256,512]{1,0:T(8,128)(2,1)S(1)} %copy-done.1, s32[3,4096]{1,0:T(4,128)S(1)} %copy-done, s32[3,4096]{1,0:T(4,128)S(1)} %collective-permute-done.4.refs_1_), custom_call_target="tpu_custom_call" | custom-call | flops 2147483648 | bytes 1000000 | tf_op jit(solution)/shard_map/pick/pallas_call | solution.py:526
  31.4 0.1 collective-permute-start.5
  31.5 0.0 collective-permute-done.2
  31.5 0.6 %collective-permute-done.3 = bf16[2,4096]{1,0:T(2,128)(2,1)S(1)} collective-permute-done((bf16[2,4096]{1,0:T(2,128)(2,1)S(1)}, bf16[2,4096]{1,0:T(2,128)(2,1)S(1)}, u32[]{:S(2)}, u32[]{:S(2)}) %collective-permute-start.3) | collective-permute-done | bytes 16416 | tf_op jit(solution)/shard_map/ppermute | solution.py:548
  32.1 0.6 %collective-permute-done.5 = bf16[2,4096]{1,0:T(2,128)(2,1)S(1)} collective-permute-done((bf16[2,4096]{1,0:T(2,128)(2,1)S(1)}, bf16[2,4096]{1,0:T(2,128)(2,1)S(1)}, u32[]{:S(2)}, u32[]{:S(2)}) %collective-permute-start.5) | collective-permute-done | bytes 16416 | tf_op jit(solution)/shard_map/ppermute | solution.py:548
  32.7 0.1 broadcast_select_fusion.11
  32.8 0.7 %maximum_convert_fusion = f32[8,4096]{1,0:T(8,128)} fusion(bf16[2,4096]{1,0:T(2,128)(2,1)S(1)} %get-tuple-element.14, bf16[2,4096]{1,0:T(2,128)(2,1)S(1)} %get-tuple-element.15, bf16[2,4096]{1,0:T(2,128)(2,1)S(1)} %get-tuple-element.16, bf16[2,4096]{1,0:T(2,128)(2,1)S(1)} %get-tuple-element.13), kind=kLoop, calls=%fused_computation | loop fusion | flops 262144 | bytes 196608 | tf_op jit(solution)/shard_map/concatenate | solution.py:561
Async XLA Ops:
  0.0 23.2 %collective-permute-start = (s32[3,4096]{1,0:T(4,128)}, s32[3,4096]{1,0:T(4,128)S(1)}, u32[]{:S(2)}, u32[]{:S(2)}) collective-permute-start(s32[3,4096]{1,0:T(4,128)} %refs_0_.1), channel_id=1, source_target_pairs={{0,2},{1,3},{2,0},{3,1},{4,6},{5,7},{6,4},{7,5},{8,10},{9,11},{10,... | collective-permute-start | bytes 147464 | tf_op jit(solution)/shard_map/ppermute | solution.py:548
  3.0 20.2 %collective-permute-start.1 = (s32[3,4096]{1,0:T(4,128)}, s32[3,4096]{1,0:T(4,128)S(1)}, u32[]{:S(2)}, u32[]{:S(2)}) collective-permute-start(s32[3,4096]{1,0:T(4,128)} %refs_0_.1), channel_id=1, source_target_pairs={{0,3},{1,2},{2,1},{3,0},{4,7},{5,6},{6,5},{7,4},{8,11},{9,10},{10,... | collective-permute-start | bytes 147464 | tf_op jit(solution)/shard_map/ppermute | solution.py:548
  3.0 25.9 %collective-permute-start.4 = (s32[3,4096]{1,0:T(4,128)}, s32[3,4096]{1,0:T(4,128)S(1)}, u32[]{:S(2)}, u32[]{:S(2)}) collective-permute-start(s32[3,4096]{1,0:T(4,128)} %refs_0_.1), channel_id=1, source_target_pairs={{0,1},{1,0},{2,3},{3,2},{4,5},{5,4},{6,7},{7,6},{8,9},{9,8},{10,11... | collective-permute-start | bytes 147464 | tf_op jit(solution)/shard_map/ppermute | solution.py:548
  3.1 25.7 %copy-start = (s32[3,4096]{1,0:T(4,128)S(1)}, s32[3,4096]{1,0:T(4,128)}, u32[]{:S(2)}) copy-start(s32[3,4096]{1,0:T(4,128)} %refs_0_.1) | copy-start | bytes 147460
  23.2 1.0 %copy-start.1 = (bf16[256,512]{1,0:T(8,128)(2,1)S(1)}, bf16[256,512]{1,0:T(8,128)(2,1)}, u32[]{:S(2)}) copy-start(bf16[256,512]{1,0:T(8,128)(2,1)} %solve.1.models_ref) | copy-start | bytes 786436
  26.7 4.8 %collective-permute-start.2 = (bf16[2,4096]{1,0:T(2,128)(2,1)S(1)}, bf16[2,4096]{1,0:T(2,128)(2,1)S(1)}, u32[]{:S(2)}, u32[]{:S(2)}) collective-permute-start(bf16[2,4096]{1,0:T(2,128)(2,1)S(1)} %get-tuple-element.9), channel_id=1, source_target_pairs={{0,3},{1,2},{2,1},{3,0},{4,7},{5,6},{6,5},{7,4},{8,11},{9,10},{10,... | collective-permute-start | bytes 49160 | tf_op jit(solution)/shard_map/ppermute | solution.py:548
  28.4 3.7 %collective-permute-start.3 = (bf16[2,4096]{1,0:T(2,128)(2,1)S(1)}, bf16[2,4096]{1,0:T(2,128)(2,1)S(1)}, u32[]{:S(2)}, u32[]{:S(2)}) collective-permute-start(bf16[2,4096]{1,0:T(2,128)(2,1)S(1)} %get-tuple-element.10), channel_id=1, source_target_pairs={{0,2},{1,3},{2,0},{3,1},{4,6},{5,7},{6,4},{7,5},{8,10},{9,11},{10,... | collective-permute-start | bytes 49160 | tf_op jit(solution)/shard_map/ppermute | solution.py:548
  31.4 1.2 %collective-permute-start.5 = (bf16[2,4096]{1,0:T(2,128)(2,1)S(1)}, bf16[2,4096]{1,0:T(2,128)(2,1)S(1)}, u32[]{:S(2)}, u32[]{:S(2)}) collective-permute-start(bf16[2,4096]{1,0:T(2,128)(2,1)S(1)} %get-tuple-element.11), channel_id=1, source_target_pairs={{0,1},{1,0},{2,3},{3,2},{4,5},{5,4},{6,7},{7,6},{8,9},{9,8},{10,11... | collective-permute-start | bytes 49160 | tf_op jit(solution)/shard_map/ppermute | solution.py:548

commit v13 on v12

--- a/solution.py
+++ b/solution.py
@@ -154,6 +154,7 @@
 def solve_kernel(
     grid_y,
     boots,
+    steps,
     slot_ref,
     comp_ref,
     station_ref,
@@ -195,9 +196,14 @@
         pltpu.make_async_copy(source.at[a:b], const.at[a:b], copied.at[i])
         for i, (a, b) in enumerate(zip(bounds[:-1], bounds[1:]))
     ]
-    first_step = pl.program_id(0) == 0
-
-    @pl.when(first_step)
+
+    def once(f):
+        if steps == 1:
+            f()
+        else:
+            pl.when(pl.program_id(0) == 0)(f)
+
+    @once
     def _():
         for copy in copies:
             copy.start()
@@ -238,7 +244,7 @@
     place_xt = (turned[:, 16:17] == lane.astype(F32)).astype(F32).astype(BF)
     place_yt = (turned[:, 17:18] == lane.astype(F32)).astype(F32)[:, :grid_y].astype(BF)
 
-    @pl.when(first_step)
+    @once
     def _():
         copies[0].wait()
 
@@ -250,19 +256,11 @@
         pick_y[:, odd * wide : (odd + 1) * wide] = dot(place_yt, high) + dot(place_yt, low)
     no_sum = jnp.zeros((8, LANES), F32)
 
-    @pl.when(first_step)
-    def _():
-        copies[1].wait()
-        copies[2].wait()
-        for c in range(5):
-            for z in range(DEPTHS):
-                table_wide[c, z] = table(c, z, slice(0, GRID)).astype(F32)
-
     def trig(at, odd, chunk):
         lane = odd * wide + chunk * LANES
         return pick_y[at, lane : lane + LANES]
 
-    def back_project(receive):
+    def station_spectra():
         spread = held("spread")
         spread = jnp.concatenate([spread[i * LANES : (i + 1) * LANES] for i in range(3)], axis=1)
         spreads = dot(values[...], spread[:, : 5 * LANES])
@@ -281,6 +279,7 @@
                     part = spec[hx * GRID : (hx + 1) * GRID, lane : lane + LANES]
                     spec_q[c, hx, chunk] = -part if odd_x * hx else part
 
+    def back_project(receive):
         for half in halves:
             for row in range(0, GRID, 16):
                 at = slice(row, row + 16)
@@ -361,27 +360,33 @@
         ratio = station_height / depth
         return ratio * ratio * ratio
 
-    models[...] = jnp.zeros_like(models)
-    pred[...] = jnp.zeros_like(pred)
-
-    def round_of(fresh, carry):
+    def round_of(outer, inner, carry):
+        first = outer == 0 and inner == 0
+        last = outer == IRLS - 1 and inner == CG_STEPS - 1
+        fresh = inner == 0
         old_norm, old_step, old_curve = carry
         sums = [no_sum] * 3
+
+        def penalty_at(slab, at):
+            if outer == 0:
+                return damping * depth_weight(slab) / (focusing * focusing)
+            return penalty[slab, at]
 
         def receive(half, applied):
             norm, bend, cross = sums
             for slab, at in pieces(half):
                 row = (slab - half.start) * GRID + at.start
-                g = applied[row : row + ROWS]
-                if fresh:
+                r = applied[row : row + ROWS]
+                if fresh and outer:
                     m = models[slab, at]
                     p = damping * depth_weight(slab) / (m * m + focusing * focusing)
                     penalty[slab, at] = p
-                    r = g - p * m
+                    r = r - p * m
                 else:
-                    p = penalty[slab, at]
+                    p = penalty_at(slab, at)
+                if not fresh:
                     pd = p * direction[slab, at]
-                    r = residual[slab, at] - old_step * (g + pd)
+                    r = residual[slab, at] - old_step * (r + pd)
                     cross += fold(pd * r)
                 residual[slab, at] = r
                 square = r * r
@@ -401,31 +406,42 @@
             )
             ratio = norm / old_norm
             curve = bend + ratio * (2.0 * cross + ratio * old_curve)
-            here = here + ratio * image[...]
         step = norm / curve
-        now = pred[...] + step * here
-        pred[...] = now
-        if fresh:
-            image[...] = here
-            values[...] = (weights[...] * here).astype(BF)
-        else:
-            values[...] = (weights[...] * (data[...] - now)).astype(BF)
+        if not last:
+            if not fresh:
+                here = here + ratio * image[...]
+            now = step * here if first else pred[...] + step * here
+            pred[...] = now
+            if fresh:
+                image[...] = here
+                values[...] = (weights[...] * here).astype(BF)
+            else:
+                values[...] = (weights[...] * (data[...] - now)).astype(BF)
+            station_spectra()
         for half in halves:
             for slab, at in pieces(half):
                 d = residual[slab, at]
                 if not fresh:
                     d = d + ratio * direction[slab, at]
-                direction[slab, at] = d
-                models[slab, at] += step * d
+                if fresh:
+                    direction[slab, at] = d
+                models[slab, at] = step * d if first else models[slab, at] + step * d
         return norm, step, curve
 
-    def outer(_, carry):
+    station_spectra()
+
+    @once
+    def _():
+        copies[1].wait()
+        copies[2].wait()
+        for c in range(5):
+            for z in range(DEPTHS):
+                table_wide[c, z] = table(c, z, slice(0, GRID)).astype(F32)
+
+    carry = (None, None, None)
+    for outer in range(IRLS):
         for inner in range(CG_STEPS):
-            carry = round_of(inner == 0, carry)
-        return carry
-
-    one = jnp.ones((1, LANES), F32)
-    lax.fori_loop(0, IRLS, outer, (one, one, one))
+            carry = round_of(outer, inner, carry)
 
     for group in range(slabs // boots):
         m = jnp.concatenate([models[group * boots + i].astype(BF) for i in range(boots)], axis=1)
@@ -452,7 +468,7 @@
     wide = 2 * boots * grid_y
     inputs = [station_index, observed, counts]
     return pl.pallas_call(
-        functools.partial(solve_kernel, grid_y, boots),
+        functools.partial(solve_kernel, grid_y, boots, mine // boots),
         out_shape=jax.ShapeDtypeStruct((mine * GRID, DEPTHS * grid_y), BF),
         grid=(mine // boots,),
         in_specs=[smem, smem] + [whole(a) for a in inputs] + [pl.BlockSpec(memory_space=pl.ANY)],
@@ -487,10 +503,13 @@
     )(slot, comp_weight, *inputs, const)
 
 
-def pick_kernel(grid_y, boots, count, models_ref, *refs):
-    def pick_chunk(cell_ref, out_ref, at):
-        cells = cell_ref[:, at]
-        place = cells.astype(F32)
+def pick_kernel(grid_y, boots, count, *refs):
+    models_refs, cell_ref, out_ref = refs[:count], refs[count], refs[count + 1]
+
+    @pl.loop(0, cell_ref.shape[1] // CHUNK)
+    def _(step):
+        at = pl.ds(pl.multiple_of(step * CHUNK, CHUNK), CHUNK)
+        place = cell_ref[:, at].astype(F32)
         wide = lambda row, rows: jnp.broadcast_to(row, (rows, CHUNK)).astype(BF)
         count_up = lambda rows: lax.broadcasted_iota(jnp.int32, (rows, CHUNK), 0).astype(F32).astype(BF)
         here_y = count_up(grid_y) == wide(place[1:2], grid_y)
@@ -501,7 +520,8 @@
         for z in range(DEPTHS):
             here_z = z_row == jnp.full((16, CHUNK), z, BF)
             chosen += [jnp.where(here_z, here_y[i : i + 16], none) for i in range(0, grid_y, 16)]
-        found = dot(models_ref[...], jnp.concatenate(chosen, axis=0)).astype(BF)
+        models = jnp.concatenate([ref[...] for ref in models_refs], axis=0)
+        found = dot(models, jnp.concatenate(chosen, axis=0)).astype(BF)
         at_x = count_up(GRID) == wide(place[0:1], GRID)
         parts = []
         for b in range(boots):
@@ -512,28 +532,23 @@
             parts.append(jnp.sum(part.astype(F32), axis=0, keepdims=True))
         out_ref[:, at] = jnp.concatenate(parts, axis=0).astype(BF)
 
-    @pl.loop(0, refs[0].shape[1] // CHUNK)
-    def _(step):
-        at = pl.ds(pl.multiple_of(step * CHUNK, CHUNK), CHUNK)
-        for cell_ref, out_ref in zip(refs[:count], refs[count:]):
-            pick_chunk(cell_ref, out_ref, at)
-
 
 def pick(models, cells, grid_y):
-    boots = models.shape[0] // GRID
-    count = cells[0].shape[1]
+    rows = sum(m.shape[0] for m in models)
+    boots = rows // GRID
+    count = cells.shape[1]
     vmem = pl.BlockSpec(memory_space=pltpu.VMEM)
     return pl.pallas_call(
-        functools.partial(pick_kernel, grid_y, boots, len(cells)),
-        out_shape=[jax.ShapeDtypeStruct((boots, count), BF)] * len(cells),
-        in_specs=[vmem] * (1 + len(cells)),
-        out_specs=[vmem] * len(cells),
+        functools.partial(pick_kernel, grid_y, boots, len(models)),
+        out_shape=jax.ShapeDtypeStruct((boots, count), BF),
+        in_specs=[vmem] * (len(models) + 1),
+        out_specs=vmem,
         compiler_params=pltpu.CompilerParams(vmem_limit_bytes=40 * 1024 * 1024),
         cost_estimate=pl.CostEstimate(
-            flops=2 * models.size * count * len(cells), bytes_accessed=10**6, transcendentals=0
+            flops=2 * rows * DEPTHS * grid_y * count, bytes_accessed=10**6, transcendentals=0
         ),
         name="pick",
-    )(models, *cells)
+    )(*models, cells)
 
 
 def local(wide, cell_index, station_index, observed, comp_weight, counts):
@@ -547,11 +562,15 @@
     def swap(a, k):
         return lax.ppermute(a, "wide", [(i, i ^ k) for i in range(wide)])
 
-    theirs = [swap(cell_index, k) for k in range(1, team)]
-    models = solve(slot.reshape(1), comp_weight, station_index, observed, counts, boots // team, grid_y)
-    far = [swap(a, k + 2) for k, a in enumerate(pick(models, theirs[1:], grid_y))] if team > 2 else []
-    near = pick(models, [cell_index] + theirs[:1], grid_y)
-    got = [near[0]] + [swap(a, 1) for a in near[1:]] + far
+    theirs = [swap(cell_index, k) for k in range(2, team, 2)]
+    models = [solve(slot.reshape(1), comp_weight, station_index, observed, counts, boots // team, grid_y)]
+    models, theirs = lax.optimization_barrier((models, theirs))
+    if team > 1:
+        models.append(swap(models[0], 1))
+    far = [swap(pick(models, cells, grid_y), 2 * k + 2) for k, cells in enumerate(theirs)]
+    found = [pick(models, cell_index, grid_y)] + far
+    mine = boots // team
+    got = [a[i * mine : (i + 1) * mine] for a in found for i in range(len(models))]
     blocks = []
     for member in range(team):
         block = got[member]

time: 33.7 us -> 32.6 us (0.967)
  starting transfers between devices: 5.36 us -> 3.11 us
  waiting for transfers between devices: 1.15 us -> 3.03 us
  Pallas kernels: 25.2 us -> 24.4 us
    ppermute x6 -> x3, starting transfers between devices: 5.36 us -> 3.11 us  [swap(): return lax.ppermute(a, 'wide', [(i, i ^ k) for i in range(wide)])]
    ppermute x6 -> x3, waiting for transfers between devices: 1.15 us -> 3.03 us  [swap(): return lax.ppermute(a, 'wide', [(i, i ^ k) for i in range(wide)])]
    pallas_call x3, Pallas kernels: 25.2 us -> 24.4 us  [the longest x1 19.2 us: solve(): pl.pallas_call(functools.partial(solve_kernel, grid_y, boots, mine // boo...]
  transfers between devices with their start and end apart: 6 -> 3, of which waited for: 2 -> 2; matrix products, arithmetic and copies ran while one was open for 0% -> 0% of each run, Pallas kernels for 75% -> 67%
where the time goes in v13:
time: 32.6 us; the launch traced here: 32.4 us
  Pallas kernels  24.4 us (75%)
  starting transfers between devices  3.11 us (10%)
  waiting for transfers between devices  3.03 us (9%)
  local copies, waits for them, and re-layouts  0.95 us (3%)
  other arithmetic  0.83 us (3%)
    pallas_call x1, Pallas kernels, solve(): pl.pallas_call(functools.partial(solve_kernel, grid_y, boots, mine // boo...  19.2 us
    pallas_call x2, Pallas kernels, pick(): pl.pallas_call(functools.partial(pick_kernel, grid_y, boots, len(models))...  5.13 us
    ppermute x3, starting transfers between devices, swap(): return lax.ppermute(a, 'wide', [(i, i ^ k) for i in range(wide)])  3.11 us
    ppermute x3, waiting for transfers between devices, swap(): return lax.ppermute(a, 'wide', [(i, i ^ k) for i in range(wide)])  3.03 us
    unnamed x4, local copies, waits for them, and re-layouts  0.95 us
    concatenate x1, other arithmetic, local(): return jnp.concatenate(blocks, axis=0)  0.73 us
  transfers between devices with their start and end apart: 3, of which 2 were waited for; matrix products, arithmetic and copies ran while one was open for 0% of the time, Pallas kernels for 67%

profile of v13, /device:TPU:0, one launch (start us, length us, event | category | flops | bytes accessed | tf_op | source)
XLA Modules:
  0.0 32.4 jit_solution(14192457129041293102)
XLA Ops:
  0.0 3.0 %collective-permute-start = (s32[3,4096]{1,0:T(4,128)}, s32[3,4096]{1,0:T(4,128)S(1)}, u32[]{:S(2)}, u32[]{:S(2)}) collective-permute-start(s32[3,4096]{1,0:T(4,128)} %refs_2_.1), channel_id=1, source_target_pairs={{0,2},{1,3},{2,0},{3,1},{4,6},{5,7},{6,4},{7,5},{8,10},{9,11},{10,... | collective-permute-start | bytes 147464 | tf_op jit(solution)/shard_map/ppermute | solution.py:563
  3.0 0.0 copy-start.1
  3.0 19.2 %solve.1.refs_0_ = bf16[256,512]{1,0:T(8,128)(2,1)} custom-call(s32[1]{0:T(128)} %bitcast.slot_ref, f32[5]{0:T(128)} %comp_ref.1, s32[2,512]{1,0:T(2,128)} %station_ref.1, f32[5,512]{1,0:T(8,128)} %observed_ref.1, s32[8,512]{1,0:T(8,128)} %counts_ref.1, bf16[16384,256]{1,0:T(8,128)(2,1)} %constant.12.clone.source), custom_call_target="tpu_custom_call" | custom-call | flops 10000000000 | bytes 10000000 | tf_op jit(solution)/shard_map/solve/pallas_call | solution.py:470
  22.2 0.0 collective-permute-done.refs_2_
  22.2 0.1 collective-permute-start.1
  22.3 1.7 %collective-permute-done.1.refs_1_ = bf16[256,512]{1,0:T(8,128)(2,1)S(1)} collective-permute-done((bf16[256,512]{1,0:T(8,128)(2,1)}, bf16[256,512]{1,0:T(8,128)(2,1)S(1)}, u32[]{:S(2)}, u32[]{:S(2)}) %collective-permute-start.1) | collective-permute-done | bytes 262176 | tf_op jit(solution)/shard_map/ppermute | solution.py:563
  24.0 0.0 copy-start
  24.0 0.9 %copy-done = bf16[256,512]{1,0:T(8,128)(2,1)S(1)} copy-done((bf16[256,512]{1,0:T(8,128)(2,1)S(1)}, bf16[256,512]{1,0:T(8,128)(2,1)}, u32[]{:S(2)}) %copy-start) | copy-done | bytes 262168
  25.0 2.6 %pick.2 = bf16[4,4096]{1,0:T(4,128)(2,1)S(1)} custom-call(bf16[256,512]{1,0:T(8,128)(2,1)S(1)} %copy-done, bf16[256,512]{1,0:T(8,128)(2,1)S(1)} %collective-permute-done.1.refs_1_, s32[3,4096]{1,0:T(4,128)S(1)} %collective-permute-done.refs_2_), custom_call_target="tpu_custom_call" | custom-call | flops 2147483648 | bytes 1000000 | tf_op jit(solution)/shard_map/pick/pallas_call | solution.py:541
  27.6 0.1 collective-permute-start.2
  27.6 0.0 copy-done.1
  27.6 2.6 %pick.3 = bf16[4,4096]{1,0:T(4,128)(2,1)S(1)} custom-call(bf16[256,512]{1,0:T(8,128)(2,1)S(1)} %copy-done, bf16[256,512]{1,0:T(8,128)(2,1)S(1)} %collective-permute-done.1.refs_1_, s32[3,4096]{1,0:T(4,128)S(1)} %copy-done.1), custom_call_target="tpu_custom_call" | custom-call | flops 2147483648 | bytes 1000000 | tf_op jit(solution)/shard_map/pick/pallas_call | solution.py:541
  30.2 1.3 %collective-permute-done.2 = bf16[4,4096]{1,0:T(4,128)(2,1)S(1)} collective-permute-done((bf16[4,4096]{1,0:T(4,128)(2,1)S(1)}, bf16[4,4096]{1,0:T(4,128)(2,1)S(1)}, u32[]{:S(2)}, u32[]{:S(2)}) %collective-permute-start.2) | collective-permute-done | bytes 32800 | tf_op jit(solution)/shard_map/ppermute | solution.py:563
  31.5 0.1 broadcast_select_fusion.11
  31.6 0.7 %maximum_convert_fusion = f32[8,4096]{1,0:T(8,128)} fusion(bf16[2,4096]{1,0:T(2,128)(2,1)S(1)} %get-tuple-element.12, bf16[2,4096]{1,0:T(2,128)(2,1)S(1)} %get-tuple-element.11, bf16[2,4096]{1,0:T(2,128)(2,1)S(1)} %get-tuple-element.10, bf16[2,4096]{1,0:T(2,128)(2,1)S(1)} %get-tuple-element.9), kind=kLoop, calls=%fused_computation | loop fusion | flops 262144 | bytes 196608 | tf_op jit(solution)/shard_map/concatenate | solution.py:580
Async XLA Ops:
  0.0 22.2 %collective-permute-start = (s32[3,4096]{1,0:T(4,128)}, s32[3,4096]{1,0:T(4,128)S(1)}, u32[]{:S(2)}, u32[]{:S(2)}) collective-permute-start(s32[3,4096]{1,0:T(4,128)} %refs_2_.1), channel_id=1, source_target_pairs={{0,2},{1,3},{2,0},{3,1},{4,6},{5,7},{6,4},{7,5},{8,10},{9,11},{10,... | collective-permute-start | bytes 147464 | tf_op jit(solution)/shard_map/ppermute | solution.py:563
  3.0 24.7 %copy-start.1 = (s32[3,4096]{1,0:T(4,128)S(1)}, s32[3,4096]{1,0:T(4,128)}, u32[]{:S(2)}) copy-start(s32[3,4096]{1,0:T(4,128)} %refs_2_.1) | copy-start | bytes 147460
  22.2 1.8 %collective-permute-start.1 = (bf16[256,512]{1,0:T(8,128)(2,1)}, bf16[256,512]{1,0:T(8,128)(2,1)S(1)}, u32[]{:S(2)}, u32[]{:S(2)}) collective-permute-start(bf16[256,512]{1,0:T(8,128)(2,1)} %solve.1.refs_0_), channel_id=1, source_target_pairs={{0,1},{1,0},{2,3},{3,2},{4,5},{5,4},{6,7},{7,6},{8,9},{9,8},{10,11... | collective-permute-start | bytes 786440 | tf_op jit(solution)/shard_map/ppermute | solution.py:563
  24.0 1.0 %copy-start = (bf16[256,512]{1,0:T(8,128)(2,1)S(1)}, bf16[256,512]{1,0:T(8,128)(2,1)}, u32[]{:S(2)}) copy-start(bf16[256,512]{1,0:T(8,128)(2,1)} %solve.1.refs_0_) | copy-start | bytes 786436
  27.6 4.0 %collective-permute-start.2 = (bf16[4,4096]{1,0:T(4,128)(2,1)S(1)}, bf16[4,4096]{1,0:T(4,128)(2,1)S(1)}, u32[]{:S(2)}, u32[]{:S(2)}) collective-permute-start(bf16[4,4096]{1,0:T(4,128)(2,1)S(1)} %pick.2), channel_id=1, source_target_pairs={{0,2},{1,3},{2,0},{3,1},{4,6},{5,7},{6,4},{7,5},{8,10},{9,11},{10,... | collective-permute-start | bytes 98312 | tf_op jit(solution)/shard_map/ppermute | solution.py:563

commit v14 on v13

--- a/solution.py
+++ b/solution.py
@@ -15,6 +15,7 @@
 DEPTHS = 16
 LANES = 128
 TEAM = 4
+PARTS = 4
 CHUNK = 2048
 ROWS = 32
 
@@ -218,11 +219,12 @@
 
     stations = station_ref.shape[1]
     first = (slot_ref[0] * pl.num_programs(0) + pl.program_id(0)) * boots
-    halves = [range(half, half + slabs // 2) for half in (0, slabs // 2)]
-    half_lanes = slabs // 2 * 2 * LANES
-
-    def pieces(half):
-        return [(slab, slice(row, row + ROWS)) for slab in half for row in range(0, GRID, ROWS)]
+    size = slabs // PARTS
+    shares = [range(start, start + size) for start in range(0, slabs, size)]
+    share_lanes = size * 2 * LANES
+
+    def pieces(share):
+        return [(slab, slice(row, row + ROWS)) for slab in share for row in range(0, GRID, ROWS)]
 
 
     rows[...] = jnp.zeros_like(rows)
@@ -280,12 +282,12 @@
                     spec_q[c, hx, chunk] = -part if odd_x * hx else part
 
     def back_project(receive):
-        for half in halves:
+        for share in shares:
             for row in range(0, GRID, 16):
                 at = slice(row, row + 16)
                 for chunk in chunks:
                     q = [[spec_q[c, hx, chunk, at, :] for hx in range(2)] for c in range(5)]
-                    for z in range(half.start * deep, half.stop * deep):
+                    for z in range(share.start * deep, share.stop * deep):
                         t = [table_wide[c, z, at, :] for c in range(5)]
                         lane = z * wide + chunk * LANES
                         for hx in range(2):
@@ -293,24 +295,24 @@
                             for c in range(1, 5):
                                 total = total + t[c] * q[c][hx ^ PARITY[c][0]]
                             spec_g[hx * GRID + row : hx * GRID + row + 16, lane : lane + LANES] = total.astype(BF)
-            lane = half.start * 2 * LANES
-            along_x = dot(held("base_x"), spec_g[:, lane : lane + half_lanes]).astype(BF)
-            along_x = [along_x[:, lane : lane + 2 * LANES] for lane in range(0, half_lanes, 2 * LANES)]
-            receive(half, dot(jnp.concatenate(along_x, axis=0), held("field_yt", LANES)))
+            lane = share.start * 2 * LANES
+            along_x = dot(held("base_x"), spec_g[:, lane : lane + share_lanes]).astype(BF)
+            along_x = [along_x[:, lane : lane + 2 * LANES] for lane in range(0, share_lanes, 2 * LANES)]
+            receive(share, dot(jnp.concatenate(along_x, axis=0), held("field_yt", LANES)))
 
     def predict():
-        for half in halves:
-            r = residual[half.start : half.stop].reshape(len(half) * GRID, LANES).astype(BF)
+        for share in shares:
+            r = residual[share.start : share.stop].reshape(len(share) * GRID, LANES).astype(BF)
             y = dot(jnp.concatenate([r, r], axis=1), held("field_y2")).astype(BF)
-            y = jnp.concatenate([y[i * GRID : (i + 1) * GRID] for i in range(len(half))], axis=1)
-            lane = half.start * 2 * LANES
-            spec_f[:, lane : lane + half_lanes] = dot(held("base_xt2"), jnp.concatenate([y, y], axis=0)).astype(BF)
+            y = jnp.concatenate([y[i * GRID : (i + 1) * GRID] for i in range(len(share))], axis=1)
+            lane = share.start * 2 * LANES
+            spec_f[:, lane : lane + share_lanes] = dot(held("base_xt2"), jnp.concatenate([y, y], axis=0)).astype(BF)
 
             for row in range(0, GRID, 16):
                 at = [slice(hx * GRID + row, hx * GRID + row + 16) for hx in range(2)]
                 for chunk in chunks:
                     total = [[None] * 2 for _ in range(5)]
-                    for z in range(half.start * deep, half.stop * deep):
+                    for z in range(share.start * deep, share.stop * deep):
                         lane = z * wide + chunk * LANES
                         f = [spec_f[at[hx], lane : lane + LANES] for hx in range(2)]
                         for c, (odd_x, _) in enumerate(PARITY):
@@ -322,9 +324,10 @@
                         lane = c * wide + chunk * LANES
                         for hx in range(2):
                             part = total[c][hx]
-                            if half is not halves[0]:
+                            if share is not shares[0]:
                                 part = part + spec_i[at[hx], lane : lane + LANES]
-                                part = -part if odd_x * hx else part
+                            if share is shares[-1] and odd_x * hx:
+                                part = -part
                             spec_i[at[hx], lane : lane + LANES] = part
 
         picked = dot(pick_x[...], spec_i[...])
@@ -372,10 +375,10 @@
                 return damping * depth_weight(slab) / (focusing * focusing)
             return penalty[slab, at]
 
-        def receive(half, applied):
+        def receive(share, applied):
             norm, bend, cross = sums
-            for slab, at in pieces(half):
-                row = (slab - half.start) * GRID + at.start
+            for slab, at in pieces(share):
+                row = (slab - share.start) * GRID + at.start
                 r = applied[row : row + ROWS]
                 if fresh and outer:
                     m = models[slab, at]
@@ -418,8 +421,8 @@
             else:
                 values[...] = (weights[...] * (data[...] - now)).astype(BF)
             station_spectra()
-        for half in halves:
-            for slab, at in pieces(half):
+        for share in shares:
+            for slab, at in pieces(share):
                 d = residual[slab, at]
                 if not fresh:
                     d = d + ratio * direction[slab, at]
@@ -503,12 +506,8 @@
     )(slot, comp_weight, *inputs, const)
 
 
-def pick_kernel(grid_y, boots, count, *refs):
-    models_refs, cell_ref, out_ref = refs[:count], refs[count], refs[count + 1]
-
-    @pl.loop(0, cell_ref.shape[1] // CHUNK)
-    def _(step):
-        at = pl.ds(pl.multiple_of(step * CHUNK, CHUNK), CHUNK)
+def pick_kernel(grid_y, boots, count, models_ref, *refs):
+    def pick_chunk(cell_ref, out_ref, at):
         place = cell_ref[:, at].astype(F32)
         wide = lambda row, rows: jnp.broadcast_to(row, (rows, CHUNK)).astype(BF)
         count_up = lambda rows: lax.broadcasted_iota(jnp.int32, (rows, CHUNK), 0).astype(F32).astype(BF)
@@ -520,8 +519,7 @@
         for z in range(DEPTHS):
             here_z = z_row == jnp.full((16, CHUNK), z, BF)
             chosen += [jnp.where(here_z, here_y[i : i + 16], none) for i in range(0, grid_y, 16)]
-        models = jnp.concatenate([ref[...] for ref in models_refs], axis=0)
-        found = dot(models, jnp.concatenate(chosen, axis=0)).astype(BF)
+        found = dot(models_ref[...], jnp.concatenate(chosen, axis=0)).astype(BF)
         at_x = count_up(GRID) == wide(place[0:1], GRID)
         parts = []
         for b in range(boots):
@@ -532,23 +530,28 @@
             parts.append(jnp.sum(part.astype(F32), axis=0, keepdims=True))
         out_ref[:, at] = jnp.concatenate(parts, axis=0).astype(BF)
 
+    @pl.loop(0, refs[0].shape[1] // CHUNK)
+    def _(step):
+        at = pl.ds(pl.multiple_of(step * CHUNK, CHUNK), CHUNK)
+        for cell_ref, out_ref in zip(refs[:count], refs[count:]):
+            pick_chunk(cell_ref, out_ref, at)
+
 
 def pick(models, cells, grid_y):
-    rows = sum(m.shape[0] for m in models)
-    boots = rows // GRID
-    count = cells.shape[1]
+    boots = models.shape[0] // GRID
+    count = cells[0].shape[1]
     vmem = pl.BlockSpec(memory_space=pltpu.VMEM)
     return pl.pallas_call(
-        functools.partial(pick_kernel, grid_y, boots, len(models)),
-        out_shape=jax.ShapeDtypeStruct((boots, count), BF),
-        in_specs=[vmem] * (len(models) + 1),
-        out_specs=vmem,
+        functools.partial(pick_kernel, grid_y, boots, len(cells)),
+        out_shape=[jax.ShapeDtypeStruct((boots, count), BF)] * len(cells),
+        in_specs=[vmem] * (1 + len(cells)),
+        out_specs=[vmem] * len(cells),
         compiler_params=pltpu.CompilerParams(vmem_limit_bytes=40 * 1024 * 1024),
         cost_estimate=pl.CostEstimate(
-            flops=2 * rows * DEPTHS * grid_y * count, bytes_accessed=10**6, transcendentals=0
+            flops=2 * models.size * count * len(cells), bytes_accessed=10**6, transcendentals=0
         ),
         name="pick",
-    )(*models, cells)
+    )(models, *cells)
 
 
 def local(wide, cell_index, station_index, observed, comp_weight, counts):
@@ -563,14 +566,18 @@
         return lax.ppermute(a, "wide", [(i, i ^ k) for i in range(wide)])
 
     theirs = [swap(cell_index, k) for k in range(2, team, 2)]
-    models = [solve(slot.reshape(1), comp_weight, station_index, observed, counts, boots // team, grid_y)]
+    models = solve(slot.reshape(1), comp_weight, station_index, observed, counts, boots // team, grid_y)
     models, theirs = lax.optimization_barrier((models, theirs))
     if team > 1:
-        models.append(swap(models[0], 1))
-    far = [swap(pick(models, cells, grid_y), 2 * k + 2) for k, cells in enumerate(theirs)]
-    found = [pick(models, cell_index, grid_y)] + far
-    mine = boots // team
-    got = [a[i * mine : (i + 1) * mine] for a in found for i in range(len(models))]
+        shared = swap(models, 1)
+        *ours_far, ours_near = pick(models, [*theirs, cell_index], grid_y)
+        ours_far = [swap(a, 2 * k + 2) for k, a in enumerate(ours_far)]
+        shared_far = [swap(a, 2 * k + 2) for k, a in enumerate(pick(shared, theirs, grid_y))]
+        got = [ours_near, pick(shared, [cell_index], grid_y)[0]]
+        for pair in zip(ours_far, shared_far):
+            got += pair
+    else:
+        got = pick(models, [cell_index], grid_y)
     blocks = []
     for member in range(team):
         block = got[member]

time: 32.6 us -> 33 us (1.012)
  waiting for transfers between devices: 3.03 us -> 0.25 us
  starting transfers between devices: 3.11 us -> 5.18 us
  Pallas kernels: 24.4 us -> 25.5 us
    ppermute x3 -> x4, waiting for transfers between devices: 3.03 us -> 0.25 us  [swap(): return lax.ppermute(a, 'wide', [(i, i ^ k) for i in range(wide)])]
    ppermute x3 -> x4, starting transfers between devices: 3.11 us -> 5.18 us  [swap(): return lax.ppermute(a, 'wide', [(i, i ^ k) for i in range(wide)])]
    pallas_call x1, Pallas kernels: 19.2 us -> 20 us  [solve(): pl.pallas_call(functools.partial(solve_kernel, grid_y, boots, mine // boo...]
    pallas_call x2 -> x3, Pallas kernels: 5.13 us -> 5.52 us  [pick(): pl.pallas_call(functools.partial(pick_kernel, grid_y, boots, len(cells)),...]
  transfers between devices with their start and end apart: 3 -> 4, of which waited for: 2 -> 1; matrix products, arithmetic and copies ran while one was open for 0% -> 0% of each run, Pallas kernels for 67% -> 78%
where the time goes in v14:
time: 33 us; the launch traced here: 32.8 us
  Pallas kernels  25.5 us (77%)
  starting transfers between devices  5.18 us (16%)
  local copies, waits for them, and re-layouts  0.95 us (3%)
  other arithmetic  0.81 us (2%)
    pallas_call x1, Pallas kernels, solve(): pl.pallas_call(functools.partial(solve_kernel, grid_y, boots, mine // boo...  20 us
    pallas_call x3, Pallas kernels, pick(): pl.pallas_call(functools.partial(pick_kernel, grid_y, boots, len(cells)),...  5.52 us
    ppermute x4, starting transfers between devices, swap(): return lax.ppermute(a, 'wide', [(i, i ^ k) for i in range(wide)])  5.18 us
    unnamed x4, local copies, waits for them, and re-layouts  0.95 us
    concatenate x1, other arithmetic, local(): return jnp.concatenate(blocks, axis=0)  0.73 us
  transfers between devices with their start and end apart: 4, of which 1 were waited for; matrix products, arithmetic and copies ran while one was open for 0% of the time, Pallas kernels for 78%

profile of v14, /device:TPU:0, one launch (start us, length us, event | category | flops | bytes accessed | tf_op | source)
XLA Modules:
  0.0 32.8 jit_solution(1495441371118822560)
XLA Ops:
  0.0 3.0 %collective-permute-start = (s32[3,4096]{1,0:T(4,128)}, s32[3,4096]{1,0:T(4,128)S(1)}, u32[]{:S(2)}, u32[]{:S(2)}) collective-permute-start(s32[3,4096]{1,0:T(4,128)} %refs_0_.1), channel_id=1, source_target_pairs={{0,2},{1,3},{2,0},{3,1},{4,6},{5,7},{6,4},{7,5},{8,10},{9,11},{10,... | collective-permute-start | bytes 147464 | tf_op jit(solution)/shard_map/ppermute | solution.py:566
  3.0 0.0 copy-start.1
  3.0 20.0 %solve.1.models_ref = bf16[256,512]{1,0:T(8,128)(2,1)} custom-call(s32[1]{0:T(128)} %bitcast.slot_ref, f32[5]{0:T(128)} %comp_ref.1, s32[2,512]{1,0:T(2,128)} %station_ref.1, f32[5,512]{1,0:T(8,128)} %observed_ref.1, s32[8,512]{1,0:T(8,128)} %counts_ref.1, bf16[16384,256]{1,0:T(8,128)(2,1)} %constant.12.clone.source), custom_call_target="tpu_custom_call" | custom-call | flops 10000000000 | bytes 10000000 | tf_op jit(solution)/shard_map/solve/pallas_call | solution.py:473
  23.0 0.0 collective-permute-done.refs_0_
  23.0 0.1 collective-permute-start.1
  23.1 0.0 copy-done.1
  23.1 0.0 copy-start
  23.1 0.9 %copy-done = bf16[256,512]{1,0:T(8,128)(2,1)S(1)} copy-done((bf16[256,512]{1,0:T(8,128)(2,1)S(1)}, bf16[256,512]{1,0:T(8,128)(2,1)}, u32[]{:S(2)}) %copy-start) | copy-done | bytes 262168
  24.0 2.6 %pick.4 = (bf16[2,4096]{1,0:T(2,128)(2,1)S(1)}, bf16[2,4096]{1,0:T(2,128)(2,1)S(1)}) custom-call(bf16[256,512]{1,0:T(8,128)(2,1)S(1)} %copy-done, s32[3,4096]{1,0:T(4,128)S(1)} %collective-permute-done.refs_0_, s32[3,4096]{1,0:T(4,128)S(1)} %copy-done.1), custom_call_target="tpu_custom_call" | custom-call | flops 2147483648 | bytes 1000000 | tf_op jit(solution)/shard_map/pick/pallas_call | solution.py:544
  26.6 0.1 collective-permute-start.3
  26.7 0.0 collective-permute-done.1.models_ref
  26.7 1.5 %pick.3 = bf16[2,4096]{1,0:T(2,128)(2,1)S(1)} custom-call(bf16[256,512]{1,0:T(8,128)(2,1)S(1)} %collective-permute-done.1.models_ref, s32[3,4096]{1,0:T(4,128)S(1)} %collective-permute-done.refs_0_), custom_call_target="tpu_custom_call" | custom-call | flops 1073741824 | bytes 1000000 | tf_op jit(solution)/shard_map/pick/pallas_call | solution.py:544
  28.2 2.1 %collective-permute-start.2 = (bf16[2,4096]{1,0:T(2,128)(2,1)S(1)}, bf16[2,4096]{1,0:T(2,128)(2,1)S(1)}, u32[]{:S(2)}, u32[]{:S(2)}) collective-permute-start(bf16[2,4096]{1,0:T(2,128)(2,1)S(1)} %pick.3), channel_id=1, source_target_pairs={{0,2},{1,3},{2,0},{3,1},{4,6},{5,7},{6,4},{7,5},{8,10},{9,11},{10,... | collective-permute-start | bytes 49160 | tf_op jit(solution)/shard_map/ppermute | solution.py:566
  30.3 1.5 %pick.5 = bf16[2,4096]{1,0:T(2,128)(2,1)S(1)} custom-call(bf16[256,512]{1,0:T(8,128)(2,1)S(1)} %collective-permute-done.1.models_ref, s32[3,4096]{1,0:T(4,128)S(1)} %copy-done.1), custom_call_target="tpu_custom_call" | custom-call | flops 1073741824 | bytes 1000000 | tf_op jit(solution)/shard_map/pick/pallas_call | solution.py:544
  31.7 0.0 collective-permute-done.3
  31.8 0.2 collective-permute-done.2
  32.0 0.1 broadcast_select_fusion.11
  32.1 0.7 %maximum_convert_fusion = f32[8,4096]{1,0:T(8,128)} fusion(bf16[2,4096]{1,0:T(2,128)(2,1)S(1)} %get-tuple-element.14, bf16[2,4096]{1,0:T(2,128)(2,1)S(1)} %get-tuple-element.15, bf16[2,4096]{1,0:T(2,128)(2,1)S(1)} %get-tuple-element.16, bf16[2,4096]{1,0:T(2,128)(2,1)S(1)} %get-tuple-element.13), kind=kLoop, calls=%fused_computation | loop fusion | flops 262144 | bytes 196608 | tf_op jit(solution)/shard_map/concatenate | solution.py:587
Async XLA Ops:
  0.0 23.0 %collective-permute-start = (s32[3,4096]{1,0:T(4,128)}, s32[3,4096]{1,0:T(4,128)S(1)}, u32[]{:S(2)}, u32[]{:S(2)}) collective-permute-start(s32[3,4096]{1,0:T(4,128)} %refs_0_.1), channel_id=1, source_target_pairs={{0,2},{1,3},{2,0},{3,1},{4,6},{5,7},{6,4},{7,5},{8,10},{9,11},{10,... | collective-permute-start | bytes 147464 | tf_op jit(solution)/shard_map/ppermute | solution.py:566
  3.0 20.1 %copy-start.1 = (s32[3,4096]{1,0:T(4,128)S(1)}, s32[3,4096]{1,0:T(4,128)}, u32[]{:S(2)}) copy-start(s32[3,4096]{1,0:T(4,128)} %refs_0_.1) | copy-start | bytes 147460
  23.0 3.7 %collective-permute-start.1 = (bf16[256,512]{1,0:T(8,128)(2,1)}, bf16[256,512]{1,0:T(8,128)(2,1)S(1)}, u32[]{:S(2)}, u32[]{:S(2)}) collective-permute-start(bf16[256,512]{1,0:T(8,128)(2,1)} %solve.1.models_ref), channel_id=1, source_target_pairs={{0,1},{1,0},{2,3},{3,2},{4,5},{5,4},{6,7},{7,6},{8,9},{9,8},{10,11... | collective-permute-start | bytes 786440 | tf_op jit(solution)/shard_map/ppermute | solution.py:566
  23.1 1.0 %copy-start = (bf16[256,512]{1,0:T(8,128)(2,1)S(1)}, bf16[256,512]{1,0:T(8,128)(2,1)}, u32[]{:S(2)}) copy-start(bf16[256,512]{1,0:T(8,128)(2,1)} %solve.1.models_ref) | copy-start | bytes 786436
  26.6 5.1 %collective-permute-start.3 = (bf16[2,4096]{1,0:T(2,128)(2,1)S(1)}, bf16[2,4096]{1,0:T(2,128)(2,1)S(1)}, u32[]{:S(2)}, u32[]{:S(2)}) collective-permute-start(bf16[2,4096]{1,0:T(2,128)(2,1)S(1)} %get-tuple-element.11), channel_id=1, source_target_pairs={{0,2},{1,3},{2,0},{3,1},{4,6},{5,7},{6,4},{7,5},{8,10},{9,11},{10,... | collective-permute-start | bytes 49160 | tf_op jit(solution)/shard_map/ppermute | solution.py:566
  28.2 3.8 %collective-permute-start.2 = (bf16[2,4096]{1,0:T(2,128)(2,1)S(1)}, bf16[2,4096]{1,0:T(2,128)(2,1)S(1)}, u32[]{:S(2)}, u32[]{:S(2)}) collective-permute-start(bf16[2,4096]{1,0:T(2,128)(2,1)S(1)} %pick.3), channel_id=1, source_target_pairs={{0,2},{1,3},{2,0},{3,1},{4,6},{5,7},{6,4},{7,5},{8,10},{9,11},{10,... | collective-permute-start | bytes 49160 | tf_op jit(solution)/shard_map/ppermute | solution.py:566

commit v15 on v14

--- a/solution.py
+++ b/solution.py
@@ -15,7 +15,7 @@
 DEPTHS = 16
 LANES = 128
 TEAM = 4
-PARTS = 4
+PARTS = 2
 CHUNK = 2048
 ROWS = 32
 
@@ -431,8 +431,6 @@
                 models[slab, at] = step * d if first else models[slab, at] + step * d
         return norm, step, curve
 
-    station_spectra()
-
     @once
     def _():
         copies[1].wait()
@@ -440,6 +438,8 @@
         for c in range(5):
             for z in range(DEPTHS):
                 table_wide[c, z] = table(c, z, slice(0, GRID)).astype(F32)
+
+    station_spectra()
 
     carry = (None, None, None)
     for outer in range(IRLS):
@@ -506,8 +506,15 @@
     )(slot, comp_weight, *inputs, const)
 
 
-def pick_kernel(grid_y, boots, count, models_ref, *refs):
-    def pick_chunk(cell_ref, out_ref, at):
+def pick_kernel(grid_y, n_models, n_before, keep, cell_ref, *refs):
+    models_refs, refs = refs[:n_models], refs[n_models:]
+    before_refs, refs = refs[:n_before], refs[n_before:]
+    if keep:
+        refs[1][...] = models_refs[0][...]
+
+    @pl.loop(0, cell_ref.shape[1] // CHUNK)
+    def _(step):
+        at = pl.ds(pl.multiple_of(step * CHUNK, CHUNK), CHUNK)
         place = cell_ref[:, at].astype(F32)
         wide = lambda row, rows: jnp.broadcast_to(row, (rows, CHUNK)).astype(BF)
         count_up = lambda rows: lax.broadcasted_iota(jnp.int32, (rows, CHUNK), 0).astype(F32).astype(BF)
@@ -519,39 +526,39 @@
         for z in range(DEPTHS):
             here_z = z_row == jnp.full((16, CHUNK), z, BF)
             chosen += [jnp.where(here_z, here_y[i : i + 16], none) for i in range(0, grid_y, 16)]
-        found = dot(models_ref[...], jnp.concatenate(chosen, axis=0)).astype(BF)
+        models = jnp.concatenate([ref[...] for ref in models_refs], axis=0)
+        found = dot(models, jnp.concatenate(chosen, axis=0)).astype(BF)
         at_x = count_up(GRID) == wide(place[0:1], GRID)
-        parts = []
-        for b in range(boots):
+        parts = [ref[:, at].astype(F32) for ref in before_refs]
+        for b in range(models.shape[0] // GRID):
             part = jnp.where(at_x, found[b * GRID : (b + 1) * GRID], jnp.zeros((GRID, CHUNK), BF))
             while part.shape[0] > 16:
                 half = part.shape[0] // 2
                 part = part[:half] + part[half:]
             parts.append(jnp.sum(part.astype(F32), axis=0, keepdims=True))
-        out_ref[:, at] = jnp.concatenate(parts, axis=0).astype(BF)
-
-    @pl.loop(0, refs[0].shape[1] // CHUNK)
-    def _(step):
-        at = pl.ds(pl.multiple_of(step * CHUNK, CHUNK), CHUNK)
-        for cell_ref, out_ref in zip(refs[:count], refs[count:]):
-            pick_chunk(cell_ref, out_ref, at)
-
-
-def pick(models, cells, grid_y):
-    boots = models.shape[0] // GRID
-    count = cells[0].shape[1]
+        refs[0][:, at] = jnp.concatenate(parts, axis=0).astype(BF)
+
+
+def pick(cells, models, before=(), grid_y=0, keep=False):
+    rows = sum(m.shape[0] for m in models)
+    boots = rows // GRID + sum(a.shape[0] for a in before)
+    count = cells.shape[1]
     vmem = pl.BlockSpec(memory_space=pltpu.VMEM)
-    return pl.pallas_call(
-        functools.partial(pick_kernel, grid_y, boots, len(cells)),
-        out_shape=[jax.ShapeDtypeStruct((boots, count), BF)] * len(cells),
-        in_specs=[vmem] * (1 + len(cells)),
-        out_specs=[vmem] * len(cells),
+    shapes = [jax.ShapeDtypeStruct((boots, count), BF)]
+    if keep:
+        shapes.append(jax.ShapeDtypeStruct(models[0].shape, BF))
+    found = pl.pallas_call(
+        functools.partial(pick_kernel, grid_y, len(models), len(before), keep),
+        out_shape=shapes,
+        in_specs=[vmem] * (1 + len(models) + len(before)),
+        out_specs=[vmem] * len(shapes),
         compiler_params=pltpu.CompilerParams(vmem_limit_bytes=40 * 1024 * 1024),
         cost_estimate=pl.CostEstimate(
-            flops=2 * models.size * count * len(cells), bytes_accessed=10**6, transcendentals=0
+            flops=2 * rows * DEPTHS * grid_y * count, bytes_accessed=10**6, transcendentals=0
         ),
         name="pick",
-    )(models, *cells)
+    )(cells, *models, *before)
+    return found if keep else found[0]
 
 
 def local(wide, cell_index, station_index, observed, comp_weight, counts):
@@ -570,14 +577,17 @@
     models, theirs = lax.optimization_barrier((models, theirs))
     if team > 1:
         shared = swap(models, 1)
-        *ours_far, ours_near = pick(models, [*theirs, cell_index], grid_y)
-        ours_far = [swap(a, 2 * k + 2) for k, a in enumerate(ours_far)]
-        shared_far = [swap(a, 2 * k + 2) for k, a in enumerate(pick(shared, theirs, grid_y))]
-        got = [ours_near, pick(shared, [cell_index], grid_y)[0]]
-        for pair in zip(ours_far, shared_far):
-            got += pair
+        far = []
+        for k, cells in enumerate(theirs):
+            ours = pick(cells, [models], grid_y=grid_y, keep=k == 0)
+            if k == 0:
+                ours, models = ours
+            far.append(swap(pick(cells, [shared], [ours], grid_y=grid_y), 2 * k + 2))
+        found = [pick(cell_index, [models, shared], grid_y=grid_y)] + far
     else:
-        got = pick(models, [cell_index], grid_y)
+        found = [pick(cell_index, [models], grid_y=grid_y)]
+    mine = boots // team
+    got = [a[i * mine : (i + 1) * mine] for a in found for i in range(a.shape[0] // mine)]
     blocks = []
     for member in range(team):
         block = got[member]

time: 33 us -> 31.8 us (0.964)
  starting transfers between devices: 5.18 us -> 3.11 us
  waiting for transfers between devices: 0.25 us -> 1.31 us
    ppermute x4 -> x3, starting transfers between devices: 5.18 us -> 3.11 us  [swap(): return lax.ppermute(a, 'wide', [(i, i ^ k) for i in range(wide)])]
    ppermute x4 -> x3, waiting for transfers between devices: 0.25 us -> 1.31 us  [swap(): return lax.ppermute(a, 'wide', [(i, i ^ k) for i in range(wide)])]
  transfers between devices with their start and end apart: 4 -> 3, of which waited for: 1 -> 1; matrix products, arithmetic and copies ran while one was open for 0% -> 0% of each run, Pallas kernels for 78% -> 75%
where the time goes in v15:
time: 31.8 us; the launch traced here: 31.6 us
  Pallas kernels  25.3 us (80%)
  starting transfers between devices  3.11 us (10%)
  waiting for transfers between devices  1.31 us (4%)
  local copies, waits for them, and re-layouts  0.95 us (3%)
  other arithmetic  0.83 us (3%)
    pallas_call x1, Pallas kernels, solve(): pl.pallas_call(functools.partial(solve_kernel, grid_y, boots, mine // boo...  19.8 us
    pallas_call x3, Pallas kernels, pick(): pl.pallas_call(functools.partial(pick_kernel, grid_y, len(models), len(be...  5.54 us
    ppermute x3, starting transfers between devices, swap(): return lax.ppermute(a, 'wide', [(i, i ^ k) for i in range(wide)])  3.11 us
    ppermute x3, waiting for transfers between devices, swap(): return lax.ppermute(a, 'wide', [(i, i ^ k) for i in range(wide)])  1.31 us
    unnamed x4, local copies, waits for them, and re-layouts  0.95 us
    concatenate x1, other arithmetic, local(): return jnp.concatenate(blocks, axis=0)  0.73 us
  transfers between devices with their start and end apart: 3, of which 1 were waited for; matrix products, arithmetic and copies ran while one was open for 0% of the time, Pallas kernels for 75%

profile of v15, /device:TPU:0, one launch (start us, length us, event | category | flops | bytes accessed | tf_op | source)
XLA Modules:
  0.0 31.6 jit_solution(17944464474254695997)
XLA Ops:
  0.0 3.0 %collective-permute-start = (s32[3,4096]{1,0:T(4,128)}, s32[3,4096]{1,0:T(4,128)S(1)}, u32[]{:S(2)}, u32[]{:S(2)}) collective-permute-start(s32[3,4096]{1,0:T(4,128)} %cell_ref.1), channel_id=1, source_target_pairs={{0,2},{1,3},{2,0},{3,1},{4,6},{5,7},{6,4},{7,5},{8,10},{9,11},{10,... | collective-permute-start | bytes 147464 | tf_op jit(solution)/shard_map/ppermute | solution.py:573
  3.0 0.0 copy-start.1
  3.0 19.8 %solve.1.refs_0_ = bf16[256,512]{1,0:T(8,128)(2,1)} custom-call(s32[1]{0:T(128)} %bitcast.slot_ref, f32[5]{0:T(128)} %comp_ref.1, s32[2,512]{1,0:T(2,128)} %station_ref.1, f32[5,512]{1,0:T(8,128)} %observed_ref.1, s32[8,512]{1,0:T(8,128)} %counts_ref.1, bf16[16384,256]{1,0:T(8,128)(2,1)} %constant.12.clone.source), custom_call_target="tpu_custom_call" | custom-call | flops 10000000000 | bytes 10000000 | tf_op jit(solution)/shard_map/solve/pallas_call | solution.py:473
  22.8 0.0 collective-permute-done.cell_ref
  22.8 0.1 collective-permute-start.1
  22.9 0.0 copy-start
  22.9 0.9 %copy-done = bf16[256,512]{1,0:T(8,128)(2,1)S(1)} copy-done((bf16[256,512]{1,0:T(8,128)(2,1)S(1)}, bf16[256,512]{1,0:T(8,128)(2,1)}, u32[]{:S(2)}) %copy-start) | copy-done | bytes 262168
  23.8 1.5 %pick.3 = (bf16[2,4096]{1,0:T(2,128)(2,1)S(1)}, bf16[256,512]{1,0:T(8,128)(2,1)S(1)}) custom-call(s32[3,4096]{1,0:T(4,128)S(1)} %collective-permute-done.cell_ref, bf16[256,512]{1,0:T(8,128)(2,1)S(1)} %copy-done), custom_call_target="tpu_custom_call" | custom-call | flops 1073741824 | bytes 1000000 | tf_op jit(solution)/shard_map/pick/pallas_call | solution.py:550
  25.3 0.0 collective-permute-done.1.refs_0_.refs_1_
  25.3 1.5 %pick.4 = bf16[4,4096]{1,0:T(4,128)(2,1)S(1)} custom-call(s32[3,4096]{1,0:T(4,128)S(1)} %collective-permute-done.cell_ref, bf16[256,512]{1,0:T(8,128)(2,1)S(1)} %collective-permute-done.1.refs_0_.refs_1_, bf16[2,4096]{1,0:T(2,128)(2,1)S(1)} %get-tuple-element.11.refs_1_), custom_call_target="tpu_custom_call" | custom-call | flops 1073741824 | bytes 1000000 | tf_op jit(solution)/shard_map/pick/pallas_call | solution.py:550
  26.8 0.1 collective-permute-start.2
  26.9 0.0 copy-done.1
  26.9 2.6 %pick.5 = bf16[4,4096]{1,0:T(4,128)(2,1)S(1)} custom-call(s32[3,4096]{1,0:T(4,128)S(1)} %copy-done.1, bf16[256,512]{1,0:T(8,128)(2,1)S(1)} %get-tuple-element.12.refs_0_, bf16[256,512]{1,0:T(8,128)(2,1)S(1)} %collective-permute-done.1.refs_0_.refs_1_), custom_call_target="tpu_custom_call" | custom-call | flops 2147483648 | bytes 1000000 | tf_op jit(solution)/shard_map/pick/pallas_call | solution.py:550
  29.5 1.3 %collective-permute-done.2 = bf16[4,4096]{1,0:T(4,128)(2,1)S(1)} collective-permute-done((bf16[4,4096]{1,0:T(4,128)(2,1)S(1)}, bf16[4,4096]{1,0:T(4,128)(2,1)S(1)}, u32[]{:S(2)}, u32[]{:S(2)}) %collective-permute-start.2) | collective-permute-done | bytes 32800 | tf_op jit(solution)/shard_map/ppermute | solution.py:573
  30.8 0.1 broadcast_select_fusion.11
  30.9 0.7 %maximum_convert_fusion = f32[8,4096]{1,0:T(8,128)} fusion(bf16[2,4096]{1,0:T(2,128)(2,1)S(1)} %get-tuple-element.16, bf16[2,4096]{1,0:T(2,128)(2,1)S(1)} %get-tuple-element.15, bf16[2,4096]{1,0:T(2,128)(2,1)S(1)} %get-tuple-element.14, bf16[2,4096]{1,0:T(2,128)(2,1)S(1)} %get-tuple-element.13), kind=kLoop, calls=%fused_computation | loop fusion | flops 262144 | bytes 196608 | tf_op jit(solution)/shard_map/concatenate | solution.py:597
Async XLA Ops:
  0.0 22.8 %collective-permute-start = (s32[3,4096]{1,0:T(4,128)}, s32[3,4096]{1,0:T(4,128)S(1)}, u32[]{:S(2)}, u32[]{:S(2)}) collective-permute-start(s32[3,4096]{1,0:T(4,128)} %cell_ref.1), channel_id=1, source_target_pairs={{0,2},{1,3},{2,0},{3,1},{4,6},{5,7},{6,4},{7,5},{8,10},{9,11},{10,... | collective-permute-start | bytes 147464 | tf_op jit(solution)/shard_map/ppermute | solution.py:573
  3.0 23.9 %copy-start.1 = (s32[3,4096]{1,0:T(4,128)S(1)}, s32[3,4096]{1,0:T(4,128)}, u32[]{:S(2)}) copy-start(s32[3,4096]{1,0:T(4,128)} %cell_ref.1) | copy-start | bytes 147460
  22.8 2.5 %collective-permute-start.1 = (bf16[256,512]{1,0:T(8,128)(2,1)}, bf16[256,512]{1,0:T(8,128)(2,1)S(1)}, u32[]{:S(2)}, u32[]{:S(2)}) collective-permute-start(bf16[256,512]{1,0:T(8,128)(2,1)} %solve.1.refs_0_), channel_id=1, source_target_pairs={{0,1},{1,0},{2,3},{3,2},{4,5},{5,4},{6,7},{7,6},{8,9},{9,8},{10,11... | collective-permute-start | bytes 786440 | tf_op jit(solution)/shard_map/ppermute | solution.py:573
  22.9 1.0 %copy-start = (bf16[256,512]{1,0:T(8,128)(2,1)S(1)}, bf16[256,512]{1,0:T(8,128)(2,1)}, u32[]{:S(2)}) copy-start(bf16[256,512]{1,0:T(8,128)(2,1)} %solve.1.refs_0_) | copy-start | bytes 786436
  26.8 4.0 %collective-permute-start.2 = (bf16[4,4096]{1,0:T(4,128)(2,1)S(1)}, bf16[4,4096]{1,0:T(4,128)(2,1)S(1)}, u32[]{:S(2)}, u32[]{:S(2)}) collective-permute-start(bf16[4,4096]{1,0:T(4,128)(2,1)S(1)} %pick.4), channel_id=1, source_target_pairs={{0,2},{1,3},{2,0},{3,1},{4,6},{5,7},{6,4},{7,5},{8,10},{9,11},{10,... | collective-permute-start | bytes 98312 | tf_op jit(solution)/shard_map/ppermute | solution.py:573

commit v16 on v15

--- a/solution.py
+++ b/solution.py
@@ -85,12 +85,14 @@
             ("base_xt2", 2 * GRID),
             ("station_y2", 4 * grid_y),
             ("spread", 3 * LANES),
-            ("table", 5 * DEPTHS // 2 * GRID),
+            ("widen", LANES * max(1, LANES // grid_y // 2)),
+            ("compact", 5 * DEPTHS * grid_y // LANES // 2 * GRID),
             ("field_y2", 2 * LANES),
             ("field_yt", 2 * LANES),
             ("back", 5 * LANES),
             ("same", LANES),
             ("regroup", boots * LANES * max(1, boots // 2)),
+            ("table", 5 * DEPTHS // 2 * GRID),
         ]
     )
 
@@ -103,8 +105,15 @@
     for values, (odd_x, odd_y) in zip(offset_table(grid_y), PARITY):
         t = spectrum(values, odd_x, GRID)
         t = np.moveaxis(spectrum(np.moveaxis(t, 1, 0), odd_y, grid_y), 0, 1)
-        table.append(np.tile(np.moveaxis(t, 2, 0), (1, 1, copies)))
-    table = np.stack(table).reshape(5, DEPTHS // 2, 2, GRID, LANES).transpose(0, 1, 3, 2, 4)
+        table.append(np.moveaxis(t, 2, 0))
+    table = np.stack(table)
+    compact = table.reshape(-1, copies, GRID, grid_y).transpose(0, 2, 1, 3).reshape(-1, 2, GRID, LANES)
+    compact = compact.transpose(0, 2, 1, 3).reshape(-1, 2 * LANES)
+    widen = np.einsum("de,yz,c->dyecz", np.eye(copies), np.eye(grid_y), np.ones(copies)).reshape(LANES, -1)
+    if copies > 1:
+        widen = np.concatenate(np.split(widen, copies // 2, axis=1), axis=0)
+    table = np.tile(table, (1, 1, 1, copies))
+    table = table.reshape(5, DEPTHS // 2, 2, GRID, LANES).transpose(0, 1, 3, 2, 4)
 
     base_x = basis(GRID)
     base_y = basis(grid_y).reshape(grid_y, 2, grid_y)
@@ -137,6 +146,8 @@
         back=back,
         same=same,
         regroup=regroup,
+        widen=widen,
+        compact=compact,
         table=table.reshape(-1, 2 * LANES),
     )
     where = layout(grid_y, boots)
@@ -189,10 +200,10 @@
     deep = LANES // grid_y // boots
     slabs = DEPTHS // deep
     where = layout(grid_y, boots)
-    table_row, table_rows = where.at["table"]
+    table_row = where.at["table"][0]
     wide = 2 * boots * grid_y
     chunks = range(wide // LANES)
-    bounds = [0, table_row, table_row + table_rows, where.rows]
+    bounds = [0, where.at["field_y2"][0], table_row, where.rows]
     copies = [
         pltpu.make_async_copy(source.at[a:b], const.at[a:b], copied.at[i])
         for i, (a, b) in enumerate(zip(bounds[:-1], bounds[1:]))
@@ -398,6 +409,8 @@
             sums[:] = [norm, bend, cross]
 
         back_project(receive)
+        if first:
+            once(copies[2].wait)
         here = predict()
         weighted = weights[...] * here
         norm, bend, cross = sums
@@ -433,13 +446,30 @@
 
     @once
     def _():
+        per = LANES // grid_y
+        widen = held("widen")
+        if per > 1:
+            widen = jnp.concatenate([widen[i * LANES : (i + 1) * LANES] for i in range(per // 2)], axis=1)
+        else:
+            widen = widen[:, :LANES]
+        compact = held("compact")
+        blocks = 5 * DEPTHS // per
+        compact = jnp.concatenate(
+            [compact[i // 2 * GRID : (i // 2 + 1) * GRID, i % 2 * LANES : (i % 2 + 1) * LANES] for i in range(blocks)],
+            axis=0,
+        )
+        widened = dot(compact, widen)
+        for i in range(blocks):
+            for z in range(per):
+                table_wide[i * per // DEPTHS, i * per % DEPTHS + z] = widened[
+                    i * GRID : (i + 1) * GRID, z * LANES : (z + 1) * LANES
+                ]
+
+    station_spectra()
+
+    @once
+    def _():
         copies[1].wait()
-        copies[2].wait()
-        for c in range(5):
-            for z in range(DEPTHS):
-                table_wide[c, z] = table(c, z, slice(0, GRID)).astype(F32)
-
-    station_spectra()
 
     carry = (None, None, None)
     for outer in range(IRLS):

time: 31.8 us -> 32.2 us (1.013)
  Pallas kernels: 25.3 us -> 25.7 us
    pallas_call x1, Pallas kernels: 19.8 us -> 20.2 us  [solve(): pl.pallas_call(functools.partial(solve_kernel, grid_y, boots, mine // boo...]
  transfers between devices with their start and end apart: 3 -> 3, of which waited for: 1 -> 1; matrix products, arithmetic and copies ran while one was open for 0% -> 0% of each run, Pallas kernels for 75% -> 76%
where the time goes in v16:
time: 32.2 us; the launch traced here: 32 us
  Pallas kernels  25.7 us (80%)
  starting transfers between devices  3.11 us (10%)
  waiting for transfers between devices  1.31 us (4%)
  local copies, waits for them, and re-layouts  0.95 us (3%)
  other arithmetic  0.83 us (3%)
    pallas_call x1, Pallas kernels, solve(): pl.pallas_call(functools.partial(solve_kernel, grid_y, boots, mine // boo...  20.2 us
    pallas_call x3, Pallas kernels, pick(): pl.pallas_call(functools.partial(pick_kernel, grid_y, len(models), len(be...  5.54 us
    ppermute x3, starting transfers between devices, swap(): return lax.ppermute(a, 'wide', [(i, i ^ k) for i in range(wide)])  3.11 us
    ppermute x3, waiting for transfers between devices, swap(): return lax.ppermute(a, 'wide', [(i, i ^ k) for i in range(wide)])  1.31 us
    unnamed x4, local copies, waits for them, and re-layouts  0.95 us
    concatenate x1, other arithmetic, local(): return jnp.concatenate(blocks, axis=0)  0.73 us
  transfers between devices with their start and end apart: 3, of which 1 were waited for; matrix products, arithmetic and copies ran while one was open for 0% of the time, Pallas kernels for 76%

profile of v16, /device:TPU:0, one launch (start us, length us, event | category | flops | bytes accessed | tf_op | source)
XLA Modules:
  0.0 32.0 jit_solution(17902511689676483391)
XLA Ops:
  0.0 3.0 %collective-permute-start = (s32[3,4096]{1,0:T(4,128)}, s32[3,4096]{1,0:T(4,128)S(1)}, u32[]{:S(2)}, u32[]{:S(2)}) collective-permute-start(s32[3,4096]{1,0:T(4,128)} %cell_ref.1), channel_id=1, source_target_pairs={{0,2},{1,3},{2,0},{3,1},{4,6},{5,7},{6,4},{7,5},{8,10},{9,11},{10,... | collective-permute-start | bytes 147464 | tf_op jit(solution)/shard_map/ppermute | solution.py:603
  3.0 0.0 copy-start.1
  3.0 20.2 %solve.1.refs_0_ = bf16[256,512]{1,0:T(8,128)(2,1)} custom-call(s32[1]{0:T(128)} %bitcast.slot_ref, f32[5]{0:T(128)} %comp_ref.1, s32[2,512]{1,0:T(2,128)} %station_ref.1, f32[5,512]{1,0:T(8,128)} %observed_ref.1, s32[8,512]{1,0:T(8,128)} %counts_ref.1, bf16[16384,256]{1,0:T(8,128)(2,1)} %constant.12.clone.source), custom_call_target="tpu_custom_call" | custom-call | flops 10000000000 | bytes 10000000 | tf_op jit(solution)/shard_map/solve/pallas_call | solution.py:503
  23.1 0.0 collective-permute-done.cell_ref
  23.1 0.1 collective-permute-start.1
  23.2 0.0 copy-start
  23.2 0.9 %copy-done = bf16[256,512]{1,0:T(8,128)(2,1)S(1)} copy-done((bf16[256,512]{1,0:T(8,128)(2,1)S(1)}, bf16[256,512]{1,0:T(8,128)(2,1)}, u32[]{:S(2)}) %copy-start) | copy-done | bytes 262168
  24.2 1.5 %pick.3 = (bf16[2,4096]{1,0:T(2,128)(2,1)S(1)}, bf16[256,512]{1,0:T(8,128)(2,1)S(1)}) custom-call(s32[3,4096]{1,0:T(4,128)S(1)} %collective-permute-done.cell_ref, bf16[256,512]{1,0:T(8,128)(2,1)S(1)} %copy-done), custom_call_target="tpu_custom_call" | custom-call | flops 1073741824 | bytes 1000000 | tf_op jit(solution)/shard_map/pick/pallas_call | solution.py:580
  25.7 0.0 collective-permute-done.1.refs_0_.refs_1_
  25.7 1.5 %pick.4 = bf16[4,4096]{1,0:T(4,128)(2,1)S(1)} custom-call(s32[3,4096]{1,0:T(4,128)S(1)} %collective-permute-done.cell_ref, bf16[256,512]{1,0:T(8,128)(2,1)S(1)} %collective-permute-done.1.refs_0_.refs_1_, bf16[2,4096]{1,0:T(2,128)(2,1)S(1)} %get-tuple-element.11.refs_1_), custom_call_target="tpu_custom_call" | custom-call | flops 1073741824 | bytes 1000000 | tf_op jit(solution)/shard_map/pick/pallas_call | solution.py:580
  27.2 0.1 collective-permute-start.2
  27.3 0.0 copy-done.1
  27.3 2.6 %pick.5 = bf16[4,4096]{1,0:T(4,128)(2,1)S(1)} custom-call(s32[3,4096]{1,0:T(4,128)S(1)} %copy-done.1, bf16[256,512]{1,0:T(8,128)(2,1)S(1)} %get-tuple-element.12.refs_0_, bf16[256,512]{1,0:T(8,128)(2,1)S(1)} %collective-permute-done.1.refs_0_.refs_1_), custom_call_target="tpu_custom_call" | custom-call | flops 2147483648 | bytes 1000000 | tf_op jit(solution)/shard_map/pick/pallas_call | solution.py:580
  29.8 1.3 %collective-permute-done.2 = bf16[4,4096]{1,0:T(4,128)(2,1)S(1)} collective-permute-done((bf16[4,4096]{1,0:T(4,128)(2,1)S(1)}, bf16[4,4096]{1,0:T(4,128)(2,1)S(1)}, u32[]{:S(2)}, u32[]{:S(2)}) %collective-permute-start.2) | collective-permute-done | bytes 32800 | tf_op jit(solution)/shard_map/ppermute | solution.py:603
  31.2 0.1 broadcast_select_fusion.11
  31.3 0.7 %maximum_convert_fusion = f32[8,4096]{1,0:T(8,128)} fusion(bf16[2,4096]{1,0:T(2,128)(2,1)S(1)} %get-tuple-element.16, bf16[2,4096]{1,0:T(2,128)(2,1)S(1)} %get-tuple-element.15, bf16[2,4096]{1,0:T(2,128)(2,1)S(1)} %get-tuple-element.14, bf16[2,4096]{1,0:T(2,128)(2,1)S(1)} %get-tuple-element.13), kind=kLoop, calls=%fused_computation | loop fusion | flops 262144 | bytes 196608 | tf_op jit(solution)/shard_map/concatenate | solution.py:627
Async XLA Ops:
  0.0 23.1 %collective-permute-start = (s32[3,4096]{1,0:T(4,128)}, s32[3,4096]{1,0:T(4,128)S(1)}, u32[]{:S(2)}, u32[]{:S(2)}) collective-permute-start(s32[3,4096]{1,0:T(4,128)} %cell_ref.1), channel_id=1, source_target_pairs={{0,2},{1,3},{2,0},{3,1},{4,6},{5,7},{6,4},{7,5},{8,10},{9,11},{10,... | collective-permute-start | bytes 147464 | tf_op jit(solution)/shard_map/ppermute | solution.py:603
  3.0 24.3 %copy-start.1 = (s32[3,4096]{1,0:T(4,128)S(1)}, s32[3,4096]{1,0:T(4,128)}, u32[]{:S(2)}) copy-start(s32[3,4096]{1,0:T(4,128)} %cell_ref.1) | copy-start | bytes 147460
  23.1 2.5 %collective-permute-start.1 = (bf16[256,512]{1,0:T(8,128)(2,1)}, bf16[256,512]{1,0:T(8,128)(2,1)S(1)}, u32[]{:S(2)}, u32[]{:S(2)}) collective-permute-start(bf16[256,512]{1,0:T(8,128)(2,1)} %solve.1.refs_0_), channel_id=1, source_target_pairs={{0,1},{1,0},{2,3},{3,2},{4,5},{5,4},{6,7},{7,6},{8,9},{9,8},{10,11... | collective-permute-start | bytes 786440 | tf_op jit(solution)/shard_map/ppermute | solution.py:603
  23.2 1.0 %copy-start = (bf16[256,512]{1,0:T(8,128)(2,1)S(1)}, bf16[256,512]{1,0:T(8,128)(2,1)}, u32[]{:S(2)}) copy-start(bf16[256,512]{1,0:T(8,128)(2,1)} %solve.1.refs_0_) | copy-start | bytes 786436
  27.2 4.0 %collective-permute-start.2 = (bf16[4,4096]{1,0:T(4,128)(2,1)S(1)}, bf16[4,4096]{1,0:T(4,128)(2,1)S(1)}, u32[]{:S(2)}, u32[]{:S(2)}) collective-permute-start(bf16[4,4096]{1,0:T(4,128)(2,1)S(1)} %pick.4), channel_id=1, source_target_pairs={{0,2},{1,3},{2,0},{3,1},{4,6},{5,7},{6,4},{7,5},{8,10},{9,11},{10,... | collective-permute-start | bytes 98312 | tf_op jit(solution)/shard_map/ppermute | solution.py:603

commit v17 on v15

--- a/solution.py
+++ b/solution.py
@@ -431,6 +431,8 @@
                 models[slab, at] = step * d if first else models[slab, at] + step * d
         return norm, step, curve
 
+    station_spectra()
+
     @once
     def _():
         copies[1].wait()
@@ -438,8 +440,6 @@
         for c in range(5):
             for z in range(DEPTHS):
                 table_wide[c, z] = table(c, z, slice(0, GRID)).astype(F32)
-
-    station_spectra()
 
     carry = (None, None, None)
     for outer in range(IRLS):

time: 31.8 us -> 31.3 us (0.984)
  Pallas kernels: 25.3 us -> 24.8 us
    pallas_call x1, Pallas kernels: 19.8 us -> 19.2 us  [solve(): pl.pallas_call(functools.partial(solve_kernel, grid_y, boots, mine // boo...]
where the time goes in v17:
time: 31.3 us; the launch traced here: 31.1 us
  Pallas kernels  24.8 us (79%)
  starting transfers between devices  3.11 us (10%)
  waiting for transfers between devices  1.31 us (4%)
  local copies, waits for them, and re-layouts  0.95 us (3%)
  other arithmetic  0.83 us (3%)
    pallas_call x1, Pallas kernels, solve(): pl.pallas_call(functools.partial(solve_kernel, grid_y, boots, mine // boo...  19.2 us
    pallas_call x3, Pallas kernels, pick(): pl.pallas_call(functools.partial(pick_kernel, grid_y, len(models), len(be...  5.54 us
    ppermute x3, starting transfers between devices, swap(): return lax.ppermute(a, 'wide', [(i, i ^ k) for i in range(wide)])  3.11 us
    ppermute x3, waiting for transfers between devices, swap(): return lax.ppermute(a, 'wide', [(i, i ^ k) for i in range(wide)])  1.31 us
    unnamed x4, local copies, waits for them, and re-layouts  0.95 us
    concatenate x1, other arithmetic, local(): return jnp.concatenate(blocks, axis=0)  0.73 us
  transfers between devices with their start and end apart: 3, of which 1 were waited for; matrix products, arithmetic and copies ran while one was open for 0% of the time, Pallas kernels for 75%

profile of v17, /device:TPU:0, one launch (start us, length us, event | category | flops | bytes accessed | tf_op | source)
XLA Modules:
  0.0 31.1 jit_solution(7110075071779750100)
XLA Ops:
  0.0 3.0 %collective-permute-start = (s32[3,4096]{1,0:T(4,128)}, s32[3,4096]{1,0:T(4,128)S(1)}, u32[]{:S(2)}, u32[]{:S(2)}) collective-permute-start(s32[3,4096]{1,0:T(4,128)} %cell_ref.1), channel_id=1, source_target_pairs={{0,2},{1,3},{2,0},{3,1},{4,6},{5,7},{6,4},{7,5},{8,10},{9,11},{10,... | collective-permute-start | bytes 147464 | tf_op jit(solution)/shard_map/ppermute | solution.py:573
  3.0 0.0 copy-start.1
  3.0 19.2 %solve.1.refs_0_ = bf16[256,512]{1,0:T(8,128)(2,1)} custom-call(s32[1]{0:T(128)} %bitcast.slot_ref, f32[5]{0:T(128)} %comp_ref.1, s32[2,512]{1,0:T(2,128)} %station_ref.1, f32[5,512]{1,0:T(8,128)} %observed_ref.1, s32[8,512]{1,0:T(8,128)} %counts_ref.1, bf16[16384,256]{1,0:T(8,128)(2,1)} %constant.12.clone.source), custom_call_target="tpu_custom_call" | custom-call | flops 10000000000 | bytes 10000000 | tf_op jit(solution)/shard_map/solve/pallas_call | solution.py:473
  22.2 0.0 collective-permute-done.cell_ref
  22.2 0.1 collective-permute-start.1
  22.3 0.0 copy-start
  22.3 0.9 %copy-done = bf16[256,512]{1,0:T(8,128)(2,1)S(1)} copy-done((bf16[256,512]{1,0:T(8,128)(2,1)S(1)}, bf16[256,512]{1,0:T(8,128)(2,1)}, u32[]{:S(2)}) %copy-start) | copy-done | bytes 262168
  23.3 1.5 %pick.3 = (bf16[2,4096]{1,0:T(2,128)(2,1)S(1)}, bf16[256,512]{1,0:T(8,128)(2,1)S(1)}) custom-call(s32[3,4096]{1,0:T(4,128)S(1)} %collective-permute-done.cell_ref, bf16[256,512]{1,0:T(8,128)(2,1)S(1)} %copy-done), custom_call_target="tpu_custom_call" | custom-call | flops 1073741824 | bytes 1000000 | tf_op jit(solution)/shard_map/pick/pallas_call | solution.py:550
  24.8 0.0 collective-permute-done.1.refs_0_.refs_1_
  24.8 1.5 %pick.4 = bf16[4,4096]{1,0:T(4,128)(2,1)S(1)} custom-call(s32[3,4096]{1,0:T(4,128)S(1)} %collective-permute-done.cell_ref, bf16[256,512]{1,0:T(8,128)(2,1)S(1)} %collective-permute-done.1.refs_0_.refs_1_, bf16[2,4096]{1,0:T(2,128)(2,1)S(1)} %get-tuple-element.11.refs_1_), custom_call_target="tpu_custom_call" | custom-call | flops 1073741824 | bytes 1000000 | tf_op jit(solution)/shard_map/pick/pallas_call | solution.py:550
  26.3 0.1 collective-permute-start.2
  26.3 0.0 copy-done.1
  26.4 2.6 %pick.5 = bf16[4,4096]{1,0:T(4,128)(2,1)S(1)} custom-call(s32[3,4096]{1,0:T(4,128)S(1)} %copy-done.1, bf16[256,512]{1,0:T(8,128)(2,1)S(1)} %get-tuple-element.12.refs_0_, bf16[256,512]{1,0:T(8,128)(2,1)S(1)} %collective-permute-done.1.refs_0_.refs_1_), custom_call_target="tpu_custom_call" | custom-call | flops 2147483648 | bytes 1000000 | tf_op jit(solution)/shard_map/pick/pallas_call | solution.py:550
  28.9 1.3 %collective-permute-done.2 = bf16[4,4096]{1,0:T(4,128)(2,1)S(1)} collective-permute-done((bf16[4,4096]{1,0:T(4,128)(2,1)S(1)}, bf16[4,4096]{1,0:T(4,128)(2,1)S(1)}, u32[]{:S(2)}, u32[]{:S(2)}) %collective-permute-start.2) | collective-permute-done | bytes 32800 | tf_op jit(solution)/shard_map/ppermute | solution.py:573
  30.2 0.1 broadcast_select_fusion.11
  30.3 0.7 %maximum_convert_fusion = f32[8,4096]{1,0:T(8,128)} fusion(bf16[2,4096]{1,0:T(2,128)(2,1)S(1)} %get-tuple-element.16, bf16[2,4096]{1,0:T(2,128)(2,1)S(1)} %get-tuple-element.15, bf16[2,4096]{1,0:T(2,128)(2,1)S(1)} %get-tuple-element.14, bf16[2,4096]{1,0:T(2,128)(2,1)S(1)} %get-tuple-element.13), kind=kLoop, calls=%fused_computation | loop fusion | flops 262144 | bytes 196608 | tf_op jit(solution)/shard_map/concatenate | solution.py:597
Async XLA Ops:
  0.0 22.2 %collective-permute-start = (s32[3,4096]{1,0:T(4,128)}, s32[3,4096]{1,0:T(4,128)S(1)}, u32[]{:S(2)}, u32[]{:S(2)}) collective-permute-start(s32[3,4096]{1,0:T(4,128)} %cell_ref.1), channel_id=1, source_target_pairs={{0,2},{1,3},{2,0},{3,1},{4,6},{5,7},{6,4},{7,5},{8,10},{9,11},{10,... | collective-permute-start | bytes 147464 | tf_op jit(solution)/shard_map/ppermute | solution.py:573
  3.0 23.4 %copy-start.1 = (s32[3,4096]{1,0:T(4,128)S(1)}, s32[3,4096]{1,0:T(4,128)}, u32[]{:S(2)}) copy-start(s32[3,4096]{1,0:T(4,128)} %cell_ref.1) | copy-start | bytes 147460
  22.2 2.5 %collective-permute-start.1 = (bf16[256,512]{1,0:T(8,128)(2,1)}, bf16[256,512]{1,0:T(8,128)(2,1)S(1)}, u32[]{:S(2)}, u32[]{:S(2)}) collective-permute-start(bf16[256,512]{1,0:T(8,128)(2,1)} %solve.1.refs_0_), channel_id=1, source_target_pairs={{0,1},{1,0},{2,3},{3,2},{4,5},{5,4},{6,7},{7,6},{8,9},{9,8},{10,11... | collective-permute-start | bytes 786440 | tf_op jit(solution)/shard_map/ppermute | solution.py:573
  22.3 1.0 %copy-start = (bf16[256,512]{1,0:T(8,128)(2,1)S(1)}, bf16[256,512]{1,0:T(8,128)(2,1)}, u32[]{:S(2)}) copy-start(bf16[256,512]{1,0:T(8,128)(2,1)} %solve.1.refs_0_) | copy-start | bytes 786436
  26.3 4.0 %collective-permute-start.2 = (bf16[4,4096]{1,0:T(4,128)(2,1)S(1)}, bf16[4,4096]{1,0:T(4,128)(2,1)S(1)}, u32[]{:S(2)}, u32[]{:S(2)}) collective-permute-start(bf16[4,4096]{1,0:T(4,128)(2,1)S(1)} %pick.4), channel_id=1, source_target_pairs={{0,2},{1,3},{2,0},{3,1},{4,6},{5,7},{6,4},{7,5},{8,10},{9,11},{10,... | collective-permute-start | bytes 98312 | tf_op jit(solution)/shard_map/ppermute | solution.py:573

commit v18 on v17

--- a/solution.py
+++ b/solution.py
@@ -150,6 +150,11 @@
 
 def dot(a, b):
     return jnp.dot(a, b, preferred_element_type=F32)
+
+
+def dot_in_halves(a, b):
+    half = a.shape[0] // 2
+    return jnp.concatenate([dot(a[:half], b), dot(a[half:], b)], axis=0)
 
 
 def solve_kernel(
@@ -298,12 +303,12 @@
             lane = share.start * 2 * LANES
             along_x = dot(held("base_x"), spec_g[:, lane : lane + share_lanes]).astype(BF)
             along_x = [along_x[:, lane : lane + 2 * LANES] for lane in range(0, share_lanes, 2 * LANES)]
-            receive(share, dot(jnp.concatenate(along_x, axis=0), held("field_yt", LANES)))
+            receive(share, dot_in_halves(jnp.concatenate(along_x, axis=0), held("field_yt", LANES)))
 
     def predict():
         for share in shares:
             r = residual[share.start : share.stop].reshape(len(share) * GRID, LANES).astype(BF)
-            y = dot(jnp.concatenate([r, r], axis=1), held("field_y2")).astype(BF)
+            y = dot_in_halves(jnp.concatenate([r, r], axis=1), held("field_y2")).astype(BF)
             y = jnp.concatenate([y[i * GRID : (i + 1) * GRID] for i in range(len(share))], axis=1)
             lane = share.start * 2 * LANES
             spec_f[:, lane : lane + share_lanes] = dot(held("base_xt2"), jnp.concatenate([y, y], axis=0)).astype(BF)
@@ -340,7 +345,7 @@
                     term = picked[at, lane : lane + LANES] * trig(at, odd_y, chunk)
                     part = term if part is None else part + term
                 picked_in[at, c * LANES : (c + 1) * LANES] = part.astype(BF)
-        return dot(picked_in[...], held("back", LANES))
+        return dot_in_halves(picked_in[...], held("back", LANES))
 
     def fold(a):
         return jnp.sum(a.reshape(a.shape[0] // 8, 8, LANES), axis=0)

time: 31.3 us -> 31.8 us (1.016)
  Pallas kernels: 24.8 us -> 25.3 us
    pallas_call x1, Pallas kernels: 19.2 us -> 19.8 us  [solve(): pl.pallas_call(functools.partial(solve_kernel, grid_y, boots, mine // boo...]
where the time goes in v18:
time: 31.8 us; the launch traced here: 31.6 us
  Pallas kernels  25.3 us (80%)
  starting transfers between devices  3.11 us (10%)
  waiting for transfers between devices  1.31 us (4%)
  local copies, waits for them, and re-layouts  0.95 us (3%)
  other arithmetic  0.83 us (3%)
    pallas_call x1, Pallas kernels, solve(): pl.pallas_call(functools.partial(solve_kernel, grid_y, boots, mine // boo...  19.8 us
    pallas_call x3, Pallas kernels, pick(): pl.pallas_call(functools.partial(pick_kernel, grid_y, len(models), len(be...  5.54 us
    ppermute x3, starting transfers between devices, swap(): return lax.ppermute(a, 'wide', [(i, i ^ k) for i in range(wide)])  3.11 us
    ppermute x3, waiting for transfers between devices, swap(): return lax.ppermute(a, 'wide', [(i, i ^ k) for i in range(wide)])  1.31 us
    unnamed x4, local copies, waits for them, and re-layouts  0.95 us
    concatenate x1, other arithmetic, local(): return jnp.concatenate(blocks, axis=0)  0.73 us
  transfers between devices with their start and end apart: 3, of which 1 were waited for; matrix products, arithmetic and copies ran while one was open for 0% of the time, Pallas kernels for 75%

profile of v18, /device:TPU:0, one launch (start us, length us, event | category | flops | bytes accessed | tf_op | source)
XLA Modules:
  0.0 31.6 jit_solution(15858426293768015844)
XLA Ops:
  0.0 3.0 %collective-permute-start = (s32[3,4096]{1,0:T(4,128)}, s32[3,4096]{1,0:T(4,128)S(1)}, u32[]{:S(2)}, u32[]{:S(2)}) collective-permute-start(s32[3,4096]{1,0:T(4,128)} %cell_ref.1), channel_id=1, source_target_pairs={{0,2},{1,3},{2,0},{3,1},{4,6},{5,7},{6,4},{7,5},{8,10},{9,11},{10,... | collective-permute-start | bytes 147464 | tf_op jit(solution)/shard_map/ppermute | solution.py:578
  3.0 0.0 copy-start.1
  3.0 19.8 %solve.1.refs_0_ = bf16[256,512]{1,0:T(8,128)(2,1)} custom-call(s32[1]{0:T(128)} %bitcast.slot_ref, f32[5]{0:T(128)} %comp_ref.1, s32[2,512]{1,0:T(2,128)} %station_ref.1, f32[5,512]{1,0:T(8,128)} %observed_ref.1, s32[8,512]{1,0:T(8,128)} %counts_ref.1, bf16[16384,256]{1,0:T(8,128)(2,1)} %constant.12.clone.source), custom_call_target="tpu_custom_call" | custom-call | flops 10000000000 | bytes 10000000 | tf_op jit(solution)/shard_map/solve/pallas_call | solution.py:478
  22.7 0.0 collective-permute-done.cell_ref
  22.8 0.1 collective-permute-start.1
  22.8 0.0 copy-start
  22.9 0.9 %copy-done = bf16[256,512]{1,0:T(8,128)(2,1)S(1)} copy-done((bf16[256,512]{1,0:T(8,128)(2,1)S(1)}, bf16[256,512]{1,0:T(8,128)(2,1)}, u32[]{:S(2)}) %copy-start) | copy-done | bytes 262168
  23.8 1.5 %pick.3 = (bf16[2,4096]{1,0:T(2,128)(2,1)S(1)}, bf16[256,512]{1,0:T(8,128)(2,1)S(1)}) custom-call(s32[3,4096]{1,0:T(4,128)S(1)} %collective-permute-done.cell_ref, bf16[256,512]{1,0:T(8,128)(2,1)S(1)} %copy-done), custom_call_target="tpu_custom_call" | custom-call | flops 1073741824 | bytes 1000000 | tf_op jit(solution)/shard_map/pick/pallas_call | solution.py:555
  25.3 0.0 collective-permute-done.1.refs_0_.refs_1_
  25.3 1.5 %pick.4 = bf16[4,4096]{1,0:T(4,128)(2,1)S(1)} custom-call(s32[3,4096]{1,0:T(4,128)S(1)} %collective-permute-done.cell_ref, bf16[256,512]{1,0:T(8,128)(2,1)S(1)} %collective-permute-done.1.refs_0_.refs_1_, bf16[2,4096]{1,0:T(2,128)(2,1)S(1)} %get-tuple-element.11.refs_1_), custom_call_target="tpu_custom_call" | custom-call | flops 1073741824 | bytes 1000000 | tf_op jit(solution)/shard_map/pick/pallas_call | solution.py:555
  26.8 0.1 collective-permute-start.2
  26.9 0.0 copy-done.1
  26.9 2.6 %pick.5 = bf16[4,4096]{1,0:T(4,128)(2,1)S(1)} custom-call(s32[3,4096]{1,0:T(4,128)S(1)} %copy-done.1, bf16[256,512]{1,0:T(8,128)(2,1)S(1)} %get-tuple-element.12.refs_0_, bf16[256,512]{1,0:T(8,128)(2,1)S(1)} %collective-permute-done.1.refs_0_.refs_1_), custom_call_target="tpu_custom_call" | custom-call | flops 2147483648 | bytes 1000000 | tf_op jit(solution)/shard_map/pick/pallas_call | solution.py:555
  29.5 1.3 %collective-permute-done.2 = bf16[4,4096]{1,0:T(4,128)(2,1)S(1)} collective-permute-done((bf16[4,4096]{1,0:T(4,128)(2,1)S(1)}, bf16[4,4096]{1,0:T(4,128)(2,1)S(1)}, u32[]{:S(2)}, u32[]{:S(2)}) %collective-permute-start.2) | collective-permute-done | bytes 32800 | tf_op jit(solution)/shard_map/ppermute | solution.py:578
  30.8 0.1 broadcast_select_fusion.11
  30.9 0.7 %maximum_convert_fusion = f32[8,4096]{1,0:T(8,128)} fusion(bf16[2,4096]{1,0:T(2,128)(2,1)S(1)} %get-tuple-element.16, bf16[2,4096]{1,0:T(2,128)(2,1)S(1)} %get-tuple-element.15, bf16[2,4096]{1,0:T(2,128)(2,1)S(1)} %get-tuple-element.14, bf16[2,4096]{1,0:T(2,128)(2,1)S(1)} %get-tuple-element.13), kind=kLoop, calls=%fused_computation | loop fusion | flops 262144 | bytes 196608 | tf_op jit(solution)/shard_map/concatenate | solution.py:602
Async XLA Ops:
  0.0 22.7 %collective-permute-start = (s32[3,4096]{1,0:T(4,128)}, s32[3,4096]{1,0:T(4,128)S(1)}, u32[]{:S(2)}, u32[]{:S(2)}) collective-permute-start(s32[3,4096]{1,0:T(4,128)} %cell_ref.1), channel_id=1, source_target_pairs={{0,2},{1,3},{2,0},{3,1},{4,6},{5,7},{6,4},{7,5},{8,10},{9,11},{10,... | collective-permute-start | bytes 147464 | tf_op jit(solution)/shard_map/ppermute | solution.py:578
  3.0 23.9 %copy-start.1 = (s32[3,4096]{1,0:T(4,128)S(1)}, s32[3,4096]{1,0:T(4,128)}, u32[]{:S(2)}) copy-start(s32[3,4096]{1,0:T(4,128)} %cell_ref.1) | copy-start | bytes 147460
  22.8 2.5 %collective-permute-start.1 = (bf16[256,512]{1,0:T(8,128)(2,1)}, bf16[256,512]{1,0:T(8,128)(2,1)S(1)}, u32[]{:S(2)}, u32[]{:S(2)}) collective-permute-start(bf16[256,512]{1,0:T(8,128)(2,1)} %solve.1.refs_0_), channel_id=1, source_target_pairs={{0,1},{1,0},{2,3},{3,2},{4,5},{5,4},{6,7},{7,6},{8,9},{9,8},{10,11... | collective-permute-start | bytes 786440 | tf_op jit(solution)/shard_map/ppermute | solution.py:578
  22.8 1.0 %copy-start = (bf16[256,512]{1,0:T(8,128)(2,1)S(1)}, bf16[256,512]{1,0:T(8,128)(2,1)}, u32[]{:S(2)}) copy-start(bf16[256,512]{1,0:T(8,128)(2,1)} %solve.1.refs_0_) | copy-start | bytes 786436
  26.8 4.0 %collective-permute-start.2 = (bf16[4,4096]{1,0:T(4,128)(2,1)S(1)}, bf16[4,4096]{1,0:T(4,128)(2,1)S(1)}, u32[]{:S(2)}, u32[]{:S(2)}) collective-permute-start(bf16[4,4096]{1,0:T(4,128)(2,1)S(1)} %pick.4), channel_id=1, source_target_pairs={{0,2},{1,3},{2,0},{3,1},{4,6},{5,7},{6,4},{7,5},{8,10},{9,11},{10,... | collective-permute-start | bytes 98312 | tf_op jit(solution)/shard_map/ppermute | solution.py:578

commit v19 on v17

--- a/solution.py
+++ b/solution.py
@@ -158,11 +158,14 @@
     steps,
     slot_ref,
     comp_ref,
+    station_source,
+    observed_source,
+    counts_source,
+    source,
+    out_ref,
     station_ref,
     observed_ref,
     counts_ref,
-    source,
-    out_ref,
     const,
     copied,
     pick_x,
@@ -198,6 +201,9 @@
         for i, (a, b) in enumerate(zip(bounds[:-1], bounds[1:]))
     ]
 
+    small = [(station_source, station_ref), (observed_source, observed_ref), (counts_source, counts_ref)]
+    small = [pltpu.make_async_copy(a, b, copied.at[len(copies) + i]) for i, (a, b) in enumerate(small)]
+
     def once(f):
         if steps == 1:
             f()
@@ -206,8 +212,10 @@
 
     @once
     def _():
-        for copy in copies:
+        for copy in small + copies:
             copy.start()
+        for copy in small:
+            copy.wait()
 
     def held(name, width=2 * LANES):
         row, count = where.at[name]
@@ -464,7 +472,6 @@
     stations = station_index.shape[1]
     const = jnp.asarray(constants(grid_y, boots))
     vmem = pltpu.VMEM
-    whole = lambda a: pl.BlockSpec(a.shape, lambda i, n=a.ndim: (0,) * n)
     smem = pl.BlockSpec(memory_space=pltpu.SMEM)
     field = vmem((slabs, GRID, LANES), F32)
     at_stations = vmem((stations, LANES), F32)
@@ -474,11 +481,12 @@
         functools.partial(solve_kernel, grid_y, boots, mine // boots),
         out_shape=jax.ShapeDtypeStruct((mine * GRID, DEPTHS * grid_y), BF),
         grid=(mine // boots,),
-        in_specs=[smem, smem] + [whole(a) for a in inputs] + [pl.BlockSpec(memory_space=pl.ANY)],
+        in_specs=[smem, smem] + [pl.BlockSpec(memory_space=pl.ANY)] * (len(inputs) + 1),
         out_specs=pl.BlockSpec((boots * GRID, DEPTHS * grid_y), lambda i: (i, 0)),
-        scratch_shapes=[
+        scratch_shapes=[vmem(a.shape, a.dtype) for a in inputs]
+        + [
             vmem((layout(grid_y, boots).rows, 2 * LANES), BF),
-            pltpu.SemaphoreType.DMA((3,)),
+            pltpu.SemaphoreType.DMA((6,)),
             vmem((stations, 2 * GRID), BF),
             vmem((2 * GRID, stations), BF),
             vmem((stations, 2 * wide), F32),

time: 31.3 us -> 31.3 us (level)
  no operation moved by 1% of the time
where the time goes in v19:
time: 31.3 us; the launch traced here: 31.1 us
  Pallas kernels  24.8 us (79%)
  starting transfers between devices  3.11 us (10%)
  waiting for transfers between devices  1.33 us (4%)
  local copies, waits for them, and re-layouts  0.95 us (3%)
  other arithmetic  0.83 us (3%)
    pallas_call x1, Pallas kernels, solve(): pl.pallas_call(functools.partial(solve_kernel, grid_y, boots, mine // boo...  19.3 us
    pallas_call x3, Pallas kernels, pick(): pl.pallas_call(functools.partial(pick_kernel, grid_y, len(models), len(be...  5.53 us
    ppermute x3, starting transfers between devices, swap(): return lax.ppermute(a, 'wide', [(i, i ^ k) for i in range(wide)])  3.11 us
    ppermute x3, waiting for transfers between devices, swap(): return lax.ppermute(a, 'wide', [(i, i ^ k) for i in range(wide)])  1.33 us
    unnamed x4, local copies, waits for them, and re-layouts  0.95 us
    concatenate x1, other arithmetic, local(): return jnp.concatenate(blocks, axis=0)  0.73 us
  transfers between devices with their start and end apart: 3, of which 1 were waited for; matrix products, arithmetic and copies ran while one was open for 0% of the time, Pallas kernels for 75%

profile of v19, /device:TPU:0, one launch (start us, length us, event | category | flops | bytes accessed | tf_op | source)
XLA Modules:
  0.0 31.1 jit_solution(17575942913434682625)
XLA Ops:
  0.0 3.0 %collective-permute-start = (s32[3,4096]{1,0:T(4,128)}, s32[3,4096]{1,0:T(4,128)S(1)}, u32[]{:S(2)}, u32[]{:S(2)}) collective-permute-start(s32[3,4096]{1,0:T(4,128)} %cell_ref.1), channel_id=1, source_target_pairs={{0,2},{1,3},{2,0},{3,1},{4,6},{5,7},{6,4},{7,5},{8,10},{9,11},{10,... | collective-permute-start | bytes 147464 | tf_op jit(solution)/shard_map/ppermute | solution.py:581
  3.0 0.0 copy-start.1
  3.0 19.3 %solve.1.refs_0_ = bf16[256,512]{1,0:T(8,128)(2,1)} custom-call(s32[1]{0:T(128)} %bitcast.slot_ref, f32[5]{0:T(128)} %comp_ref.1, s32[2,512]{1,0:T(2,128)} %station_source.1, f32[5,512]{1,0:T(8,128)} %observed_source.1, s32[8,512]{1,0:T(8,128)} %counts_source.1, bf16[16384,256]{1,0:T(8,128)(2,1)} %constant.12.clone.source), custom_call_target="tpu_custom_call" | custom-call | flops 10000000000 | bytes 10000000 | tf_op jit(solution)/shard_map/solve/pallas_call | solution.py:480
  22.3 0.0 collective-permute-done.cell_ref
  22.3 0.1 collective-permute-start.1
  22.4 0.0 copy-start
  22.4 0.9 %copy-done = bf16[256,512]{1,0:T(8,128)(2,1)S(1)} copy-done((bf16[256,512]{1,0:T(8,128)(2,1)S(1)}, bf16[256,512]{1,0:T(8,128)(2,1)}, u32[]{:S(2)}) %copy-start) | copy-done | bytes 262168
  23.3 1.5 %pick.3 = (bf16[2,4096]{1,0:T(2,128)(2,1)S(1)}, bf16[256,512]{1,0:T(8,128)(2,1)S(1)}) custom-call(s32[3,4096]{1,0:T(4,128)S(1)} %collective-permute-done.cell_ref, bf16[256,512]{1,0:T(8,128)(2,1)S(1)} %copy-done), custom_call_target="tpu_custom_call" | custom-call | flops 1073741824 | bytes 1000000 | tf_op jit(solution)/shard_map/pick/pallas_call | solution.py:558
  24.8 0.0 collective-permute-done.1.refs_0_.refs_1_
  24.8 1.5 %pick.4 = bf16[4,4096]{1,0:T(4,128)(2,1)S(1)} custom-call(s32[3,4096]{1,0:T(4,128)S(1)} %collective-permute-done.cell_ref, bf16[256,512]{1,0:T(8,128)(2,1)S(1)} %collective-permute-done.1.refs_0_.refs_1_, bf16[2,4096]{1,0:T(2,128)(2,1)S(1)} %get-tuple-element.11.refs_1_), custom_call_target="tpu_custom_call" | custom-call | flops 1073741824 | bytes 1000000 | tf_op jit(solution)/shard_map/pick/pallas_call | solution.py:558
  26.3 0.1 collective-permute-start.2
  26.4 0.0 copy-done.1
  26.4 2.6 %pick.5 = bf16[4,4096]{1,0:T(4,128)(2,1)S(1)} custom-call(s32[3,4096]{1,0:T(4,128)S(1)} %copy-done.1, bf16[256,512]{1,0:T(8,128)(2,1)S(1)} %get-tuple-element.12.refs_0_, bf16[256,512]{1,0:T(8,128)(2,1)S(1)} %collective-permute-done.1.refs_0_.refs_1_), custom_call_target="tpu_custom_call" | custom-call | flops 2147483648 | bytes 1000000 | tf_op jit(solution)/shard_map/pick/pallas_call | solution.py:558
  29.0 1.3 %collective-permute-done.2 = bf16[4,4096]{1,0:T(4,128)(2,1)S(1)} collective-permute-done((bf16[4,4096]{1,0:T(4,128)(2,1)S(1)}, bf16[4,4096]{1,0:T(4,128)(2,1)S(1)}, u32[]{:S(2)}, u32[]{:S(2)}) %collective-permute-start.2) | collective-permute-done | bytes 32800 | tf_op jit(solution)/shard_map/ppermute | solution.py:581
  30.3 0.1 broadcast_select_fusion.11
  30.4 0.7 %maximum_convert_fusion = f32[8,4096]{1,0:T(8,128)} fusion(bf16[2,4096]{1,0:T(2,128)(2,1)S(1)} %get-tuple-element.16, bf16[2,4096]{1,0:T(2,128)(2,1)S(1)} %get-tuple-element.15, bf16[2,4096]{1,0:T(2,128)(2,1)S(1)} %get-tuple-element.14, bf16[2,4096]{1,0:T(2,128)(2,1)S(1)} %get-tuple-element.13), kind=kLoop, calls=%fused_computation | loop fusion | flops 262144 | bytes 196608 | tf_op jit(solution)/shard_map/concatenate | solution.py:605
Async XLA Ops:
  0.0 22.3 %collective-permute-start = (s32[3,4096]{1,0:T(4,128)}, s32[3,4096]{1,0:T(4,128)S(1)}, u32[]{:S(2)}, u32[]{:S(2)}) collective-permute-start(s32[3,4096]{1,0:T(4,128)} %cell_ref.1), channel_id=1, source_target_pairs={{0,2},{1,3},{2,0},{3,1},{4,6},{5,7},{6,4},{7,5},{8,10},{9,11},{10,... | collective-permute-start | bytes 147464 | tf_op jit(solution)/shard_map/ppermute | solution.py:581
  3.0 23.4 %copy-start.1 = (s32[3,4096]{1,0:T(4,128)S(1)}, s32[3,4096]{1,0:T(4,128)}, u32[]{:S(2)}) copy-start(s32[3,4096]{1,0:T(4,128)} %cell_ref.1) | copy-start | bytes 147460
  22.3 2.5 %collective-permute-start.1 = (bf16[256,512]{1,0:T(8,128)(2,1)}, bf16[256,512]{1,0:T(8,128)(2,1)S(1)}, u32[]{:S(2)}, u32[]{:S(2)}) collective-permute-start(bf16[256,512]{1,0:T(8,128)(2,1)} %solve.1.refs_0_), channel_id=1, source_target_pairs={{0,1},{1,0},{2,3},{3,2},{4,5},{5,4},{6,7},{7,6},{8,9},{9,8},{10,11... | collective-permute-start | bytes 786440 | tf_op jit(solution)/shard_map/ppermute | solution.py:581
  22.4 1.0 %copy-start = (bf16[256,512]{1,0:T(8,128)(2,1)S(1)}, bf16[256,512]{1,0:T(8,128)(2,1)}, u32[]{:S(2)}) copy-start(bf16[256,512]{1,0:T(8,128)(2,1)} %solve.1.refs_0_) | copy-start | bytes 786436
  26.3 4.0 %collective-permute-start.2 = (bf16[4,4096]{1,0:T(4,128)(2,1)S(1)}, bf16[4,4096]{1,0:T(4,128)(2,1)S(1)}, u32[]{:S(2)}, u32[]{:S(2)}) collective-permute-start(bf16[4,4096]{1,0:T(4,128)(2,1)S(1)} %pick.4), channel_id=1, source_target_pairs={{0,2},{1,3},{2,0},{3,1},{4,6},{5,7},{6,4},{7,5},{8,10},{9,11},{10,... | collective-permute-start | bytes 98312 | tf_op jit(solution)/shard_map/ppermute | solution.py:581

commit v20 on v19

--- a/solution.py
+++ b/solution.py
@@ -16,7 +16,7 @@
 LANES = 128
 TEAM = 4
 PARTS = 2
-CHUNK = 2048
+CHUNK = 4096
 ROWS = 32
 
 station_height = 2.0
@@ -177,7 +177,6 @@
     image,
     values,
     rows,
-    table_wide,
     spread_out,
     spec_q,
     spec_i,
@@ -296,7 +295,7 @@
                 for chunk in chunks:
                     q = [[spec_q[c, hx, chunk, at, :] for hx in range(2)] for c in range(5)]
                     for z in range(share.start * deep, share.stop * deep):
-                        t = [table_wide[c, z, at, :] for c in range(5)]
+                        t = [table(c, z, at).astype(F32) for c in range(5)]
                         lane = z * wide + chunk * LANES
                         for hx in range(2):
                             total = t[0] * q[0][hx]
@@ -445,9 +444,6 @@
     def _():
         copies[1].wait()
         copies[2].wait()
-        for c in range(5):
-            for z in range(DEPTHS):
-                table_wide[c, z] = table(c, z, slice(0, GRID)).astype(F32)
 
     carry = (None, None, None)
     for outer in range(IRLS):
@@ -496,7 +492,6 @@
             at_stations,
             vmem((stations, LANES), BF),
             vmem((LANES, stations), F32),
-            vmem((5, DEPTHS, GRID, LANES), F32),
             vmem((stations, 5 * wide), BF),
             vmem((5, 2, wide // LANES, GRID, LANES), F32),
             vmem((2 * GRID, 5 * wide), BF),

time: 31.3 us -> 31.5 us (level)
    pallas_call x1, Pallas kernels: 19.3 us -> 19.9 us  [solve(): pl.pallas_call(functools.partial(solve_kernel, grid_y, boots, mine // boo...]
    pallas_call x3, Pallas kernels: 5.53 us -> 4.98 us  [pick(): pl.pallas_call(functools.partial(pick_kernel, grid_y, len(models), len(be...]
where the time goes in v20:
time: 31.5 us; the launch traced here: 31.3 us
  Pallas kernels  24.8 us (79%)
  starting transfers between devices  3.11 us (10%)
  waiting for transfers between devices  1.51 us (5%)
  local copies, waits for them, and re-layouts  0.95 us (3%)
  other arithmetic  0.83 us (3%)
    pallas_call x1, Pallas kernels, solve(): pl.pallas_call(functools.partial(solve_kernel, grid_y, boots, mine // boo...  19.9 us
    pallas_call x3, Pallas kernels, pick(): pl.pallas_call(functools.partial(pick_kernel, grid_y, len(models), len(be...  4.98 us
    ppermute x3, starting transfers between devices, swap(): return lax.ppermute(a, 'wide', [(i, i ^ k) for i in range(wide)])  3.11 us
    ppermute x3, waiting for transfers between devices, swap(): return lax.ppermute(a, 'wide', [(i, i ^ k) for i in range(wide)])  1.51 us
    unnamed x4, local copies, waits for them, and re-layouts  0.95 us
    concatenate x1, other arithmetic, local(): return jnp.concatenate(blocks, axis=0)  0.73 us
  transfers between devices with their start and end apart: 3, of which 1 were waited for; matrix products, arithmetic and copies ran while one was open for 0% of the time, Pallas kernels for 75%

profile of v20, /device:TPU:0, one launch (start us, length us, event | category | flops | bytes accessed | tf_op | source)
XLA Modules:
  0.0 31.3 jit_solution(4029674989005690108)
XLA Ops:
  0.0 3.0 %collective-permute-start = (s32[3,4096]{1,0:T(4,128)}, s32[3,4096]{1,0:T(4,128)S(1)}, u32[]{:S(2)}, u32[]{:S(2)}) collective-permute-start(s32[3,4096]{1,0:T(4,128)} %cell_ref.1), channel_id=1, source_target_pairs={{0,2},{1,3},{2,0},{3,1},{4,6},{5,7},{6,4},{7,5},{8,10},{9,11},{10,... | collective-permute-start | bytes 147464 | tf_op jit(solution)/shard_map/ppermute | solution.py:576
  3.0 0.0 copy-start.1
  3.0 19.9 %solve.1.refs_0_ = bf16[256,512]{1,0:T(8,128)(2,1)} custom-call(s32[1]{0:T(128)} %bitcast.slot_ref, f32[5]{0:T(128)} %comp_ref.1, s32[2,512]{1,0:T(2,128)} %station_source.1, f32[5,512]{1,0:T(8,128)} %observed_source.1, s32[8,512]{1,0:T(8,128)} %counts_source.1, bf16[16384,256]{1,0:T(8,128)(2,1)} %constant.12.clone.source), custom_call_target="tpu_custom_call" | custom-call | flops 10000000000 | bytes 10000000 | tf_op jit(solution)/shard_map/solve/pallas_call | solution.py:476
  22.8 0.0 collective-permute-done.cell_ref
  22.9 0.1 collective-permute-start.1
  22.9 0.0 copy-start
  23.0 0.9 %copy-done = bf16[256,512]{1,0:T(8,128)(2,1)S(1)} copy-done((bf16[256,512]{1,0:T(8,128)(2,1)S(1)}, bf16[256,512]{1,0:T(8,128)(2,1)}, u32[]{:S(2)}) %copy-start) | copy-done | bytes 262168
  23.9 1.3 %pick.3 = (bf16[2,4096]{1,0:T(2,128)(2,1)S(1)}, bf16[256,512]{1,0:T(8,128)(2,1)S(1)}) custom-call(s32[3,4096]{1,0:T(4,128)S(1)} %collective-permute-done.cell_ref, bf16[256,512]{1,0:T(8,128)(2,1)S(1)} %copy-done), custom_call_target="tpu_custom_call" | custom-call | flops 1073741824 | bytes 1000000 | tf_op jit(solution)/shard_map/pick/pallas_call | solution.py:553
  25.2 0.0 collective-permute-done.1.refs_0_.refs_1_
  25.2 1.3 %pick.4 = bf16[4,4096]{1,0:T(4,128)(2,1)S(1)} custom-call(s32[3,4096]{1,0:T(4,128)S(1)} %collective-permute-done.cell_ref, bf16[256,512]{1,0:T(8,128)(2,1)S(1)} %collective-permute-done.1.refs_0_.refs_1_, bf16[2,4096]{1,0:T(2,128)(2,1)S(1)} %get-tuple-element.11.refs_1_), custom_call_target="tpu_custom_call" | custom-call | flops 1073741824 | bytes 1000000 | tf_op jit(solution)/shard_map/pick/pallas_call | solution.py:553
  26.5 0.1 collective-permute-start.2
  26.6 0.0 copy-done.1
  26.6 2.4 %pick.5 = bf16[4,4096]{1,0:T(4,128)(2,1)S(1)} custom-call(s32[3,4096]{1,0:T(4,128)S(1)} %copy-done.1, bf16[256,512]{1,0:T(8,128)(2,1)S(1)} %get-tuple-element.12.refs_0_, bf16[256,512]{1,0:T(8,128)(2,1)S(1)} %collective-permute-done.1.refs_0_.refs_1_), custom_call_target="tpu_custom_call" | custom-call | flops 2147483648 | bytes 1000000 | tf_op jit(solution)/shard_map/pick/pallas_call | solution.py:553
  29.0 1.5 %collective-permute-done.2 = bf16[4,4096]{1,0:T(4,128)(2,1)S(1)} collective-permute-done((bf16[4,4096]{1,0:T(4,128)(2,1)S(1)}, bf16[4,4096]{1,0:T(4,128)(2,1)S(1)}, u32[]{:S(2)}, u32[]{:S(2)}) %collective-permute-start.2) | collective-permute-done | bytes 32800 | tf_op jit(solution)/shard_map/ppermute | solution.py:576
  30.5 0.1 broadcast_select_fusion.11
  30.6 0.7 %maximum_convert_fusion = f32[8,4096]{1,0:T(8,128)} fusion(bf16[2,4096]{1,0:T(2,128)(2,1)S(1)} %get-tuple-element.16, bf16[2,4096]{1,0:T(2,128)(2,1)S(1)} %get-tuple-element.15, bf16[2,4096]{1,0:T(2,128)(2,1)S(1)} %get-tuple-element.14, bf16[2,4096]{1,0:T(2,128)(2,1)S(1)} %get-tuple-element.13), kind=kLoop, calls=%fused_computation | loop fusion | flops 262144 | bytes 196608 | tf_op jit(solution)/shard_map/concatenate | solution.py:600
Async XLA Ops:
  0.0 22.8 %collective-permute-start = (s32[3,4096]{1,0:T(4,128)}, s32[3,4096]{1,0:T(4,128)S(1)}, u32[]{:S(2)}, u32[]{:S(2)}) collective-permute-start(s32[3,4096]{1,0:T(4,128)} %cell_ref.1), channel_id=1, source_target_pairs={{0,2},{1,3},{2,0},{3,1},{4,6},{5,7},{6,4},{7,5},{8,10},{9,11},{10,... | collective-permute-start | bytes 147464 | tf_op jit(solution)/shard_map/ppermute | solution.py:576
  3.0 23.6 %copy-start.1 = (s32[3,4096]{1,0:T(4,128)S(1)}, s32[3,4096]{1,0:T(4,128)}, u32[]{:S(2)}) copy-start(s32[3,4096]{1,0:T(4,128)} %cell_ref.1) | copy-start | bytes 147460
  22.9 2.4 %collective-permute-start.1 = (bf16[256,512]{1,0:T(8,128)(2,1)}, bf16[256,512]{1,0:T(8,128)(2,1)S(1)}, u32[]{:S(2)}, u32[]{:S(2)}) collective-permute-start(bf16[256,512]{1,0:T(8,128)(2,1)} %solve.1.refs_0_), channel_id=1, source_target_pairs={{0,1},{1,0},{2,3},{3,2},{4,5},{5,4},{6,7},{7,6},{8,9},{9,8},{10,11... | collective-permute-start | bytes 786440 | tf_op jit(solution)/shard_map/ppermute | solution.py:576
  22.9 1.0 %copy-start = (bf16[256,512]{1,0:T(8,128)(2,1)S(1)}, bf16[256,512]{1,0:T(8,128)(2,1)}, u32[]{:S(2)}) copy-start(bf16[256,512]{1,0:T(8,128)(2,1)} %solve.1.refs_0_) | copy-start | bytes 786436
  26.5 4.0 %collective-permute-start.2 = (bf16[4,4096]{1,0:T(4,128)(2,1)S(1)}, bf16[4,4096]{1,0:T(4,128)(2,1)S(1)}, u32[]{:S(2)}, u32[]{:S(2)}) collective-permute-start(bf16[4,4096]{1,0:T(4,128)(2,1)S(1)} %pick.4), channel_id=1, source_target_pairs={{0,2},{1,3},{2,0},{3,1},{4,6},{5,7},{6,4},{7,5},{8,10},{9,11},{10,... | collective-permute-start | bytes 98312 | tf_op jit(solution)/shard_map/ppermute | solution.py:576

commit v21 on v19

--- a/solution.py
+++ b/solution.py
@@ -16,7 +16,7 @@
 LANES = 128
 TEAM = 4
 PARTS = 2
-CHUNK = 2048
+CHUNK = 4096
 ROWS = 32
 
 station_height = 2.0
@@ -173,7 +173,6 @@
     pick_y,
     weights,
     data,
-    pred,
     image,
     values,
     rows,
@@ -308,9 +307,9 @@
             along_x = [along_x[:, lane : lane + 2 * LANES] for lane in range(0, share_lanes, 2 * LANES)]
             receive(share, dot(jnp.concatenate(along_x, axis=0), held("field_yt", LANES)))
 
-    def predict():
+    def predict(field):
         for share in shares:
-            r = residual[share.start : share.stop].reshape(len(share) * GRID, LANES).astype(BF)
+            r = field[share.start : share.stop].reshape(len(share) * GRID, LANES).astype(BF)
             y = dot(jnp.concatenate([r, r], axis=1), held("field_y2")).astype(BF)
             y = jnp.concatenate([y[i * GRID : (i + 1) * GRID] for i in range(len(share))], axis=1)
             lane = share.start * 2 * LANES
@@ -372,71 +371,75 @@
         return ratio * ratio * ratio
 
     def round_of(outer, inner, carry):
-        first = outer == 0 and inner == 0
         last = outer == IRLS - 1 and inner == CG_STEPS - 1
         fresh = inner == 0
         old_norm, old_step, old_curve = carry
         sums = [no_sum] * 3
 
-        def penalty_at(slab, at):
-            if outer == 0:
-                return damping * depth_weight(slab) / (focusing * focusing)
-            return penalty[slab, at]
-
         def receive(share, applied):
             norm, bend, cross = sums
-            for slab, at in pieces(share):
-                row = (slab - share.start) * GRID + at.start
-                r = applied[row : row + ROWS]
-                if fresh and outer:
-                    m = models[slab, at]
-                    p = damping * depth_weight(slab) / (m * m + focusing * focusing)
-                    penalty[slab, at] = p
-                    r = r - p * m
-                else:
-                    p = penalty_at(slab, at)
-                if not fresh:
-                    pd = p * direction[slab, at]
-                    r = residual[slab, at] - old_step * (r + pd)
-                    cross += fold(pd * r)
-                residual[slab, at] = r
-                square = r * r
-                norm += fold(square)
-                bend += fold(p * square)
+            for slab in share:
+                if outer == 0:
+                    p = damping * depth_weight(slab) / (focusing * focusing)
+                squares = products = no_sum
+                for at in (slice(row, row + ROWS) for row in range(0, GRID, ROWS)):
+                    row = (slab - share.start) * GRID + at.start
+                    r = applied[row : row + ROWS]
+                    if fresh and outer:
+                        m = models[slab, at]
+                        p = damping * depth_weight(slab) / (m * m + focusing * focusing)
+                        penalty[slab, at] = p
+                        r = r - p * m
+                    elif outer:
+                        p = penalty[slab, at]
+                    if fresh:
+                        direction[slab, at] = r
+                    else:
+                        d = direction[slab, at]
+                        pd = p * d
+                        r = d - old_step * (r + pd)
+                        residual[slab, at] = r
+                        if outer:
+                            cross += fold(pd * r)
+                        else:
+                            products += fold(d * r)
+                    square = r * r
+                    squares += fold(square)
+                    if outer:
+                        bend += fold(p * square)
+                norm += squares
+                if outer == 0:
+                    bend += p * squares
+                    cross += p * products
             sums[:] = [norm, bend, cross]
 
         back_project(receive)
-        here = predict()
+        here = predict(direction if fresh else residual)
         weighted = weights[...] * here
         norm, bend, cross = sums
         if fresh:
             norm, curve = totals_of([norm, bend + fold(weighted * here)])
-        else:
-            norm, bend, cross = totals_of(
-                [norm, bend + fold(weighted * here), cross + fold(weighted * image[...])]
-            )
-            ratio = norm / old_norm
-            curve = bend + ratio * (2.0 * cross + ratio * old_curve)
+            step = norm / curve
+            image[...] = here
+            values[...] = weighted.astype(BF)
+            station_spectra()
+            return norm, step, curve
+        norm, bend, cross = totals_of(
+            [norm, bend + fold(weighted * here), cross + fold(weighted * image[...])]
+        )
+        ratio = norm / old_norm
+        curve = bend + ratio * (2.0 * cross + ratio * old_curve)
         step = norm / curve
+        along = old_step + step * ratio
         if not last:
-            if not fresh:
-                here = here + ratio * image[...]
-            now = step * here if first else pred[...] + step * here
-            pred[...] = now
-            if fresh:
-                image[...] = here
-                values[...] = (weights[...] * here).astype(BF)
-            else:
-                values[...] = (weights[...] * (data[...] - now)).astype(BF)
+            left = data[...] - (along * image[...] + step * here)
+            data[...] = left
+            values[...] = (weights[...] * left).astype(BF)
             station_spectra()
         for share in shares:
             for slab, at in pieces(share):
-                d = residual[slab, at]
-                if not fresh:
-                    d = d + ratio * direction[slab, at]
-                if fresh:
-                    direction[slab, at] = d
-                models[slab, at] = step * d if first else models[slab, at] + step * d
+                move = along * direction[slab, at] + step * residual[slab, at]
+                models[slab, at] = models[slab, at] + move if outer else move
         return norm, step, curve
 
     station_spectra()
@@ -493,7 +496,6 @@
             at_stations,
             at_stations,
             at_stations,
-            at_stations,
             vmem((stations, LANES), BF),
             vmem((LANES, stations), F32),
             vmem((5, DEPTHS, GRID, LANES), F32),

time: 31.3 us -> 30.9 us (0.987)
  Pallas kernels: 24.8 us -> 24.2 us
    pallas_call x3, Pallas kernels: 5.53 us -> 4.98 us  [pick(): pl.pallas_call(functools.partial(pick_kernel, grid_y, len(models), len(be...]
where the time goes in v21:
time: 30.9 us; the launch traced here: 30.7 us
  Pallas kernels  24.2 us (78%)
  starting transfers between devices  3.11 us (10%)
  waiting for transfers between devices  1.51 us (5%)
  local copies, waits for them, and re-layouts  0.95 us (3%)
  other arithmetic  0.83 us (3%)
    pallas_call x1, Pallas kernels, solve(): pl.pallas_call(functools.partial(solve_kernel, grid_y, boots, mine // boo...  19.3 us
    pallas_call x3, Pallas kernels, pick(): pl.pallas_call(functools.partial(pick_kernel, grid_y, len(models), len(be...  4.98 us
    ppermute x3, starting transfers between devices, swap(): return lax.ppermute(a, 'wide', [(i, i ^ k) for i in range(wide)])  3.11 us
    ppermute x3, waiting for transfers between devices, swap(): return lax.ppermute(a, 'wide', [(i, i ^ k) for i in range(wide)])  1.51 us
    unnamed x4, local copies, waits for them, and re-layouts  0.95 us
    concatenate x1, other arithmetic, local(): return jnp.concatenate(blocks, axis=0)  0.73 us
  transfers between devices with their start and end apart: 3, of which 1 were waited for; matrix products, arithmetic and copies ran while one was open for 0% of the time, Pallas kernels for 75%

profile of v21, /device:TPU:0, one launch (start us, length us, event | category | flops | bytes accessed | tf_op | source)
XLA Modules:
  0.0 30.7 jit_solution(3625657095778400359)
XLA Ops:
  0.0 3.0 %collective-permute-start = (s32[3,4096]{1,0:T(4,128)}, s32[3,4096]{1,0:T(4,128)S(1)}, u32[]{:S(2)}, u32[]{:S(2)}) collective-permute-start(s32[3,4096]{1,0:T(4,128)} %cell_ref.1), channel_id=1, source_target_pairs={{0,2},{1,3},{2,0},{3,1},{4,6},{5,7},{6,4},{7,5},{8,10},{9,11},{10,... | collective-permute-start | bytes 147464 | tf_op jit(solution)/shard_map/ppermute | solution.py:583
  3.0 0.0 copy-start.1
  3.0 19.3 %solve.1.refs_0_ = bf16[256,512]{1,0:T(8,128)(2,1)} custom-call(s32[1]{0:T(128)} %bitcast.slot_ref, f32[5]{0:T(128)} %comp_ref.1, s32[2,512]{1,0:T(2,128)} %station_source.1, f32[5,512]{1,0:T(8,128)} %observed_source.1, s32[8,512]{1,0:T(8,128)} %counts_source.1, bf16[16384,256]{1,0:T(8,128)(2,1)} %constant.12.clone.source), custom_call_target="tpu_custom_call" | custom-call | flops 10000000000 | bytes 10000000 | tf_op jit(solution)/shard_map/solve/pallas_call | solution.py:483
  22.2 0.0 collective-permute-done.cell_ref
  22.2 0.1 collective-permute-start.1
  22.3 0.0 copy-start
  22.3 0.9 %copy-done = bf16[256,512]{1,0:T(8,128)(2,1)S(1)} copy-done((bf16[256,512]{1,0:T(8,128)(2,1)S(1)}, bf16[256,512]{1,0:T(8,128)(2,1)}, u32[]{:S(2)}) %copy-start) | copy-done | bytes 262168
  23.3 1.3 %pick.3 = (bf16[2,4096]{1,0:T(2,128)(2,1)S(1)}, bf16[256,512]{1,0:T(8,128)(2,1)S(1)}) custom-call(s32[3,4096]{1,0:T(4,128)S(1)} %collective-permute-done.cell_ref, bf16[256,512]{1,0:T(8,128)(2,1)S(1)} %copy-done), custom_call_target="tpu_custom_call" | custom-call | flops 1073741824 | bytes 1000000 | tf_op jit(solution)/shard_map/pick/pallas_call | solution.py:560
  24.6 0.0 collective-permute-done.1.refs_0_.refs_1_
  24.6 1.3 %pick.4 = bf16[4,4096]{1,0:T(4,128)(2,1)S(1)} custom-call(s32[3,4096]{1,0:T(4,128)S(1)} %collective-permute-done.cell_ref, bf16[256,512]{1,0:T(8,128)(2,1)S(1)} %collective-permute-done.1.refs_0_.refs_1_, bf16[2,4096]{1,0:T(2,128)(2,1)S(1)} %get-tuple-element.11.refs_1_), custom_call_target="tpu_custom_call" | custom-call | flops 1073741824 | bytes 1000000 | tf_op jit(solution)/shard_map/pick/pallas_call | solution.py:560
  25.9 0.1 collective-permute-start.2
  26.0 0.0 copy-done.1
  26.0 2.4 %pick.5 = bf16[4,4096]{1,0:T(4,128)(2,1)S(1)} custom-call(s32[3,4096]{1,0:T(4,128)S(1)} %copy-done.1, bf16[256,512]{1,0:T(8,128)(2,1)S(1)} %get-tuple-element.12.refs_0_, bf16[256,512]{1,0:T(8,128)(2,1)S(1)} %collective-permute-done.1.refs_0_.refs_1_), custom_call_target="tpu_custom_call" | custom-call | flops 2147483648 | bytes 1000000 | tf_op jit(solution)/shard_map/pick/pallas_call | solution.py:560
  28.4 1.5 %collective-permute-done.2 = bf16[4,4096]{1,0:T(4,128)(2,1)S(1)} collective-permute-done((bf16[4,4096]{1,0:T(4,128)(2,1)S(1)}, bf16[4,4096]{1,0:T(4,128)(2,1)S(1)}, u32[]{:S(2)}, u32[]{:S(2)}) %collective-permute-start.2) | collective-permute-done | bytes 32800 | tf_op jit(solution)/shard_map/ppermute | solution.py:583
  29.9 0.1 broadcast_select_fusion.11
  30.0 0.7 %maximum_convert_fusion = f32[8,4096]{1,0:T(8,128)} fusion(bf16[2,4096]{1,0:T(2,128)(2,1)S(1)} %get-tuple-element.16, bf16[2,4096]{1,0:T(2,128)(2,1)S(1)} %get-tuple-element.15, bf16[2,4096]{1,0:T(2,128)(2,1)S(1)} %get-tuple-element.14, bf16[2,4096]{1,0:T(2,128)(2,1)S(1)} %get-tuple-element.13), kind=kLoop, calls=%fused_computation | loop fusion | flops 262144 | bytes 196608 | tf_op jit(solution)/shard_map/concatenate | solution.py:607
Async XLA Ops:
  0.0 22.2 %collective-permute-start = (s32[3,4096]{1,0:T(4,128)}, s32[3,4096]{1,0:T(4,128)S(1)}, u32[]{:S(2)}, u32[]{:S(2)}) collective-permute-start(s32[3,4096]{1,0:T(4,128)} %cell_ref.1), channel_id=1, source_target_pairs={{0,2},{1,3},{2,0},{3,1},{4,6},{5,7},{6,4},{7,5},{8,10},{9,11},{10,... | collective-permute-start | bytes 147464 | tf_op jit(solution)/shard_map/ppermute | solution.py:583
  3.0 23.0 %copy-start.1 = (s32[3,4096]{1,0:T(4,128)S(1)}, s32[3,4096]{1,0:T(4,128)}, u32[]{:S(2)}) copy-start(s32[3,4096]{1,0:T(4,128)} %cell_ref.1) | copy-start | bytes 147460
  22.2 2.4 %collective-permute-start.1 = (bf16[256,512]{1,0:T(8,128)(2,1)}, bf16[256,512]{1,0:T(8,128)(2,1)S(1)}, u32[]{:S(2)}, u32[]{:S(2)}) collective-permute-start(bf16[256,512]{1,0:T(8,128)(2,1)} %solve.1.refs_0_), channel_id=1, source_target_pairs={{0,1},{1,0},{2,3},{3,2},{4,5},{5,4},{6,7},{7,6},{8,9},{9,8},{10,11... | collective-permute-start | bytes 786440 | tf_op jit(solution)/shard_map/ppermute | solution.py:583
  22.3 1.0 %copy-start = (bf16[256,512]{1,0:T(8,128)(2,1)S(1)}, bf16[256,512]{1,0:T(8,128)(2,1)}, u32[]{:S(2)}) copy-start(bf16[256,512]{1,0:T(8,128)(2,1)} %solve.1.refs_0_) | copy-start | bytes 786436
  25.9 4.0 %collective-permute-start.2 = (bf16[4,4096]{1,0:T(4,128)(2,1)S(1)}, bf16[4,4096]{1,0:T(4,128)(2,1)S(1)}, u32[]{:S(2)}, u32[]{:S(2)}) collective-permute-start(bf16[4,4096]{1,0:T(4,128)(2,1)S(1)} %pick.4), channel_id=1, source_target_pairs={{0,2},{1,3},{2,0},{3,1},{4,6},{5,7},{6,4},{7,5},{8,10},{9,11},{10,... | collective-permute-start | bytes 98312 | tf_op jit(solution)/shard_map/ppermute | solution.py:583

commit v22 on v21

--- a/solution.py
+++ b/solution.py
@@ -15,7 +15,7 @@
 DEPTHS = 16
 LANES = 128
 TEAM = 4
-PARTS = 2
+PARTS = 1
 CHUNK = 4096
 ROWS = 32
 
@@ -319,14 +319,20 @@
                 at = [slice(hx * GRID + row, hx * GRID + row + 16) for hx in range(2)]
                 for chunk in chunks:
                     total = [[None] * 2 for _ in range(5)]
-                    for z in range(share.start * deep, share.stop * deep):
-                        lane = z * wide + chunk * LANES
-                        f = [spec_f[at[hx], lane : lane + LANES] for hx in range(2)]
-                        for c, (odd_x, _) in enumerate(PARITY):
-                            t = table(c, z, at[0])
+                    for eight in range(share.start * deep, share.stop * deep, 8):
+                        some = [[None] * 2 for _ in range(5)]
+                        for z in range(eight, eight + 8):
+                            lane = z * wide + chunk * LANES
+                            f = [spec_f[at[hx], lane : lane + LANES] for hx in range(2)]
+                            for c, (odd_x, _) in enumerate(PARITY):
+                                t = table(c, z, at[0])
+                                for hx in range(2):
+                                    term = t * f[hx ^ odd_x]
+                                    some[c][hx] = term if z == eight else some[c][hx] + term
+                        for c in range(5):
                             for hx in range(2):
-                                term = t * f[hx ^ odd_x]
-                                total[c][hx] = term if total[c][hx] is None else total[c][hx] + term
+                                old = total[c][hx]
+                                total[c][hx] = some[c][hx] if old is None else old + some[c][hx]
                     for c, (odd_x, _) in enumerate(PARITY):
                         lane = c * wide + chunk * LANES
                         for hx in range(2):

time: 30.9 us -> 30.6 us (level)
    pallas_call x1, Pallas kernels: 19.3 us -> 18.9 us  [solve(): pl.pallas_call(functools.partial(solve_kernel, grid_y, boots, mine // boo...]
  transfers between devices with their start and end apart: 3 -> 3, of which waited for: 1 -> 1; matrix products, arithmetic and copies ran while one was open for 0% -> 0% of each run, Pallas kernels for 75% -> 74%
where the time goes in v22:
time: 30.6 us; the launch traced here: 30.4 us
  Pallas kernels  23.9 us (78%)
  starting transfers between devices  3.11 us (10%)
  waiting for transfers between devices  1.51 us (5%)
  local copies, waits for them, and re-layouts  0.95 us (3%)
  other arithmetic  0.83 us (3%)
    pallas_call x1, Pallas kernels, solve(): pl.pallas_call(functools.partial(solve_kernel, grid_y, boots, mine // boo...  18.9 us
    pallas_call x3, Pallas kernels, pick(): pl.pallas_call(functools.partial(pick_kernel, grid_y, len(models), len(be...  4.98 us
    ppermute x3, starting transfers between devices, swap(): return lax.ppermute(a, 'wide', [(i, i ^ k) for i in range(wide)])  3.11 us
    ppermute x3, waiting for transfers between devices, swap(): return lax.ppermute(a, 'wide', [(i, i ^ k) for i in range(wide)])  1.51 us
    unnamed x4, local copies, waits for them, and re-layouts  0.95 us
    concatenate x1, other arithmetic, local(): return jnp.concatenate(blocks, axis=0)  0.73 us
  transfers between devices with their start and end apart: 3, of which 1 were waited for; matrix products, arithmetic and copies ran while one was open for 0% of the time, Pallas kernels for 74%

profile of v22, /device:TPU:0, one launch (start us, length us, event | category | flops | bytes accessed | tf_op | source)
XLA Modules:
  0.0 30.4 jit_solution(18078949557991823804)
XLA Ops:
  0.0 3.0 %collective-permute-start = (s32[3,4096]{1,0:T(4,128)}, s32[3,4096]{1,0:T(4,128)S(1)}, u32[]{:S(2)}, u32[]{:S(2)}) collective-permute-start(s32[3,4096]{1,0:T(4,128)} %cell_ref.1), channel_id=1, source_target_pairs={{0,2},{1,3},{2,0},{3,1},{4,6},{5,7},{6,4},{7,5},{8,10},{9,11},{10,... | collective-permute-start | bytes 147464 | tf_op jit(solution)/shard_map/ppermute | solution.py:589
  3.0 0.0 copy-start.1
  3.0 18.9 %solve.1.refs_0_ = bf16[256,512]{1,0:T(8,128)(2,1)} custom-call(s32[1]{0:T(128)} %bitcast.slot_ref, f32[5]{0:T(128)} %comp_ref.1, s32[2,512]{1,0:T(2,128)} %station_source.1, f32[5,512]{1,0:T(8,128)} %observed_source.1, s32[8,512]{1,0:T(8,128)} %counts_source.1, bf16[16384,256]{1,0:T(8,128)(2,1)} %constant.12.clone.source), custom_call_target="tpu_custom_call" | custom-call | flops 10000000000 | bytes 10000000 | tf_op jit(solution)/shard_map/solve/pallas_call | solution.py:489
  21.9 0.0 collective-permute-done.cell_ref
  21.9 0.1 collective-permute-start.1
  22.0 0.0 copy-start
  22.0 0.9 %copy-done = bf16[256,512]{1,0:T(8,128)(2,1)S(1)} copy-done((bf16[256,512]{1,0:T(8,128)(2,1)S(1)}, bf16[256,512]{1,0:T(8,128)(2,1)}, u32[]{:S(2)}) %copy-start) | copy-done | bytes 262168
  23.0 1.3 %pick.3 = (bf16[2,4096]{1,0:T(2,128)(2,1)S(1)}, bf16[256,512]{1,0:T(8,128)(2,1)S(1)}) custom-call(s32[3,4096]{1,0:T(4,128)S(1)} %collective-permute-done.cell_ref, bf16[256,512]{1,0:T(8,128)(2,1)S(1)} %copy-done), custom_call_target="tpu_custom_call" | custom-call | flops 1073741824 | bytes 1000000 | tf_op jit(solution)/shard_map/pick/pallas_call | solution.py:566
  24.3 0.0 collective-permute-done.1.refs_0_.refs_1_
  24.3 1.3 %pick.4 = bf16[4,4096]{1,0:T(4,128)(2,1)S(1)} custom-call(s32[3,4096]{1,0:T(4,128)S(1)} %collective-permute-done.cell_ref, bf16[256,512]{1,0:T(8,128)(2,1)S(1)} %collective-permute-done.1.refs_0_.refs_1_, bf16[2,4096]{1,0:T(2,128)(2,1)S(1)} %get-tuple-element.11.refs_1_), custom_call_target="tpu_custom_call" | custom-call | flops 1073741824 | bytes 1000000 | tf_op jit(solution)/shard_map/pick/pallas_call | solution.py:566
  25.6 0.1 collective-permute-start.2
  25.6 0.0 copy-done.1
  25.7 2.4 %pick.5 = bf16[4,4096]{1,0:T(4,128)(2,1)S(1)} custom-call(s32[3,4096]{1,0:T(4,128)S(1)} %copy-done.1, bf16[256,512]{1,0:T(8,128)(2,1)S(1)} %get-tuple-element.12.refs_0_, bf16[256,512]{1,0:T(8,128)(2,1)S(1)} %collective-permute-done.1.refs_0_.refs_1_), custom_call_target="tpu_custom_call" | custom-call | flops 2147483648 | bytes 1000000 | tf_op jit(solution)/shard_map/pick/pallas_call | solution.py:566
  28.0 1.5 %collective-permute-done.2 = bf16[4,4096]{1,0:T(4,128)(2,1)S(1)} collective-permute-done((bf16[4,4096]{1,0:T(4,128)(2,1)S(1)}, bf16[4,4096]{1,0:T(4,128)(2,1)S(1)}, u32[]{:S(2)}, u32[]{:S(2)}) %collective-permute-start.2) | collective-permute-done | bytes 32800 | tf_op jit(solution)/shard_map/ppermute | solution.py:589
  29.6 0.1 broadcast_select_fusion.11
  29.7 0.7 %maximum_convert_fusion = f32[8,4096]{1,0:T(8,128)} fusion(bf16[2,4096]{1,0:T(2,128)(2,1)S(1)} %get-tuple-element.16, bf16[2,4096]{1,0:T(2,128)(2,1)S(1)} %get-tuple-element.15, bf16[2,4096]{1,0:T(2,128)(2,1)S(1)} %get-tuple-element.14, bf16[2,4096]{1,0:T(2,128)(2,1)S(1)} %get-tuple-element.13), kind=kLoop, calls=%fused_computation | loop fusion | flops 262144 | bytes 196608 | tf_op jit(solution)/shard_map/concatenate | solution.py:613
Async XLA Ops:
  0.0 21.9 %collective-permute-start = (s32[3,4096]{1,0:T(4,128)}, s32[3,4096]{1,0:T(4,128)S(1)}, u32[]{:S(2)}, u32[]{:S(2)}) collective-permute-start(s32[3,4096]{1,0:T(4,128)} %cell_ref.1), channel_id=1, source_target_pairs={{0,2},{1,3},{2,0},{3,1},{4,6},{5,7},{6,4},{7,5},{8,10},{9,11},{10,... | collective-permute-start | bytes 147464 | tf_op jit(solution)/shard_map/ppermute | solution.py:589
  3.0 22.7 %copy-start.1 = (s32[3,4096]{1,0:T(4,128)S(1)}, s32[3,4096]{1,0:T(4,128)}, u32[]{:S(2)}) copy-start(s32[3,4096]{1,0:T(4,128)} %cell_ref.1) | copy-start | bytes 147460
  21.9 2.4 %collective-permute-start.1 = (bf16[256,512]{1,0:T(8,128)(2,1)}, bf16[256,512]{1,0:T(8,128)(2,1)S(1)}, u32[]{:S(2)}, u32[]{:S(2)}) collective-permute-start(bf16[256,512]{1,0:T(8,128)(2,1)} %solve.1.refs_0_), channel_id=1, source_target_pairs={{0,1},{1,0},{2,3},{3,2},{4,5},{5,4},{6,7},{7,6},{8,9},{9,8},{10,11... | collective-permute-start | bytes 786440 | tf_op jit(solution)/shard_map/ppermute | solution.py:589
  22.0 1.0 %copy-start = (bf16[256,512]{1,0:T(8,128)(2,1)S(1)}, bf16[256,512]{1,0:T(8,128)(2,1)}, u32[]{:S(2)}) copy-start(bf16[256,512]{1,0:T(8,128)(2,1)} %solve.1.refs_0_) | copy-start | bytes 786436
  25.6 4.0 %collective-permute-start.2 = (bf16[4,4096]{1,0:T(4,128)(2,1)S(1)}, bf16[4,4096]{1,0:T(4,128)(2,1)S(1)}, u32[]{:S(2)}, u32[]{:S(2)}) collective-permute-start(bf16[4,4096]{1,0:T(4,128)(2,1)S(1)} %pick.4), channel_id=1, source_target_pairs={{0,2},{1,3},{2,0},{3,1},{4,6},{5,7},{6,4},{7,5},{8,10},{9,11},{10,... | collective-permute-start | bytes 98312 | tf_op jit(solution)/shard_map/ppermute | solution.py:589

commit v23 on v22

--- a/solution.py
+++ b/solution.py
@@ -17,7 +17,7 @@
 TEAM = 4
 PARTS = 1
 CHUNK = 4096
-ROWS = 32
+ROWS = 64
 
 station_height = 2.0
 focusing = 0.1

time: 30.6 us -> 30.5 us (level)
  no operation moved by 1% of the time
where the time goes in v23:
time: 30.5 us; the launch traced here: 30.4 us
  Pallas kernels  23.9 us (78%)
  starting transfers between devices  3.11 us (10%)
  waiting for transfers between devices  1.51 us (5%)
  local copies, waits for them, and re-layouts  0.95 us (3%)
  other arithmetic  0.83 us (3%)
    pallas_call x1, Pallas kernels, solve(): pl.pallas_call(functools.partial(solve_kernel, grid_y, boots, mine // boo...  18.9 us
    pallas_call x3, Pallas kernels, pick(): pl.pallas_call(functools.partial(pick_kernel, grid_y, len(models), len(be...  4.97 us
    ppermute x3, starting transfers between devices, swap(): return lax.ppermute(a, 'wide', [(i, i ^ k) for i in range(wide)])  3.11 us
    ppermute x3, waiting for transfers between devices, swap(): return lax.ppermute(a, 'wide', [(i, i ^ k) for i in range(wide)])  1.51 us
    unnamed x4, local copies, waits for them, and re-layouts  0.95 us
    concatenate x1, other arithmetic, local(): return jnp.concatenate(blocks, axis=0)  0.73 us
  transfers between devices with their start and end apart: 3, of which 1 were waited for; matrix products, arithmetic and copies ran while one was open for 0% of the time, Pallas kernels for 74%

profile of v23, /device:TPU:0, one launch (start us, length us, event | category | flops | bytes accessed | tf_op | source)
XLA Modules:
  0.0 30.4 jit_solution(16584651088212927415)
XLA Ops:
  0.0 3.0 %collective-permute-start = (s32[3,4096]{1,0:T(4,128)}, s32[3,4096]{1,0:T(4,128)S(1)}, u32[]{:S(2)}, u32[]{:S(2)}) collective-permute-start(s32[3,4096]{1,0:T(4,128)} %cell_ref.1), channel_id=1, source_target_pairs={{0,2},{1,3},{2,0},{3,1},{4,6},{5,7},{6,4},{7,5},{8,10},{9,11},{10,... | collective-permute-start | bytes 147464 | tf_op jit(solution)/shard_map/ppermute | solution.py:589
  3.0 0.0 copy-start.1
  3.0 18.9 %solve.1.refs_0_ = bf16[256,512]{1,0:T(8,128)(2,1)} custom-call(s32[1]{0:T(128)} %bitcast.slot_ref, f32[5]{0:T(128)} %comp_ref.1, s32[2,512]{1,0:T(2,128)} %station_source.1, f32[5,512]{1,0:T(8,128)} %observed_source.1, s32[8,512]{1,0:T(8,128)} %counts_source.1, bf16[16384,256]{1,0:T(8,128)(2,1)} %constant.12.clone.source), custom_call_target="tpu_custom_call" | custom-call | flops 10000000000 | bytes 10000000 | tf_op jit(solution)/shard_map/solve/pallas_call | solution.py:489
  21.9 0.0 collective-permute-done.cell_ref
  21.9 0.1 collective-permute-start.1
  22.0 0.0 copy-start
  22.0 0.9 %copy-done = bf16[256,512]{1,0:T(8,128)(2,1)S(1)} copy-done((bf16[256,512]{1,0:T(8,128)(2,1)S(1)}, bf16[256,512]{1,0:T(8,128)(2,1)}, u32[]{:S(2)}) %copy-start) | copy-done | bytes 262168
  22.9 1.3 %pick.3 = (bf16[2,4096]{1,0:T(2,128)(2,1)S(1)}, bf16[256,512]{1,0:T(8,128)(2,1)S(1)}) custom-call(s32[3,4096]{1,0:T(4,128)S(1)} %collective-permute-done.cell_ref, bf16[256,512]{1,0:T(8,128)(2,1)S(1)} %copy-done), custom_call_target="tpu_custom_call" | custom-call | flops 1073741824 | bytes 1000000 | tf_op jit(solution)/shard_map/pick/pallas_call | solution.py:566
  24.2 0.0 collective-permute-done.1.refs_0_.refs_1_
  24.2 1.3 %pick.4 = bf16[4,4096]{1,0:T(4,128)(2,1)S(1)} custom-call(s32[3,4096]{1,0:T(4,128)S(1)} %collective-permute-done.cell_ref, bf16[256,512]{1,0:T(8,128)(2,1)S(1)} %collective-permute-done.1.refs_0_.refs_1_, bf16[2,4096]{1,0:T(2,128)(2,1)S(1)} %get-tuple-element.11.refs_1_), custom_call_target="tpu_custom_call" | custom-call | flops 1073741824 | bytes 1000000 | tf_op jit(solution)/shard_map/pick/pallas_call | solution.py:566
  25.5 0.1 collective-permute-start.2
  25.6 0.0 copy-done.1
  25.6 2.4 %pick.5 = bf16[4,4096]{1,0:T(4,128)(2,1)S(1)} custom-call(s32[3,4096]{1,0:T(4,128)S(1)} %copy-done.1, bf16[256,512]{1,0:T(8,128)(2,1)S(1)} %get-tuple-element.12.refs_0_, bf16[256,512]{1,0:T(8,128)(2,1)S(1)} %collective-permute-done.1.refs_0_.refs_1_), custom_call_target="tpu_custom_call" | custom-call | flops 2147483648 | bytes 1000000 | tf_op jit(solution)/shard_map/pick/pallas_call | solution.py:566
  28.0 1.5 %collective-permute-done.2 = bf16[4,4096]{1,0:T(4,128)(2,1)S(1)} collective-permute-done((bf16[4,4096]{1,0:T(4,128)(2,1)S(1)}, bf16[4,4096]{1,0:T(4,128)(2,1)S(1)}, u32[]{:S(2)}, u32[]{:S(2)}) %collective-permute-start.2) | collective-permute-done | bytes 32800 | tf_op jit(solution)/shard_map/ppermute | solution.py:589
  29.5 0.1 broadcast_select_fusion.11
  29.6 0.7 %maximum_convert_fusion = f32[8,4096]{1,0:T(8,128)} fusion(bf16[2,4096]{1,0:T(2,128)(2,1)S(1)} %get-tuple-element.16, bf16[2,4096]{1,0:T(2,128)(2,1)S(1)} %get-tuple-element.15, bf16[2,4096]{1,0:T(2,128)(2,1)S(1)} %get-tuple-element.14, bf16[2,4096]{1,0:T(2,128)(2,1)S(1)} %get-tuple-element.13), kind=kLoop, calls=%fused_computation | loop fusion | flops 262144 | bytes 196608 | tf_op jit(solution)/shard_map/concatenate | solution.py:613
Async XLA Ops:
  0.0 21.9 %collective-permute-start = (s32[3,4096]{1,0:T(4,128)}, s32[3,4096]{1,0:T(4,128)S(1)}, u32[]{:S(2)}, u32[]{:S(2)}) collective-permute-start(s32[3,4096]{1,0:T(4,128)} %cell_ref.1), channel_id=1, source_target_pairs={{0,2},{1,3},{2,0},{3,1},{4,6},{5,7},{6,4},{7,5},{8,10},{9,11},{10,... | collective-permute-start | bytes 147464 | tf_op jit(solution)/shard_map/ppermute | solution.py:589
  3.0 22.7 %copy-start.1 = (s32[3,4096]{1,0:T(4,128)S(1)}, s32[3,4096]{1,0:T(4,128)}, u32[]{:S(2)}) copy-start(s32[3,4096]{1,0:T(4,128)} %cell_ref.1) | copy-start | bytes 147460
  21.9 2.3 %collective-permute-start.1 = (bf16[256,512]{1,0:T(8,128)(2,1)}, bf16[256,512]{1,0:T(8,128)(2,1)S(1)}, u32[]{:S(2)}, u32[]{:S(2)}) collective-permute-start(bf16[256,512]{1,0:T(8,128)(2,1)} %solve.1.refs_0_), channel_id=1, source_target_pairs={{0,1},{1,0},{2,3},{3,2},{4,5},{5,4},{6,7},{7,6},{8,9},{9,8},{10,11... | collective-permute-start | bytes 786440 | tf_op jit(solution)/shard_map/ppermute | solution.py:589
  22.0 1.0 %copy-start = (bf16[256,512]{1,0:T(8,128)(2,1)S(1)}, bf16[256,512]{1,0:T(8,128)(2,1)}, u32[]{:S(2)}) copy-start(bf16[256,512]{1,0:T(8,128)(2,1)} %solve.1.refs_0_) | copy-start | bytes 786436
  25.5 4.0 %collective-permute-start.2 = (bf16[4,4096]{1,0:T(4,128)(2,1)S(1)}, bf16[4,4096]{1,0:T(4,128)(2,1)S(1)}, u32[]{:S(2)}, u32[]{:S(2)}) collective-permute-start(bf16[4,4096]{1,0:T(4,128)(2,1)S(1)} %pick.4), channel_id=1, source_target_pairs={{0,2},{1,3},{2,0},{3,1},{4,6},{5,7},{6,4},{7,5},{8,10},{9,11},{10,... | collective-permute-start | bytes 98312 | tf_op jit(solution)/shard_map/ppermute | solution.py:589
